TPU v7x, 32 devices: a whole 2x2x4 slice. The times are simulated.
32 devices in a mesh: dp: 8 (over z, x), tensor: 4 (over y, core).
Axes of the slice: x: 2, y: 2, z: 4, core: 2. Of those that a mesh axis runs over, the one named last changes fastest.
Arguments:
- latents: float32 [24, 4096], P('dp', 'tensor'), may hold values from -6 to 6
- target_noise: float32 [24, 4096], P('dp', 'tensor'), may hold values from -6 to 6
- timesteps: int32 [24], P('dp'), may hold values from 1 to 999
- labels: int32 [24], P('dp'), may hold values from 0 to 1000
- step_count: int32 [], replicated, may hold values from 1 to 20
- embed_table: float32 [3640, 768], P(None, ('dp', 'tensor')), may hold values from -6 to 6
- layer_in: float32 [3, 768, 4, 1344], P(None, 'dp', 'tensor'), may hold values from -0.21875 to 0.21875
- layer_out: float32 [3, 4, 960, 768], P(None, 'tensor', 'dp'), may hold values from -0.21875 to 0.21875
- layer_ada: float32 [3, 768, 4608], P(None, 'dp', 'tensor'), may hold values from -0.21875 to 0.21875
- embed_first: float32 [3640, 768], P(None, ('dp', 'tensor')), may hold values from -0.00024 to 0.00024
- embed_second: float32 [3640, 768], P(None, ('dp', 'tensor')), may hold values from 3e-10 to 1e-08
- input_first: float32 [3, 768, 4, 1344], P(None, 'dp', 'tensor'), may hold values from -0.00024 to 0.00024
- input_second: float32 [3, 768, 4, 1344], P(None, 'dp', 'tensor'), may hold values from 3e-10 to 1e-08
- output_first: float32 [3, 4, 960, 768], P(None, 'tensor', 'dp'), may hold values from -0.00024 to 0.00024
- output_second: float32 [3, 4, 960, 768], P(None, 'tensor', 'dp'), may hold values from 3e-10 to 1e-08
- mod_first: float32 [3, 768, 4608], P(None, 'dp', 'tensor'), may hold values from -0.00024 to 0.00024
- mod_second: float32 [3, 768, 4608], P(None, 'dp', 'tensor'), may hold values from 3e-10 to 1e-08
Outputs:
- loss_value: float32 [], replicated
- grad_norm: float32 [], replicated
- embed_step: float32 [3640, 768], P(None, ('dp', 'tensor'))
- embed_first_new: float32 [3640, 768], P(None, ('dp', 'tensor'))
- embed_second_new: float32 [3640, 768], P(None, ('dp', 'tensor'))
- input_master: float32 [3, 768, 4, 1344], P(None, 'dp', 'tensor')
- input_first_new: float32 [3, 768, 4, 1344], P(None, 'dp', 'tensor')
- input_second_new: float32 [3, 768, 4, 1344], P(None, 'dp', 'tensor')
- input_copy: bfloat16 [3, 768, 4, 1344], P(None, 'dp', 'tensor')
- output_master: float32 [3, 4, 960, 768], P(None, 'tensor', 'dp')
- output_first_new: float32 [3, 4, 960, 768], P(None, 'tensor', 'dp')
- output_second_new: float32 [3, 4, 960, 768], P(None, 'tensor', 'dp')
- output_copy: bfloat16 [3, 4, 960, 768], P(None, 'tensor', 'dp')
- mod_master: float32 [3, 768, 4608], P(None, 'dp', 'tensor')
- mod_first_new: float32 [3, 768, 4608], P(None, 'dp', 'tensor')
- mod_second_new: float32 [3, 768, 4608], P(None, 'dp', 'tensor')
- mod_copy: bfloat16 [3, 768, 4608], P(None, 'dp', 'tensor')
All inputs are finite; a program needn't handle non-finite values.
Results may differ from a plain program's by a relative error of at most 0.008.
The roundings to bfloat16 on the way count: a program that leaves them out, or rounds other values in their place, can miss the bound.
Values may be sent and summed in bfloat16 or wider, within the bound.
A program may use at most 256 MiB of HBM per device.

v0:
```python
import math

import jax
import jax.numpy as jnp
from jax import lax
from jax.sharding import PartitionSpec as P

D = 768
HEADS = 12
HEAD_DIM = 64
FF = 3072
CLASSES = 1001
FREQ = 256
CHANNELS = 4
PATCH = 2
SIDE = 32
LAYERS = 3


EPS_NORM = 1e-06
LEARN_RATE = 0.01
DECAY = 0.01
BETA_ONE = 0.5
BETA_TWO = 0.5
ADAM_EPS = 1e-08
CLIP_NORM = 0.25
PRECISE = lax.Precision.HIGHEST


def dense(left_op, right_op):
    return jnp.dot(left_op, right_op, precision=PRECISE, preferred_element_type=jnp.float32)


def layer_norm(values):
    center = values - jnp.mean(values, axis=-1, keepdims=True)
    return center * lax.rsqrt(jnp.mean(center * center, axis=-1, keepdims=True) + EPS_NORM)


def modulate(values, shift_vec, scale_vec):
    return layer_norm(values) * (1.0 + scale_vec[:, None, :]) + shift_vec[:, None, :]


def gelu_tanh(values):
    return jax.nn.gelu(values, approximate=True)


def silu_slope(values):
    sigmoid_val = jax.nn.sigmoid(values)
    return sigmoid_val * (1.0 + values * (1.0 - sigmoid_val))


def time_features(step_ints):
    half_width = FREQ // 2
    frequency = jnp.exp(-math.log(10000.0) * jnp.arange(half_width, dtype=jnp.float32) / half_width)
    angles = step_ints.astype(jnp.float32)[:, None] * frequency[None, :]
    return jnp.concatenate([jnp.cos(angles), jnp.sin(angles)], axis=1)


def noise_levels(step_ints):
    base_cos = math.cos(0.008 / 1.008 * math.pi / 2)
    angles = (step_ints.astype(jnp.float32) / 1000.0 + 0.008) / 1.008 * (math.pi / 2)
    signal_level = jnp.cos(angles) ** 2 / base_cos**2
    return (jnp.sqrt(signal_level), jnp.sqrt(1.0 - signal_level))


def position_table(first_row, row_count):
    grid_side = SIDE // PATCH
    quarter = D // 4
    omegas = jnp.exp(-math.log(10000.0) * jnp.arange(quarter, dtype=jnp.float32) / quarter)
    token_index = jnp.arange(row_count * grid_side, dtype=jnp.int32)
    row_angle = (first_row + token_index // grid_side).astype(jnp.float32)[:, None] * omegas[
        None, :
    ]
    col_angle = (token_index % grid_side).astype(jnp.float32)[:, None] * omegas[None, :]
    return jnp.concatenate(
        [jnp.sin(row_angle), jnp.cos(row_angle), jnp.sin(col_angle), jnp.cos(col_angle)], axis=1
    )


def patchify(flat_pixels, row_count):
    grid_side = SIDE // PATCH
    shaped = flat_pixels.reshape(flat_pixels.shape[0], row_count, PATCH, grid_side, PATCH, CHANNELS)
    return shaped.transpose(0, 1, 3, 2, 4, 5).reshape(
        flat_pixels.shape[0], row_count * grid_side, PATCH * PATCH * CHANNELS
    )


def table_starts():
    patch_in = PATCH * PATCH * CHANNELS
    patch_start = CLASSES
    time_start = patch_start + patch_in
    second_start = time_start + FREQ
    final_start = second_start + D
    head_start = final_start + 2 * D
    vector_start = head_start + patch_in
    layer_start = vector_start + 5
    return (
        patch_start,
        time_start,
        second_start,
        final_start,
        head_start,
        vector_start,
        layer_start,
    )


def gather_tokens(values):
    return lax.all_gather(values, "tensor", axis=1, tiled=True)


def sum_tokens(values):
    return lax.psum_scatter(
        values.astype(jnp.bfloat16), "tensor", scatter_dimension=1, tiled=True
    ).astype(jnp.float32)


def adam_update(weight, first, second, grad, factor, first_fix, second_fix):
    clipped = grad * factor
    first_new = BETA_ONE * first + (1.0 - BETA_ONE) * clipped
    second_new = BETA_TWO * second + (1.0 - BETA_TWO) * clipped * clipped
    step_size = first_new / first_fix / (jnp.sqrt(second_new / second_fix) + ADAM_EPS)
    change = -LEARN_RATE * (step_size + DECAY * weight)
    master = weight + change
    return (master, first_new, second_new, master.astype(jnp.bfloat16), change)


def local(
    latents,
    target_noise,
    timesteps,
    labels,
    step_count,
    embed_table,
    layer_in,
    layer_out,
    layer_ada,
    embed_first,
    embed_second,
    input_first,
    input_second,
    output_first,
    output_second,
    mod_first,
    mod_second,
):
    tensor_size = lax.axis_size("tensor")
    tensor_rank = lax.axis_index("tensor")
    images = latents.shape[0]
    grid_side = SIDE // PATCH
    local_rows = grid_side // tensor_size
    tokens_all = grid_side * grid_side
    heads_local = HEADS // tensor_size
    group_width = heads_local * HEAD_DIM
    unit_count = FF // tensor_size
    patch_in = PATCH * PATCH * CHANNELS
    count_all = images * lax.axis_size("dp") * tokens_all * patch_in
    scale_dot = HEAD_DIM ** (-0.5)
    patch_start, time_start, second_start, final_start, head_start, vector_start, layer_start = (
        table_starts()
    )
    layer_rows = 10 + FF // D
    head_shape = (images, tokens_all, heads_local, HEAD_DIM)
    flat_shape = (images, tokens_all, group_width)
    table = lax.all_gather(embed_table.astype(jnp.bfloat16), ("dp", "tensor"), axis=1, tiled=True)
    mod_weights = lax.all_gather(layer_ada.astype(jnp.bfloat16), "dp", axis=1, tiled=True)

    def table_block(row_start, row_count):
        return table[row_start : row_start + row_count].astype(jnp.float32)

    vectors = table_block(vector_start, 5)
    time_feats = time_features(timesteps)
    onehot = (labels[:, None] == jnp.arange(CLASSES, dtype=jnp.int32)[None, :]).astype(jnp.float32)
    time_w = table_block(time_start, FREQ)
    second_w = table_block(second_start, D)
    shift_w = table_block(final_start, D)
    scale_w = table_block(final_start + D, D)
    pre_time = dense(time_feats, time_w) + vectors[1]
    hidden = jax.nn.silu(pre_time)
    pre_signal = dense(hidden, second_w) + vectors[2] + dense(onehot, table_block(0, CLASSES))
    signal = jax.nn.silu(pre_signal)
    final_shift = dense(signal, shift_w) + vectors[3]
    final_scale = dense(signal, scale_w) + vectors[4]
    signal_low = signal.astype(jnp.bfloat16)
    mod_local = jnp.einsum(
        "bd,lde->lbe", signal_low, mod_weights, preferred_element_type=jnp.float32
    )
    mod_full = lax.all_gather(mod_local.astype(jnp.bfloat16), "tensor", axis=2, tiled=True).astype(
        mod_local.dtype
    )
    pixels = patchify(latents, local_rows)
    targets = patchify(target_noise, local_rows)
    keep_coef, drop_coef = noise_levels(timesteps)
    noisy = keep_coef[:, None, None] * pixels + drop_coef[:, None, None] * targets
    residual = (
        jnp.einsum("btp,pd->btd", noisy, table_block(patch_start, patch_in), precision=PRECISE)
        + vectors[0]
        + position_table(tensor_rank * local_rows, local_rows)[None]
    )
    saved_acts = []
    for layer_idx in range(LAYERS):
        weight_in, weight_out = (
            lax.all_gather(
                layer_in[layer_idx]
                .astype(jnp.bfloat16)
                .reshape(layer_in.shape[1], layer_in.shape[3]),
                "dp",
                axis=0,
                tiled=True,
            ),
            lax.all_gather(
                layer_out[layer_idx].astype(jnp.bfloat16).reshape(layer_out.shape[2], D),
                "dp",
                axis=0,
                tiled=True,
            ),
        )
        bias_rows = table_block(layer_start + layer_idx * layer_rows, layer_rows)
        up_all = bias_rows[10:].reshape(FF)
        ada_bias = bias_rows[0:6].reshape(6 * D)
        out_bias = bias_rows[6]
        down_bias = bias_rows[7]
        query_bias = lax.dynamic_slice_in_dim(bias_rows[8], tensor_rank * group_width, group_width)
        value_bias = lax.dynamic_slice_in_dim(bias_rows[9], tensor_rank * group_width, group_width)
        up_bias = lax.dynamic_slice_in_dim(up_all, tensor_rank * unit_count, unit_count)
        modulation = mod_full[layer_idx] + ada_bias
        shift_a, scale_a, gate_a, shift_m, scale_m, gate_m = [
            modulation[:, piece_idx * D : (piece_idx + 1) * D] for piece_idx in range(6)
        ]
        w_qkv = weight_in[:, : 3 * group_width]
        w_up = weight_in[:, 3 * group_width :]
        w_attn = weight_out[:group_width]
        w_down = weight_out[group_width:]
        normed_a, norm_pull_a = jax.vjp(modulate, residual, shift_a, scale_a)
        rows_a = gather_tokens(normed_a.astype(jnp.bfloat16))
        projected = jnp.einsum("btd,de->bte", rows_a, w_qkv, preferred_element_type=jnp.float32)
        queries = (
            (projected[..., :group_width] + query_bias).astype(jnp.bfloat16).reshape(head_shape)
        )
        keys_low = (
            projected[..., group_width : 2 * group_width].astype(jnp.bfloat16).reshape(head_shape)
        )
        values_low = (
            (projected[..., 2 * group_width :] + value_bias)
            .astype(jnp.bfloat16)
            .reshape(head_shape)
        )
        scores = (
            jnp.einsum("bqhd,bkhd->bhqk", queries, keys_low, preferred_element_type=jnp.float32)
            * scale_dot
        )
        row_max = jnp.max(scores, axis=-1, keepdims=True)
        exponent = jnp.exp(scores - row_max)
        row_total = jnp.sum(exponent, axis=-1, keepdims=True)
        log_total = row_max + jnp.log(row_total)
        probs_low = (exponent / row_total).astype(jnp.bfloat16)
        mixed_out = (
            jnp.einsum("bhqk,bkhd->bqhd", probs_low, values_low, preferred_element_type=jnp.float32)
            .astype(jnp.bfloat16)
            .reshape(flat_shape)
        )
        branch = (
            sum_tokens(
                jnp.einsum("bte,ed->btd", mixed_out, w_attn, preferred_element_type=jnp.float32)
            )
            + out_bias
        )
        residual_mid = residual + gate_a[:, None, :] * branch
        normed_m, norm_pull_m = jax.vjp(modulate, residual_mid, shift_m, scale_m)
        rows_m = gather_tokens(normed_m.astype(jnp.bfloat16))
        upper_pre = (
            jnp.einsum("btd,df->btf", rows_m, w_up, preferred_element_type=jnp.float32) + up_bias
        )
        activated, gelu_pull = jax.vjp(gelu_tanh, upper_pre)
        act_low = activated.astype(jnp.bfloat16)
        down_out = (
            sum_tokens(
                jnp.einsum("btf,fd->btd", act_low, w_down, preferred_element_type=jnp.float32)
            )
            + down_bias
        )
        residual = residual_mid + gate_m[:, None, :] * down_out
        saved_acts.append(
            (
                norm_pull_a,
                rows_a,
                queries,
                keys_low,
                values_low,
                log_total,
                mixed_out,
                branch,
                gate_a,
                norm_pull_m,
                rows_m,
                gelu_pull,
                act_low,
                down_out,
                gate_m,
            )
        )
    final_in, final_norm_pull = jax.vjp(modulate, residual, final_shift, final_scale)
    head_w = table_block(head_start, patch_in)
    predicted = jnp.einsum("btd,pd->btp", final_in, head_w, precision=PRECISE)
    error_all = predicted - targets
    loss_part = jnp.sum(error_all * error_all) / count_all
    loss_value = lax.psum(loss_part, ("dp", "tensor"))
    d_pred = 2.0 * error_all / count_all
    d_head = jnp.einsum("btp,btd->pd", d_pred, final_in, precision=PRECISE)
    d_final = jnp.einsum("btp,pd->btd", d_pred, head_w, precision=PRECISE)
    d_residual, d_final_shift, d_final_scale = final_norm_pull(d_final)
    d_signal = jnp.zeros((images, D), jnp.float32)
    grads_in = []
    grads_out = []
    grads_mod = []
    bias_blocks = []
    for layer_idx in reversed(range(LAYERS)):
        weight_in, weight_out = (
            lax.all_gather(
                layer_in[layer_idx]
                .astype(jnp.bfloat16)
                .reshape(layer_in.shape[1], layer_in.shape[3]),
                "dp",
                axis=0,
                tiled=True,
            ),
            lax.all_gather(
                layer_out[layer_idx].astype(jnp.bfloat16).reshape(layer_out.shape[2], D),
                "dp",
                axis=0,
                tiled=True,
            ),
        )
        (
            norm_pull_a,
            rows_a,
            queries,
            keys_low,
            values_low,
            log_total,
            mixed_out,
            branch,
            gate_a,
            norm_pull_m,
            rows_m,
            gelu_pull,
            act_low,
            down_out,
            gate_m,
        ) = saved_acts[layer_idx]
        w_qkv = weight_in[:, : 3 * group_width]
        w_up = weight_in[:, 3 * group_width :]
        w_attn = weight_out[:group_width]
        w_down = weight_out[group_width:]
        d_gate_m = jnp.sum(d_residual * down_out, axis=1)
        d_down = d_residual * gate_m[:, None, :]
        d_down_bias = jnp.sum(d_down, axis=(0, 1))
        d_down_rows = gather_tokens(d_down.astype(jnp.bfloat16))
        d_w_down = jnp.einsum(
            "btf,btd->fd", act_low, d_down_rows, preferred_element_type=jnp.float32
        )
        d_act = jnp.einsum("btd,fd->btf", d_down_rows, w_down, preferred_element_type=jnp.float32)
        d_upper = gelu_pull(d_act)[0]
        d_up_bias = jnp.sum(d_upper, axis=(0, 1))
        d_upper_low = d_upper.astype(jnp.bfloat16)
        d_w_up = jnp.einsum("btd,btf->df", rows_m, d_upper_low, preferred_element_type=jnp.float32)
        d_normed_m = sum_tokens(
            jnp.einsum("btf,df->btd", d_upper_low, w_up, preferred_element_type=jnp.float32)
        )
        d_mid, d_shift_m, d_scale_m = norm_pull_m(d_normed_m)
        d_residual = d_residual + d_mid
        d_gate_a = jnp.sum(d_residual * branch, axis=1)
        d_branch = d_residual * gate_a[:, None, :]
        d_out_bias = jnp.sum(d_branch, axis=(0, 1))
        d_branch_rows = gather_tokens(d_branch.astype(jnp.bfloat16))
        d_w_attn = jnp.einsum(
            "bte,btd->ed", mixed_out, d_branch_rows, preferred_element_type=jnp.float32
        )
        d_mixed = (
            jnp.einsum("btd,ed->bte", d_branch_rows, w_attn, preferred_element_type=jnp.float32)
            .astype(jnp.bfloat16)
            .reshape(head_shape)
        )
        scores = (
            jnp.einsum("bqhd,bkhd->bhqk", queries, keys_low, preferred_element_type=jnp.float32)
            * scale_dot
        )
        probs_row = jnp.exp(scores - log_total)
        d_probs = jnp.einsum(
            "bqhd,bkhd->bhqk", d_mixed, values_low, preferred_element_type=jnp.float32
        )
        d_values = jnp.einsum(
            "bhqk,bqhd->bkhd",
            probs_row.astype(jnp.bfloat16),
            d_mixed,
            preferred_element_type=jnp.float32,
        )
        d_scores = (
            probs_row * (d_probs - jnp.sum(probs_row * d_probs, axis=-1, keepdims=True))
        ).astype(jnp.bfloat16)
        d_queries = (
            jnp.einsum("bhqk,bkhd->bqhd", d_scores, keys_low, preferred_element_type=jnp.float32)
            * scale_dot
        )
        d_keys = (
            jnp.einsum("bhqk,bqhd->bkhd", d_scores, queries, preferred_element_type=jnp.float32)
            * scale_dot
        )
        d_query_bias = jnp.sum(d_queries.reshape(flat_shape), axis=(0, 1))
        d_value_bias = jnp.sum(d_values.reshape(flat_shape), axis=(0, 1))
        d_projected = jnp.concatenate(
            [
                d_queries.reshape(flat_shape),
                d_keys.reshape(flat_shape),
                d_values.reshape(flat_shape),
            ],
            axis=2,
        ).astype(jnp.bfloat16)
        d_w_qkv = jnp.einsum("btd,bte->de", rows_a, d_projected, preferred_element_type=jnp.float32)
        d_normed_a = sum_tokens(
            jnp.einsum("bte,de->btd", d_projected, w_qkv, preferred_element_type=jnp.float32)
        )
        d_before, d_shift_a, d_scale_a = norm_pull_a(d_normed_a)
        d_residual = d_residual + d_before
        d_modulation = jnp.concatenate(
            [d_shift_a, d_scale_a, d_gate_a, d_shift_m, d_scale_m, d_gate_m], axis=1
        )
        d_mod_local = lax.psum_scatter(
            d_modulation, "tensor", scatter_dimension=1, tiled=True
        ).astype(jnp.bfloat16)
        d_signal = d_signal + jnp.einsum(
            "be,de->bd", d_mod_local, mod_weights[layer_idx], preferred_element_type=jnp.float32
        )
        d_w_ada = jnp.einsum(
            "bd,be->de", signal_low, d_mod_local, preferred_element_type=jnp.float32
        )
        grad_in, grad_out, grad_ada = (
            lax.psum_scatter(
                jnp.concatenate([d_w_qkv, d_w_up], axis=1), "dp", scatter_dimension=0, tiled=True
            ),
            lax.psum_scatter(
                jnp.concatenate([d_w_attn, d_w_down], axis=0), "dp", scatter_dimension=0, tiled=True
            ),
            lax.psum_scatter(d_w_ada, "dp", scatter_dimension=0, tiled=True),
        )
        grads_in.insert(0, grad_in)
        grads_out.insert(0, grad_out)
        grads_mod.insert(0, grad_ada)
        query_row = lax.dynamic_update_slice_in_dim(
            jnp.zeros((D,), jnp.float32), d_query_bias, tensor_rank * group_width, 0
        )
        value_row = lax.dynamic_update_slice_in_dim(
            jnp.zeros((D,), jnp.float32), d_value_bias, tensor_rank * group_width, 0
        )
        up_rows = lax.dynamic_update_slice_in_dim(
            jnp.zeros((FF,), jnp.float32), d_up_bias, tensor_rank * unit_count, 0
        ).reshape(FF // D, D)
        bias_blocks.insert(
            0,
            jnp.concatenate(
                [
                    jnp.sum(d_modulation, axis=0).reshape(6, D),
                    d_out_bias[None],
                    d_down_bias[None],
                    query_row[None],
                    value_row[None],
                    up_rows,
                ],
                axis=0,
            ),
        )
    d_signal_total = d_signal + dense(d_final_shift, shift_w.T) + dense(d_final_scale, scale_w.T)
    d_pre_signal = d_signal_total * silu_slope(pre_signal)
    d_hidden = dense(d_pre_signal, second_w.T) * silu_slope(pre_time)
    d_patch_w = jnp.einsum("btp,btd->pd", noisy, d_residual, precision=PRECISE)
    d_patch_b = jnp.sum(d_residual, axis=(0, 1))
    vector_grads = jnp.stack(
        [
            d_patch_b,
            jnp.sum(d_hidden, axis=0),
            jnp.sum(d_pre_signal, axis=0),
            jnp.sum(d_final_shift, axis=0),
            jnp.sum(d_final_scale, axis=0),
        ]
    )
    grad_table = jnp.concatenate(
        [
            dense(onehot.T, d_pre_signal),
            d_patch_w,
            dense(time_feats.T, d_hidden),
            dense(hidden.T, d_pre_signal),
            dense(signal.T, d_final_shift),
            dense(signal.T, d_final_scale),
            d_head,
            vector_grads,
        ]
        + bias_blocks,
        axis=0,
    )
    table_grad = lax.psum_scatter(grad_table, ("dp", "tensor"), scatter_dimension=1, tiled=True)
    input_grad = jnp.stack(grads_in).reshape(layer_in.shape)
    output_grad = jnp.stack(grads_out).reshape(layer_out.shape)
    mod_grad = jnp.stack(grads_mod)
    local_squares = (
        jnp.sum(table_grad * table_grad)
        + jnp.sum(input_grad * input_grad)
        + jnp.sum(output_grad * output_grad)
        + jnp.sum(mod_grad * mod_grad)
    )
    square_total = lax.psum(local_squares, ("dp", "tensor"))
    grad_norm = jnp.sqrt(square_total)
    factor = jnp.minimum(1.0, CLIP_NORM / grad_norm)
    first_fix = 1.0 - BETA_ONE ** step_count.astype(jnp.float32)
    second_fix = 1.0 - BETA_TWO ** step_count.astype(jnp.float32)
    embed_out = adam_update(
        embed_table, embed_first, embed_second, table_grad, factor, first_fix, second_fix
    )
    input_out = adam_update(
        layer_in, input_first, input_second, input_grad, factor, first_fix, second_fix
    )
    output_out = adam_update(
        layer_out, output_first, output_second, output_grad, factor, first_fix, second_fix
    )
    mod_out = adam_update(layer_ada, mod_first, mod_second, mod_grad, factor, first_fix, second_fix)
    return (
        (loss_value, grad_norm, embed_out[4], embed_out[1], embed_out[2])
        + input_out[0:4]
        + output_out[0:4]
        + mod_out[0:4]
    )


def solution(mesh):
    placed = (
        P("dp", "tensor"),
        P("dp", "tensor"),
        P("dp"),
        P("dp"),
        P(),
        P(None, ("dp", "tensor")),
        P(None, "dp", "tensor", None),
        P(None, "tensor", "dp", None),
        P(None, "dp", "tensor"),
        P(None, ("dp", "tensor")),
        P(None, ("dp", "tensor")),
        P(None, "dp", "tensor", None),
        P(None, "dp", "tensor", None),
        P(None, "tensor", "dp", None),
        P(None, "tensor", "dp", None),
        P(None, "dp", "tensor"),
        P(None, "dp", "tensor"),
    )
    return jax.shard_map(
        local,
        mesh=mesh,
        in_specs=placed,
        out_specs=(
            P(),
            P(),
            P(None, ("dp", "tensor")),
            P(None, ("dp", "tensor")),
            P(None, ("dp", "tensor")),
            P(None, "dp", "tensor", None),
            P(None, "dp", "tensor", None),
            P(None, "dp", "tensor", None),
            P(None, "dp", "tensor", None),
            P(None, "tensor", "dp", None),
            P(None, "tensor", "dp", None),
            P(None, "tensor", "dp", None),
            P(None, "tensor", "dp", None),
            P(None, "dp", "tensor"),
            P(None, "dp", "tensor"),
            P(None, "dp", "tensor"),
            P(None, "dp", "tensor"),
        ),
        check_vma=False,
    )
```

profile of v0, /device:TPU:0, one launch (start us, length us, event | category | flops | bytes accessed | tf_op | source)
XLA Modules:
  0.0 2289.3 jit_solution(6731740812102349512)
XLA Ops:
  15.8 65.4 %all-gather.27.cloned.1.call-done = bf16[3640,768]{0,1:T(8,128)(2,1)} async-done(((bf16[3640,24]{0,1:T(8,128)(2,1)}), bf16[3640,768]{0,1:T(8,128)(2,1)}) %all-gather.27.cloned.1.call-update) | async-done | bytes 5591056 | tf_op jit(solution)/shard_map/all_gather | solution.py:165
  89.5 80.4 %all-gather.29.cloned.1.call-done = bf16[3,768,1152]{2,1,0:T(8,128)(2,1)} async-done(((bf16[3,96,1152]{2,1,0:T(8,128)(2,1)}), bf16[3,768,1152]{2,1,0:T(8,128)(2,1)}) %all-gather.29.cloned.1.call-update) | async-done | bytes 5308432 | tf_op jit(solution)/shard_map/all_gather | solution.py:166
  170.0 3.3 fusion.18
  173.3 5.4 all_gather.71
  186.2 34.8 %all-gather.55.cloned.1.call-done = bf16[1,768,1,1344]{3,1,2,0:T(8,128)(2,1)} async-done(((bf16[1,96,1,1344]{3,1,2,0:T(8,128)(2,1)}), bf16[1,768,1,1344]{3,1,2,0:T(8,128)(2,1)}) %all-gather.55.cloned.1.call-update) | async-done | bytes 2064400 | tf_op jit(solution)/shard_map/all_gather | solution.py:203
  220.9 4.1 copy.221
  226.5 12.4 all-gather.31.cloned.1.call-done
  243.8 41.3 %all-gather.57.cloned.1.call-done = bf16[1,1,960,768]{3,2,1,0:T(8,128)(2,1)} async-done(((bf16[1,1,120,768]{3,2,1,0:T(8,128)(2,1)}), bf16[1,1,960,768]{3,2,1,0:T(8,128)(2,1)}) %all-gather.57.cloned.1.call-update) | async-done | bytes 1474576 | tf_op jit(solution)/shard_map/all_gather | solution.py:211
  287.7 24.5 %reduce-scatter.38.cloned.1.call-done = bf16[3,64,768]{2,1,0:T(8,128)(2,1)} async-done(((bf16[3,256,768]{2,1,0:T(8,128)(2,1)}), bf16[3,64,768]{2,1,0:T(8,128)(2,1)}) %reduce-scatter.38.cloned.1.call-update) | async-done | bytes 294928 | tf_op jit(solution)/shard_map/reduce_scatter | solution.py:113
  322.8 11.1 all-gather.33.cloned.1.call-done
  343.1 23.7 %reduce-scatter.40.cloned.1.call-done = bf16[3,64,768]{2,1,0:T(8,128)(2,1)} async-done(((bf16[3,256,768]{2,1,0:T(8,128)(2,1)}), bf16[3,64,768]{2,1,0:T(8,128)(2,1)}) %reduce-scatter.40.cloned.1.call-update) | async-done | bytes 294928 | tf_op jit(solution)/shard_map/reduce_scatter | solution.py:113
  371.0 48.5 %all-gather.59.cloned.1.call-done = bf16[1,768,1,1344]{3,1,2,0:T(8,128)(2,1)} async-done(((bf16[1,96,1,1344]{3,1,2,0:T(8,128)(2,1)}), bf16[1,768,1,1344]{3,1,2,0:T(8,128)(2,1)}) %all-gather.59.cloned.1.call-update) | async-done | bytes 2064400 | tf_op jit(solution)/shard_map/all_gather | solution.py:203
  419.5 4.1 copy.226
  427.4 10.1 all-gather.35.cloned.1.call-done
  444.1 39.7 %all-gather.61.cloned.1.call-done = bf16[1,1,960,768]{3,2,1,0:T(8,128)(2,1)} async-done(((bf16[1,1,120,768]{3,2,1,0:T(8,128)(2,1)}), bf16[1,1,960,768]{3,2,1,0:T(8,128)(2,1)}) %all-gather.61.cloned.1.call-update) | async-done | bytes 1474576 | tf_op jit(solution)/shard_map/all_gather | solution.py:211
  486.5 24.4 %reduce-scatter.42.cloned.1.call-done = bf16[3,64,768]{2,1,0:T(8,128)(2,1)} async-done(((bf16[3,256,768]{2,1,0:T(8,128)(2,1)}), bf16[3,64,768]{2,1,0:T(8,128)(2,1)}) %reduce-scatter.42.cloned.1.call-update) | async-done | bytes 294928 | tf_op jit(solution)/shard_map/reduce_scatter | solution.py:113
  520.9 11.2 all-gather.37.cloned.1.call-done
  541.1 23.8 %reduce-scatter.44.cloned.1.call-done = bf16[3,64,768]{2,1,0:T(8,128)(2,1)} async-done(((bf16[3,256,768]{2,1,0:T(8,128)(2,1)}), bf16[3,64,768]{2,1,0:T(8,128)(2,1)}) %reduce-scatter.44.cloned.1.call-update) | async-done | bytes 294928 | tf_op jit(solution)/shard_map/reduce_scatter | solution.py:113
  569.6 48.0 %all-gather.63.cloned.1.call-done = bf16[1,768,1,1344]{3,1,2,0:T(8,128)(2,1)} async-done(((bf16[1,96,1,1344]{3,1,2,0:T(8,128)(2,1)}), bf16[1,768,1,1344]{3,1,2,0:T(8,128)(2,1)}) %all-gather.63.cloned.1.call-update) | async-done | bytes 2064400 | tf_op jit(solution)/shard_map/all_gather | solution.py:203
  617.6 4.2 copy.231
  625.3 10.3 all-gather.39.cloned.1.call-done
  642.2 39.5 %all-gather.65.cloned.1.call-done = bf16[1,1,960,768]{3,2,1,0:T(8,128)(2,1)} async-done(((bf16[1,1,120,768]{3,2,1,0:T(8,128)(2,1)}), bf16[1,1,960,768]{3,2,1,0:T(8,128)(2,1)}) %all-gather.65.cloned.1.call-update) | async-done | bytes 1474576 | tf_op jit(solution)/shard_map/all_gather | solution.py:211
  684.4 24.4 %reduce-scatter.46.cloned.1.call-done = bf16[3,64,768]{2,1,0:T(8,128)(2,1)} async-done(((bf16[3,256,768]{2,1,0:T(8,128)(2,1)}), bf16[3,64,768]{2,1,0:T(8,128)(2,1)}) %reduce-scatter.46.cloned.1.call-update) | async-done | bytes 294928 | tf_op jit(solution)/shard_map/reduce_scatter | solution.py:113
  718.9 11.2 all-gather.41.cloned.1.call-done
  743.3 19.6 reduce-scatter.48.cloned.1.call-done
  772.4 17.2 all-gather.43.cloned.1.call-done
  789.6 5.4 fusion.220
  798.2 25.8 %reduce-scatter.50.cloned.1.call-done = bf16[3,64,768]{2,1,0:T(8,128)(2,1)} async-done(((bf16[3,256,768]{2,1,0:T(8,128)(2,1)}), bf16[3,64,768]{2,1,0:T(8,128)(2,1)}) %reduce-scatter.50.cloned.1.call-update) | async-done | bytes 294928 | tf_op jit(solution)/shard_map/reduce_scatter | solution.py:113
  833.4 16.2 all-gather.45.cloned.1.call-done
  861.8 25.8 %reduce-scatter.52.cloned.1.call-done = bf16[3,64,768]{2,1,0:T(8,128)(2,1)} async-done(((bf16[3,256,768]{2,1,0:T(8,128)(2,1)}), bf16[3,64,768]{2,1,0:T(8,128)(2,1)}) %reduce-scatter.52.cloned.1.call-update) | async-done | bytes 294928 | tf_op jit(solution)/shard_map/reduce_scatter | solution.py:113
  895.8 17.4 all-gather.47.cloned.1.call-done
  913.2 5.4 fusion.219
  921.9 25.8 %reduce-scatter.54.cloned.1.call-done = bf16[3,64,768]{2,1,0:T(8,128)(2,1)} async-done(((bf16[3,256,768]{2,1,0:T(8,128)(2,1)}), bf16[3,64,768]{2,1,0:T(8,128)(2,1)}) %reduce-scatter.54.cloned.1.call-update) | async-done | bytes 294928 | tf_op jit(solution)/shard_map/reduce_scatter | solution.py:113
  957.0 16.2 all-gather.49.cloned.1.call-done
  985.3 25.8 %reduce-scatter.56.cloned.1.call-done = bf16[3,64,768]{2,1,0:T(8,128)(2,1)} async-done(((bf16[3,256,768]{2,1,0:T(8,128)(2,1)}), bf16[3,64,768]{2,1,0:T(8,128)(2,1)}) %reduce-scatter.56.cloned.1.call-update) | async-done | bytes 294928 | tf_op jit(solution)/shard_map/reduce_scatter | solution.py:113
  1019.1 17.6 all-gather.51.cloned.1.call-done
  1036.7 5.4 fusion.218
  1045.5 25.6 %reduce-scatter.58.cloned.1.call-done = bf16[3,64,768]{2,1,0:T(8,128)(2,1)} async-done(((bf16[3,256,768]{2,1,0:T(8,128)(2,1)}), bf16[3,64,768]{2,1,0:T(8,128)(2,1)}) %reduce-scatter.58.cloned.1.call-update) | async-done | bytes 294928 | tf_op jit(solution)/shard_map/reduce_scatter | solution.py:113
  1078.6 16.2 all-gather.53.cloned.1.call-done
  1101.9 3.4 convolution_convert_fusion.1
  1105.5 5.0 convolution_bitcast_fusion
  1116.0 15.2 reduce-scatter.60.cloned.1.call-done
  1138.2 3.7 pad_maximum_fusion.5
  1142.6 3.5 convolution_bitcast_fusion.1
  1149.0 3.5 convolution_bitcast_fusion.2
  1161.2 3.5 fusion.179
  1197.1 5.4 reduce-scatter.76.cloned.1.call-done
  1224.7 13.5 reduce-scatter.78.cloned.1.call-done
  1252.0 3.5 fusion.174
  1259.1 45.1 %concatenate.92 = f32[3640,768]{1,0:T(8,128)} concatenate(f32[1001,768]{1,0:T(8,128)} %fusion.130, f32[16,768]{1,0:T(8,128)S(1)} %copy-done.117, f32[256,768]{1,0:T(8,128)} %fusion.147, f32[768,768]{1,0:T(8,128)} %fusion.174, f32[768,768]{1,0:T(8,128)} %fusion.179, f32[768,768]{1,0:T(8,128)S(1)} %fusion.177, f32[16,768]{1,0:T(8,128)S(1)} %copy-done.118, ...), dimensions={0} | concatenate | bytes 22364160 | tf_op jit(solution)/shard_map/concatenate | solution.py:486
  1310.6 5.7 copy.307
  1322.4 5.7 copy.305
  1334.3 5.7 copy.303
  1349.7 39.8 %reduce-scatter.64.cloned.1.call-done = f32[120,768]{1,0:T(8,128)} async-done(((f32[960,768]{1,0:T(8,128)}), f32[120,768]{1,0:T(8,128)}) %reduce-scatter.64.cloned.1.call-update) | async-done | bytes 368656 | tf_op jit(solution)/shard_map/reduce_scatter | solution.py:441
  1389.5 75.5 %reduce-scatter.62.cloned.1.call-done = f32[120,768]{1,0:T(8,128)} async-done(((f32[960,768]{1,0:T(8,128)}), f32[120,768]{1,0:T(8,128)}) %reduce-scatter.62.cloned.1.call-update) | async-done | bytes 368656 | tf_op jit(solution)/shard_map/reduce_scatter | solution.py:441
  1467.1 220.6 %all-reduce.4.cloned.1.call-done = f32[3640,768]{1,0:T(8,128)} async-done(((f32[3640,768]{1,0:T(8,128)}), f32[3640,768]{1,0:T(8,128)}) %all-reduce.4.cloned.1.call-update) | async-done | bytes 11182096
  1690.8 89.0 %reduce-scatter.84.cloned.1.call-done = f32[96,1344]{1,0:T(8,128)} async-done(((f32[768,1344]{1,0:T(8,128)}), f32[96,1344]{1,0:T(8,128)}) %reduce-scatter.84.cloned.1.call-update) | async-done | bytes 516112 | tf_op jit(solution)/shard_map/reduce_scatter | solution.py:438
  1779.8 93.8 %reduce-scatter.82.cloned.1.call-done = f32[96,1344]{1,0:T(8,128)} async-done(((f32[768,1344]{1,0:T(8,128)}), f32[96,1344]{1,0:T(8,128)}) %reduce-scatter.82.cloned.1.call-update) | async-done | bytes 516112 | tf_op jit(solution)/shard_map/reduce_scatter | solution.py:438
  1873.6 93.2 %reduce-scatter.80.cloned.1.call-done = f32[96,1344]{1,0:T(8,128)} async-done(((f32[768,1344]{1,0:T(8,128)}), f32[96,1344]{1,0:T(8,128)}) %reduce-scatter.80.cloned.1.call-update) | async-done | bytes 516112 | tf_op jit(solution)/shard_map/reduce_scatter | solution.py:438
  1971.3 78.2 %reduce-scatter.72.cloned.1.call-done = f32[96,1152]{1,0:T(8,128)} async-done(((f32[768,1152]{1,0:T(8,128)}), f32[96,1152]{1,0:T(8,128)}) %reduce-scatter.72.cloned.1.call-update) | async-done | bytes 442384 | tf_op jit(solution)/shard_map/reduce_scatter | solution.py:444
  2049.5 82.7 %reduce-scatter.70.cloned.1.call-done = f32[96,1152]{1,0:T(8,128)} async-done(((f32[768,1152]{1,0:T(8,128)}), f32[96,1152]{1,0:T(8,128)}) %reduce-scatter.70.cloned.1.call-update) | async-done | bytes 442384 | tf_op jit(solution)/shard_map/reduce_scatter | solution.py:444
  2132.2 82.4 %reduce-scatter.68.cloned.1.call-done = f32[96,1152]{1,0:T(8,128)} async-done(((f32[768,1152]{1,0:T(8,128)}), f32[96,1152]{1,0:T(8,128)}) %reduce-scatter.68.cloned.1.call-update) | async-done | bytes 442384 | tf_op jit(solution)/shard_map/reduce_scatter | solution.py:444
  2218.8 40.4 %all-reduce.1 = (f32[]{:T(128)}, f32[]{:T(128)}) all-reduce(f32[]{:T(128)S(6)} %div.276, f32[]{:T(128)S(6)} %add.819), channel_id=1, replica_groups=mesh['dp'=8,'tensor'=4] {'dp','tensor'}, use_global_device_ids=true, to_apply=%region_27.28 | all-reduce | flops 2 | bytes 16 | tf_op jit(solution)/shard_map/psum | solution.py:307
  2260.0 4.6 fusion.193
  (872 shorter events, 371.5 us)
Async XLA Ops:
  7.2 74.0 %all-gather.27.cloned.1.call-start = ((), (), s32[]{:S(2)}) async-start(), calls=%async_computation.24 | async-start | bytes 5879808 | tf_op jit(solution)/shard_map/all_gather | solution.py:165
  9.1 160.9 %all-gather.29.cloned.1.call-start = ((), (), s32[]{:S(2)}) async-start(), calls=%async_computation.25 | async-start | bytes 5971968 | tf_op jit(solution)/shard_map/all_gather | solution.py:166
  11.4 209.5 %all-gather.55.cloned.1.call-start = ((), (), s32[]{:S(2)}) async-start(), calls=%async_computation.56 | async-start | bytes 2433024 | tf_op jit(solution)/shard_map/all_gather | solution.py:203
  12.5 226.4 %all-gather.31.cloned.1.call-start = ((), (), s32[]{:S(2)}) async-start(), calls=%async_computation.26 | async-start | bytes 1474560 | tf_op jit(solution)/shard_map/all_gather | solution.py:109
  12.6 168.4 %copy-start.232 = (f32[3]{0:T(128)}, f32[3]{0:T(128)S(1)}, u32[]{:S(2)}) copy-start(f32[3]{0:T(128)S(1)} %get-tuple-element.187) | copy-start | bytes 40
  12.7 168.3 %copy-start.233 = (f32[3]{0:T(128)}, f32[3]{0:T(128)S(1)}, u32[]{:S(2)}) copy-start(f32[3]{0:T(128)S(1)} %subtract_sqrt_fusion) | copy-start | bytes 40
  13.8 167.2 %copy-start.108 = (f32[3,64,16]{1,2,0:T(8,128)}, f32[3,64,16]{1,2,0:T(8,128)S(1)}, u32[]{:S(2)}) copy-start(f32[3,64,16]{1,2,0:T(8,128)S(1)} %reshape.818) | copy-start | bytes 36868
  15.0 166.1 %copy-start.79 = (f32[3,64,16]{1,2,0:T(8,128)}, f32[3,64,16]{1,2,0:T(8,128)S(1)}, u32[]{:S(2)}) copy-start(f32[3,64,16]{1,2,0:T(8,128)S(1)} %reshape.820) | copy-start | bytes 36868
  15.1 72.5 %copy-start.186 = (f32[3,128]{1,0:T(4,128)}, f32[3,128]{1,0:T(4,128)S(1)}, u32[]{:S(2)}) copy-start(f32[3,128]{1,0:T(4,128)S(1)} %get-tuple-element.248) | copy-start | bytes 4612
  15.1 72.5 %copy-start.188 = (f32[3,128]{1,0:T(4,128)}, f32[3,128]{1,0:T(4,128)S(1)}, u32[]{:S(2)}) copy-start(f32[3,128]{1,0:T(4,128)S(1)} %get-tuple-element.249) | copy-start | bytes 4612
  15.7 71.9 %copy-start.230 = (s32[3]{0:T(128)S(1)}, s32[3]{0:T(128)}, u32[]{:S(2)}) copy-start(s32[3]{0:T(128)} %param.20) | copy-start | bytes 40
  85.1 88.2 %copy-start.147 = (f32[3,768]{1,0:T(4,128)}, f32[3,768]{1,0:T(4,128)S(1)}, u32[]{:S(2)}) copy-start(f32[3,768]{1,0:T(4,128)S(1)} %convolution_add_fusion.6) | copy-start | bytes 27652
  180.2 44.9 %copy-start.14 = (f32[14,768]{0,1:T(8,128)}, f32[14,768]{0,1:T(8,128)S(1)}, u32[]{:S(2)}) copy-start(f32[14,768]{0,1:T(8,128)S(1)} %get-tuple-element.191) | copy-start | bytes 129028
  185.1 100.0 %all-gather.57.cloned.1.call-start = ((), (), s32[]{:S(2)}) async-start(), calls=%async_computation.57 | async-start | bytes 1658880 | tf_op jit(solution)/shard_map/all_gather | solution.py:211
  186.1 126.1 %reduce-scatter.38.cloned.1.call-start = ((), (), s32[]{:S(2)}) async-start(), calls=%async_computation.27 | async-start | bytes 1474560 | tf_op jit(solution)/shard_map/reduce_scatter | solution.py:113
  243.8 68.4 %copy-start.60 = (bf16[3,3,64,256]{3,2,1,0:T(8,128)(2,1)}, bf16[3,3,64,256]{3,2,1,0:T(8,128)(2,1)S(1)}, u32[]{:S(2)}) copy-start(bf16[3,3,64,256]{3,2,1,0:T(8,128)(2,1)S(1)} %convolution_convert_fusion.18) | copy-start | bytes 884740
  287.6 46.3 %all-gather.33.cloned.1.call-start = ((), (), s32[]{:S(2)}) async-start(), calls=%async_computation.28 | async-start | bytes 1474560 | tf_op jit(solution)/shard_map/all_gather | solution.py:109
  316.3 50.5 %reduce-scatter.40.cloned.1.call-start = ((), (), s32[]{:S(2)}) async-start(), calls=%async_computation.29 | async-start | bytes 1474560 | tf_op jit(solution)/shard_map/reduce_scatter | solution.py:113
  340.9 78.6 %all-gather.59.cloned.1.call-start = ((), (), s32[]{:S(2)}) async-start(), calls=%async_computation.58 | async-start | bytes 2433024 | tf_op jit(solution)/shard_map/all_gather | solution.py:203
  341.6 95.9 %all-gather.35.cloned.1.call-start = ((), (), s32[]{:S(2)}) async-start(), calls=%async_computation.30 | async-start | bytes 1474560 | tf_op jit(solution)/shard_map/all_gather | solution.py:109
  370.2 113.6 %all-gather.61.cloned.1.call-start = ((), (), s32[]{:S(2)}) async-start(), calls=%async_computation.59 | async-start | bytes 1658880 | tf_op jit(solution)/shard_map/all_gather | solution.py:211
  371.0 140.0 %reduce-scatter.42.cloned.1.call-start = ((), (), s32[]{:S(2)}) async-start(), calls=%async_computation.31 | async-start | bytes 1474560 | tf_op jit(solution)/shard_map/reduce_scatter | solution.py:113
  486.5 45.7 %all-gather.37.cloned.1.call-start = ((), (), s32[]{:S(2)}) async-start(), calls=%async_computation.32 | async-start | bytes 1474560 | tf_op jit(solution)/shard_map/all_gather | solution.py:109
  514.5 50.4 %reduce-scatter.44.cloned.1.call-start = ((), (), s32[]{:S(2)}) async-start(), calls=%async_computation.33 | async-start | bytes 1474560 | tf_op jit(solution)/shard_map/reduce_scatter | solution.py:113
  539.1 78.5 %all-gather.63.cloned.1.call-start = ((), (), s32[]{:S(2)}) async-start(), calls=%async_computation.60 | async-start | bytes 2433024 | tf_op jit(solution)/shard_map/all_gather | solution.py:203
  539.7 95.9 %all-gather.39.cloned.1.call-start = ((), (), s32[]{:S(2)}) async-start(), calls=%async_computation.34 | async-start | bytes 1474560 | tf_op jit(solution)/shard_map/all_gather | solution.py:109
  568.7 113.0 %all-gather.65.cloned.1.call-start = ((), (), s32[]{:S(2)}) async-start(), calls=%async_computation.61 | async-start | bytes 1658880 | tf_op jit(solution)/shard_map/all_gather | solution.py:211
  569.3 139.5 %reduce-scatter.46.cloned.1.call-start = ((), (), s32[]{:S(2)}) async-start(), calls=%async_computation.35 | async-start | bytes 1474560 | tf_op jit(solution)/shard_map/reduce_scatter | solution.py:113
  684.4 45.7 %all-gather.41.cloned.1.call-start = ((), (), s32[]{:S(2)}) async-start(), calls=%async_computation.36 | async-start | bytes 1474560 | tf_op jit(solution)/shard_map/all_gather | solution.py:109
  712.5 50.4 %reduce-scatter.48.cloned.1.call-start = ((), (), s32[]{:S(2)}) async-start(), calls=%async_computation.37 | async-start | bytes 1474560 | tf_op jit(solution)/shard_map/reduce_scatter | solution.py:113
  737.0 52.6 %all-gather.43.cloned.1.call-start = ((), (), s32[]{:S(2)}) async-start(), calls=%async_computation.38 | async-start | bytes 1474560 | tf_op jit(solution)/shard_map/all_gather | solution.py:109
  772.0 52.1 %reduce-scatter.50.cloned.1.call-start = ((), (), s32[]{:S(2)}) async-start(), calls=%async_computation.39 | async-start | bytes 1474560 | tf_op jit(solution)/shard_map/reduce_scatter | solution.py:113
  798.2 51.4 %all-gather.45.cloned.1.call-start = ((), (), s32[]{:S(2)}) async-start(), calls=%async_computation.40 | async-start | bytes 1474560 | tf_op jit(solution)/shard_map/all_gather | solution.py:109
  832.0 55.7 %reduce-scatter.52.cloned.1.call-start = ((), (), s32[]{:S(2)}) async-start(), calls=%async_computation.41 | async-start | bytes 1474560 | tf_op jit(solution)/shard_map/reduce_scatter | solution.py:113
  861.8 51.5 %all-gather.47.cloned.1.call-start = ((), (), s32[]{:S(2)}) async-start(), calls=%async_computation.42 | async-start | bytes 1474560 | tf_op jit(solution)/shard_map/all_gather | solution.py:109
  895.6 52.1 %reduce-scatter.54.cloned.1.call-start = ((), (), s32[]{:S(2)}) async-start(), calls=%async_computation.43 | async-start | bytes 1474560 | tf_op jit(solution)/shard_map/reduce_scatter | solution.py:113
  921.8 51.4 %all-gather.49.cloned.1.call-start = ((), (), s32[]{:S(2)}) async-start(), calls=%async_computation.44 | async-start | bytes 1474560 | tf_op jit(solution)/shard_map/all_gather | solution.py:109
  955.6 55.6 %reduce-scatter.56.cloned.1.call-start = ((), (), s32[]{:S(2)}) async-start(), calls=%async_computation.45 | async-start | bytes 1474560 | tf_op jit(solution)/shard_map/reduce_scatter | solution.py:113
  985.3 51.4 %all-gather.51.cloned.1.call-start = ((), (), s32[]{:S(2)}) async-start(), calls=%async_computation.46 | async-start | bytes 1474560 | tf_op jit(solution)/shard_map/all_gather | solution.py:109
  1019.1 52.1 %reduce-scatter.58.cloned.1.call-start = ((), (), s32[]{:S(2)}) async-start(), calls=%async_computation.47 | async-start | bytes 1474560 | tf_op jit(solution)/shard_map/reduce_scatter | solution.py:113
  1045.3 49.6 %all-gather.53.cloned.1.call-start = ((), (), s32[]{:S(2)}) async-start(), calls=%async_computation.48 | async-start | bytes 1474560 | tf_op jit(solution)/shard_map/all_gather | solution.py:109
  1077.2 54.0 %reduce-scatter.60.cloned.1.call-start = ((), (), s32[]{:S(2)}) async-start(), calls=%async_computation.49 | async-start | bytes 1474560 | tf_op jit(solution)/shard_map/reduce_scatter | solution.py:113
  1078.6 20.1 copy-start.70
  1105.4 74.6 %reduce-scatter.74.cloned.1.call-start = ((), (), s32[]{:S(2)}) async-start(), calls=%async_computation.62 | async-start | bytes 2949120
  1113.5 89.0 %reduce-scatter.76.cloned.1.call-start = ((), (), s32[]{:S(2)}) async-start(), calls=%async_computation.63 | async-start | bytes 2949120
  1115.9 17.8 copy-start.62
  1115.9 17.8 copy-start.109
  1116.0 20.0 copy-start.166
  1116.0 20.0 copy-start.164
  1116.0 20.0 copy-start.163
  1116.0 122.2 %reduce-scatter.78.cloned.1.call-start = ((), (), s32[]{:S(2)}) async-start(), calls=%async_computation.64 | async-start | bytes 2949120
  1138.2 211.5 %reduce-scatter.66.cloned.1.call-start = ((), (), s32[]{:S(2)}) async-start(), calls=%async_computation.52 | async-start | bytes 3317760 | tf_op jit(solution)/shard_map/reduce_scatter | solution.py:441
  1142.0 247.5 %reduce-scatter.64.cloned.1.call-start = ((), (), s32[]{:S(2)}) async-start(), calls=%async_computation.51 | async-start | bytes 3317760 | tf_op jit(solution)/shard_map/reduce_scatter | solution.py:441
  1148.4 316.6 %reduce-scatter.62.cloned.1.call-start = ((), (), s32[]{:S(2)}) async-start(), calls=%async_computation.50 | async-start | bytes 3317760 | tf_op jit(solution)/shard_map/reduce_scatter | solution.py:441
  1154.8 532.8 %all-reduce.4.cloned.1.call-start = ((), (), s32[]{:S(2)}) async-start(), calls=%async_computation.68 | async-start | bytes 22364160
  1304.2 475.6 %reduce-scatter.84.cloned.1.call-start = ((), (), s32[]{:S(2)}) async-start(), calls=%async_computation.67 | async-start | bytes 4866048 | tf_op jit(solution)/shard_map/reduce_scatter | solution.py:438
  1316.4 557.2 %reduce-scatter.82.cloned.1.call-start = ((), (), s32[]{:S(2)}) async-start(), calls=%async_computation.66 | async-start | bytes 4866048 | tf_op jit(solution)/shard_map/reduce_scatter | solution.py:438
  1328.2 638.6 %reduce-scatter.80.cloned.1.call-start = ((), (), s32[]{:S(2)}) async-start(), calls=%async_computation.65 | async-start | bytes 4866048 | tf_op jit(solution)/shard_map/reduce_scatter | solution.py:438
  1340.1 709.4 %reduce-scatter.72.cloned.1.call-start = ((), (), s32[]{:S(2)}) async-start(), calls=%async_computation.55 | async-start | bytes 3981312 | tf_op jit(solution)/shard_map/reduce_scatter | solution.py:444
  1342.6 789.7 %reduce-scatter.70.cloned.1.call-start = ((), (), s32[]{:S(2)}) async-start(), calls=%async_computation.54 | async-start | bytes 3981312 | tf_op jit(solution)/shard_map/reduce_scatter | solution.py:444
  1345.7 868.9 %reduce-scatter.68.cloned.1.call-start = ((), (), s32[]{:S(2)}) async-start(), calls=%async_computation.53 | async-start | bytes 3981312 | tf_op jit(solution)/shard_map/reduce_scatter | solution.py:444
  1969.2 290.8 %copy-start.44 = (f32[96,1344]{1,0:T(8,128)S(1)}, f32[96,1344]{1,0:T(8,128)}, u32[]{:S(2)}) copy-start(f32[96,1344]{1,0:T(8,128)} %reduce-scatter.84.cloned.1.call-done) | copy-start | bytes 1548292
  1969.2 290.8 %copy-start.45 = (f32[96,1344]{1,0:T(8,128)S(1)}, f32[96,1344]{1,0:T(8,128)}, u32[]{:S(2)}) copy-start(f32[96,1344]{1,0:T(8,128)} %reduce-scatter.82.cloned.1.call-done) | copy-start | bytes 1548292
  1969.2 290.8 %copy-start.46 = (f32[96,1344]{1,0:T(8,128)S(1)}, f32[96,1344]{1,0:T(8,128)}, u32[]{:S(2)}) copy-start(f32[96,1344]{1,0:T(8,128)} %reduce-scatter.80.cloned.1.call-done) | copy-start | bytes 1548292
  (225 other events, 731.6 us)
Sparse Core Ops, SparseCore 0:
  11.4 69.6 all-gather.26
  83.9 86.0 all-gather.28
  172.7 48.1 all-gather.54
  222.9 15.9 all-gather.30
  241.5 43.5 all-gather.56
  288.1 24.0 reduce-scatter.37
  316.4 17.4 all-gather.32
  341.0 25.7 reduce-scatter.39
  369.5 49.9 all-gather.58
  421.5 15.9 all-gather.34
  440.3 43.5 all-gather.60
  486.9 24.0 reduce-scatter.41
  514.7 17.4 all-gather.36
  539.2 25.7 reduce-scatter.43
  567.6 49.9 all-gather.62
  619.5 15.9 all-gather.38
  638.1 43.5 all-gather.64
  684.8 24.0 reduce-scatter.45
  712.6 17.4 all-gather.40
  737.1 25.7 reduce-scatter.47
  772.1 17.4 all-gather.42
  798.3 25.7 reduce-scatter.49
  832.1 17.4 all-gather.44
  861.9 25.7 reduce-scatter.51
  895.7 17.4 all-gather.46
  921.9 25.7 reduce-scatter.53
  955.7 17.4 all-gather.48
  985.4 25.7 reduce-scatter.55
  1019.2 17.4 all-gather.50
  1045.4 25.7 reduce-scatter.57
  1077.4 17.4 all-gather.52
  1105.5 25.7 reduce-scatter.59
  1133.6 33.0 reduce-scatter.73
  1169.4 33.0 reduce-scatter.75
  1205.1 33.0 reduce-scatter.77
  1242.0 72.4 reduce-scatter.65
  1317.9 71.5 reduce-scatter.63
  1393.5 71.4 reduce-scatter.61
  1471.0 216.6 all-reduce.3
  1691.2 88.5 reduce-scatter.83
  1783.8 89.7 reduce-scatter.81
  1877.2 89.5 reduce-scatter.79
  1970.7 78.7 reduce-scatter.71
  2053.6 78.6 reduce-scatter.69
  2136.2 78.4 reduce-scatter.67
where the time goes:
time: 2300 us; the launch traced here: 2290 us
  waiting for transfers between devices  1730 us (75%)
  local copies, waits for them, and re-layouts  201 us (9%)
  matrix products  174 us (8%)
  other arithmetic  115 us (5%)
  blocking collectives  45.8 us (2%)
  between operations  23.5 us (1%)
    reduce_scatter x12, waiting for transfers between devices, sum_tokens(): lax.psum_scatter(values.astype(jnp.bfloat16), 'tensor', scatter_dimension...  285 us
    reduce_scatter x3, waiting for transfers between devices, local(): lax.psum_scatter(jnp.concatenate([d_w_qkv, d_w_up], axis=1), 'dp', scatte...  276 us
    reduce_scatter x3, waiting for transfers between devices, local(): lax.psum_scatter(d_w_ada, 'dp', scatter_dimension=0, tiled=True)  243 us
    unnamed x49, waiting for transfers between devices  243 us
    all_gather x12, waiting for transfers between devices, gather_tokens(): return lax.all_gather(values, 'tensor', axis=1, tiled=True)  167 us
    all_gather x3, waiting for transfers between devices, local(): lax.all_gather(layer_in[layer_idx].astype(jnp.bfloat16).reshape(layer_in....  131 us
    all_gather x3, waiting for transfers between devices, local(): lax.all_gather(layer_out[layer_idx].astype(jnp.bfloat16).reshape(layer_ou...  121 us
    reduce_scatter x3, waiting for transfers between devices, local(): lax.psum_scatter(jnp.concatenate([d_w_attn, d_w_down], axis=0), 'dp', sca...  115 us
  transfers between devices with their start and end apart: 45, of which 43 were waited for; matrix products, arithmetic and copies ran while one was open for 13% of the time, Pallas kernels for 0%

commit v1 on v0

--- a/solution.py
+++ b/solution.py
@@ -1,8 +1,11 @@
+import functools
 import math
 
 import jax
 import jax.numpy as jnp
 from jax import lax
+from jax.experimental import pallas as pl
+from jax.experimental.pallas import tpu as pltpu
 from jax.sharding import PartitionSpec as P
 
 D = 768
@@ -103,6 +106,77 @@
         vector_start,
         layer_start,
     )
+
+
+def group_place(group):
+    if group == "all":
+        width = lax.axis_size("tensor")
+        place = lax.axis_index("dp") * width + lax.axis_index("tensor")
+        size = lax.axis_size("dp") * width
+        return place, size, lambda at: {"dp": at // width, "tensor": lax.rem(at, width)}
+    return lax.axis_index(group), lax.axis_size(group), lambda at: {group: at}
+
+
+def exchange_kernel(group, spread, source, target, send_sems, recv_sems, local_sem):
+    place, size, coords = group_place(group)
+    barrier = pltpu.get_barrier_semaphore()
+
+    def greet(step, carry):
+        peer = coords(lax.rem(place + step, size))
+        pl.semaphore_signal(barrier, inc=1, device_id=peer, device_id_type=pl.DeviceIdType.MESH)
+        return carry
+
+    def copy_to(step):
+        there = lax.rem(place + step, size)
+        return pltpu.make_async_remote_copy(
+            src_ref=source.at[there] if spread else source,
+            dst_ref=target.at[place],
+            send_sem=send_sems.at[step],
+            recv_sem=recv_sems.at[step],
+            device_id=coords(there),
+            device_id_type=pl.DeviceIdType.MESH,
+        )
+
+    def begin(step, carry):
+        copy_to(step).start()
+        return carry
+
+    def finish(step, carry):
+        copy_to(step).wait()
+        return carry
+
+    lax.fori_loop(1, size, greet, 0)
+    mine = pltpu.make_async_copy(
+        source.at[place] if spread else source, target.at[place], local_sem
+    )
+    mine.start()
+    pl.semaphore_wait(barrier, size - 1)
+    lax.fori_loop(1, size, begin, 0)
+    mine.wait()
+    lax.fori_loop(1, size, finish, 0)
+
+
+def exchange(values, group, spread, call_id):
+    if group == "all":
+        size = lax.axis_size("dp") * lax.axis_size("tensor")
+    else:
+        size = lax.axis_size(group)
+    block = values.shape[1:] if spread else values.shape
+    return pl.pallas_call(
+        functools.partial(exchange_kernel, group, spread),
+        out_shape=jax.ShapeDtypeStruct((size,) + block, values.dtype),
+        in_specs=[pl.BlockSpec(memory_space=pltpu.VMEM)],
+        out_specs=pl.BlockSpec(memory_space=pltpu.VMEM),
+        scratch_shapes=[
+            pltpu.SemaphoreType.DMA((size,)),
+            pltpu.SemaphoreType.DMA((size,)),
+            pltpu.SemaphoreType.DMA,
+        ],
+        compiler_params=pltpu.CompilerParams(
+            collective_id=call_id, has_side_effects=True, vmem_limit_bytes=32 * 2**20
+        ),
+        name="exchange_" + group,
+    )(values)
 
 
 def gather_tokens(values):
@@ -162,38 +236,84 @@
     layer_rows = 10 + FF // D
     head_shape = (images, tokens_all, heads_local, HEAD_DIM)
     flat_shape = (images, tokens_all, group_width)
-    table = lax.all_gather(embed_table.astype(jnp.bfloat16), ("dp", "tensor"), axis=1, tiled=True)
-    mod_weights = lax.all_gather(layer_ada.astype(jnp.bfloat16), "dp", axis=1, tiled=True)
-
-    def table_block(row_start, row_count):
-        return table[row_start : row_start + row_count].astype(jnp.float32)
-
-    vectors = table_block(vector_start, 5)
-    time_feats = time_features(timesteps)
-    onehot = (labels[:, None] == jnp.arange(CLASSES, dtype=jnp.int32)[None, :]).astype(jnp.float32)
-    time_w = table_block(time_start, FREQ)
-    second_w = table_block(second_start, D)
-    shift_w = table_block(final_start, D)
-    scale_w = table_block(final_start + D, D)
-    pre_time = dense(time_feats, time_w) + vectors[1]
-    hidden = jax.nn.silu(pre_time)
-    pre_signal = dense(hidden, second_w) + vectors[2] + dense(onehot, table_block(0, CLASSES))
-    signal = jax.nn.silu(pre_signal)
-    final_shift = dense(signal, shift_w) + vectors[3]
-    final_scale = dense(signal, scale_w) + vectors[4]
-    signal_low = signal.astype(jnp.bfloat16)
-    mod_local = jnp.einsum(
-        "bd,lde->lbe", signal_low, mod_weights, preferred_element_type=jnp.float32
-    )
-    mod_full = lax.all_gather(mod_local.astype(jnp.bfloat16), "tensor", axis=2, tiled=True).astype(
-        mod_local.dtype
-    )
+    dp_rank = lax.axis_index("dp")
+    dp_size = lax.axis_size("dp")
+    place_count = dp_size * tensor_size
+    images_all = images * dp_size
+    table_cols = embed_table.T.astype(jnp.bfloat16).astype(jnp.float32)
+    cols = table_cols.shape[0]
+    mod_rows = layer_ada.shape[1]
+    mod_cols = layer_ada.shape[2]
+    mod_low = layer_ada.astype(jnp.bfloat16)
+
+    def col_block(row_start, row_count):
+        return table_cols[:, row_start : row_start + row_count]
+
+    vector_count = 5 + LAYERS * layer_rows
+    small_count = 2 * patch_in + vector_count
+    lanes = -(-(small_count + 2 * images) // 128) * 128
+    scalar_lanes = jnp.concatenate([timesteps, labels]).astype(jnp.float32)
+    small_send = jnp.concatenate(
+        [
+            col_block(patch_start, patch_in),
+            col_block(head_start, patch_in + vector_count),
+            jnp.broadcast_to(scalar_lanes[None, :], (cols, 2 * images)),
+            jnp.zeros((cols, lanes - small_count - 2 * images), jnp.float32),
+        ],
+        axis=1,
+    )
+    small_all = exchange(small_send, "all", False, 1)
+    small_rows = small_all.reshape(D, lanes).T
+    patch_w = small_rows[0:patch_in]
+    head_w = small_rows[patch_in : 2 * patch_in]
+    vectors = small_rows[2 * patch_in : 2 * patch_in + 5]
+    bias_all = small_rows[2 * patch_in + 5 : small_count]
+    scalars_all = small_all[::tensor_size, 0, small_count : small_count + 2 * images].astype(
+        jnp.int32
+    )
+    timesteps_all = scalars_all[:, :images].reshape(images_all)
+    labels_all = scalars_all[:, images:].reshape(images_all)
+    time_feats = time_features(timesteps_all)
+    onehot = (labels_all[:, None] == jnp.arange(CLASSES, dtype=jnp.int32)[None, :]).astype(
+        jnp.float32
+    )
+    pre_time = dense(col_block(time_start, FREQ), time_feats.T) + col_block(vector_start + 1, 1)
+    hidden = exchange(jax.nn.silu(pre_time), "all", False, 2).reshape(D, images_all)
+    second_cols = col_block(second_start, D)
+    shift_cols = col_block(final_start, D)
+    scale_cols = col_block(final_start + D, D)
+    pre_signal = (
+        dense(second_cols, hidden)
+        + col_block(vector_start + 2, 1)
+        + dense(col_block(0, CLASSES), onehot.T)
+    )
+    signal = exchange(jax.nn.silu(pre_signal), "all", False, 3).reshape(D, images_all)
+    final_send = jnp.concatenate(
+        [
+            dense(shift_cols, signal) + col_block(vector_start + 3, 1),
+            dense(scale_cols, signal) + col_block(vector_start + 4, 1),
+        ],
+        axis=0,
+    )
+    final_all = exchange(final_send, "all", False, 4).reshape(place_count, 2, cols, images_all)
+    final_own = lax.dynamic_slice_in_dim(final_all, dp_rank * images, images, 3)
+    final_own = final_own.transpose(1, 3, 0, 2).reshape(2, images, D)
+    final_shift, final_scale = final_own[0], final_own[1]
+    signal_low = lax.dynamic_slice_in_dim(
+        signal.astype(jnp.bfloat16), dp_rank * mod_rows, mod_rows, 0
+    )
+    mod_part = jnp.einsum("db,lde->ble", signal_low, mod_low, preferred_element_type=jnp.float32)
+    mod_part = mod_part.reshape(dp_size, images * LAYERS, mod_cols)
+    mod_local = jnp.sum(exchange(mod_part, "dp", True, 5), axis=0)
+    mod_full = exchange(mod_local, "tensor", False, 6)
+    mod_full = mod_full.reshape(tensor_size, images, LAYERS, mod_cols)
+    mod_full = mod_full.transpose(2, 1, 0, 3).reshape(LAYERS, images, tensor_size * mod_cols)
     pixels = patchify(latents, local_rows)
     targets = patchify(target_noise, local_rows)
     keep_coef, drop_coef = noise_levels(timesteps)
     noisy = keep_coef[:, None, None] * pixels + drop_coef[:, None, None] * targets
     residual = (
-        jnp.einsum("btp,pd->btd", noisy, table_block(patch_start, patch_in), precision=PRECISE)
+        jnp.einsum("btp,pd->btd", noisy, patch_w, precision=PRECISE)
         + vectors[0]
         + position_table(tensor_rank * local_rows, local_rows)[None]
     )
@@ -215,7 +335,7 @@
                 tiled=True,
             ),
         )
-        bias_rows = table_block(layer_start + layer_idx * layer_rows, layer_rows)
+        bias_rows = bias_all[layer_idx * layer_rows : (layer_idx + 1) * layer_rows]
         up_all = bias_rows[10:].reshape(FF)
         ada_bias = bias_rows[0:6].reshape(6 * D)
         out_bias = bias_rows[6]
@@ -297,40 +417,25 @@
                 act_low,
                 down_out,
                 gate_m,
+                w_qkv,
+                w_up,
+                w_attn,
+                w_down,
             )
         )
     final_in, final_norm_pull = jax.vjp(modulate, residual, final_shift, final_scale)
-    head_w = table_block(head_start, patch_in)
     predicted = jnp.einsum("btd,pd->btp", final_in, head_w, precision=PRECISE)
     error_all = predicted - targets
     loss_part = jnp.sum(error_all * error_all) / count_all
-    loss_value = lax.psum(loss_part, ("dp", "tensor"))
     d_pred = 2.0 * error_all / count_all
     d_head = jnp.einsum("btp,btd->pd", d_pred, final_in, precision=PRECISE)
     d_final = jnp.einsum("btp,pd->btd", d_pred, head_w, precision=PRECISE)
     d_residual, d_final_shift, d_final_scale = final_norm_pull(d_final)
-    d_signal = jnp.zeros((images, D), jnp.float32)
     grads_in = []
     grads_out = []
-    grads_mod = []
+    mod_parts = []
     bias_blocks = []
     for layer_idx in reversed(range(LAYERS)):
-        weight_in, weight_out = (
-            lax.all_gather(
-                layer_in[layer_idx]
-                .astype(jnp.bfloat16)
-                .reshape(layer_in.shape[1], layer_in.shape[3]),
-                "dp",
-                axis=0,
-                tiled=True,
-            ),
-            lax.all_gather(
-                layer_out[layer_idx].astype(jnp.bfloat16).reshape(layer_out.shape[2], D),
-                "dp",
-                axis=0,
-                tiled=True,
-            ),
-        )
         (
             norm_pull_a,
             rows_a,
@@ -347,11 +452,11 @@
             act_low,
             down_out,
             gate_m,
+            w_qkv,
+            w_up,
+            w_attn,
+            w_down,
         ) = saved_acts[layer_idx]
-        w_qkv = weight_in[:, : 3 * group_width]
-        w_up = weight_in[:, 3 * group_width :]
-        w_attn = weight_out[:group_width]
-        w_down = weight_out[group_width:]
         d_gate_m = jnp.sum(d_residual * down_out, axis=1)
         d_down = d_residual * gate_m[:, None, :]
         d_down_bias = jnp.sum(d_down, axis=(0, 1))
@@ -425,27 +530,23 @@
         d_modulation = jnp.concatenate(
             [d_shift_a, d_scale_a, d_gate_a, d_shift_m, d_scale_m, d_gate_m], axis=1
         )
-        d_mod_local = lax.psum_scatter(
-            d_modulation, "tensor", scatter_dimension=1, tiled=True
-        ).astype(jnp.bfloat16)
-        d_signal = d_signal + jnp.einsum(
-            "be,de->bd", d_mod_local, mod_weights[layer_idx], preferred_element_type=jnp.float32
-        )
-        d_w_ada = jnp.einsum(
-            "bd,be->de", signal_low, d_mod_local, preferred_element_type=jnp.float32
-        )
-        grad_in, grad_out, grad_ada = (
+        mod_parts.insert(0, d_modulation)
+        grad_in, grad_out = (
             lax.psum_scatter(
-                jnp.concatenate([d_w_qkv, d_w_up], axis=1), "dp", scatter_dimension=0, tiled=True
-            ),
+                jnp.concatenate([d_w_qkv, d_w_up], axis=1).astype(jnp.bfloat16),
+                "dp",
+                scatter_dimension=0,
+                tiled=True,
+            ).astype(jnp.float32),
             lax.psum_scatter(
-                jnp.concatenate([d_w_attn, d_w_down], axis=0), "dp", scatter_dimension=0, tiled=True
-            ),
-            lax.psum_scatter(d_w_ada, "dp", scatter_dimension=0, tiled=True),
+                jnp.concatenate([d_w_attn, d_w_down], axis=0).astype(jnp.bfloat16),
+                "dp",
+                scatter_dimension=0,
+                tiled=True,
+            ).astype(jnp.float32),
         )
         grads_in.insert(0, grad_in)
         grads_out.insert(0, grad_out)
-        grads_mod.insert(0, grad_ada)
         query_row = lax.dynamic_update_slice_in_dim(
             jnp.zeros((D,), jnp.float32), d_query_bias, tensor_rank * group_width, 0
         )
@@ -469,51 +570,84 @@
                 axis=0,
             ),
         )
-    d_signal_total = d_signal + dense(d_final_shift, shift_w.T) + dense(d_final_scale, scale_w.T)
-    d_pre_signal = d_signal_total * silu_slope(pre_signal)
-    d_hidden = dense(d_pre_signal, second_w.T) * silu_slope(pre_time)
     d_patch_w = jnp.einsum("btp,btd->pd", noisy, d_residual, precision=PRECISE)
     d_patch_b = jnp.sum(d_residual, axis=(0, 1))
-    vector_grads = jnp.stack(
+    row_parts = jnp.concatenate(
+        [d_patch_w, d_head, d_patch_b[None]] + bias_blocks + [d_final_shift, d_final_scale],
+        axis=0,
+    )
+    row_count = row_parts.shape[0]
+    row_lanes = -(-row_count // 128) * 128
+    row_parts = jnp.pad(row_parts, ((0, row_lanes - row_count), (0, 0)))
+    row_all = exchange(row_parts.T.reshape(place_count, cols, row_lanes), "all", True, 7)
+    row_sums = jnp.sum(row_all, axis=0)
+    final_at = row_count - 2 * images
+    final_sums = jnp.sum(
+        row_all[:, :, final_at:row_count].reshape(dp_size, tensor_size, cols, 2, images), axis=1
+    )
+    final_sums = final_sums.transpose(2, 1, 0, 3).reshape(2, cols, images_all)
+    d_shift_cols, d_scale_cols = final_sums[0], final_sums[1]
+    mod_parts = jnp.stack(mod_parts).reshape(LAYERS * images, tensor_size, mod_cols)
+    d_mod_own = jnp.sum(exchange(mod_parts.transpose(1, 0, 2), "tensor", True, 8), axis=0)
+    d_mod_low = exchange(d_mod_own.astype(jnp.bfloat16), "dp", False, 9)
+    d_mod_low = d_mod_low.reshape(dp_size, LAYERS, images, mod_cols)
+    d_mod_low = d_mod_low.transpose(1, 0, 2, 3).reshape(LAYERS, images_all, mod_cols)
+    mod_grad = jnp.einsum(
+        "db,lbe->lde", signal_low, d_mod_low, preferred_element_type=jnp.float32
+    )
+    d_signal_rows = jnp.einsum(
+        "lbe,lde->db", d_mod_low, mod_low, preferred_element_type=jnp.float32
+    )
+    d_signal_part = dense(shift_cols.T, d_shift_cols) + dense(scale_cols.T, d_scale_cols)
+    d_signal_part = d_signal_part + lax.dynamic_update_slice_in_dim(
+        jnp.zeros((D, images_all), jnp.float32), d_signal_rows, dp_rank * mod_rows, 0
+    )
+    d_signal_cols = jnp.sum(
+        exchange(d_signal_part.reshape(place_count, cols, images_all), "all", True, 10), axis=0
+    )
+    d_pre_signal = d_signal_cols * silu_slope(pre_signal)
+    d_hidden_part = dense(second_cols.T, d_pre_signal)
+    d_hidden_cols = jnp.sum(
+        exchange(d_hidden_part.reshape(place_count, cols, images_all), "all", True, 11), axis=0
+    )
+    d_hidden = d_hidden_cols * silu_slope(pre_time)
+    table_grad = jnp.concatenate(
         [
-            d_patch_b,
-            jnp.sum(d_hidden, axis=0),
-            jnp.sum(d_pre_signal, axis=0),
-            jnp.sum(d_final_shift, axis=0),
-            jnp.sum(d_final_scale, axis=0),
-        ]
-    )
-    grad_table = jnp.concatenate(
-        [
-            dense(onehot.T, d_pre_signal),
-            d_patch_w,
-            dense(time_feats.T, d_hidden),
-            dense(hidden.T, d_pre_signal),
-            dense(signal.T, d_final_shift),
-            dense(signal.T, d_final_scale),
-            d_head,
-            vector_grads,
-        ]
-        + bias_blocks,
-        axis=0,
-    )
-    table_grad = lax.psum_scatter(grad_table, ("dp", "tensor"), scatter_dimension=1, tiled=True)
+            dense(d_pre_signal, onehot),
+            row_sums[:, 0:patch_in],
+            dense(d_hidden, time_feats),
+            dense(d_pre_signal, hidden.T),
+            dense(d_shift_cols, signal.T),
+            dense(d_scale_cols, signal.T),
+            row_sums[:, patch_in : 2 * patch_in + 1],
+            jnp.sum(d_hidden, axis=1, keepdims=True),
+            jnp.sum(d_pre_signal, axis=1, keepdims=True),
+            jnp.sum(d_shift_cols, axis=1, keepdims=True),
+            jnp.sum(d_scale_cols, axis=1, keepdims=True),
+            row_sums[:, 2 * patch_in + 1 : final_at],
+        ],
+        axis=1,
+    )
     input_grad = jnp.stack(grads_in).reshape(layer_in.shape)
     output_grad = jnp.stack(grads_out).reshape(layer_out.shape)
-    mod_grad = jnp.stack(grads_mod)
     local_squares = (
         jnp.sum(table_grad * table_grad)
         + jnp.sum(input_grad * input_grad)
         + jnp.sum(output_grad * output_grad)
         + jnp.sum(mod_grad * mod_grad)
     )
-    square_total = lax.psum(local_squares, ("dp", "tensor"))
+    scalar_send = jnp.where(
+        lax.broadcasted_iota(jnp.int32, (8, 128), 1) == 0, loss_part, local_squares
+    )
+    scalar_sums = jnp.sum(exchange(scalar_send, "all", False, 12)[:, 0, 0:2], axis=0)
+    loss_value = scalar_sums[0]
+    square_total = scalar_sums[1]
     grad_norm = jnp.sqrt(square_total)
     factor = jnp.minimum(1.0, CLIP_NORM / grad_norm)
     first_fix = 1.0 - BETA_ONE ** step_count.astype(jnp.float32)
     second_fix = 1.0 - BETA_TWO ** step_count.astype(jnp.float32)
     embed_out = adam_update(
-        embed_table, embed_first, embed_second, table_grad, factor, first_fix, second_fix
+        embed_table.T, embed_first.T, embed_second.T, table_grad, factor, first_fix, second_fix
     )
     input_out = adam_update(
         layer_in, input_first, input_second, input_grad, factor, first_fix, second_fix
@@ -523,7 +657,7 @@
     )
     mod_out = adam_update(layer_ada, mod_first, mod_second, mod_grad, factor, first_fix, second_fix)
     return (
-        (loss_value, grad_norm, embed_out[4], embed_out[1], embed_out[2])
+        (loss_value, grad_norm, embed_out[4].T, embed_out[1].T, embed_out[2].T)
         + input_out[0:4]
         + output_out[0:4]
         + mod_out[0:4]

time: 2300 us -> 1500 us (0.65)
  waiting for transfers between devices: 1730 us -> 962 us
  Pallas kernels: 0 us -> 173 us
  local copies, waits for them, and re-layouts: 201 us -> 115 us
  matrix products: 174 us -> 126 us
  blocking collectives: 45.8 us -> 0 us
  other arithmetic: 115 us -> 84.9 us
    reduce_scatter x9 -> x3, waiting for transfers between devices: 635 us -> 131 us  [local(): lax.psum_scatter(jnp.concatenate([d_w_attn, d_w_down], axis=0).astype(jnp...]
    pallas_call x0 -> x12, Pallas kernels: none -> 173 us  [exchange(): pl.pallas_call(functools.partial(exchange_kernel, group, spread), out_sha...]
    all_gather x2 -> x0, waiting for transfers between devices: 146 us -> none  [the longest x1 80.4 us: local(): lax.all_gather(layer_ada.astype(jnp.bfloat16), 'dp', axis=1, tiled=True)]
    unnamed x49 -> x39, waiting for transfers between devices: 243 us -> 164 us
    concatenate x1 -> x4, local copies, waits for them, and re-layouts: 45.1 us -> 0.94 us  [the longest x1 0.58 us: local(): jnp.concatenate([d_patch_w, d_head, d_patch_b[None]] + bias_blocks + [d_f...]
    psum x1 -> x0, blocking collectives: 40.4 us -> none  [local(): loss_value = lax.psum(loss_part, ('dp', 'tensor'))]
    all_gather x3, waiting for transfers between devices: 131 us -> 95.7 us  [local(): lax.all_gather(layer_in[layer_idx].astype(jnp.bfloat16).reshape(layer_in....]
    dot_general x13, matrix products: 33.4 us -> 4.8 us  [dense(): jnp.dot(left_op, right_op, precision=PRECISE, preferred_element_type=jnp....]
  transfers between devices with their start and end apart: 45 -> 36, of which waited for: 43 -> 33; matrix products, arithmetic and copies ran while one was open for 13% -> 10% of each run, Pallas kernels for 0% -> 11%
where the time goes in v1:
time: 1500 us; the launch traced here: 1490 us
  waiting for transfers between devices  962 us (64%)
  Pallas kernels  173 us (12%)
  matrix products  126 us (8%)
  local copies, waits for them, and re-layouts  115 us (8%)
  other arithmetic  84.9 us (6%)
  between operations  24.3 us (2%)
    reduce_scatter x12, waiting for transfers between devices, sum_tokens(): lax.psum_scatter(values.astype(jnp.bfloat16), 'tensor', scatter_dimension...  266 us
    all_gather x12, waiting for transfers between devices, gather_tokens(): return lax.all_gather(values, 'tensor', axis=1, tiled=True)  185 us
    pallas_call x12, Pallas kernels, exchange(): pl.pallas_call(functools.partial(exchange_kernel, group, spread), out_sha...  173 us
    unnamed x39, waiting for transfers between devices  164 us
    reduce_scatter x3, waiting for transfers between devices, local(): lax.psum_scatter(jnp.concatenate([d_w_attn, d_w_down], axis=0).astype(jnp...  131 us
    all_gather x3, waiting for transfers between devices, local(): lax.all_gather(layer_out[layer_idx].astype(jnp.bfloat16).reshape(layer_ou...  120 us
    all_gather x3, waiting for transfers between devices, local(): lax.all_gather(layer_in[layer_idx].astype(jnp.bfloat16).reshape(layer_in....  95.7 us
    unnamed x557, local copies, waits for them, and re-layouts  75.4 us
  transfers between devices with their start and end apart: 36, of which 33 were waited for; matrix products, arithmetic and copies ran while one was open for 10% of the time, Pallas kernels for 11%

profile of v1, /device:TPU:0, one launch (start us, length us, event | category | flops | bytes accessed | tf_op | source)
XLA Modules:
  0.0 1487.4 jit_solution(10538842363409195180)
XLA Ops:
  10.4 16.8 %exchange_all.8 = f32[32,24,128]{2,1,0:T(8,128)S(1)} custom-call(f32[24,128]{1,0:T(8,128)S(1)} %maximum_maximum_fusion.source), custom_call_target="tpu_custom_call" | custom-call | tf_op jit(solution)/shard_map/exchange_all/pallas_call | solution.py:165
  29.3 19.6 %exchange_all.9 = f32[32,24,24]{2,1,0:T(8,128)S(1)} custom-call(f32[24,24]{1,0:T(8,128)S(1)} %get-tuple-element.238.source), custom_call_target="tpu_custom_call" | custom-call | tf_op jit(solution)/shard_map/exchange_all/pallas_call | solution.py:165
  50.0 19.7 %exchange_all.10 = f32[32,24,24]{2,1,0:T(8,128)S(1)} custom-call(f32[24,24]{1,0:T(8,128)S(1)} %get-tuple-element.240.source), custom_call_target="tpu_custom_call" | custom-call | tf_op jit(solution)/shard_map/exchange_all/pallas_call | solution.py:165
  70.4 17.8 %exchange_dp.2 = f32[8,9,1152]{2,1,0:T(8,128)S(1)} custom-call(f32[8,9,1152]{2,1,0:T(8,128)S(1)} %reshape.910.source), custom_call_target="tpu_custom_call" | custom-call | tf_op jit(solution)/shard_map/exchange_dp/pallas_call | solution.py:165
  88.2 5.4 exchange_tensor.2
  106.6 17.5 %all-gather.25.cloned.1.call-done = bf16[3,256,768]{2,1,0:T(8,128)(2,1)} async-done(((bf16[3,64,768]{2,1,0:T(8,128)(2,1)}), bf16[3,256,768]{2,1,0:T(8,128)(2,1)}) %all-gather.25.cloned.1.call-update) | async-done | bytes 1179664 | tf_op jit(solution)/shard_map/all_gather | solution.py:183
  130.0 40.4 %all-gather.51.cloned.1.call-done = bf16[1,1,960,768]{3,2,1,0:T(8,128)(2,1)} async-done(((bf16[1,1,120,768]{3,2,1,0:T(8,128)(2,1)}), bf16[1,1,960,768]{3,2,1,0:T(8,128)(2,1)}) %all-gather.51.cloned.1.call-update) | async-done | bytes 1474576 | tf_op jit(solution)/shard_map/all_gather | solution.py:331
  173.1 24.4 %reduce-scatter.25.cloned.1.call-done = bf16[3,64,768]{2,1,0:T(8,128)(2,1)} async-done(((bf16[3,256,768]{2,1,0:T(8,128)(2,1)}), bf16[3,64,768]{2,1,0:T(8,128)(2,1)}) %reduce-scatter.25.cloned.1.call-update) | async-done | bytes 294928 | tf_op jit(solution)/shard_map/reduce_scatter | solution.py:187
  202.6 16.0 %all-gather.27.cloned.1.call-done = bf16[3,256,768]{2,1,0:T(8,128)(2,1)} async-done(((bf16[3,64,768]{2,1,0:T(8,128)(2,1)}), bf16[3,256,768]{2,1,0:T(8,128)(2,1)}) %all-gather.27.cloned.1.call-update) | async-done | bytes 1179664 | tf_op jit(solution)/shard_map/all_gather | solution.py:183
  231.2 20.3 %reduce-scatter.27.cloned.1.call-done = bf16[3,64,768]{2,1,0:T(8,128)(2,1)} async-done(((bf16[3,256,768]{2,1,0:T(8,128)(2,1)}), bf16[3,64,768]{2,1,0:T(8,128)(2,1)}) %reduce-scatter.27.cloned.1.call-update) | async-done | bytes 294928 | tf_op jit(solution)/shard_map/reduce_scatter | solution.py:187
  256.4 47.8 %all-gather.53.cloned.1.call-done = bf16[1,768,1,1344]{3,1,2,0:T(8,128)(2,1)} async-done(((bf16[1,96,1,1344]{3,1,2,0:T(8,128)(2,1)}), bf16[1,768,1,1344]{3,1,2,0:T(8,128)(2,1)}) %all-gather.53.cloned.1.call-update) | async-done | bytes 2064400 | tf_op jit(solution)/shard_map/all_gather | solution.py:323
  304.2 4.1 copy.157
  308.3 14.0 all-gather.29.cloned.1.call-done
  329.0 39.7 %all-gather.55.cloned.1.call-done = bf16[1,1,960,768]{3,2,1,0:T(8,128)(2,1)} async-done(((bf16[1,1,120,768]{3,2,1,0:T(8,128)(2,1)}), bf16[1,1,960,768]{3,2,1,0:T(8,128)(2,1)}) %all-gather.55.cloned.1.call-update) | async-done | bytes 1474576 | tf_op jit(solution)/shard_map/all_gather | solution.py:331
  371.3 24.4 %reduce-scatter.29.cloned.1.call-done = bf16[3,64,768]{2,1,0:T(8,128)(2,1)} async-done(((bf16[3,256,768]{2,1,0:T(8,128)(2,1)}), bf16[3,64,768]{2,1,0:T(8,128)(2,1)}) %reduce-scatter.29.cloned.1.call-update) | async-done | bytes 294928 | tf_op jit(solution)/shard_map/reduce_scatter | solution.py:187
  400.0 16.8 %all-gather.31.cloned.1.call-done = bf16[3,256,768]{2,1,0:T(8,128)(2,1)} async-done(((bf16[3,64,768]{2,1,0:T(8,128)(2,1)}), bf16[3,256,768]{2,1,0:T(8,128)(2,1)}) %all-gather.31.cloned.1.call-update) | async-done | bytes 1179664 | tf_op jit(solution)/shard_map/all_gather | solution.py:183
  428.9 20.7 %reduce-scatter.31.cloned.1.call-done = bf16[3,64,768]{2,1,0:T(8,128)(2,1)} async-done(((bf16[3,256,768]{2,1,0:T(8,128)(2,1)}), bf16[3,64,768]{2,1,0:T(8,128)(2,1)}) %reduce-scatter.31.cloned.1.call-update) | async-done | bytes 294928 | tf_op jit(solution)/shard_map/reduce_scatter | solution.py:187
  454.5 47.9 %all-gather.57.cloned.1.call-done = bf16[1,768,1,1344]{3,1,2,0:T(8,128)(2,1)} async-done(((bf16[1,96,1,1344]{3,1,2,0:T(8,128)(2,1)}), bf16[1,768,1,1344]{3,1,2,0:T(8,128)(2,1)}) %all-gather.57.cloned.1.call-update) | async-done | bytes 2064400 | tf_op jit(solution)/shard_map/all_gather | solution.py:323
  502.4 4.2 copy.160
  506.6 13.8 all-gather.33.cloned.1.call-done
  527.0 39.6 %all-gather.59.cloned.1.call-done = bf16[1,1,960,768]{3,2,1,0:T(8,128)(2,1)} async-done(((bf16[1,1,120,768]{3,2,1,0:T(8,128)(2,1)}), bf16[1,1,960,768]{3,2,1,0:T(8,128)(2,1)}) %all-gather.59.cloned.1.call-update) | async-done | bytes 1474576 | tf_op jit(solution)/shard_map/all_gather | solution.py:331
  569.3 24.4 %reduce-scatter.33.cloned.1.call-done = bf16[3,64,768]{2,1,0:T(8,128)(2,1)} async-done(((bf16[3,256,768]{2,1,0:T(8,128)(2,1)}), bf16[3,64,768]{2,1,0:T(8,128)(2,1)}) %reduce-scatter.33.cloned.1.call-update) | async-done | bytes 294928 | tf_op jit(solution)/shard_map/reduce_scatter | solution.py:187
  598.2 16.6 %all-gather.35.cloned.1.call-done = bf16[3,256,768]{2,1,0:T(8,128)(2,1)} async-done(((bf16[3,64,768]{2,1,0:T(8,128)(2,1)}), bf16[3,256,768]{2,1,0:T(8,128)(2,1)}) %all-gather.35.cloned.1.call-update) | async-done | bytes 1179664 | tf_op jit(solution)/shard_map/all_gather | solution.py:183
  622.3 18.2 %exchange_all.11 = f32[32,48,24]{2,1,0:T(8,128)S(1)} custom-call(f32[48,24]{1,0:T(8,128)S(1)} %pad_maximum_fusion.20.source), custom_call_target="tpu_custom_call" | custom-call | tf_op jit(solution)/shard_map/exchange_all/pallas_call | solution.py:165
  644.1 3.6 reduce-scatter.35.cloned.1.call-done
  656.3 21.4 %all-gather.37.cloned.1.call-done = bf16[3,256,768]{2,1,0:T(8,128)(2,1)} async-done(((bf16[3,64,768]{2,1,0:T(8,128)(2,1)}), bf16[3,256,768]{2,1,0:T(8,128)(2,1)}) %all-gather.37.cloned.1.call-update) | async-done | bytes 1179664 | tf_op jit(solution)/shard_map/all_gather | solution.py:183
  677.7 5.4 fusion.206
  686.4 25.8 %reduce-scatter.37.cloned.1.call-done = bf16[3,64,768]{2,1,0:T(8,128)(2,1)} async-done(((bf16[3,256,768]{2,1,0:T(8,128)(2,1)}), bf16[3,64,768]{2,1,0:T(8,128)(2,1)}) %reduce-scatter.37.cloned.1.call-update) | async-done | bytes 294928 | tf_op jit(solution)/shard_map/reduce_scatter | solution.py:187
  718.9 17.3 %all-gather.39.cloned.1.call-done = bf16[3,256,768]{2,1,0:T(8,128)(2,1)} async-done(((bf16[3,64,768]{2,1,0:T(8,128)(2,1)}), bf16[3,256,768]{2,1,0:T(8,128)(2,1)}) %all-gather.39.cloned.1.call-update) | async-done | bytes 1179664 | tf_op jit(solution)/shard_map/all_gather | solution.py:183
  745.1 3.4 convolution_convert_fusion.4
  748.5 25.8 %reduce-scatter.39.cloned.1.call-done = bf16[3,64,768]{2,1,0:T(8,128)(2,1)} async-done(((bf16[3,256,768]{2,1,0:T(8,128)(2,1)}), bf16[3,64,768]{2,1,0:T(8,128)(2,1)}) %reduce-scatter.39.cloned.1.call-update) | async-done | bytes 294928 | tf_op jit(solution)/shard_map/reduce_scatter | solution.py:187
  780.7 17.6 %all-gather.41.cloned.1.call-done = bf16[3,256,768]{2,1,0:T(8,128)(2,1)} async-done(((bf16[3,64,768]{2,1,0:T(8,128)(2,1)}), bf16[3,256,768]{2,1,0:T(8,128)(2,1)}) %all-gather.41.cloned.1.call-update) | async-done | bytes 1179664 | tf_op jit(solution)/shard_map/all_gather | solution.py:183
  798.3 5.4 fusion.205
  806.9 25.8 %reduce-scatter.41.cloned.1.call-done = bf16[3,64,768]{2,1,0:T(8,128)(2,1)} async-done(((bf16[3,256,768]{2,1,0:T(8,128)(2,1)}), bf16[3,64,768]{2,1,0:T(8,128)(2,1)}) %reduce-scatter.41.cloned.1.call-update) | async-done | bytes 294928 | tf_op jit(solution)/shard_map/reduce_scatter | solution.py:187
  840.8 16.4 %all-gather.43.cloned.1.call-done = bf16[3,256,768]{2,1,0:T(8,128)(2,1)} async-done(((bf16[3,64,768]{2,1,0:T(8,128)(2,1)}), bf16[3,256,768]{2,1,0:T(8,128)(2,1)}) %all-gather.43.cloned.1.call-update) | async-done | bytes 1179664 | tf_op jit(solution)/shard_map/all_gather | solution.py:183
  866.1 3.4 convolution_convert_fusion.2
  869.6 25.8 %reduce-scatter.43.cloned.1.call-done = bf16[3,64,768]{2,1,0:T(8,128)(2,1)} async-done(((bf16[3,256,768]{2,1,0:T(8,128)(2,1)}), bf16[3,64,768]{2,1,0:T(8,128)(2,1)}) %reduce-scatter.43.cloned.1.call-update) | async-done | bytes 294928 | tf_op jit(solution)/shard_map/reduce_scatter | solution.py:187
  903.0 17.6 %all-gather.45.cloned.1.call-done = bf16[3,256,768]{2,1,0:T(8,128)(2,1)} async-done(((bf16[3,64,768]{2,1,0:T(8,128)(2,1)}), bf16[3,256,768]{2,1,0:T(8,128)(2,1)}) %all-gather.45.cloned.1.call-update) | async-done | bytes 1179664 | tf_op jit(solution)/shard_map/all_gather | solution.py:183
  920.6 5.4 fusion.204
  929.2 25.8 %reduce-scatter.45.cloned.1.call-done = bf16[3,64,768]{2,1,0:T(8,128)(2,1)} async-done(((bf16[3,256,768]{2,1,0:T(8,128)(2,1)}), bf16[3,64,768]{2,1,0:T(8,128)(2,1)}) %reduce-scatter.45.cloned.1.call-update) | async-done | bytes 294928 | tf_op jit(solution)/shard_map/reduce_scatter | solution.py:187
  965.9 4.2 copy.246
  975.6 4.1 copy.244
  986.9 3.3 convolution_convert_fusion
  990.3 3.5 bitcast_convert_fusion
  995.5 3.5 bitcast_convert_fusion.1
  1000.8 3.6 bitcast_convert_fusion.2
  1010.7 5.1 copy.198
  1024.6 25.5 %reduce-scatter.59.cloned.1.call-done = bf16[96,1344]{1,0:T(8,128)(2,1)} async-done(((bf16[768,1344]{1,0:T(8,128)(2,1)}), bf16[96,1344]{1,0:T(8,128)(2,1)}) %reduce-scatter.59.cloned.1.call-update) | async-done | bytes 258064
  1054.1 67.0 %reduce-scatter.57.cloned.1.call-done = bf16[96,1344]{1,0:T(8,128)(2,1)} async-done(((bf16[768,1344]{1,0:T(8,128)(2,1)}), bf16[96,1344]{1,0:T(8,128)(2,1)}) %reduce-scatter.57.cloned.1.call-update) | async-done | bytes 258064
  1130.0 19.1 %reduce-scatter.47.cloned.1.call-done = bf16[3,64,768]{2,1,0:T(8,128)(2,1)} async-done(((bf16[3,256,768]{2,1,0:T(8,128)(2,1)}), bf16[3,64,768]{2,1,0:T(8,128)(2,1)}) %reduce-scatter.47.cloned.1.call-update) | async-done | bytes 294928 | tf_op jit(solution)/shard_map/reduce_scatter | solution.py:187
  1155.1 14.2 exchange_all.12
  1169.8 5.8 exchange_tensor.3
  1175.7 15.6 %exchange_dp.3 = bf16[8,9,1152]{2,1,0:T(8,128)(2,1)S(1)} custom-call(bf16[9,1152]{1,0:T(8,128)(2,1)S(1)} %reduce_sum.989.source), custom_call_target="tpu_custom_call" | custom-call | tf_op jit(solution)/shard_map/exchange_dp/pallas_call | solution.py:165
  1193.4 13.8 exchange_all.13
  1207.8 17.0 %exchange_all.14 = f32[32,24,24]{2,1,0:T(8,128)S(1)} custom-call(f32[32,24,24]{2,1,0:T(8,128)S(1)} %bitcast.398), custom_call_target="tpu_custom_call" | custom-call | tf_op jit(solution)/shard_map/exchange_all/pallas_call | solution.py:165
  1230.1 64.9 %reduce-scatter.51.cloned.1.call-done = bf16[120,768]{1,0:T(8,128)(2,1)} async-done(((bf16[960,768]{1,0:T(8,128)(2,1)}), bf16[120,768]{1,0:T(8,128)(2,1)}) %reduce-scatter.51.cloned.1.call-update) | async-done | bytes 184336 | tf_op jit(solution)/shard_map/reduce_scatter | solution.py:541
  1295.0 66.4 %reduce-scatter.49.cloned.1.call-done = bf16[120,768]{1,0:T(8,128)(2,1)} async-done(((bf16[960,768]{1,0:T(8,128)(2,1)}), bf16[120,768]{1,0:T(8,128)(2,1)}) %reduce-scatter.49.cloned.1.call-update) | async-done | bytes 184336 | tf_op jit(solution)/shard_map/reduce_scatter | solution.py:541
  1363.4 68.5 %reduce-scatter.55.cloned.1.call-done = bf16[96,1344]{1,0:T(8,128)(2,1)} async-done(((bf16[768,1344]{1,0:T(8,128)(2,1)}), bf16[96,1344]{1,0:T(8,128)(2,1)}) %reduce-scatter.55.cloned.1.call-update) | async-done | bytes 258064
  1438.4 8.9 exchange_all.15
  1448.7 5.5 fusion.176
  1454.2 5.1 copy.202
  1459.2 5.2 copy.203
  1464.5 3.4 copy.204
  1470.3 4.4 fusion.174
  (930 shorter events, 249.6 us)
Async XLA Ops:
  7.2 96.6 %all-gather.49.cloned.1.call-start = ((), (), s32[]{:S(2)}) async-start(), calls=%async_computation.45 | async-start | bytes 2433024 | tf_op jit(solution)/shard_map/all_gather | solution.py:323
  9.8 60.1 %copy-start.24 = (f32[3,96,1152]{2,1,0:T(8,128)S(1)}, f32[3,96,1152]{2,1,0:T(8,128)}, u32[]{:S(2)}) copy-start(f32[3,96,1152]{2,1,0:T(8,128)} %param.25) | copy-start | bytes 3981316
  9.8 114.3 %all-gather.25.cloned.1.call-start = ((), (), s32[]{:S(2)}) async-start(), calls=%async_computation.18 | async-start | bytes 1474560 | tf_op jit(solution)/shard_map/all_gather | solution.py:183
  9.9 612.2 %copy-start.82 = (bf16[24,3640]{1,0:T(8,128)(2,1)}, bf16[24,3640]{1,0:T(8,128)(2,1)S(1)}, u32[]{:S(2)}) copy-start(bf16[24,3640]{1,0:T(8,128)(2,1)S(1)} %get-tuple-element.151) | copy-start | bytes 524164
  27.5 71.9 %copy-start.67 = (f32[768,128]{0,1:T(8,128)}, f32[768,128]{0,1:T(8,128)S(1)}, u32[]{:S(2)}) copy-start(f32[768,128]{0,1:T(8,128)S(1)} %copy.146) | copy-start | bytes 1179652
  28.5 41.3 %copy-start.168 = (f32[24,128]{1,0:T(8,128)}, f32[24,128]{1,0:T(8,128)S(1)}, u32[]{:S(2)}) copy-start(f32[24,128]{1,0:T(8,128)S(1)} %get-tuple-element.234) | copy-start | bytes 36868
  28.5 41.3 %copy-start.170 = (f32[24,128]{1,0:T(8,128)}, f32[24,128]{1,0:T(8,128)S(1)}, u32[]{:S(2)}) copy-start(f32[24,128]{1,0:T(8,128)S(1)} %get-tuple-element.235) | copy-start | bytes 36868
  100.2 97.3 %copy-start.6 = (f32[3,64,768]{2,1,0:T(8,128)}, f32[3,64,768]{2,1,0:T(8,128)S(1)}, u32[]{:S(2)}) copy-start(f32[3,64,768]{2,1,0:T(8,128)S(1)} %get-tuple-element.243) | copy-start | bytes 1769476
  101.1 98.4 %copy-start.90 = (f32[3,768]{1,0:T(4,128)}, f32[3,768]{1,0:T(4,128)S(1)}, u32[]{:S(2)}) copy-start(f32[3,768]{1,0:T(4,128)S(1)} %get-tuple-element.218) | copy-start | bytes 27652
  102.0 68.4 %all-gather.51.cloned.1.call-start = ((), (), s32[]{:S(2)}) async-start(), calls=%async_computation.46 | async-start | bytes 1658880 | tf_op jit(solution)/shard_map/all_gather | solution.py:331
  103.0 94.5 %reduce-scatter.25.cloned.1.call-start = ((), (), s32[]{:S(2)}) async-start(), calls=%async_computation.19 | async-start | bytes 1474560 | tf_op jit(solution)/shard_map/reduce_scatter | solution.py:187
  130.0 67.5 %copy-start.175 = (f32[768]{0:T(1024)S(1)}, f32[768]{0:T(1024)}, u32[]{:S(2)}) copy-start(f32[768]{0:T(1024)} %get-tuple-element.190) | copy-start | bytes 9220
  173.0 45.6 %all-gather.27.cloned.1.call-start = ((), (), s32[]{:S(2)}) async-start(), calls=%async_computation.20 | async-start | bytes 1474560 | tf_op jit(solution)/shard_map/all_gather | solution.py:183
  201.0 50.4 %reduce-scatter.27.cloned.1.call-start = ((), (), s32[]{:S(2)}) async-start(), calls=%async_computation.21 | async-start | bytes 1474560 | tf_op jit(solution)/shard_map/reduce_scatter | solution.py:187
  225.5 78.6 %all-gather.53.cloned.1.call-start = ((), (), s32[]{:S(2)}) async-start(), calls=%async_computation.47 | async-start | bytes 2433024 | tf_op jit(solution)/shard_map/all_gather | solution.py:323
  226.3 96.0 %all-gather.29.cloned.1.call-start = ((), (), s32[]{:S(2)}) async-start(), calls=%async_computation.22 | async-start | bytes 1474560 | tf_op jit(solution)/shard_map/all_gather | solution.py:183
  231.2 77.1 %copy-start.92 = (f32[3,768]{1,0:T(4,128)}, f32[3,768]{1,0:T(4,128)S(1)}, u32[]{:S(2)}) copy-start(f32[3,768]{1,0:T(4,128)S(1)} %get-tuple-element.216) | copy-start | bytes 27652
  252.6 55.7 %copy-start.132 = (f32[3,64]{1,0:T(4,128)}, f32[3,64]{1,0:T(4,128)S(1)}, u32[]{:S(2)}) copy-start(f32[3,64]{1,0:T(4,128)S(1)} %broadcast_multiply_fusion.4) | copy-start | bytes 2308
  254.9 113.8 %all-gather.55.cloned.1.call-start = ((), (), s32[]{:S(2)}) async-start(), calls=%async_computation.48 | async-start | bytes 1658880 | tf_op jit(solution)/shard_map/all_gather | solution.py:331
  255.6 140.1 %reduce-scatter.29.cloned.1.call-start = ((), (), s32[]{:S(2)}) async-start(), calls=%async_computation.23 | async-start | bytes 1474560 | tf_op jit(solution)/shard_map/reduce_scatter | solution.py:187
  329.0 66.8 %copy-start.12 = (f32[3,64,768]{2,1,0:T(8,128)S(1)}, f32[3,64,768]{2,1,0:T(8,128)}, u32[]{:S(2)}) copy-start(f32[3,64,768]{2,1,0:T(8,128)} %copy-done.11) | copy-start | bytes 1769476
  329.0 66.8 %copy-start.178 = (f32[768]{0:T(1024)S(1)}, f32[768]{0:T(1024)}, u32[]{:S(2)}) copy-start(f32[768]{0:T(1024)} %get-tuple-element.192) | copy-start | bytes 9220
  371.3 45.5 %all-gather.31.cloned.1.call-start = ((), (), s32[]{:S(2)}) async-start(), calls=%async_computation.24 | async-start | bytes 1474560 | tf_op jit(solution)/shard_map/all_gather | solution.py:183
  399.2 50.5 %reduce-scatter.31.cloned.1.call-start = ((), (), s32[]{:S(2)}) async-start(), calls=%async_computation.25 | async-start | bytes 1474560 | tf_op jit(solution)/shard_map/reduce_scatter | solution.py:187
  423.8 78.6 %all-gather.57.cloned.1.call-start = ((), (), s32[]{:S(2)}) async-start(), calls=%async_computation.49 | async-start | bytes 2433024 | tf_op jit(solution)/shard_map/all_gather | solution.py:323
  424.5 95.9 %all-gather.33.cloned.1.call-start = ((), (), s32[]{:S(2)}) async-start(), calls=%async_computation.26 | async-start | bytes 1474560 | tf_op jit(solution)/shard_map/all_gather | solution.py:183
  428.9 77.7 %copy-start.96 = (f32[3,768]{1,0:T(4,128)}, f32[3,768]{1,0:T(4,128)S(1)}, u32[]{:S(2)}) copy-start(f32[3,768]{1,0:T(4,128)S(1)} %get-tuple-element.210) | copy-start | bytes 27652
  450.8 55.8 %copy-start.136 = (f32[3,64]{1,0:T(4,128)}, f32[3,64]{1,0:T(4,128)S(1)}, u32[]{:S(2)}) copy-start(f32[3,64]{1,0:T(4,128)S(1)} %broadcast_multiply_fusion.2) | copy-start | bytes 2308
  453.1 113.5 %all-gather.59.cloned.1.call-start = ((), (), s32[]{:S(2)}) async-start(), calls=%async_computation.50 | async-start | bytes 1658880 | tf_op jit(solution)/shard_map/all_gather | solution.py:331
  453.7 140.0 %reduce-scatter.33.cloned.1.call-start = ((), (), s32[]{:S(2)}) async-start(), calls=%async_computation.27 | async-start | bytes 1474560 | tf_op jit(solution)/shard_map/reduce_scatter | solution.py:187
  527.0 66.7 %copy-start.18 = (f32[3,64,768]{2,1,0:T(8,128)S(1)}, f32[3,64,768]{2,1,0:T(8,128)}, u32[]{:S(2)}) copy-start(f32[3,64,768]{2,1,0:T(8,128)} %copy-done.17) | copy-start | bytes 1769476
  527.0 66.7 %copy-start.180 = (f32[768]{0:T(1024)S(1)}, f32[768]{0:T(1024)}, u32[]{:S(2)}) copy-start(f32[768]{0:T(1024)} %get-tuple-element.194) | copy-start | bytes 9220
  569.2 45.6 %all-gather.35.cloned.1.call-start = ((), (), s32[]{:S(2)}) async-start(), calls=%async_computation.28 | async-start | bytes 1474560 | tf_op jit(solution)/shard_map/all_gather | solution.py:183
  597.2 50.5 %reduce-scatter.35.cloned.1.call-start = ((), (), s32[]{:S(2)}) async-start(), calls=%async_computation.29 | async-start | bytes 1474560 | tf_op jit(solution)/shard_map/reduce_scatter | solution.py:187
  621.7 56.0 %all-gather.37.cloned.1.call-start = ((), (), s32[]{:S(2)}) async-start(), calls=%async_computation.30 | async-start | bytes 1474560 | tf_op jit(solution)/shard_map/all_gather | solution.py:183
  656.2 56.0 %reduce-scatter.37.cloned.1.call-start = ((), (), s32[]{:S(2)}) async-start(), calls=%async_computation.31 | async-start | bytes 1474560 | tf_op jit(solution)/shard_map/reduce_scatter | solution.py:187
  686.4 49.9 %all-gather.39.cloned.1.call-start = ((), (), s32[]{:S(2)}) async-start(), calls=%async_computation.32 | async-start | bytes 1474560 | tf_op jit(solution)/shard_map/all_gather | solution.py:183
  718.6 55.8 %reduce-scatter.39.cloned.1.call-start = ((), (), s32[]{:S(2)}) async-start(), calls=%async_computation.33 | async-start | bytes 1474560 | tf_op jit(solution)/shard_map/reduce_scatter | solution.py:187
  748.5 49.8 %all-gather.41.cloned.1.call-start = ((), (), s32[]{:S(2)}) async-start(), calls=%async_computation.34 | async-start | bytes 1474560 | tf_op jit(solution)/shard_map/all_gather | solution.py:183
  780.7 52.1 %reduce-scatter.41.cloned.1.call-start = ((), (), s32[]{:S(2)}) async-start(), calls=%async_computation.35 | async-start | bytes 1474560 | tf_op jit(solution)/shard_map/reduce_scatter | solution.py:187
  806.9 50.4 %all-gather.43.cloned.1.call-start = ((), (), s32[]{:S(2)}) async-start(), calls=%async_computation.36 | async-start | bytes 1474560 | tf_op jit(solution)/shard_map/all_gather | solution.py:183
  839.7 55.7 %reduce-scatter.43.cloned.1.call-start = ((), (), s32[]{:S(2)}) async-start(), calls=%async_computation.37 | async-start | bytes 1474560 | tf_op jit(solution)/shard_map/reduce_scatter | solution.py:187
  869.5 51.1 %all-gather.45.cloned.1.call-start = ((), (), s32[]{:S(2)}) async-start(), calls=%async_computation.38 | async-start | bytes 1474560 | tf_op jit(solution)/shard_map/all_gather | solution.py:183
  903.0 52.1 %reduce-scatter.45.cloned.1.call-start = ((), (), s32[]{:S(2)}) async-start(), calls=%async_computation.39 | async-start | bytes 1474560 | tf_op jit(solution)/shard_map/reduce_scatter | solution.py:187
  929.2 51.3 %all-gather.47.cloned.1.call-start = ((), (), s32[]{:S(2)}) async-start(), calls=%async_computation.40 | async-start | bytes 1474560 | tf_op jit(solution)/shard_map/all_gather | solution.py:183
  960.5 89.6 %reduce-scatter.59.cloned.1.call-start = ((), (), s32[]{:S(2)}) async-start(), calls=%async_computation.53 | async-start | bytes 2433024
  970.2 151.0 %reduce-scatter.57.cloned.1.call-start = ((), (), s32[]{:S(2)}) async-start(), calls=%async_computation.52 | async-start | bytes 2433024
  979.8 169.3 %reduce-scatter.47.cloned.1.call-start = ((), (), s32[]{:S(2)}) async-start(), calls=%async_computation.41 | async-start | bytes 1474560 | tf_op jit(solution)/shard_map/reduce_scatter | solution.py:187
  990.2 239.9 %reduce-scatter.53.cloned.1.call-start = ((), (), s32[]{:S(2)}) async-start(), calls=%async_computation.44 | async-start | bytes 1658880 | tf_op jit(solution)/shard_map/reduce_scatter | solution.py:541
  995.5 299.5 %reduce-scatter.51.cloned.1.call-start = ((), (), s32[]{:S(2)}) async-start(), calls=%async_computation.43 | async-start | bytes 1658880 | tf_op jit(solution)/shard_map/reduce_scatter | solution.py:541
  1000.7 360.7 %reduce-scatter.49.cloned.1.call-start = ((), (), s32[]{:S(2)}) async-start(), calls=%async_computation.42 | async-start | bytes 1658880 | tf_op jit(solution)/shard_map/reduce_scatter | solution.py:541
  1006.0 425.8 %reduce-scatter.55.cloned.1.call-start = ((), (), s32[]{:S(2)}) async-start(), calls=%async_computation.51 | async-start | bytes 2433024
  1015.9 36.5 %copy-start.160 = (f32[3,768]{1,0:T(4,128)S(1)}, f32[3,768]{1,0:T(4,128)}, u32[]{:S(2)}) copy-start(f32[3,768]{1,0:T(4,128)} %get-tuple-element.109) | copy-start | bytes 27652
  1015.9 36.5 %copy-start.159 = (f32[3,768]{1,0:T(4,128)S(1)}, f32[3,768]{1,0:T(4,128)}, u32[]{:S(2)}) copy-start(f32[3,768]{1,0:T(4,128)} %get-tuple-element.76) | copy-start | bytes 27652
  1015.9 36.6 %copy-start.156 = (f32[3,768]{1,0:T(4,128)S(1)}, f32[3,768]{1,0:T(4,128)}, u32[]{:S(2)}) copy-start(f32[3,768]{1,0:T(4,128)} %get-tuple-element.92) | copy-start | bytes 27652
  1015.9 36.6 %copy-start.155 = (f32[3,768]{1,0:T(4,128)S(1)}, f32[3,768]{1,0:T(4,128)}, u32[]{:S(2)}) copy-start(f32[3,768]{1,0:T(4,128)} %get-tuple-element.108) | copy-start | bytes 27652
  1015.9 36.6 %copy-start.154 = (f32[3,768]{1,0:T(4,128)S(1)}, f32[3,768]{1,0:T(4,128)}, u32[]{:S(2)}) copy-start(f32[3,768]{1,0:T(4,128)} %get-tuple-element.74) | copy-start | bytes 27652
  1016.0 36.6 %copy-start.152 = (f32[3,768]{1,0:T(4,128)S(1)}, f32[3,768]{1,0:T(4,128)}, u32[]{:S(2)}) copy-start(f32[3,768]{1,0:T(4,128)} %get-tuple-element.90) | copy-start | bytes 27652
  1016.0 36.7 %copy-start.208 = (f32[768]{0:T(1024)S(1)}, f32[768]{0:T(1024)}, u32[]{:S(2)}) copy-start(f32[768]{0:T(1024)} %get-tuple-element.93) | copy-start | bytes 9220
  1016.0 37.3 %copy-start.241 = (f32[768]{0:T(1024)S(1)}, f32[768]{0:T(1024)}, u32[]{:S(2)}) copy-start(f32[768]{0:T(1024)} %get-tuple-element.263) | copy-start | bytes 9220
  1052.2 73.7 %copy-start.220 = (f32[1,768]{1,0:T(1,128)}, f32[1,768]{1,0:T(1,128)S(1)}, u32[]{:S(2)}) copy-start(f32[1,768]{1,0:T(1,128)S(1)} %dynamic_update_slice.41) | copy-start | bytes 9220
  1052.4 73.5 %copy-start.222 = (f32[1,768]{1,0:T(1,128)}, f32[1,768]{1,0:T(1,128)S(1)}, u32[]{:S(2)}) copy-start(f32[1,768]{1,0:T(1,128)S(1)} %dynamic_update_slice.42) | copy-start | bytes 9220
  1226.7 207.0 %copy-start.45 = (bf16[96,1344]{0,1:T(8,128)(2,1)S(1)}, bf16[96,1344]{0,1:T(8,128)(2,1)}, u32[]{:S(2)}) copy-start(bf16[96,1344]{0,1:T(8,128)(2,1)} %copy.245) | copy-start | bytes 774148
  1227.3 221.3 %copy-start.27 = (f32[3,96,1,1344]{1,3,2,0:T(8,128)S(1)}, f32[3,96,1,1344]{1,3,2,0:T(8,128)}, u32[]{:S(2)}) copy-start(f32[3,96,1,1344]{1,3,2,0:T(8,128)} %copy.201) | copy-start | bytes 4644868
  (233 other events, 2416.8 us)
Sparse Core Ops, SparseCore 0:
  10.8 60.5 all-gather.48
  102.1 21.8 all-gather.24
  126.8 43.5 all-gather.50
  173.4 24.0 reduce-scatter.24
  201.1 17.4 all-gather.26
  225.7 25.7 reduce-scatter.26
  254.2 49.9 all-gather.52
  306.3 15.9 all-gather.28
  325.0 43.5 all-gather.54
  371.7 24.0 reduce-scatter.28
  399.3 17.4 all-gather.30
  423.9 25.7 reduce-scatter.30
  452.4 49.9 all-gather.56
  504.4 15.9 all-gather.32
  523.0 43.5 all-gather.58
  569.6 24.0 reduce-scatter.32
  597.3 17.4 all-gather.34
  621.9 25.7 reduce-scatter.34
  656.4 21.3 all-gather.36
  686.5 25.7 reduce-scatter.36
  718.7 17.4 all-gather.38
  748.6 25.7 reduce-scatter.38
  780.8 17.4 all-gather.40
  807.0 25.7 reduce-scatter.40
  839.8 17.4 all-gather.42
  869.6 25.7 reduce-scatter.42
  903.1 17.4 all-gather.44
  929.3 25.7 reduce-scatter.44
  960.6 17.4 all-gather.46
  981.9 68.2 reduce-scatter.58
  1054.0 67.0 reduce-scatter.56
  1124.4 24.6 reduce-scatter.46
  1153.0 75.0 reduce-scatter.52
  1232.2 62.7 reduce-scatter.50
  1299.1 62.2 reduce-scatter.48
  1364.7 67.0 reduce-scatter.54

commit v2 on v1

--- a/solution.py
+++ b/solution.py
@@ -179,14 +179,554 @@
     )(values)
 
 
-def gather_tokens(values):
-    return lax.all_gather(values, "tensor", axis=1, tiled=True)
-
-
-def sum_tokens(values):
-    return lax.psum_scatter(
-        values.astype(jnp.bfloat16), "tensor", scatter_dimension=1, tiled=True
-    ).astype(jnp.float32)
+MESH = pl.DeviceIdType.MESH
+ACT_VMEM = 60 * 2**20
+
+
+def dot_nn(left_op, right_op):
+    return jnp.dot(left_op, right_op, preferred_element_type=jnp.float32)
+
+
+def dot_nt(left_op, right_op):
+    return lax.dot_general(
+        left_op, right_op, (((1,), (1,)), ((), ())), preferred_element_type=jnp.float32
+    )
+
+
+def dot_tn(left_op, right_op):
+    return lax.dot_general(
+        left_op, right_op, (((0,), (0,)), ((), ())), preferred_element_type=jnp.float32
+    )
+
+
+def norm_parts(values):
+    center = values - jnp.mean(values, axis=-1, keepdims=True)
+    rstd = lax.rsqrt(jnp.mean(center * center, axis=-1, keepdims=True) + EPS_NORM)
+    return center * rstd, rstd
+
+
+def greet_tensor():
+    rank = lax.axis_index("tensor")
+    half = lax.axis_size("tensor") // 2
+    core_peer = {"tensor": rank + 1 - 2 * lax.rem(rank, 2)}
+    chip_peer = {"tensor": lax.rem(rank + half, 2 * half)}
+    barrier = pltpu.get_barrier_semaphore()
+    for peer in (core_peer, chip_peer):
+        pl.semaphore_signal(barrier, inc=1, device_id=peer, device_id_type=MESH)
+    pl.semaphore_wait(barrier, 2)
+
+
+class Spread:
+    def __init__(self, rows_ref, send_sems, recv_sems):
+        self.rows, self.send, self.recv = rows_ref, send_sems, recv_sems
+        self.rank = lax.axis_index("tensor")
+        self.own_core = lax.rem(self.rank, 2)
+        self.core_peer = self.rank + 1 - 2 * self.own_core
+        self.chip_peer = lax.rem(self.rank + 2, 4)
+        self.count = rows_ref.shape[1] // 4
+
+    def block(self, image, owner):
+        return self.rows.at[image, pl.ds(pl.multiple_of(owner * self.count, 16), self.count), :]
+
+    def copy(self, image, owner, peer, which):
+        return pltpu.make_async_remote_copy(
+            src_ref=self.block(image, owner),
+            dst_ref=self.block(image, owner),
+            send_sem=self.send.at[image, which],
+            recv_sem=self.recv.at[image, which],
+            device_id={"tensor": peer},
+            device_id_type=MESH,
+        )
+
+    def put(self, image, values):
+        self.rows[image, pl.ds(pl.multiple_of(self.rank * self.count, 16), self.count), :] = values
+        self.copy(image, self.rank, self.chip_peer, 0).start()
+        self.copy(image, self.rank, self.core_peer, 1).start()
+
+    def forward(self, image):
+        self.copy(image, self.rank, self.chip_peer, 0).wait_recv()
+        self.copy(image, self.chip_peer, self.core_peer, 2).start()
+
+    def wait(self, image):
+        self.copy(image, self.rank, self.core_peer, 1).wait_recv()
+        self.copy(image, self.chip_peer, self.core_peer, 2).wait_recv()
+
+    def close(self, image):
+        self.copy(image, self.rank, self.chip_peer, 0).wait_send()
+        self.copy(image, self.rank, self.core_peer, 1).wait_send()
+        self.copy(image, self.chip_peer, self.core_peer, 2).wait_send()
+
+
+class Collect:
+    def __init__(self, part, near, far_out, far_in, send_sems, recv_sems):
+        self.part, self.near, self.far_out, self.far_in = part, near, far_out, far_in
+        self.send, self.recv = send_sems, recv_sems
+        self.rank = lax.axis_index("tensor")
+        self.own_core = lax.rem(self.rank, 2)
+        self.own_chip = self.rank // 2
+        self.core_peer = self.rank + 1 - 2 * self.own_core
+        self.chip_peer = lax.rem(self.rank + 2, 4)
+        self.count = part.shape[1] // 4
+
+    def block(self, image, owner):
+        return self.part.at[image, pl.ds(pl.multiple_of(owner * self.count, 16), self.count), :]
+
+    def near_copy(self, image, far):
+        chip = 1 - self.own_chip if far else self.own_chip
+        return pltpu.make_async_remote_copy(
+            src_ref=self.block(image, 2 * chip + 1 - self.own_core),
+            dst_ref=self.near.at[image, far],
+            send_sem=self.send.at[image, far],
+            recv_sem=self.recv.at[image, far],
+            device_id={"tensor": self.core_peer},
+            device_id_type=MESH,
+        )
+
+    def far_copy(self, image):
+        return pltpu.make_async_remote_copy(
+            src_ref=self.far_out.at[image],
+            dst_ref=self.far_in.at[image],
+            send_sem=self.send.at[image, 2],
+            recv_sem=self.recv.at[image, 2],
+            device_id={"tensor": self.chip_peer},
+            device_id_type=MESH,
+        )
+
+    def put(self, image, values):
+        self.part[image] = values.astype(jnp.bfloat16)
+        self.near_copy(image, 1).start()
+        self.near_copy(image, 0).start()
+
+    def load(self, image, owner):
+        at = pl.ds(pl.multiple_of(owner * self.count, 16), self.count)
+        return self.part[image, at, :].astype(jnp.float32)
+
+    def forward(self, image):
+        self.near_copy(image, 1).wait_recv()
+        total = self.load(image, self.chip_peer) + self.near[image, 1].astype(jnp.float32)
+        self.far_out[image] = total.astype(jnp.bfloat16)
+        self.far_copy(image).start()
+
+    def take(self, image):
+        self.near_copy(image, 0).wait_recv()
+        total = self.load(image, self.rank) + self.near[image, 0].astype(jnp.float32)
+        self.far_copy(image).wait_recv()
+        return total + self.far_in[image].astype(jnp.float32)
+
+    def close(self, image):
+        self.near_copy(image, 1).wait_send()
+        self.near_copy(image, 0).wait_send()
+        self.far_copy(image).wait_send()
+
+
+def collect_scratch(images, tokens):
+    count = tokens // 4
+    return [
+        pltpu.VMEM((images, tokens, D), jnp.bfloat16),
+        pltpu.VMEM((images, 2, count, D), jnp.bfloat16),
+        pltpu.VMEM((images, count, D), jnp.bfloat16),
+        pltpu.VMEM((images, count, D), jnp.bfloat16),
+    ]
+
+
+def each(count, body):
+    def step(index, carry):
+        body(index)
+        return carry
+
+    lax.fori_loop(0, count, step, 0)
+
+
+def head_slice(matrix, head):
+    return matrix[:, head * HEAD_DIM : (head + 1) * HEAD_DIM]
+
+
+def soft_rows(queries, keys_in):
+    scores = dot_nt(queries, keys_in) * (HEAD_DIM ** (-0.5))
+    exponent = jnp.exp(scores - jnp.max(scores, axis=-1, keepdims=True))
+    return exponent / jnp.sum(exponent, axis=-1, keepdims=True)
+
+
+def forward_kernel(
+    res_ref,
+    mod_ref,
+    vec_ref,
+    qkv_bias_ref,
+    up_bias_ref,
+    w_qkv_ref,
+    w_up_ref,
+    w_attn_ref,
+    w_down_ref,
+    res_out,
+    rows_a,
+    qkv_out,
+    mixed_out,
+    branch_out,
+    mid_out,
+    rows_m,
+    upper_out,
+    down_out,
+    part_a,
+    near_a,
+    far_out_a,
+    far_in_a,
+    part_m,
+    near_m,
+    far_out_m,
+    far_in_m,
+    sends,
+    recvs,
+):
+    images = res_ref.shape[0]
+    group_width = w_attn_ref.shape[0]
+    greet_tensor()
+    spread_a = Spread(rows_a, sends.at[0], recvs.at[0])
+    spread_m = Spread(rows_m, sends.at[1], recvs.at[1])
+    collect_a = Collect(part_a, near_a, far_out_a, far_in_a, sends.at[2], recvs.at[2])
+    collect_m = Collect(part_m, near_m, far_out_m, far_in_m, sends.at[3], recvs.at[3])
+
+    def mod_row(image, piece):
+        return mod_ref[image, pl.ds(piece, 1), :]
+
+    def start_norm(image):
+        normed, _ = norm_parts(res_ref[image])
+        normed = normed * (1.0 + mod_row(image, 1)) + mod_row(image, 0)
+        spread_a.put(image, normed.astype(jnp.bfloat16))
+
+    def attend(image):
+        spread_a.wait(image)
+        rows = rows_a[image]
+        projected = dot_nn(rows, w_qkv_ref[...]) + qkv_bias_ref[...]
+        qkv = projected.astype(jnp.bfloat16)
+        qkv_out[image] = qkv
+        heads = []
+        for head in range(group_width // HEAD_DIM):
+            probs = soft_rows(
+                head_slice(qkv[:, :group_width], head),
+                head_slice(qkv[:, group_width : 2 * group_width], head),
+            )
+            heads.append(
+                dot_nn(probs.astype(jnp.bfloat16), head_slice(qkv[:, 2 * group_width :], head))
+            )
+        mixed = jnp.concatenate(heads, axis=1).astype(jnp.bfloat16)
+        mixed_out[image] = mixed
+        collect_a.put(image, dot_nn(mixed, w_attn_ref[...]))
+
+    def middle(image):
+        branch = collect_a.take(image) + vec_ref[0:1, :]
+        branch_out[image] = branch
+        mid = res_ref[image] + mod_row(image, 2) * branch
+        mid_out[image] = mid
+        normed, _ = norm_parts(mid)
+        normed = normed * (1.0 + mod_row(image, 4)) + mod_row(image, 3)
+        spread_m.put(image, normed.astype(jnp.bfloat16))
+
+    def feed(image):
+        spread_m.wait(image)
+        upper = dot_nn(rows_m[image], w_up_ref[...]) + up_bias_ref[...]
+        upper_out[image] = upper
+        collect_m.put(image, dot_nn(gelu_tanh(upper).astype(jnp.bfloat16), w_down_ref[...]))
+
+    def finish(image):
+        down = collect_m.take(image) + vec_ref[1:2, :]
+        down_out[image] = down
+        res_out[image] = mid_out[image] + mod_row(image, 5) * down
+
+    def close(image):
+        spread_a.close(image)
+        spread_m.close(image)
+        collect_a.close(image)
+        collect_m.close(image)
+
+    each(images, start_norm)
+    each(images, spread_a.forward)
+    each(images, attend)
+    each(images, collect_a.forward)
+    each(images, middle)
+    each(images, spread_m.forward)
+    each(images, feed)
+    each(images, collect_m.forward)
+    each(images, finish)
+    each(images, close)
+
+
+def forward_layer(residual, mod_vec, vec_bias, qkv_bias, up_bias, w_qkv, w_up, w_attn, w_down):
+    images, count, _ = residual.shape
+    tokens = 4 * count
+    low, full = jnp.bfloat16, jnp.float32
+    shapes = [
+        ((images, count, D), full),
+        ((images, tokens, D), low),
+        ((images, tokens, w_qkv.shape[1]), low),
+        ((images, tokens, w_attn.shape[0]), low),
+        ((images, count, D), full),
+        ((images, count, D), full),
+        ((images, tokens, D), low),
+        ((images, tokens, w_up.shape[1]), full),
+        ((images, count, D), full),
+    ]
+    return pl.pallas_call(
+        forward_kernel,
+        out_shape=[jax.ShapeDtypeStruct(*shape) for shape in shapes],
+        in_specs=[pl.BlockSpec(memory_space=pltpu.VMEM)] * 9,
+        out_specs=[pl.BlockSpec(memory_space=pltpu.VMEM)] * 9,
+        scratch_shapes=collect_scratch(images, tokens)
+        + collect_scratch(images, tokens)
+        + [
+            pltpu.SemaphoreType.DMA((4, images, 3)),
+            pltpu.SemaphoreType.DMA((4, images, 3)),
+        ],
+        compiler_params=pltpu.CompilerParams(
+            collective_id=20, has_side_effects=True, vmem_limit_bytes=ACT_VMEM
+        ),
+        cost_estimate=pl.CostEstimate(
+            flops=30 * 10**9, bytes_accessed=15 * 2**20, transcendentals=0
+        ),
+        name="block_forward",
+    )(residual, mod_vec, vec_bias, qkv_bias, up_bias, w_qkv, w_up, w_attn, w_down)
+
+
+def gelu_slope(values):
+    root = math.sqrt(2.0 / math.pi)
+    square = values * values
+    tanh = jnp.tanh(root * (values + 0.044715 * values * square))
+    half = 0.5 * (1.0 + tanh)
+    slope = half + 0.5 * values * (1.0 - tanh * tanh) * root * (1.0 + 3.0 * 0.044715 * square)
+    return values * half, slope
+
+
+def norm_pull(values, scale_row, d_normed):
+    normed, rstd = norm_parts(values)
+    d_shift = jnp.sum(d_normed, axis=0, keepdims=True)
+    d_scale = jnp.sum(d_normed * normed, axis=0, keepdims=True)
+    inner = d_normed * (1.0 + scale_row)
+    mean_one = jnp.mean(inner, axis=-1, keepdims=True)
+    mean_two = jnp.mean(inner * normed, axis=-1, keepdims=True)
+    return (inner - mean_one - normed * mean_two) * rstd, d_shift, d_scale
+
+
+def backward_kernel(
+    d_res_ref,
+    mod_ref,
+    res_ref,
+    rows_a,
+    qkv_ref,
+    mixed_ref,
+    branch_ref,
+    mid_ref,
+    rows_m,
+    upper_ref,
+    down_ref,
+    w_qkv_ref,
+    w_up_ref,
+    w_attn_ref,
+    w_down_ref,
+    d_res_out,
+    d_in,
+    d_out,
+    d_mod,
+    d_vec,
+    d_qkv_bias,
+    d_up_bias,
+    d_mid,
+    d_rows_m,
+    d_rows_a,
+    act_low,
+    d_upper,
+    d_qkv,
+    part_a,
+    near_a,
+    far_out_a,
+    far_in_a,
+    part_m,
+    near_m,
+    far_out_m,
+    far_in_m,
+    sends,
+    recvs,
+):
+    images = res_ref.shape[0]
+    tokens = rows_a.shape[1]
+    group_width = w_attn_ref.shape[0]
+    qkv_width = 3 * group_width
+    units = w_up_ref.shape[1]
+    greet_tensor()
+    spread_m = Spread(d_rows_m, sends.at[0], recvs.at[0])
+    spread_a = Spread(d_rows_a, sends.at[1], recvs.at[1])
+    collect_m = Collect(part_m, near_m, far_out_m, far_in_m, sends.at[2], recvs.at[2])
+    collect_a = Collect(part_a, near_a, far_out_a, far_in_a, sends.at[3], recvs.at[3])
+    d_vec[...] = jnp.zeros_like(d_vec)
+    d_qkv_bias[...] = jnp.zeros_like(d_qkv_bias)
+    d_up_bias[...] = jnp.zeros_like(d_up_bias)
+
+    def mod_row(image, piece):
+        return mod_ref[image, pl.ds(piece, 1), :]
+
+    def start_down(image):
+        d_res = d_res_ref[image]
+        d_mod[image, pl.ds(5, 1), :] = jnp.sum(d_res * down_ref[image], axis=0, keepdims=True)
+        d_down = d_res * mod_row(image, 5)
+        d_vec[1:2, :] += jnp.sum(d_down, axis=0, keepdims=True)
+        spread_m.put(image, d_down.astype(jnp.bfloat16))
+
+    def feed(image):
+        spread_m.wait(image)
+        d_act = dot_nt(d_rows_m[image], w_down_ref[...])
+        act, slope = gelu_slope(upper_ref[image])
+        act_low[image] = act.astype(jnp.bfloat16)
+        d_up = d_act * slope
+        d_up_bias[...] += jnp.sum(d_up, axis=0, keepdims=True)
+        d_up_low = d_up.astype(jnp.bfloat16)
+        d_upper[image] = d_up_low
+        collect_m.put(image, dot_nt(d_up_low, w_up_ref[...]))
+
+    def rows_of(ref, width):
+        return ref[...].reshape(images * tokens, width)
+
+    def feed_weights():
+        tile = 256
+
+        def step(index, carry):
+            at = pl.ds(pl.multiple_of(index * tile, tile), tile)
+            grad = dot_tn(
+                act_low[:, :, at].reshape(images * tokens, tile), rows_of(d_rows_m, D)
+            )
+            d_out[pl.ds(pl.multiple_of(group_width + index * tile, 64), tile), :] = grad.astype(
+                jnp.bfloat16
+            )
+            grad = dot_tn(
+                rows_m[:, :, at].reshape(images * tokens, tile), rows_of(d_upper, units)
+            )
+            d_in[pl.ds(pl.multiple_of(index * tile, tile), tile), qkv_width:] = grad.astype(
+                jnp.bfloat16
+            )
+            return carry
+
+        lax.fori_loop(0, units // tile, step, 0)
+
+    def middle(image):
+        d_value, d_shift, d_scale = norm_pull(
+            mid_ref[image], mod_row(image, 4), collect_m.take(image)
+        )
+        d_mod[image, pl.ds(3, 1), :] = d_shift
+        d_mod[image, pl.ds(4, 1), :] = d_scale
+        d_value = d_res_ref[image] + d_value
+        d_mid[image] = d_value
+        d_mod[image, pl.ds(2, 1), :] = jnp.sum(d_value * branch_ref[image], axis=0, keepdims=True)
+        d_branch = d_value * mod_row(image, 2)
+        d_vec[0:1, :] += jnp.sum(d_branch, axis=0, keepdims=True)
+        spread_a.put(image, d_branch.astype(jnp.bfloat16))
+
+    def attend(image):
+        spread_a.wait(image)
+        d_mixed = dot_nt(d_rows_a[image], w_attn_ref[...]).astype(jnp.bfloat16)
+        qkv = qkv_ref[image]
+        d_queries, d_keys, d_values = [], [], []
+        scale_dot = HEAD_DIM ** (-0.5)
+        for head in range(group_width // HEAD_DIM):
+            queries = head_slice(qkv[:, :group_width], head)
+            keys_in = head_slice(qkv[:, group_width : 2 * group_width], head)
+            values_in = head_slice(qkv[:, 2 * group_width :], head)
+            d_head = head_slice(d_mixed, head)
+            probs = soft_rows(queries, keys_in)
+            d_probs = dot_nt(d_head, values_in)
+            d_values.append(dot_tn(probs.astype(jnp.bfloat16), d_head))
+            inner = jnp.sum(probs * d_probs, axis=-1, keepdims=True)
+            d_scores = (probs * (d_probs - inner)).astype(jnp.bfloat16)
+            d_queries.append(dot_nn(d_scores, keys_in) * scale_dot)
+            d_keys.append(dot_tn(d_scores, queries) * scale_dot)
+        joined = jnp.concatenate(d_queries + d_keys + d_values, axis=1)
+        d_qkv_bias[...] += jnp.sum(joined, axis=0, keepdims=True)
+        joined = joined.astype(jnp.bfloat16)
+        d_qkv[image] = joined
+        collect_a.put(image, dot_nt(joined, w_qkv_ref[...]))
+
+    def attend_weights():
+        d_out[0:group_width, :] = dot_tn(
+            rows_of(mixed_ref, group_width), rows_of(d_rows_a, D)
+        ).astype(jnp.bfloat16)
+        tile = 256
+
+        def step(index, carry):
+            at = pl.ds(pl.multiple_of(index * tile, tile), tile)
+            grad = dot_tn(
+                rows_a[:, :, at].reshape(images * tokens, tile), rows_of(d_qkv, qkv_width)
+            )
+            d_in[at, 0:qkv_width] = grad.astype(jnp.bfloat16)
+            return carry
+
+        lax.fori_loop(0, D // tile, step, 0)
+
+    def finish(image):
+        d_value, d_shift, d_scale = norm_pull(
+            res_ref[image], mod_row(image, 1), collect_a.take(image)
+        )
+        d_mod[image, pl.ds(0, 1), :] = d_shift
+        d_mod[image, pl.ds(1, 1), :] = d_scale
+        d_res_out[image] = d_mid[image] + d_value
+
+    def close(image):
+        spread_a.close(image)
+        spread_m.close(image)
+        collect_a.close(image)
+        collect_m.close(image)
+
+    each(images, start_down)
+    each(images, spread_m.forward)
+    each(images, feed)
+    each(images, collect_m.forward)
+    feed_weights()
+    each(images, middle)
+    each(images, spread_a.forward)
+    each(images, attend)
+    each(images, collect_a.forward)
+    attend_weights()
+    each(images, finish)
+    each(images, close)
+
+
+def backward_layer(d_residual, mod_vec, saved, weights):
+    images, count, _ = d_residual.shape
+    tokens = 4 * count
+    low, full = jnp.bfloat16, jnp.float32
+    w_qkv, w_up, w_attn, w_down = weights
+    group_width, units = w_attn.shape[0], w_up.shape[1]
+    shapes = [
+        ((images, count, D), full),
+        ((D, 3 * group_width + units), low),
+        ((group_width + units, D), low),
+        ((images, 6, D), full),
+        ((2, D), full),
+        ((1, 3 * group_width), full),
+        ((1, units), full),
+    ]
+    return pl.pallas_call(
+        backward_kernel,
+        out_shape=[jax.ShapeDtypeStruct(*shape) for shape in shapes],
+        in_specs=[pl.BlockSpec(memory_space=pltpu.VMEM)] * 15,
+        out_specs=[pl.BlockSpec(memory_space=pltpu.VMEM)] * 7,
+        scratch_shapes=[
+            pltpu.VMEM((images, count, D), full),
+            pltpu.VMEM((images, tokens, D), low),
+            pltpu.VMEM((images, tokens, D), low),
+            pltpu.VMEM((images, tokens, units), low),
+            pltpu.VMEM((images, tokens, units), low),
+            pltpu.VMEM((images, tokens, 3 * group_width), low),
+        ]
+        + collect_scratch(images, tokens)
+        + collect_scratch(images, tokens)
+        + [
+            pltpu.SemaphoreType.DMA((4, images, 3)),
+            pltpu.SemaphoreType.DMA((4, images, 3)),
+        ],
+        compiler_params=pltpu.CompilerParams(
+            collective_id=21, has_side_effects=True, vmem_limit_bytes=ACT_VMEM
+        ),
+        cost_estimate=pl.CostEstimate(
+            flops=60 * 10**9, bytes_accessed=25 * 2**20, transcendentals=0
+        ),
+        name="block_backward",
+    )(d_residual, mod_vec, *saved, *weights)
 
 
 def adam_update(weight, first, second, grad, factor, first_fix, second_fix):
@@ -229,13 +769,10 @@
     unit_count = FF // tensor_size
     patch_in = PATCH * PATCH * CHANNELS
     count_all = images * lax.axis_size("dp") * tokens_all * patch_in
-    scale_dot = HEAD_DIM ** (-0.5)
     patch_start, time_start, second_start, final_start, head_start, vector_start, layer_start = (
         table_starts()
     )
     layer_rows = 10 + FF // D
-    head_shape = (images, tokens_all, heads_local, HEAD_DIM)
-    flat_shape = (images, tokens_all, group_width)
     dp_rank = lax.axis_index("dp")
     dp_size = lax.axis_size("dp")
     place_count = dp_size * tensor_size
@@ -343,86 +880,26 @@
         query_bias = lax.dynamic_slice_in_dim(bias_rows[8], tensor_rank * group_width, group_width)
         value_bias = lax.dynamic_slice_in_dim(bias_rows[9], tensor_rank * group_width, group_width)
         up_bias = lax.dynamic_slice_in_dim(up_all, tensor_rank * unit_count, unit_count)
-        modulation = mod_full[layer_idx] + ada_bias
-        shift_a, scale_a, gate_a, shift_m, scale_m, gate_m = [
-            modulation[:, piece_idx * D : (piece_idx + 1) * D] for piece_idx in range(6)
-        ]
-        w_qkv = weight_in[:, : 3 * group_width]
-        w_up = weight_in[:, 3 * group_width :]
-        w_attn = weight_out[:group_width]
-        w_down = weight_out[group_width:]
-        normed_a, norm_pull_a = jax.vjp(modulate, residual, shift_a, scale_a)
-        rows_a = gather_tokens(normed_a.astype(jnp.bfloat16))
-        projected = jnp.einsum("btd,de->bte", rows_a, w_qkv, preferred_element_type=jnp.float32)
-        queries = (
-            (projected[..., :group_width] + query_bias).astype(jnp.bfloat16).reshape(head_shape)
-        )
-        keys_low = (
-            projected[..., group_width : 2 * group_width].astype(jnp.bfloat16).reshape(head_shape)
-        )
-        values_low = (
-            (projected[..., 2 * group_width :] + value_bias)
-            .astype(jnp.bfloat16)
-            .reshape(head_shape)
-        )
-        scores = (
-            jnp.einsum("bqhd,bkhd->bhqk", queries, keys_low, preferred_element_type=jnp.float32)
-            * scale_dot
-        )
-        row_max = jnp.max(scores, axis=-1, keepdims=True)
-        exponent = jnp.exp(scores - row_max)
-        row_total = jnp.sum(exponent, axis=-1, keepdims=True)
-        log_total = row_max + jnp.log(row_total)
-        probs_low = (exponent / row_total).astype(jnp.bfloat16)
-        mixed_out = (
-            jnp.einsum("bhqk,bkhd->bqhd", probs_low, values_low, preferred_element_type=jnp.float32)
-            .astype(jnp.bfloat16)
-            .reshape(flat_shape)
-        )
-        branch = (
-            sum_tokens(
-                jnp.einsum("bte,ed->btd", mixed_out, w_attn, preferred_element_type=jnp.float32)
-            )
-            + out_bias
-        )
-        residual_mid = residual + gate_a[:, None, :] * branch
-        normed_m, norm_pull_m = jax.vjp(modulate, residual_mid, shift_m, scale_m)
-        rows_m = gather_tokens(normed_m.astype(jnp.bfloat16))
-        upper_pre = (
-            jnp.einsum("btd,df->btf", rows_m, w_up, preferred_element_type=jnp.float32) + up_bias
-        )
-        activated, gelu_pull = jax.vjp(gelu_tanh, upper_pre)
-        act_low = activated.astype(jnp.bfloat16)
-        down_out = (
-            sum_tokens(
-                jnp.einsum("btf,fd->btd", act_low, w_down, preferred_element_type=jnp.float32)
-            )
-            + down_bias
-        )
-        residual = residual_mid + gate_m[:, None, :] * down_out
-        saved_acts.append(
-            (
-                norm_pull_a,
-                rows_a,
-                queries,
-                keys_low,
-                values_low,
-                log_total,
-                mixed_out,
-                branch,
-                gate_a,
-                norm_pull_m,
-                rows_m,
-                gelu_pull,
-                act_low,
-                down_out,
-                gate_m,
-                w_qkv,
-                w_up,
-                w_attn,
-                w_down,
-            )
-        )
+        mod_vec = (mod_full[layer_idx] + ada_bias).reshape(images, 6, D)
+        weights = (
+            weight_in[:, : 3 * group_width],
+            weight_in[:, 3 * group_width :],
+            weight_out[:group_width],
+            weight_out[group_width:],
+        )
+        qkv_bias = jnp.concatenate(
+            [query_bias, jnp.zeros((group_width,), jnp.float32), value_bias]
+        )[None]
+        outs = forward_layer(
+            residual,
+            mod_vec,
+            jnp.stack([out_bias, down_bias]),
+            qkv_bias,
+            up_bias[None],
+            *weights,
+        )
+        saved_acts.append((mod_vec, (residual,) + tuple(outs[1:]), weights))
+        residual = outs[0]
     final_in, final_norm_pull = jax.vjp(modulate, residual, final_shift, final_scale)
     predicted = jnp.einsum("btd,pd->btp", final_in, head_w, precision=PRECISE)
     error_all = predicted - targets
@@ -436,110 +913,25 @@
     mod_parts = []
     bias_blocks = []
     for layer_idx in reversed(range(LAYERS)):
-        (
-            norm_pull_a,
-            rows_a,
-            queries,
-            keys_low,
-            values_low,
-            log_total,
-            mixed_out,
-            branch,
-            gate_a,
-            norm_pull_m,
-            rows_m,
-            gelu_pull,
-            act_low,
-            down_out,
-            gate_m,
-            w_qkv,
-            w_up,
-            w_attn,
-            w_down,
-        ) = saved_acts[layer_idx]
-        d_gate_m = jnp.sum(d_residual * down_out, axis=1)
-        d_down = d_residual * gate_m[:, None, :]
-        d_down_bias = jnp.sum(d_down, axis=(0, 1))
-        d_down_rows = gather_tokens(d_down.astype(jnp.bfloat16))
-        d_w_down = jnp.einsum(
-            "btf,btd->fd", act_low, d_down_rows, preferred_element_type=jnp.float32
-        )
-        d_act = jnp.einsum("btd,fd->btf", d_down_rows, w_down, preferred_element_type=jnp.float32)
-        d_upper = gelu_pull(d_act)[0]
-        d_up_bias = jnp.sum(d_upper, axis=(0, 1))
-        d_upper_low = d_upper.astype(jnp.bfloat16)
-        d_w_up = jnp.einsum("btd,btf->df", rows_m, d_upper_low, preferred_element_type=jnp.float32)
-        d_normed_m = sum_tokens(
-            jnp.einsum("btf,df->btd", d_upper_low, w_up, preferred_element_type=jnp.float32)
-        )
-        d_mid, d_shift_m, d_scale_m = norm_pull_m(d_normed_m)
-        d_residual = d_residual + d_mid
-        d_gate_a = jnp.sum(d_residual * branch, axis=1)
-        d_branch = d_residual * gate_a[:, None, :]
-        d_out_bias = jnp.sum(d_branch, axis=(0, 1))
-        d_branch_rows = gather_tokens(d_branch.astype(jnp.bfloat16))
-        d_w_attn = jnp.einsum(
-            "bte,btd->ed", mixed_out, d_branch_rows, preferred_element_type=jnp.float32
-        )
-        d_mixed = (
-            jnp.einsum("btd,ed->bte", d_branch_rows, w_attn, preferred_element_type=jnp.float32)
-            .astype(jnp.bfloat16)
-            .reshape(head_shape)
-        )
-        scores = (
-            jnp.einsum("bqhd,bkhd->bhqk", queries, keys_low, preferred_element_type=jnp.float32)
-            * scale_dot
-        )
-        probs_row = jnp.exp(scores - log_total)
-        d_probs = jnp.einsum(
-            "bqhd,bkhd->bhqk", d_mixed, values_low, preferred_element_type=jnp.float32
-        )
-        d_values = jnp.einsum(
-            "bhqk,bqhd->bkhd",
-            probs_row.astype(jnp.bfloat16),
-            d_mixed,
-            preferred_element_type=jnp.float32,
-        )
-        d_scores = (
-            probs_row * (d_probs - jnp.sum(probs_row * d_probs, axis=-1, keepdims=True))
-        ).astype(jnp.bfloat16)
-        d_queries = (
-            jnp.einsum("bhqk,bkhd->bqhd", d_scores, keys_low, preferred_element_type=jnp.float32)
-            * scale_dot
-        )
-        d_keys = (
-            jnp.einsum("bhqk,bqhd->bkhd", d_scores, queries, preferred_element_type=jnp.float32)
-            * scale_dot
-        )
-        d_query_bias = jnp.sum(d_queries.reshape(flat_shape), axis=(0, 1))
-        d_value_bias = jnp.sum(d_values.reshape(flat_shape), axis=(0, 1))
-        d_projected = jnp.concatenate(
-            [
-                d_queries.reshape(flat_shape),
-                d_keys.reshape(flat_shape),
-                d_values.reshape(flat_shape),
-            ],
-            axis=2,
-        ).astype(jnp.bfloat16)
-        d_w_qkv = jnp.einsum("btd,bte->de", rows_a, d_projected, preferred_element_type=jnp.float32)
-        d_normed_a = sum_tokens(
-            jnp.einsum("bte,de->btd", d_projected, w_qkv, preferred_element_type=jnp.float32)
-        )
-        d_before, d_shift_a, d_scale_a = norm_pull_a(d_normed_a)
-        d_residual = d_residual + d_before
-        d_modulation = jnp.concatenate(
-            [d_shift_a, d_scale_a, d_gate_a, d_shift_m, d_scale_m, d_gate_m], axis=1
-        )
+        mod_vec, saved, weights = saved_acts[layer_idx]
+        d_residual, d_w_in, d_w_out, d_mod_vec, d_vec, d_qkv_bias, d_up_bias = backward_layer(
+            d_residual, mod_vec, saved, weights
+        )
+        d_modulation = d_mod_vec.reshape(images, 6 * D)
+        d_out_bias, d_down_bias = d_vec[0], d_vec[1]
+        d_query_bias = d_qkv_bias[0, :group_width]
+        d_value_bias = d_qkv_bias[0, 2 * group_width :]
+        d_up_bias = d_up_bias[0]
         mod_parts.insert(0, d_modulation)
         grad_in, grad_out = (
             lax.psum_scatter(
-                jnp.concatenate([d_w_qkv, d_w_up], axis=1).astype(jnp.bfloat16),
+                d_w_in,
                 "dp",
                 scatter_dimension=0,
                 tiled=True,
             ).astype(jnp.float32),
             lax.psum_scatter(
-                jnp.concatenate([d_w_attn, d_w_down], axis=0).astype(jnp.bfloat16),
+                d_w_out,
                 "dp",
                 scatter_dimension=0,
                 tiled=True,

time: 1500 us -> 1090 us (0.73)
  waiting for transfers between devices: 962 us -> 502 us
  Pallas kernels: 173 us -> 464 us
  matrix products: 126 us -> 13.1 us
  local copies, waits for them, and re-layouts: 115 us -> 52.3 us
  other arithmetic: 84.9 us -> 26 us
    pallas_call x0 -> x6, Pallas kernels: none -> 281 us  [the longest x3 147 us: backward_layer(): pl.pallas_call(backward_kernel, out_shape=[jax.ShapeDtypeStruct(*shape) f...]
    all_gather x12 -> x0, waiting for transfers between devices: 185 us -> none  [gather_tokens(): return lax.all_gather(values, 'tensor', axis=1, tiled=True)]
    unnamed x39 -> x12, waiting for transfers between devices: 164 us -> 4.97 us
    dot_general x54 -> x0, matrix products: 112 us -> none  [the longest x3 16.3 us: local(): jnp.einsum('btd,fd->btf', d_down_rows, w_down, preferred_element_type=jnp...]
    all_gather x3, waiting for transfers between devices: 120 us -> 30.9 us  [local(): lax.all_gather(layer_out[layer_idx].astype(jnp.bfloat16).reshape(layer_ou...]
    reduce_scatter x15 -> x6, waiting for transfers between devices: 397 us -> 329 us  [the longest x3 210 us: local(): lax.psum_scatter(d_w_in, 'dp', scatter_dimension=0, tiled=True)]
    unnamed x557 -> x157, local copies, waits for them, and re-layouts: 75.4 us -> 12.7 us
    all_gather x3, waiting for transfers between devices: 95.7 us -> 137 us  [local(): lax.all_gather(layer_in[layer_idx].astype(jnp.bfloat16).reshape(layer_in....]
  transfers between devices with their start and end apart: 36 -> 12, of which waited for: 33 -> 9; matrix products, arithmetic and copies ran while one was open for 10% -> 5% of each run, Pallas kernels for 11% -> 16%
where the time goes in v2:
time: 1090 us; the launch traced here: 1080 us
  waiting for transfers between devices  502 us (46%)
  Pallas kernels  464 us (43%)
  local copies, waits for them, and re-layouts  52.3 us (5%)
  other arithmetic  26 us (2%)
  between operations  22.2 us (2%)
  matrix products  13.1 us (1%)
    reduce_scatter x3, waiting for transfers between devices, local(): lax.psum_scatter(d_w_in, 'dp', scatter_dimension=0, tiled=True)  210 us
    pallas_call x12, Pallas kernels, exchange(): pl.pallas_call(functools.partial(exchange_kernel, group, spread), out_sha...  184 us
    pallas_call x3, Pallas kernels, backward_layer(): pl.pallas_call(backward_kernel, out_shape=[jax.ShapeDtypeStruct(*shape) f...  147 us
    all_gather x3, waiting for transfers between devices, local(): lax.all_gather(layer_in[layer_idx].astype(jnp.bfloat16).reshape(layer_in....  137 us
    pallas_call x3, Pallas kernels, forward_layer(): pl.pallas_call(forward_kernel, out_shape=[jax.ShapeDtypeStruct(*shape) fo...  133 us
    reduce_scatter x3, waiting for transfers between devices, local(): lax.psum_scatter(d_w_out, 'dp', scatter_dimension=0, tiled=True)  119 us
    all_gather x3, waiting for transfers between devices, local(): lax.all_gather(layer_out[layer_idx].astype(jnp.bfloat16).reshape(layer_ou...  30.9 us
  transfers between devices with their start and end apart: 12, of which 9 were waited for; matrix products, arithmetic and copies ran while one was open for 5% of the time, Pallas kernels for 16%

profile of v2, /device:TPU:0, one launch (start us, length us, event | category | flops | bytes accessed | tf_op | source)
XLA Modules:
  0.0 1080.1 jit_solution(8748151486886907563)
XLA Ops:
  7.2 1.4 convert.19
  8.7 0.8 fusion.78
  11.2 0.9 fusion.77
  13.9 17.9 %exchange_all.8 = f32[32,24,128]{2,1,0:T(8,128)S(1)} custom-call(f32[24,128]{1,0:T(8,128)S(1)} %maximum_maximum_fusion.source), custom_call_target="tpu_custom_call" | custom-call | tf_op jit(solution)/shard_map/exchange_all/pallas_call | solution.py:165
  35.0 0.8 fusion.50
  35.8 20.4 %exchange_all.9 = f32[32,24,24]{2,1,0:T(8,128)S(1)} custom-call(f32[24,24]{1,0:T(8,128)S(1)} %get-tuple-element.246.source), custom_call_target="tpu_custom_call" | custom-call | tf_op jit(solution)/shard_map/exchange_all/pallas_call | solution.py:165
  56.5 0.8 fusion.49
  57.3 19.2 %exchange_all.10 = f32[32,24,24]{2,1,0:T(8,128)S(1)} custom-call(f32[24,24]{1,0:T(8,128)S(1)} %get-tuple-element.248.source), custom_call_target="tpu_custom_call" | custom-call | tf_op jit(solution)/shard_map/exchange_all/pallas_call | solution.py:165
  77.8 18.6 %exchange_dp.2 = f32[8,9,1152]{2,1,0:T(8,128)S(1)} custom-call(f32[8,9,1152]{2,1,0:T(8,128)S(1)} %reshape.583.source), custom_call_target="tpu_custom_call" | custom-call | tf_op jit(solution)/shard_map/exchange_dp/pallas_call | solution.py:165
  96.4 5.4 exchange_tensor.2
  102.0 26.6 %exchange_all.11 = f32[32,48,24]{2,1,0:T(8,128)S(1)} custom-call(f32[48,24]{1,0:T(8,128)S(1)} %pad_maximum_fusion.5.source), custom_call_target="tpu_custom_call" | custom-call | tf_op jit(solution)/shard_map/exchange_all/pallas_call | solution.py:165
  136.9 1.6 fusion.3.res_ref
  138.5 1.8 slice_bitcast_fusion.5.w_attn_ref
  140.3 1.7 slice_bitcast_fusion.4.w_attn_ref
  142.0 30.9 %all-gather.23.cloned.1.call-done = bf16[1,1,960,768]{3,2,1,0:T(8,128)(2,1)} async-done(((bf16[1,1,120,768]{3,2,1,0:T(8,128)(2,1)}), bf16[1,1,960,768]{3,2,1,0:T(8,128)(2,1)}) %all-gather.23.cloned.1.call-update) | async-done | bytes 1474576 | tf_op jit(solution)/shard_map/all_gather | solution.py:868
  172.9 1.7 slice_bitcast_fusion.3.w_attn_ref
  174.6 1.1 slice_bitcast_fusion.2.w_down_ref
  175.7 0.7 copy-done.14
  176.4 1.1 slice_bitcast_fusion.1.w_down_ref
  177.5 0.7 copy-done.15
  178.2 1.1 slice_bitcast_fusion.w_down_ref
  179.3 44.6 %all-gather.13.cloned.1.call-done = bf16[1,768,1,1344]{3,1,2,0:T(8,128)(2,1)} async-done(((bf16[1,96,1,1344]{3,1,2,0:T(8,128)(2,1)}), bf16[1,768,1,1344]{3,1,2,0:T(8,128)(2,1)}) %all-gather.13.cloned.1.call-update) | async-done | bytes 2064400 | tf_op jit(solution)/shard_map/all_gather | solution.py:860
  223.9 2.2 slice.347.w_qkv_ref
  226.1 2.9 slice.348.w_up_ref
  228.9 46.0 %all-gather.17.cloned.1.call-done = bf16[1,768,1,1344]{3,1,2,0:T(8,128)(2,1)} async-done(((bf16[1,96,1,1344]{3,1,2,0:T(8,128)(2,1)}), bf16[1,768,1,1344]{3,1,2,0:T(8,128)(2,1)}) %all-gather.17.cloned.1.call-update) | async-done | bytes 2064400 | tf_op jit(solution)/shard_map/all_gather | solution.py:860
  275.0 2.2 slice.358.w_qkv_ref
  277.2 2.9 slice.359.w_up_ref
  280.0 46.0 %all-gather.21.cloned.1.call-done = bf16[1,768,1,1344]{3,1,2,0:T(8,128)(2,1)} async-done(((bf16[1,96,1,1344]{3,1,2,0:T(8,128)(2,1)}), bf16[1,768,1,1344]{3,1,2,0:T(8,128)(2,1)}) %all-gather.21.cloned.1.call-update) | async-done | bytes 2064400 | tf_op jit(solution)/shard_map/all_gather | solution.py:860
  326.1 2.2 slice.369.w_qkv_ref
  328.3 2.9 slice.370.w_up_ref
  331.2 44.3 %block_forward.3 = (f32[3,64,768]{2,1,0:T(8,128)}, bf16[3,256,768]{2,1,0:T(8,128)(2,1)}, bf16[3,256,576]{2,1,0:T(8,128)(2,1)}, bf16[3,256,192]{2,1,0:T(8,128)(2,...) custom-call(f32[3,64,768]{2,1,0:T(8,128)} %fusion.3.res_ref, ...), custom_call_target="tpu_custom_call" | custom-call | flops 30000001024 | bytes 15728640 | tf_op jit(solution)/shard_map/block_forward/pallas_call | solution.py:468
  375.4 43.2 %block_forward.4 = (f32[3,64,768]{2,1,0:T(8,128)}, bf16[3,256,768]{2,1,0:T(8,128)(2,1)}, bf16[3,256,576]{2,1,0:T(8,128)(2,1)}, bf16[3,256,192]{2,1,0:T(8,128)(2,...) custom-call(f32[3,64,768]{2,1,0:T(8,128)} %get-tuple-element.65.res_, ...), custom_call_target="tpu_custom_call" | custom-call | flops 30000001024 | bytes 15728640 | tf_op jit(solution)/shard_map/block_forward/pallas_call | solution.py:468
  418.7 45.9 %block_forward.5 = (f32[3,64,768]{2,1,0:T(8,128)}, bf16[3,256,768]{2,1,0:T(8,128)(2,1)}, bf16[3,256,576]{2,1,0:T(8,128)(2,1)}, bf16[3,256,192]{2,1,0:T(8,128)(2,...) custom-call(f32[3,64,768]{2,1,0:T(8,128)} %get-tuple-element.66.res_, ...), custom_call_target="tpu_custom_call" | custom-call | flops 30000001024 | bytes 15728640 | tf_op jit(solution)/shard_map/block_forward/pallas_call | solution.py:468
  464.6 1.2 reduce_sum.251
  465.9 1.3 multiply_reduce_fusion.3
  467.2 2.5 multiply_reduce_fusion.5
  469.7 0.8 multiply_reduce_fusion.2
  470.5 0.9 multiply_reduce_fusion.1
  471.5 1.0 broadcast_add_fusion.d_res_ref
  472.5 47.8 %block_backward.3 = (f32[3,64,768]{2,1,0:T(8,128)}, bf16[768,1344]{1,0:T(8,128)(2,1)}, bf16[960,768]{1,0:T(8,128)(2,1)}, f32[3,6,768]{2,1,0:T(8,128)}, f32[2,768...) custom-call(f32[3,64,768]{2,1,0:T(8,128)} %broadcast_add_fusion.d_res_ref, f32[3,6,768]{2,1,0:T(8,128)} %broadcast_add_fusion.1.mod_ref, ...), custom_call_target="tpu_custom_call" | custom-call | flops 60000002048 | bytes 26214400 | tf_op jit(solution)/shard_map/block_backward/pallas_call | solution.py:703
  520.3 51.5 %block_backward.4 = (f32[3,64,768]{2,1,0:T(8,128)}, bf16[768,1344]{1,0:T(8,128)(2,1)}, bf16[960,768]{1,0:T(8,128)(2,1)}, f32[3,6,768]{2,1,0:T(8,128)}, f32[2,768...) custom-call(f32[3,64,768]{2,1,0:T(8,128)} %get-tuple-element.76.d_res_ref, f32[3,6,768]{2,1,0:T(8,128)} %broadcast_add_fusion.2.mod_ref, ...), custom_call_target="tpu_custom_call" | custom-call | flops 60000002048 | bytes 26214400 | tf_op jit(solution)/shard_map/block_backward/pallas_call | solution.py:703
  571.8 47.8 %block_backward.5 = (f32[3,64,768]{2,1,0:T(8,128)}, bf16[768,1344]{1,0:T(8,128)(2,1)}, bf16[960,768]{1,0:T(8,128)(2,1)}, f32[3,6,768]{2,1,0:T(8,128)}, f32[2,768...) custom-call(f32[3,64,768]{2,1,0:T(8,128)} %get-tuple-element.85.d_res_ref, f32[3,6,768]{2,1,0:T(8,128)} %broadcast_add_fusion.3.mod_ref, ...), custom_call_target="tpu_custom_call" | custom-call | flops 60000002048 | bytes 26214400 | tf_op jit(solution)/shard_map/block_backward/pallas_call | solution.py:703
  628.1 14.4 %exchange_all.12 = f32[32,24,128]{2,1,0:T(8,128)S(1)} custom-call(f32[32,24,128]{2,1,0:T(8,128)S(1)} %bitcast.180), custom_call_target="tpu_custom_call" | custom-call | tf_op jit(solution)/shard_map/exchange_all/pallas_call | solution.py:165
  643.5 6.6 exchange_tensor.3
  650.1 14.3 %exchange_dp.3 = bf16[8,9,1152]{2,1,0:T(8,128)(2,1)S(1)} custom-call(bf16[9,1152]{1,0:T(8,128)(2,1)S(1)} %reduce_sum.263.source), custom_call_target="tpu_custom_call" | custom-call | tf_op jit(solution)/shard_map/exchange_dp/pallas_call | solution.py:165
  666.1 15.6 %exchange_all.13 = f32[32,24,24]{2,1,0:T(8,128)S(1)} custom-call(f32[32,24,24]{2,1,0:T(8,128)S(1)} %bitcast.181), custom_call_target="tpu_custom_call" | custom-call | tf_op jit(solution)/shard_map/exchange_all/pallas_call | solution.py:165
  682.5 15.6 %exchange_all.14 = f32[32,24,24]{2,1,0:T(8,128)S(1)} custom-call(f32[32,24,24]{2,1,0:T(8,128)S(1)} %bitcast.182), custom_call_target="tpu_custom_call" | custom-call | tf_op jit(solution)/shard_map/exchange_all/pallas_call | solution.py:165
  701.7 2.0 multiply_reduce_fusion
  703.7 53.3 %reduce-scatter.15.cloned.1.call-done = bf16[120,768]{1,0:T(8,128)(2,1)} async-done(((bf16[960,768]{1,0:T(8,128)(2,1)}), bf16[120,768]{1,0:T(8,128)(2,1)}) %reduce-scatter.15.cloned.1.call-update) | async-done | bytes 184336 | tf_op jit(solution)/shard_map/reduce_scatter | solution.py:933
  757.0 65.9 %reduce-scatter.17.cloned.1.call-done = bf16[120,768]{1,0:T(8,128)(2,1)} async-done(((bf16[960,768]{1,0:T(8,128)(2,1)}), bf16[120,768]{1,0:T(8,128)(2,1)}) %reduce-scatter.17.cloned.1.call-update) | async-done | bytes 184336 | tf_op jit(solution)/shard_map/reduce_scatter | solution.py:933
  823.0 2.0 fusion.10
  825.0 68.6 %reduce-scatter.7.cloned.1.call-done = bf16[96,1344]{1,0:T(8,128)(2,1)} async-done(((bf16[768,1344]{1,0:T(8,128)(2,1)}), bf16[96,1344]{1,0:T(8,128)(2,1)}) %reduce-scatter.7.cloned.1.call-update) | async-done | bytes 258064 | tf_op jit(solution)/shard_map/reduce_scatter | solution.py:927
  893.5 70.8 %reduce-scatter.9.cloned.1.call-done = bf16[96,1344]{1,0:T(8,128)(2,1)} async-done(((bf16[768,1344]{1,0:T(8,128)(2,1)}), bf16[96,1344]{1,0:T(8,128)(2,1)}) %reduce-scatter.9.cloned.1.call-update) | async-done | bytes 258064 | tf_op jit(solution)/shard_map/reduce_scatter | solution.py:927
  964.3 70.8 %reduce-scatter.11.cloned.1.call-done = bf16[96,1344]{1,0:T(8,128)(2,1)} async-done(((bf16[768,1344]{1,0:T(8,128)(2,1)}), bf16[96,1344]{1,0:T(8,128)(2,1)}) %reduce-scatter.11.cloned.1.call-update) | async-done | bytes 258064 | tf_op jit(solution)/shard_map/reduce_scatter | solution.py:927
  1035.1 2.1 fusion
  1039.9 9.1 exchange_all.15
  1050.3 4.4 fusion.71
  1054.7 2.8 copy.124
  1057.5 2.8 copy.126
  1060.4 2.8 copy.125
  1063.2 1.2 fusion.31
  1065.2 2.6 fusion.69
  1067.8 0.9 copy-done.19
  1068.7 2.9 fusion.67
  (334 shorter events, 31.0 us)
Async XLA Ops:
  7.2 3.8 copy-start.8
  7.2 131.3 %all-gather.15.cloned.1.call-start = ((), (), s32[]{:S(2)}) async-start(), calls=%async_computation.13 | async-start | bytes 1658880 | tf_op jit(solution)/shard_map/all_gather | solution.py:868
  9.5 130.8 %all-gather.19.cloned.1.call-start = ((), (), s32[]{:S(2)}) async-start(), calls=%async_computation.15 | async-start | bytes 1658880 | tf_op jit(solution)/shard_map/all_gather | solution.py:868
  10.2 162.7 %all-gather.23.cloned.1.call-start = ((), (), s32[]{:S(2)}) async-start(), calls=%async_computation.17 | async-start | bytes 1658880 | tf_op jit(solution)/shard_map/all_gather | solution.py:868
  11.0 212.9 %all-gather.13.cloned.1.call-start = ((), (), s32[]{:S(2)}) async-start(), calls=%async_computation.12 | async-start | bytes 2433024 | tf_op jit(solution)/shard_map/all_gather | solution.py:860
  11.2 2.4 copy-start.73
  12.1 262.9 %all-gather.17.cloned.1.call-start = ((), (), s32[]{:S(2)}) async-start(), calls=%async_computation.14 | async-start | bytes 2433024 | tf_op jit(solution)/shard_map/all_gather | solution.py:860
  12.7 19.4 %copy-start.54 = (f32[3,1024]{1,0:T(4,128)S(1)}, f32[3,1024]{1,0:T(4,128)}, u32[]{:S(2)}) copy-start(f32[3,1024]{1,0:T(4,128)} %param.17) | copy-start | bytes 36868
  12.7 313.4 %all-gather.21.cloned.1.call-start = ((), (), s32[]{:S(2)}) async-start(), calls=%async_computation.16 | async-start | bytes 2433024 | tf_op jit(solution)/shard_map/all_gather | solution.py:860
  13.3 690.4 %reduce-scatter.13.cloned.1.call-start = ((), (), s32[]{:S(2)}) async-start(), calls=%async_computation.9 | async-start | bytes 1658880 | tf_op jit(solution)/shard_map/reduce_scatter | solution.py:933
  13.4 63.4 %copy-start.22 = (bf16[24,3640]{1,0:T(8,128)(2,1)}, bf16[24,3640]{1,0:T(8,128)(2,1)S(1)}, u32[]{:S(2)}) copy-start(bf16[24,3640]{1,0:T(8,128)(2,1)S(1)} %get-tuple-element.190) | copy-start | bytes 524164
  13.4 19.8 %copy-start.55 = (f32[3,1024]{1,0:T(4,128)S(1)}, f32[3,1024]{1,0:T(4,128)}, u32[]{:S(2)}) copy-start(f32[3,1024]{1,0:T(4,128)} %param.18) | copy-start | bytes 36868
  33.3 103.7 %copy-start.36 = (f32[3,64,16]{1,2,0:T(8,128)}, f32[3,64,16]{1,2,0:T(8,128)S(1)}, u32[]{:S(2)}) copy-start(f32[3,64,16]{1,2,0:T(8,128)S(1)} %reshape.577) | copy-start | bytes 36868
  34.4 432.8 %copy-start.29 = (f32[3,64,16]{1,2,0:T(8,128)}, f32[3,64,16]{1,2,0:T(8,128)S(1)}, u32[]{:S(2)}) copy-start(f32[3,64,16]{1,2,0:T(8,128)S(1)} %reshape.579) | copy-start | bytes 36868
  34.4 42.8 %copy-start.6 = (f32[3,96,1152]{2,1,0:T(8,128)S(1)}, f32[3,96,1152]{2,1,0:T(8,128)}, u32[]{:S(2)}) copy-start(f32[3,96,1152]{2,1,0:T(8,128)} %param.25) | copy-start | bytes 3981316
  34.8 42.3 %copy-start.64 = (s32[24]{0:T(128)}, s32[24]{0:T(128)S(1)}, u32[]{:S(2)}) copy-start(s32[24]{0:T(128)S(1)} %eq.26) | copy-start | bytes 292
  35.0 41.5 %copy-start.50 = (f32[24,128]{1,0:T(8,128)}, f32[24,128]{1,0:T(8,128)S(1)}, u32[]{:S(2)}) copy-start(f32[24,128]{1,0:T(8,128)S(1)} %get-tuple-element.240) | copy-start | bytes 36868
  35.0 41.8 %copy-start.52 = (f32[24,128]{1,0:T(8,128)}, f32[24,128]{1,0:T(8,128)S(1)}, u32[]{:S(2)}) copy-start(f32[24,128]{1,0:T(8,128)S(1)} %get-tuple-element.241) | copy-start | bytes 36868
  134.1 337.4 %copy-start.27 = (f32[3,768]{1,0:T(4,128)}, f32[3,768]{1,0:T(4,128)S(1)}, u32[]{:S(2)}) copy-start(f32[3,768]{1,0:T(4,128)S(1)} %add.363) | copy-start | bytes 27652
  134.2 333.0 %copy-start.40 = (f32[3,768]{1,0:T(4,128)}, f32[3,768]{1,0:T(4,128)S(1)}, u32[]{:S(2)}) copy-start(f32[3,768]{1,0:T(4,128)S(1)} %add.364) | copy-start | bytes 27652
  134.4 7.6 copy-start.66
  134.4 7.6 copy-start.68
  138.5 36.1 %copy-start.13 = (bf16[1,1,960,768]{3,2,1,0:T(8,128)(2,1)S(1)}, bf16[1,1,960,768]{3,2,1,0:T(8,128)(2,1)}, u32[]{:S(2)}) copy-start(bf16[1,1,960,768]{3,2,1,0:T(8,128)(2,1)} %all-gather.15.cloned.1.call-done) | copy-start | bytes 4423684
  464.6 5.1 copy-start.4
  465.9 5.6 copy-start.42
  467.2 4.3 copy-start.46
  469.7 2.8 copy-start.38
  619.6 137.5 %reduce-scatter.15.cloned.1.call-start = ((), (), s32[]{:S(2)}) async-start(), calls=%async_computation.10 | async-start | bytes 1658880 | tf_op jit(solution)/shard_map/reduce_scatter | solution.py:933
  620.3 202.6 %reduce-scatter.17.cloned.1.call-start = ((), (), s32[]{:S(2)}) async-start(), calls=%async_computation.11 | async-start | bytes 1658880 | tf_op jit(solution)/shard_map/reduce_scatter | solution.py:933
  621.1 272.4 %reduce-scatter.7.cloned.1.call-start = ((), (), s32[]{:S(2)}) async-start(), calls=%async_computation.6 | async-start | bytes 2433024 | tf_op jit(solution)/shard_map/reduce_scatter | solution.py:927
  621.7 342.6 %reduce-scatter.9.cloned.1.call-start = ((), (), s32[]{:S(2)}) async-start(), calls=%async_computation.7 | async-start | bytes 2433024 | tf_op jit(solution)/shard_map/reduce_scatter | solution.py:927
  621.8 2.8 copy-start.35
  621.8 2.8 copy-start.34
  621.8 2.9 copy-start.33
  621.8 2.9 copy-start.5
  621.8 2.9 copy-start.28
  621.8 2.9 copy-start.39
  621.8 2.9 copy-start.41
  621.8 2.9 copy-start.43
  621.8 2.9 copy-start.47
  622.4 3.0 copy-start.72
  622.4 3.0 copy-start.71
  622.4 3.0 copy-start.70
  622.4 412.7 %reduce-scatter.11.cloned.1.call-start = ((), (), s32[]{:S(2)}) async-start(), calls=%async_computation.8 | async-start | bytes 2433024 | tf_op jit(solution)/shard_map/reduce_scatter | solution.py:927
  643.5 21.2 %copy-start.23 = (bf16[24,3640]{1,0:T(8,128)(2,1)S(1)}, bf16[24,3640]{1,0:T(8,128)(2,1)}, u32[]{:S(2)}) copy-start(bf16[24,3640]{1,0:T(8,128)(2,1)} %copy-done.22) | copy-start | bytes 524164
  643.5 21.7 %copy-start.7 = (f32[3,96,1152]{2,1,0:T(8,128)S(1)}, f32[3,96,1152]{2,1,0:T(8,128)}, u32[]{:S(2)}) copy-start(f32[3,96,1152]{2,1,0:T(8,128)} %param.25) | copy-start | bytes 3981316
  665.2 16.6 %copy-start.57 = (f32[24,24]{1,0:T(8,128)S(1)}, f32[24,24]{1,0:T(8,128)}, u32[]{:S(2)}) copy-start(f32[24,24]{1,0:T(8,128)} %get-tuple-element.249) | copy-start | bytes 6916
  666.0 32.0 %copy-start.56 = (f32[24,24]{1,0:T(8,128)S(1)}, f32[24,24]{1,0:T(8,128)}, u32[]{:S(2)}) copy-start(f32[24,24]{1,0:T(8,128)} %get-tuple-element.247) | copy-start | bytes 6916
  681.7 17.3 %copy-start.51 = (f32[24,128]{1,0:T(8,128)S(1)}, f32[24,128]{1,0:T(8,128)}, u32[]{:S(2)}) copy-start(f32[24,128]{1,0:T(8,128)} %copy-done.50) | copy-start | bytes 36868
  681.7 17.3 %copy-start.53 = (f32[24,128]{1,0:T(8,128)S(1)}, f32[24,128]{1,0:T(8,128)}, u32[]{:S(2)}) copy-start(f32[24,128]{1,0:T(8,128)} %copy-done.52) | copy-start | bytes 36868
  681.7 17.4 %copy-start.65 = (s32[24]{0:T(128)S(1)}, s32[24]{0:T(128)}, u32[]{:S(2)}) copy-start(s32[24]{0:T(128)} %copy-done.64) | copy-start | bytes 292
  681.7 17.7 %copy-start.1 = (f32[32,24,24]{2,1,0:T(8,128)S(1)}, f32[32,24,24]{2,1,0:T(8,128)}, u32[]{:S(2)}) copy-start(f32[32,24,24]{2,1,0:T(8,128)} %copy-done) | copy-start | bytes 221188
  682.3 18.1 %copy-start.3 = (f32[32,24,24]{2,1,0:T(8,128)S(1)}, f32[32,24,24]{2,1,0:T(8,128)}, u32[]{:S(2)}) copy-start(f32[32,24,24]{2,1,0:T(8,128)} %copy-done.2) | copy-start | bytes 221188
  699.2 2.5 copy-start.45
  701.7 348.6 %copy-start.9 = (f32[3,96,1,1344]{3,2,1,0:T(1,128)S(1)}, f32[3,96,1,1344]{3,2,1,0:T(1,128)}, u32[]{:S(2)}) copy-start(f32[3,96,1,1344]{3,2,1,0:T(1,128)} %param.23) | copy-start | bytes 4644868
  1060.3 2.9 copy-start.17
  1060.3 2.9 copy-start.31
  1060.3 2.9 copy-start.32
  1060.3 4.1 copy-start.21
  1060.4 4.1 copy-start.25
  1060.4 4.1 copy-start.26
  1065.2 2.6 copy-start.10
  1065.2 2.6 copy-start.18
  1065.2 3.5 copy-start.19
  (23 other events, 39.6 us)
Sparse Core Ops, SparseCore 0:
  10.8 56.7 all-gather.14
  70.3 58.9 all-gather.18
  132.1 40.7 all-gather.22
  175.5 48.2 all-gather.12
  226.5 48.4 all-gather.16
  277.6 48.4 all-gather.20
  619.7 72.7 reduce-scatter.12
  696.0 60.9 reduce-scatter.14
  760.5 62.3 reduce-scatter.16
  826.3 67.1 reduce-scatter.6
  897.0 67.2 reduce-scatter.8
  967.6 67.4 reduce-scatter.10

commit v3 on v2

--- a/solution.py
+++ b/solution.py
@@ -205,7 +205,7 @@
     return center * rstd, rstd
 
 
-def greet_tensor():
+def greet(line):
     rank = lax.axis_index("tensor")
     half = lax.axis_size("tensor") // 2
     core_peer = {"tensor": rank + 1 - 2 * lax.rem(rank, 2)}
@@ -213,7 +213,11 @@
     barrier = pltpu.get_barrier_semaphore()
     for peer in (core_peer, chip_peer):
         pl.semaphore_signal(barrier, inc=1, device_id=peer, device_id_type=MESH)
-    pl.semaphore_wait(barrier, 2)
+    count = 2
+    if line is not None:
+        line.greet()
+        count = count + line.answers()
+    pl.semaphore_wait(barrier, count)
 
 
 class Spread:
@@ -337,6 +341,225 @@
     lax.fori_loop(0, count, step, 0)
 
 
+class Line:
+    def __init__(self):
+        self.size = lax.axis_size("dp") // 2
+        self.place = lax.axis_index("dp")
+        self.at = self.place // 2
+        self.side = lax.rem(self.place, 2)
+        self.pair = self.place + 1 - 2 * self.side
+        self.has_up = self.at + 1 < self.size
+        self.has_down = self.at > 0
+
+    def greet(self):
+        barrier = pltpu.get_barrier_semaphore()
+        pl.semaphore_signal(barrier, inc=1, device_id={"dp": self.pair}, device_id_type=MESH)
+
+        @pl.when(self.has_up)
+        def _():
+            up = {"dp": self.place + 2}
+            pl.semaphore_signal(barrier, inc=1, device_id=up, device_id_type=MESH)
+
+        @pl.when(self.has_down)
+        def _():
+            down = {"dp": self.place - 2}
+            pl.semaphore_signal(barrier, inc=1, device_id=down, device_id_type=MESH)
+
+    def answers(self):
+        return 1 + self.has_up.astype(jnp.int32) + self.has_down.astype(jnp.int32)
+
+
+UP, DOWN, PAIR = 0, 1, 2
+
+
+class Gather:
+    def __init__(self, line, shards, wholes, sends, recvs, local_sems):
+        self.line, self.shards, self.wholes = line, shards, wholes
+        self.sends, self.recvs, self.local_sems = sends, recvs, local_sems
+
+    def copy(self, part, way, step, owner, fresh=False):
+        line = self.line
+        there = {UP: line.place + 2, DOWN: line.place - 2, PAIR: line.pair}[way]
+        return pltpu.make_async_remote_copy(
+            src_ref=self.shards[part] if fresh else self.wholes[part].at[owner],
+            dst_ref=self.wholes[part].at[owner],
+            send_sem=self.sends.at[way, step, part],
+            recv_sem=self.recvs.at[way, step, part],
+            device_id={"dp": there},
+            device_id_type=MESH,
+        )
+
+    def local_copy(self, part):
+        return pltpu.make_async_copy(
+            self.shards[part], self.wholes[part].at[self.line.place], self.local_sems.at[part]
+        )
+
+    def start(self):
+        line = self.line
+        parts = range(len(self.shards))
+
+        @pl.when(line.has_up)
+        def _():
+            for part in parts:
+                self.copy(part, UP, 0, line.place, True).start()
+
+        @pl.when(line.has_down)
+        def _():
+            for part in parts:
+                self.copy(part, DOWN, 0, line.place, True).start()
+
+        for part in parts:
+            self.copy(part, PAIR, line.at, line.place, True).start()
+            self.local_copy(part).start()
+
+    def tick(self, step):
+        line = self.line
+        parts = range(len(self.shards))
+        for way, there, can in ((UP, -step, line.has_up), (DOWN, step, line.has_down)):
+            owner = line.place + 2 * there
+            spot = line.at + there
+
+            @pl.when((spot >= 0) & (spot < line.size))
+            def _(way=way, can=can, owner=owner, spot=spot):
+                for part in parts:
+                    self.copy(part, way, step - 1, owner).wait_recv()
+
+                @pl.when(can)
+                def _():
+                    for part in parts:
+                        self.copy(part, way, step, owner).start()
+
+                for part in parts:
+                    self.copy(part, PAIR, spot, owner).start()
+
+    def finish(self):
+        line = self.line
+        parts = range(len(self.shards))
+        for part in parts:
+            self.local_copy(part).wait()
+
+        def side(spot):
+            for part in parts:
+                self.copy(part, PAIR, spot, 2 * spot + line.side).wait()
+
+        each(line.size, side)
+
+        def along(step):
+            for way, there, can in ((UP, -step, line.has_up), (DOWN, step, line.has_down)):
+                spot = line.at + there
+
+                @pl.when((spot >= 0) & (spot < line.size) & can)
+                def _(way=way, there=there):
+                    for part in parts:
+                        self.copy(part, way, step, line.place + 2 * there).wait_send()
+
+        each(line.size, along)
+
+
+class Reduce:
+    def __init__(self, line, terms, totals, pair_in, way_in, way_out, sends, recvs):
+        self.line, self.terms, self.totals = line, terms, totals
+        self.pair_in, self.way_in, self.way_out = pair_in, way_in, way_out
+        self.sends, self.recvs = sends, recvs
+
+    def pair_copy(self, part, spot):
+        return pltpu.make_async_remote_copy(
+            src_ref=self.terms[part].at[2 * spot + 1 - self.line.side],
+            dst_ref=self.pair_in[part].at[spot],
+            send_sem=self.sends.at[PAIR, spot, part],
+            recv_sem=self.recvs.at[PAIR, spot, part],
+            device_id={"dp": self.line.pair},
+            device_id_type=MESH,
+        )
+
+    def way_copy(self, part, way, spot):
+        there = self.line.place + 2 if way == UP else self.line.place - 2
+        return pltpu.make_async_remote_copy(
+            src_ref=self.way_out[part].at[way, spot],
+            dst_ref=self.way_in[part].at[way, spot],
+            send_sem=self.sends.at[way, spot, part],
+            recv_sem=self.recvs.at[way, spot, part],
+            device_id={"dp": there},
+            device_id_type=MESH,
+        )
+
+    def start(self):
+        last = self.line.size - 1
+
+        def outer(step):
+            for part in range(len(self.terms)):
+                self.pair_copy(part, last - step).start()
+
+            @pl.when(last - step > step)
+            def _():
+                for part in range(len(self.terms)):
+                    self.pair_copy(part, step).start()
+
+        each((self.line.size + 1) // 2, outer)
+
+    def pair_sum(self, part, spot):
+        own = self.terms[part][2 * spot + self.line.side].astype(jnp.float32)
+        return own + self.pair_in[part][spot].astype(jnp.float32)
+
+    def pass_on(self, way, spot, more):
+        for part in range(len(self.terms)):
+            self.pair_copy(part, spot).wait_recv()
+            self.way_out[part][way, spot] = self.pair_sum(part, spot).astype(jnp.bfloat16)
+
+            @pl.when(more)
+            def _(part=part):
+                self.way_copy(part, way, spot).wait_recv()
+                self.way_out[part][way, spot] = (
+                    self.pair_sum(part, spot) + self.way_in[part][way, spot].astype(jnp.float32)
+                ).astype(jnp.bfloat16)
+
+            self.way_copy(part, way, spot).start()
+
+    def tick(self, step):
+        line = self.line
+        last = line.size - 1
+
+        @pl.when(last - step > line.at)
+        def _():
+            self.pass_on(UP, last - step, line.has_down)
+
+        @pl.when(line.at > step)
+        def _():
+            self.pass_on(DOWN, step, line.has_up)
+
+    def finish(self):
+        line = self.line
+        spot = line.at
+        for part in range(len(self.terms)):
+            self.pair_copy(part, spot).wait_recv()
+            self.totals[part][...] = self.pair_sum(part, spot)
+        for way, can in ((UP, line.has_down), (DOWN, line.has_up)):
+
+            @pl.when(can)
+            def _(way=way):
+                for part in range(len(self.terms)):
+                    self.way_copy(part, way, spot).wait_recv()
+                    self.totals[part][...] += self.way_in[part][way, spot].astype(jnp.float32)
+
+        def close(spot):
+            for part in range(len(self.terms)):
+                self.pair_copy(part, spot).wait_send()
+            for way, passed in ((UP, spot > line.at), (DOWN, spot < line.at)):
+
+                @pl.when(passed)
+                def _(way=way):
+                    for part in range(len(self.terms)):
+                        self.way_copy(part, way, spot).wait_send()
+
+        each(line.size, close)
+
+
+def run_ticks(task, first, last):
+    if task is not None:
+        for step in range(first, last):
+            task.tick(step)
+
+
 def head_slice(matrix, head):
     return matrix[:, head * HEAD_DIM : (head + 1) * HEAD_DIM]
 
@@ -357,15 +580,23 @@
     w_up_ref,
     w_attn_ref,
     w_down_ref,
-    res_out,
-    rows_a,
-    qkv_out,
-    mixed_out,
-    branch_out,
-    mid_out,
-    rows_m,
-    upper_out,
-    down_out,
+    *rest,
+):
+    with_gather = len(rest) > 19
+    shards, rest = (rest[:3], rest[3:]) if with_gather else ((), rest)
+    (
+        res_out,
+        rows_a,
+        qkv_out,
+        mixed_out,
+        branch_out,
+        mid_out,
+        rows_m,
+        upper_out,
+        down_out,
+    ) = rest[:9]
+    wholes, rest = (rest[9:12], rest[12:]) if with_gather else ((), rest[9:])
+    (
     part_a,
     near_a,
     far_out_a,
@@ -376,10 +607,17 @@
     far_in_m,
     sends,
     recvs,
-):
+    ) = rest[:10]
     images = res_ref.shape[0]
     group_width = w_attn_ref.shape[0]
-    greet_tensor()
+    gather, last_step = None, 0
+    if with_gather:
+        line = Line()
+        greet(line)
+        gather = Gather(line, shards, wholes, *rest[10:])
+        last_step = line.size
+    else:
+        greet(None)
     spread_a = Spread(rows_a, sends.at[0], recvs.at[0])
     spread_m = Spread(rows_m, sends.at[1], recvs.at[1])
     collect_a = Collect(part_a, near_a, far_out_a, far_in_a, sends.at[2], recvs.at[2])
@@ -439,18 +677,28 @@
         collect_m.close(image)
 
     each(images, start_norm)
+    if with_gather:
+        gather.start()
     each(images, spread_a.forward)
     each(images, attend)
+    run_ticks(gather, 1, min(2, last_step))
     each(images, collect_a.forward)
     each(images, middle)
     each(images, spread_m.forward)
+    run_ticks(gather, 2, min(3, last_step))
     each(images, feed)
+    run_ticks(gather, 3, min(4, last_step))
     each(images, collect_m.forward)
     each(images, finish)
     each(images, close)
-
-
-def forward_layer(residual, mod_vec, vec_bias, qkv_bias, up_bias, w_qkv, w_up, w_attn, w_down):
+    if with_gather:
+        each(max(last_step - 4, 0), lambda step: gather.tick(step + 4))
+        gather.finish()
+
+
+def forward_layer(
+    residual, mod_vec, vec_bias, qkv_bias, up_bias, w_qkv, w_up, w_attn, w_down, shards
+):
     images, count, _ = residual.shape
     tokens = 4 * count
     low, full = jnp.bfloat16, jnp.float32
@@ -465,25 +713,32 @@
         ((images, tokens, w_up.shape[1]), full),
         ((images, count, D), full),
     ]
+    scratch = [
+        pltpu.SemaphoreType.DMA((4, images, 3)),
+        pltpu.SemaphoreType.DMA((4, images, 3)),
+    ]
+    if shards:
+        dp_size = lax.axis_size("dp")
+        shapes += [((dp_size,) + shard.shape, low) for shard in shards]
+        scratch += [
+            pltpu.SemaphoreType.DMA((3, dp_size // 2, 3)),
+            pltpu.SemaphoreType.DMA((3, dp_size // 2, 3)),
+            pltpu.SemaphoreType.DMA((3,)),
+        ]
     return pl.pallas_call(
         forward_kernel,
         out_shape=[jax.ShapeDtypeStruct(*shape) for shape in shapes],
-        in_specs=[pl.BlockSpec(memory_space=pltpu.VMEM)] * 9,
-        out_specs=[pl.BlockSpec(memory_space=pltpu.VMEM)] * 9,
-        scratch_shapes=collect_scratch(images, tokens)
-        + collect_scratch(images, tokens)
-        + [
-            pltpu.SemaphoreType.DMA((4, images, 3)),
-            pltpu.SemaphoreType.DMA((4, images, 3)),
-        ],
+        in_specs=[pl.BlockSpec(memory_space=pltpu.VMEM)] * (9 + len(shards)),
+        out_specs=[pl.BlockSpec(memory_space=pltpu.VMEM)] * len(shapes),
+        scratch_shapes=collect_scratch(images, tokens) + collect_scratch(images, tokens) + scratch,
         compiler_params=pltpu.CompilerParams(
-            collective_id=20, has_side_effects=True, vmem_limit_bytes=ACT_VMEM
+            collective_id=20 if shards else 22, has_side_effects=True, vmem_limit_bytes=ACT_VMEM
         ),
         cost_estimate=pl.CostEstimate(
             flops=30 * 10**9, bytes_accessed=15 * 2**20, transcendentals=0
         ),
         name="block_forward",
-    )(residual, mod_vec, vec_bias, qkv_bias, up_bias, w_qkv, w_up, w_attn, w_down)
+    )(residual, mod_vec, vec_bias, qkv_bias, up_bias, w_qkv, w_up, w_attn, w_down, *shards)
 
 
 def gelu_slope(values):
@@ -521,13 +776,22 @@
     w_up_ref,
     w_attn_ref,
     w_down_ref,
-    d_res_out,
-    d_in,
-    d_out,
-    d_mod,
-    d_vec,
-    d_qkv_bias,
-    d_up_bias,
+    *rest,
+):
+    with_reduce = len(rest) > 24
+    terms, rest = (rest[:3], rest[3:]) if with_reduce else ((), rest)
+    (
+        d_res_out,
+        d_w_qkv,
+        d_w_up,
+        d_out,
+        d_mod,
+        d_vec,
+        d_qkv_bias,
+        d_up_bias,
+    ) = rest[:8]
+    totals, rest = (rest[8:11], rest[11:]) if with_reduce else ((), rest[8:])
+    (
     d_mid,
     d_rows_m,
     d_rows_a,
@@ -544,13 +808,21 @@
     far_in_m,
     sends,
     recvs,
-):
+    ) = rest[:16]
     images = res_ref.shape[0]
     tokens = rows_a.shape[1]
     group_width = w_attn_ref.shape[0]
     qkv_width = 3 * group_width
     units = w_up_ref.shape[1]
-    greet_tensor()
+    reduce, last_step = None, 0
+    if with_reduce:
+        line = Line()
+        greet(line)
+        pair_in, way_in, way_out = rest[16:19], rest[19:22], rest[22:25]
+        reduce = Reduce(line, terms, totals, pair_in, way_in, way_out, *rest[25:])
+        last_step = line.size
+    else:
+        greet(None)
     spread_m = Spread(d_rows_m, sends.at[0], recvs.at[0])
     spread_a = Spread(d_rows_a, sends.at[1], recvs.at[1])
     collect_m = Collect(part_m, near_m, far_out_m, far_in_m, sends.at[2], recvs.at[2])
@@ -597,9 +869,7 @@
             grad = dot_tn(
                 rows_m[:, :, at].reshape(images * tokens, tile), rows_of(d_upper, units)
             )
-            d_in[pl.ds(pl.multiple_of(index * tile, tile), tile), qkv_width:] = grad.astype(
-                jnp.bfloat16
-            )
+            d_w_up[pl.ds(pl.multiple_of(index * tile, tile), tile), :] = grad.astype(jnp.bfloat16)
             return carry
 
         lax.fori_loop(0, units // tile, step, 0)
@@ -652,7 +922,7 @@
             grad = dot_tn(
                 rows_a[:, :, at].reshape(images * tokens, tile), rows_of(d_qkv, qkv_width)
             )
-            d_in[at, 0:qkv_width] = grad.astype(jnp.bfloat16)
+            d_w_qkv[at, :] = grad.astype(jnp.bfloat16)
             return carry
 
         lax.fori_loop(0, D // tile, step, 0)
@@ -672,20 +942,29 @@
         collect_m.close(image)
 
     each(images, start_down)
+    if with_reduce:
+        reduce.start()
     each(images, spread_m.forward)
     each(images, feed)
     each(images, collect_m.forward)
     feed_weights()
+    run_ticks(reduce, 0, min(1, last_step))
     each(images, middle)
     each(images, spread_a.forward)
+    run_ticks(reduce, 1, min(2, last_step))
     each(images, attend)
+    run_ticks(reduce, 2, min(3, last_step))
     each(images, collect_a.forward)
     attend_weights()
+    run_ticks(reduce, 3, min(4, last_step))
     each(images, finish)
     each(images, close)
-
-
-def backward_layer(d_residual, mod_vec, saved, weights):
+    if with_reduce:
+        each(max(last_step - 4, 0), lambda step: reduce.tick(step + 4))
+        reduce.finish()
+
+
+def backward_layer(d_residual, mod_vec, saved, weights, terms):
     images, count, _ = d_residual.shape
     tokens = 4 * count
     low, full = jnp.bfloat16, jnp.float32
@@ -693,18 +972,34 @@
     group_width, units = w_attn.shape[0], w_up.shape[1]
     shapes = [
         ((images, count, D), full),
-        ((D, 3 * group_width + units), low),
+        ((D, 3 * group_width), low),
+        ((D, units), low),
         ((group_width + units, D), low),
         ((images, 6, D), full),
         ((2, D), full),
         ((1, 3 * group_width), full),
         ((1, units), full),
     ]
+    scratch = [
+        pltpu.SemaphoreType.DMA((4, images, 3)),
+        pltpu.SemaphoreType.DMA((4, images, 3)),
+    ]
+    if terms:
+        spots = lax.axis_size("dp") // 2
+        blocks = [term.shape[1:] for term in terms]
+        shapes += [(block, full) for block in blocks]
+        scratch += [pltpu.VMEM((spots,) + block, low) for block in blocks]
+        scratch += [pltpu.VMEM((2, spots) + block, low) for block in blocks]
+        scratch += [pltpu.VMEM((2, spots) + block, low) for block in blocks]
+        scratch += [
+            pltpu.SemaphoreType.DMA((3, spots, 3)),
+            pltpu.SemaphoreType.DMA((3, spots, 3)),
+        ]
     return pl.pallas_call(
         backward_kernel,
         out_shape=[jax.ShapeDtypeStruct(*shape) for shape in shapes],
-        in_specs=[pl.BlockSpec(memory_space=pltpu.VMEM)] * 15,
-        out_specs=[pl.BlockSpec(memory_space=pltpu.VMEM)] * 7,
+        in_specs=[pl.BlockSpec(memory_space=pltpu.VMEM)] * (15 + len(terms)),
+        out_specs=[pl.BlockSpec(memory_space=pltpu.VMEM)] * len(shapes),
         scratch_shapes=[
             pltpu.VMEM((images, count, D), full),
             pltpu.VMEM((images, tokens, D), low),
@@ -715,18 +1010,15 @@
         ]
         + collect_scratch(images, tokens)
         + collect_scratch(images, tokens)
-        + [
-            pltpu.SemaphoreType.DMA((4, images, 3)),
-            pltpu.SemaphoreType.DMA((4, images, 3)),
-        ],
+        + scratch,
         compiler_params=pltpu.CompilerParams(
-            collective_id=21, has_side_effects=True, vmem_limit_bytes=ACT_VMEM
+            collective_id=21 if terms else 23, has_side_effects=True, vmem_limit_bytes=ACT_VMEM
         ),
         cost_estimate=pl.CostEstimate(
             flops=60 * 10**9, bytes_accessed=25 * 2**20, transcendentals=0
         ),
         name="block_backward",
-    )(d_residual, mod_vec, *saved, *weights)
+    )(d_residual, mod_vec, *saved, *weights, *terms)
 
 
 def adam_update(weight, first, second, grad, factor, first_fix, second_fix):
@@ -855,23 +1147,15 @@
         + position_table(tensor_rank * local_rows, local_rows)[None]
     )
     saved_acts = []
+    shards_all = []
     for layer_idx in range(LAYERS):
-        weight_in, weight_out = (
-            lax.all_gather(
-                layer_in[layer_idx]
-                .astype(jnp.bfloat16)
-                .reshape(layer_in.shape[1], layer_in.shape[3]),
-                "dp",
-                axis=0,
-                tiled=True,
-            ),
-            lax.all_gather(
-                layer_out[layer_idx].astype(jnp.bfloat16).reshape(layer_out.shape[2], D),
-                "dp",
-                axis=0,
-                tiled=True,
-            ),
-        )
+        shard_in = layer_in[layer_idx, :, 0].astype(jnp.bfloat16)
+        shard_out = layer_out[layer_idx, 0].astype(jnp.bfloat16)
+        shards_all.append(
+            (shard_in[:, : 3 * group_width], shard_in[:, 3 * group_width :], shard_out)
+        )
+    wholes = [lax.all_gather(shard, "dp") for shard in shards_all[0]]
+    for layer_idx in range(LAYERS):
         bias_rows = bias_all[layer_idx * layer_rows : (layer_idx + 1) * layer_rows]
         up_all = bias_rows[10:].reshape(FF)
         ada_bias = bias_rows[0:6].reshape(6 * D)
@@ -881,9 +1165,10 @@
         value_bias = lax.dynamic_slice_in_dim(bias_rows[9], tensor_rank * group_width, group_width)
         up_bias = lax.dynamic_slice_in_dim(up_all, tensor_rank * unit_count, unit_count)
         mod_vec = (mod_full[layer_idx] + ada_bias).reshape(images, 6, D)
+        weight_out = wholes[2].reshape(group_width + unit_count, D)
         weights = (
-            weight_in[:, : 3 * group_width],
-            weight_in[:, 3 * group_width :],
+            wholes[0].reshape(D, 3 * group_width),
+            wholes[1].reshape(D, unit_count),
             weight_out[:group_width],
             weight_out[group_width:],
         )
@@ -897,8 +1182,10 @@
             qkv_bias,
             up_bias[None],
             *weights,
-        )
-        saved_acts.append((mod_vec, (residual,) + tuple(outs[1:]), weights))
+            shards_all[layer_idx + 1] if layer_idx + 1 < LAYERS else (),
+        )
+        wholes = outs[9:]
+        saved_acts.append((mod_vec, (residual,) + tuple(outs[1:9]), weights))
         residual = outs[0]
     final_in, final_norm_pull = jax.vjp(modulate, residual, final_shift, final_scale)
     predicted = jnp.einsum("btd,pd->btp", final_in, head_w, precision=PRECISE)
@@ -908,37 +1195,25 @@
     d_head = jnp.einsum("btp,btd->pd", d_pred, final_in, precision=PRECISE)
     d_final = jnp.einsum("btp,pd->btd", d_pred, head_w, precision=PRECISE)
     d_residual, d_final_shift, d_final_scale = final_norm_pull(d_final)
-    grads_in = []
-    grads_out = []
+    totals = []
+    terms = ()
     mod_parts = []
     bias_blocks = []
     for layer_idx in reversed(range(LAYERS)):
         mod_vec, saved, weights = saved_acts[layer_idx]
-        d_residual, d_w_in, d_w_out, d_mod_vec, d_vec, d_qkv_bias, d_up_bias = backward_layer(
-            d_residual, mod_vec, saved, weights
-        )
+        outs = backward_layer(d_residual, mod_vec, saved, weights, terms)
+        d_residual, d_w_qkv, d_w_up, d_w_out, d_mod_vec, d_vec, d_qkv_bias, d_up_bias = outs[:8]
+        if terms:
+            totals.insert(0, outs[8:])
+        terms = [
+            term.reshape((dp_size, -1) + term.shape[1:]) for term in (d_w_qkv, d_w_up, d_w_out)
+        ]
         d_modulation = d_mod_vec.reshape(images, 6 * D)
         d_out_bias, d_down_bias = d_vec[0], d_vec[1]
         d_query_bias = d_qkv_bias[0, :group_width]
         d_value_bias = d_qkv_bias[0, 2 * group_width :]
         d_up_bias = d_up_bias[0]
         mod_parts.insert(0, d_modulation)
-        grad_in, grad_out = (
-            lax.psum_scatter(
-                d_w_in,
-                "dp",
-                scatter_dimension=0,
-                tiled=True,
-            ).astype(jnp.float32),
-            lax.psum_scatter(
-                d_w_out,
-                "dp",
-                scatter_dimension=0,
-                tiled=True,
-            ).astype(jnp.float32),
-        )
-        grads_in.insert(0, grad_in)
-        grads_out.insert(0, grad_out)
         query_row = lax.dynamic_update_slice_in_dim(
             jnp.zeros((D,), jnp.float32), d_query_bias, tensor_rank * group_width, 0
         )
@@ -962,6 +1237,13 @@
                 axis=0,
             ),
         )
+    totals.insert(
+        0,
+        [
+            lax.psum_scatter(term, "dp", scatter_dimension=0).astype(jnp.float32)
+            for term in terms
+        ],
+    )
     d_patch_w = jnp.einsum("btp,btd->pd", noisy, d_residual, precision=PRECISE)
     d_patch_b = jnp.sum(d_residual, axis=(0, 1))
     row_parts = jnp.concatenate(
@@ -1020,8 +1302,9 @@
         ],
         axis=1,
     )
-    input_grad = jnp.stack(grads_in).reshape(layer_in.shape)
-    output_grad = jnp.stack(grads_out).reshape(layer_out.shape)
+    input_grad = jnp.stack([jnp.concatenate(total[0:2], axis=1) for total in totals])
+    input_grad = input_grad.reshape(layer_in.shape)
+    output_grad = jnp.stack([total[2] for total in totals]).reshape(layer_out.shape)
     local_squares = (
         jnp.sum(table_grad * table_grad)
         + jnp.sum(input_grad * input_grad)

time: 1090 us -> 806 us (0.74)
  waiting for transfers between devices: 502 us -> 118 us
  Pallas kernels: 464 us -> 534 us
  blocking collectives: 0 us -> 37.2 us
    reduce_scatter x6 -> x3, waiting for transfers between devices: 329 us -> 118 us  [local(): lax.psum_scatter(term, 'dp', scatter_dimension=0).astype(jnp.float32)]
    all_gather x6 -> x2, waiting for transfers between devices: 168 us -> 0.01 us  [local(): wholes = [lax.all_gather(shard, 'dp') for shard in shards_all[0]]]
    pallas_call x3, Pallas kernels: 147 us -> 187 us  [backward_layer(): pl.pallas_call(backward_kernel, out_shape=[jax.ShapeDtypeStruct(*shape) f...]
    all_gather x0 -> x1, blocking collectives: none -> 37.2 us  [local(): wholes = [lax.all_gather(shard, 'dp') for shard in shards_all[0]]]
    pallas_call x3, Pallas kernels: 133 us -> 157 us  [forward_layer(): pl.pallas_call(forward_kernel, out_shape=[jax.ShapeDtypeStruct(*shape) fo...]
    slice x8 -> x6, local copies, waits for them, and re-layouts: 17 us -> 3.64 us  [the longest x3 2.31 us: local(): shard_in[:, 3 * group_width:]]
  transfers between devices with their start and end apart: 12 -> 5, of which waited for: 9 -> 2; matrix products, arithmetic and copies ran while one was open for 5% -> 5% of each run, Pallas kernels for 16% -> 23%
where the time goes in v3:
time: 806 us; the launch traced here: 798 us
  Pallas kernels  534 us (66%)
  waiting for transfers between devices  118 us (15%)
  local copies, waits for them, and re-layouts  44.3 us (5%)
  blocking collectives  37.2 us (5%)
  other arithmetic  29 us (4%)
  between operations  21.8 us (3%)
  matrix products  13.1 us (2%)
    pallas_call x12, Pallas kernels, exchange(): pl.pallas_call(functools.partial(exchange_kernel, group, spread), out_sha...  190 us
    pallas_call x3, Pallas kernels, backward_layer(): pl.pallas_call(backward_kernel, out_shape=[jax.ShapeDtypeStruct(*shape) f...  187 us
    pallas_call x3, Pallas kernels, forward_layer(): pl.pallas_call(forward_kernel, out_shape=[jax.ShapeDtypeStruct(*shape) fo...  157 us
    reduce_scatter x3, waiting for transfers between devices, local(): lax.psum_scatter(term, 'dp', scatter_dimension=0).astype(jnp.float32)  118 us
    all_gather x1, blocking collectives, local(): wholes = [lax.all_gather(shard, 'dp') for shard in shards_all[0]]  37.2 us
  transfers between devices with their start and end apart: 5, of which 2 were waited for; matrix products, arithmetic and copies ran while one was open for 5% of the time, Pallas kernels for 23%

profile of v3, /device:TPU:0, one launch (start us, length us, event | category | flops | bytes accessed | tf_op | source)
XLA Modules:
  0.0 798.0 jit_solution(12615156759414123864)
XLA Ops:
  7.2 1.4 convert.16
  8.7 0.8 slice_bitcast_fusion.3
  9.8 0.8 slice.342
  11.3 16.9 %exchange_all.8 = f32[32,24,128]{2,1,0:T(8,128)S(1)} custom-call(f32[24,128]{1,0:T(8,128)S(1)} %maximum_maximum_fusion.source), custom_call_target="tpu_custom_call" | custom-call | tf_op jit(solution)/shard_map/exchange_all/pallas_call | solution.py:165
  28.5 0.7 slice.358.rest_0_
  29.2 0.8 slice.359.rest_1_
  30.0 0.7 slice.347.rest_0_
  30.6 0.8 slice.348.rest_1_
  34.3 0.8 fusion.49
  35.1 19.6 %exchange_all.9 = f32[32,24,24]{2,1,0:T(8,128)S(1)} custom-call(f32[24,24]{1,0:T(8,128)S(1)} %get-tuple-element.276.source), custom_call_target="tpu_custom_call" | custom-call | tf_op jit(solution)/shard_map/exchange_all/pallas_call | solution.py:165
  55.0 0.8 fusion.48
  55.8 18.9 %exchange_all.10 = f32[32,24,24]{2,1,0:T(8,128)S(1)} custom-call(f32[24,24]{1,0:T(8,128)S(1)} %get-tuple-element.278.source), custom_call_target="tpu_custom_call" | custom-call | tf_op jit(solution)/shard_map/exchange_all/pallas_call | solution.py:165
  76.0 17.9 %exchange_dp.2 = f32[8,9,1152]{2,1,0:T(8,128)S(1)} custom-call(f32[8,9,1152]{2,1,0:T(8,128)S(1)} %reshape.611.source), custom_call_target="tpu_custom_call" | custom-call | tf_op jit(solution)/shard_map/exchange_dp/pallas_call | solution.py:165
  93.9 5.3 exchange_tensor.2
  103.5 23.1 %exchange_all.11 = f32[32,48,24]{2,1,0:T(8,128)S(1)} custom-call(f32[48,24]{1,0:T(8,128)S(1)} %pad_maximum_fusion.5.source), custom_call_target="tpu_custom_call" | custom-call | tf_op jit(solution)/shard_map/exchange_all/pallas_call | solution.py:165
  128.9 0.6 broadcast_add_fusion.3.mod_ref
  130.9 1.6 fusion.2.res_ref
  132.4 37.2 %all-gather.w_qkv_ref = bf16[768,576]{1,0:T(8,128)(2,1)} all-gather(bf16[96,576]{1,0:T(8,128)(2,1)S(1)} %slice.341), channel_id=2, replica_groups=mesh['dp'=8,'tensor'=4] {'dp'}, dimensions={0}, use_global_device_ids=true | all-gather | bytes 995328 | tf_op jit(solution)/shard_map/all_gather | solution.py:1157
  169.6 1.7 slice.344.w_attn_ref
  171.3 2.4 slice.345.w_down_ref
  173.7 59.5 %block_forward.3 = (f32[3,64,768]{2,1,0:T(8,128)}, bf16[3,256,768]{2,1,0:T(8,128)(2,1)}, bf16[3,256,576]{2,1,0:T(8,128)(2,1)}, bf16[3,256,192]{2,1,0:T(8,128)(2,...) custom-call(f32[3,64,768]{2,1,0:T(8,128)} %fusion.2.res_ref, ...), custom_call_target="tpu_custom_call" | custom-call | flops 30000001024 | bytes 15728640 | tf_op jit(solution)/shard_map/block_forward/pallas_call | solution.py:728
  233.2 1.7 slice.355.w_attn_ref
  234.9 2.4 slice.356.w_down_ref
  237.3 53.6 %block_forward.4 = (f32[3,64,768]{2,1,0:T(8,128)}, bf16[3,256,768]{2,1,0:T(8,128)(2,1)}, bf16[3,256,576]{2,1,0:T(8,128)(2,1)}, bf16[3,256,192]{2,1,0:T(8,128)(2,...) custom-call(f32[3,64,768]{2,1,0:T(8,128)} %get-tuple-element.80.res_, ...), custom_call_target="tpu_custom_call" | custom-call | flops 30000001024 | bytes 15728640 | tf_op jit(solution)/shard_map/block_forward/pallas_call | solution.py:728
  290.8 1.7 slice.366.w_attn_ref
  292.5 2.4 slice.367.w_down_ref
  294.9 43.6 %block_forward.5 = (f32[3,64,768]{2,1,0:T(8,128)}, bf16[3,256,768]{2,1,0:T(8,128)(2,1)}, bf16[3,256,576]{2,1,0:T(8,128)(2,1)}, bf16[3,256,192]{2,1,0:T(8,128)(2,...) custom-call(f32[3,64,768]{2,1,0:T(8,128)} %get-tuple-element.84.res_, ...), custom_call_target="tpu_custom_call" | custom-call | flops 30000001024 | bytes 15728640 | tf_op jit(solution)/shard_map/block_forward/pallas_call | solution.py:728
  338.5 1.2 reduce_sum.251
  339.8 1.3 multiply_reduce_fusion.5
  341.1 2.5 multiply_reduce_fusion.7
  343.6 0.8 multiply_reduce_fusion.4
  344.4 0.9 multiply_reduce_fusion.3
  345.4 1.0 broadcast_add_fusion.d_res_ref
  346.4 48.1 %block_backward.3 = (f32[3,64,768]{2,1,0:T(8,128)}, bf16[768,576]{1,0:T(8,128)(2,1)}, bf16[768,768]{1,0:T(8,128)(2,1)}, bf16[960,768]{1,0:T(8,128)(2,1)}, f32[3,...) custom-call(f32[3,64,768]{2,1,0:T(8,128)} %broadcast_add_fusion.d_res_ref, ...), custom_call_target="tpu_custom_call" | custom-call | flops 60000002048 | bytes 26214400 | tf_op jit(solution)/shard_map/block_backward/pallas_call | solution.py:998
  394.5 62.6 %block_backward.4 = (f32[3,64,768]{2,1,0:T(8,128)}, bf16[768,576]{1,0:T(8,128)(2,1)}, bf16[768,768]{1,0:T(8,128)(2,1)}, bf16[960,768]{1,0:T(8,128)(2,1)}, f32[3,...) custom-call(f32[3,64,768]{2,1,0:T(8,128)} %get-tuple-element.97.d_re, ...), custom_call_target="tpu_custom_call" | custom-call | flops 60000002048 | bytes 26214400 | tf_op jit(solution)/shard_map/block_backward/pallas_call | solution.py:998
  457.1 76.5 %block_backward.5 = (f32[3,64,768]{2,1,0:T(8,128)}, bf16[768,576]{1,0:T(8,128)(2,1)}, bf16[768,768]{1,0:T(8,128)(2,1)}, bf16[960,768]{1,0:T(8,128)(2,1)}, f32[3,...) custom-call(f32[3,64,768]{2,1,0:T(8,128)} %get-tuple-element.109.d_r, ...), custom_call_target="tpu_custom_call" | custom-call | flops 60000002048 | bytes 26214400 | tf_op jit(solution)/shard_map/block_backward/pallas_call | solution.py:998
  534.5 0.7 fusion.84
  539.4 0.7 concatenate.89
  540.3 30.7 %exchange_all.12 = f32[32,24,128]{2,1,0:T(8,128)S(1)} custom-call(f32[32,24,128]{2,1,0:T(8,128)S(1)} %bitcast.201), custom_call_target="tpu_custom_call" | custom-call | tf_op jit(solution)/shard_map/exchange_all/pallas_call | solution.py:165
  572.0 5.2 exchange_tensor.3
  577.2 13.5 %exchange_dp.3 = bf16[8,9,1152]{2,1,0:T(8,128)(2,1)S(1)} custom-call(bf16[9,1152]{1,0:T(8,128)(2,1)S(1)} %reduce_sum.263.source), custom_call_target="tpu_custom_call" | custom-call | tf_op jit(solution)/shard_map/exchange_dp/pallas_call | solution.py:165
  592.4 15.1 %exchange_all.13 = f32[32,24,24]{2,1,0:T(8,128)S(1)} custom-call(f32[32,24,24]{2,1,0:T(8,128)S(1)} %bitcast.202), custom_call_target="tpu_custom_call" | custom-call | tf_op jit(solution)/shard_map/exchange_all/pallas_call | solution.py:165
  608.3 15.1 %exchange_all.14 = f32[32,24,24]{2,1,0:T(8,128)S(1)} custom-call(f32[32,24,24]{2,1,0:T(8,128)S(1)} %bitcast.203), custom_call_target="tpu_custom_call" | custom-call | tf_op jit(solution)/shard_map/exchange_all/pallas_call | solution.py:165
  626.4 0.7 multiply_reduce_fusion.6
  627.1 1.1 maximum_bitcast_fusion
  628.2 1.1 maximum_bitcast_fusion.1
  629.3 2.0 multiply_reduce_fusion.1
  631.3 56.3 %reduce-scatter.6.cloned.1.call-done = bf16[1,96,768]{2,1,0:T(8,128)(2,1)} async-done(((bf16[8,96,768]{2,1,0:T(8,128)(2,1)}), bf16[1,96,768]{2,1,0:T(8,128)(2,1)}) %reduce-scatter.6.cloned.1.call-update) | async-done | bytes 147472 | tf_op jit(solution)/shard_map/reduce_scatter | solution.py:1243
  687.7 1.1 fusion.26
  688.8 0.8 copy-done.12
  689.6 1.0 multiply_reduce_fusion
  692.0 61.5 %reduce-scatter.8.cloned.1.call-done = bf16[1,120,768]{2,1,0:T(8,128)(2,1)} async-done(((bf16[8,120,768]{2,1,0:T(8,128)(2,1)}), bf16[1,120,768]{2,1,0:T(8,128)(2,1)}) %reduce-scatter.8.cloned.1.call-update) | async-done | bytes 184336 | tf_op jit(solution)/shard_map/reduce_scatter | solution.py:1243
  753.5 0.9 bitcast_convert_fusion
  754.5 0.7 copy-done.14
  755.2 2.0 multiply_reduce_fusion.2
  758.5 8.9 %exchange_all.15 = f32[32,8,128]{2,1,0:T(8,128)S(1)} custom-call(f32[8,128]{1,0:T(8,128)S(1)} %iota.39.source), custom_call_target="tpu_custom_call" | custom-call | tf_op jit(solution)/shard_map/exchange_all/pallas_call | solution.py:165
  768.8 4.4 fusion.70
  773.3 2.8 copy.124
  776.1 2.8 copy.126
  778.9 2.8 copy.125
  781.8 1.2 fusion.30
  783.7 2.5 fusion.68
  786.3 0.9 copy-done.24
  787.2 2.9 fusion.66
  (324 shorter events, 24.2 us)
Async XLA Ops:
  7.2 162.4 %all-gather.8.cloned.1.call-start = ((), (), s32[]{:S(2)}) async-start(), calls=%async_computation.7 | async-start | bytes 1658880 | tf_op jit(solution)/shard_map/all_gather | solution.py:1157
  9.5 164.2 %all-gather.6.cloned.1.call-start = ((), (), s32[]{:S(2)}) async-start(), calls=%async_computation.6 | async-start | bytes 1327104 | tf_op jit(solution)/shard_map/all_gather | solution.py:1157
  10.6 620.8 %reduce-scatter.4.cloned.1.call-start = ((), (), s32[]{:S(2)}) async-start(), calls=%async_computation.3 | async-start | bytes 1105920 | tf_op jit(solution)/shard_map/reduce_scatter | solution.py:1243
  10.7 64.3 %copy-start.27 = (bf16[24,3640]{1,0:T(8,128)(2,1)}, bf16[24,3640]{1,0:T(8,128)(2,1)S(1)}, u32[]{:S(2)}) copy-start(bf16[24,3640]{1,0:T(8,128)(2,1)S(1)} %get-tuple-element.220) | copy-start | bytes 524164
  10.9 119.9 %copy-start.70 = (f32[3]{0:T(128)}, f32[3]{0:T(128)S(1)}, u32[]{:S(2)}) copy-start(f32[3]{0:T(128)S(1)} %get-tuple-element.221) | copy-start | bytes 40
  11.3 20.2 %copy-start.58 = (f32[3,1024]{1,0:T(4,128)S(1)}, f32[3,1024]{1,0:T(4,128)}, u32[]{:S(2)}) copy-start(f32[3,1024]{1,0:T(4,128)} %param.17) | copy-start | bytes 36868
  28.5 4.1 copy-start.59
  32.6 98.3 %copy-start.40 = (f32[3,64,16]{1,2,0:T(8,128)}, f32[3,64,16]{1,2,0:T(8,128)S(1)}, u32[]{:S(2)}) copy-start(f32[3,64,16]{1,2,0:T(8,128)S(1)} %reshape.605) | copy-start | bytes 36868
  33.7 307.4 %copy-start.31 = (f32[3,64,16]{1,2,0:T(8,128)}, f32[3,64,16]{1,2,0:T(8,128)S(1)}, u32[]{:S(2)}) copy-start(f32[3,64,16]{1,2,0:T(8,128)S(1)} %reshape.607) | copy-start | bytes 36868
  33.7 41.7 %copy-start.6 = (f32[3,96,1152]{2,1,0:T(8,128)S(1)}, f32[3,96,1152]{2,1,0:T(8,128)}, u32[]{:S(2)}) copy-start(f32[3,96,1152]{2,1,0:T(8,128)} %param.25) | copy-start | bytes 3981316
  34.1 41.2 %copy-start.68 = (s32[24]{0:T(128)}, s32[24]{0:T(128)S(1)}, u32[]{:S(2)}) copy-start(s32[24]{0:T(128)S(1)} %eq.26) | copy-start | bytes 292
  34.3 40.4 %copy-start.54 = (f32[24,128]{1,0:T(8,128)}, f32[24,128]{1,0:T(8,128)S(1)}, u32[]{:S(2)}) copy-start(f32[24,128]{1,0:T(8,128)S(1)} %get-tuple-element.270) | copy-start | bytes 36868
  34.3 40.7 %copy-start.56 = (f32[24,128]{1,0:T(8,128)}, f32[24,128]{1,0:T(8,128)S(1)}, u32[]{:S(2)}) copy-start(f32[24,128]{1,0:T(8,128)S(1)} %get-tuple-element.271) | copy-start | bytes 36868
  127.5 217.8 %copy-start.29 = (f32[3,768]{1,0:T(4,128)}, f32[3,768]{1,0:T(4,128)S(1)}, u32[]{:S(2)}) copy-start(f32[3,768]{1,0:T(4,128)S(1)} %add.357) | copy-start | bytes 27652
  127.6 213.5 %copy-start.44 = (f32[3,768]{1,0:T(4,128)}, f32[3,768]{1,0:T(4,128)S(1)}, u32[]{:S(2)}) copy-start(f32[3,768]{1,0:T(4,128)S(1)} %add.358) | copy-start | bytes 27652
  128.3 41.3 %copy-start.72 = (f32[3]{0:T(128)}, f32[3]{0:T(128)S(1)}, u32[]{:S(2)}) copy-start(f32[3]{0:T(128)S(1)} %subtract_sqrt_fusion) | copy-start | bytes 40
  338.5 5.1 copy-start.4
  339.8 5.6 copy-start.46
  341.1 4.3 copy-start.50
  343.6 2.8 copy-start.42
  533.6 2.7 copy-start.66
  533.6 3.0 copy-start.65
  533.6 3.3 copy-start.37
  533.6 3.4 copy-start.36
  533.6 3.4 copy-start.35
  533.7 154.0 %reduce-scatter.6.cloned.1.call-start = ((), (), s32[]{:S(2)}) async-start(), calls=%async_computation.4 | async-start | bytes 1327104 | tf_op jit(solution)/shard_map/reduce_scatter | solution.py:1243
  535.1 2.7 copy-start.74
  535.1 3.1 copy-start.32
  535.1 3.1 copy-start.41
  535.2 3.1 copy-start.71
  535.2 3.1 copy-start.73
  535.2 3.6 copy-start.5
  535.2 3.6 copy-start.30
  535.2 3.6 copy-start.43
  535.2 3.6 copy-start.45
  535.2 3.6 copy-start.47
  535.3 3.6 copy-start.51
  535.3 218.3 %reduce-scatter.8.cloned.1.call-start = ((), (), s32[]{:S(2)}) async-start(), calls=%async_computation.5 | async-start | bytes 1658880 | tf_op jit(solution)/shard_map/reduce_scatter | solution.py:1243
  535.8 3.6 copy-start.52
  535.8 3.6 copy-start.53
  535.8 3.6 copy-start.62
  535.8 3.6 copy-start.63
  535.8 3.6 copy-start.64
  572.0 19.1 %copy-start.28 = (bf16[24,3640]{1,0:T(8,128)(2,1)S(1)}, bf16[24,3640]{1,0:T(8,128)(2,1)}, u32[]{:S(2)}) copy-start(bf16[24,3640]{1,0:T(8,128)(2,1)} %copy-done.27) | copy-start | bytes 524164
  572.0 19.6 %copy-start.7 = (f32[3,96,1152]{2,1,0:T(8,128)S(1)}, f32[3,96,1152]{2,1,0:T(8,128)}, u32[]{:S(2)}) copy-start(f32[3,96,1152]{2,1,0:T(8,128)} %param.25) | copy-start | bytes 3981316
  592.4 15.2 %copy-start.61 = (f32[24,24]{1,0:T(8,128)S(1)}, f32[24,24]{1,0:T(8,128)}, u32[]{:S(2)}) copy-start(f32[24,24]{1,0:T(8,128)} %get-tuple-element.279) | copy-start | bytes 6916
  607.5 15.9 %copy-start.60 = (f32[24,24]{1,0:T(8,128)S(1)}, f32[24,24]{1,0:T(8,128)}, u32[]{:S(2)}) copy-start(f32[24,24]{1,0:T(8,128)} %get-tuple-element.277) | copy-start | bytes 6916
  607.5 16.8 %copy-start.55 = (f32[24,128]{1,0:T(8,128)S(1)}, f32[24,128]{1,0:T(8,128)}, u32[]{:S(2)}) copy-start(f32[24,128]{1,0:T(8,128)} %copy-done.54) | copy-start | bytes 36868
  607.5 16.8 %copy-start.57 = (f32[24,128]{1,0:T(8,128)S(1)}, f32[24,128]{1,0:T(8,128)}, u32[]{:S(2)}) copy-start(f32[24,128]{1,0:T(8,128)} %copy-done.56) | copy-start | bytes 36868
  607.5 16.9 %copy-start.69 = (s32[24]{0:T(128)S(1)}, s32[24]{0:T(128)}, u32[]{:S(2)}) copy-start(s32[24]{0:T(128)} %copy-done.68) | copy-start | bytes 292
  607.6 17.2 %copy-start.1 = (f32[32,24,24]{2,1,0:T(8,128)S(1)}, f32[32,24,24]{2,1,0:T(8,128)}, u32[]{:S(2)}) copy-start(f32[32,24,24]{2,1,0:T(8,128)} %copy-done) | copy-start | bytes 221188
  608.1 17.6 %copy-start.3 = (f32[32,24,24]{2,1,0:T(8,128)S(1)}, f32[32,24,24]{2,1,0:T(8,128)}, u32[]{:S(2)}) copy-start(f32[32,24,24]{2,1,0:T(8,128)} %copy-done.2) | copy-start | bytes 221188
  624.5 2.6 copy-start.39
  626.4 2.9 copy-start.49
  629.3 59.5 %copy-start.11 = (f32[1,96,1,1344]{3,1,2,0:T(8,128)}, f32[1,96,1,1344]{3,1,2,0:T(8,128)S(1)}, u32[]{:S(2)}) copy-start(f32[1,96,1,1344]{3,1,2,0:T(8,128)S(1)} %maximum_bitcast_fusion.1) | copy-start | bytes 1548292
  690.6 78.3 %copy-start.9 = (f32[3,96,1,1344]{3,2,1,0:T(1,128)S(1)}, f32[3,96,1,1344]{3,2,1,0:T(1,128)}, u32[]{:S(2)}) copy-start(f32[3,96,1,1344]{3,2,1,0:T(1,128)} %param.23) | copy-start | bytes 4644868
  776.1 5.7 copy-start.33
  776.1 5.7 copy-start.34
  778.9 2.8 copy-start.17
  778.9 2.8 copy-start.22
  778.9 4.1 copy-start.25
  778.9 4.1 copy-start.26
  783.7 2.6 copy-start.23
  783.7 3.5 copy-start.24
  (19 other events, 29.0 us)
Sparse Core Ops, SparseCore 0:
  10.8 54.2 all-gather.7
  67.8 45.8 all-gather.5
  533.8 84.1 reduce-scatter.3
  621.5 66.0 reduce-scatter.5
  691.4 62.0 reduce-scatter.7

commit v4 on v3

--- a/solution.py
+++ b/solution.py
@@ -117,43 +117,78 @@
     return lax.axis_index(group), lax.axis_size(group), lambda at: {group: at}
 
 
-def exchange_kernel(group, spread, source, target, send_sems, recv_sems, local_sem):
+def greet_group(group):
     place, size, coords = group_place(group)
     barrier = pltpu.get_barrier_semaphore()
 
-    def greet(step, carry):
+    def greet_one(step, carry):
         peer = coords(lax.rem(place + step, size))
         pl.semaphore_signal(barrier, inc=1, device_id=peer, device_id_type=pl.DeviceIdType.MESH)
         return carry
 
-    def copy_to(step):
-        there = lax.rem(place + step, size)
+    lax.fori_loop(1, size, greet_one, 0)
+    pl.semaphore_wait(barrier, size - 1)
+
+
+class Crowd:
+    def __init__(self, group, source_at, target, send_sems, recv_sems, local_sem):
+        self.place, self.size, self.coords = group_place(group)
+        self.source_at, self.target = source_at, target
+        self.sends, self.recvs, self.local_sem = send_sems, recv_sems, local_sem
+
+    def copy_to(self, step):
+        there = lax.rem(self.place + step, self.size)
         return pltpu.make_async_remote_copy(
-            src_ref=source.at[there] if spread else source,
-            dst_ref=target.at[place],
-            send_sem=send_sems.at[step],
-            recv_sem=recv_sems.at[step],
-            device_id=coords(there),
+            src_ref=self.source_at(there),
+            dst_ref=self.target.at[self.place],
+            send_sem=self.sends.at[step],
+            recv_sem=self.recvs.at[step],
+            device_id=self.coords(there),
             device_id_type=pl.DeviceIdType.MESH,
         )
 
-    def begin(step, carry):
-        copy_to(step).start()
-        return carry
-
-    def finish(step, carry):
-        copy_to(step).wait()
-        return carry
-
-    lax.fori_loop(1, size, greet, 0)
-    mine = pltpu.make_async_copy(
-        source.at[place] if spread else source, target.at[place], local_sem
-    )
-    mine.start()
-    pl.semaphore_wait(barrier, size - 1)
-    lax.fori_loop(1, size, begin, 0)
-    mine.wait()
-    lax.fori_loop(1, size, finish, 0)
+    def own_copy(self):
+        return pltpu.make_async_copy(
+            self.source_at(self.place), self.target.at[self.place], self.local_sem
+        )
+
+    def start(self):
+        def begin(step, carry):
+            self.copy_to(step).start()
+            return carry
+
+        lax.fori_loop(1, self.size, begin, 0)
+        self.own_copy().start()
+
+    def wait(self):
+        def finish(step, carry):
+            self.copy_to(step).wait()
+            return carry
+
+        self.own_copy().wait()
+        lax.fori_loop(1, self.size, finish, 0)
+
+
+def crowd_scratch(size):
+    return [
+        pltpu.SemaphoreType.DMA((size,)),
+        pltpu.SemaphoreType.DMA((size,)),
+        pltpu.SemaphoreType.DMA,
+    ]
+
+
+def exchange_kernel(group, spread, source, target, send_sems, recv_sems, local_sem):
+    greet_group(group)
+    crowd = Crowd(
+        group,
+        lambda place: source.at[place] if spread else source,
+        target,
+        send_sems,
+        recv_sems,
+        local_sem,
+    )
+    crowd.start()
+    crowd.wait()
 
 
 def exchange(values, group, spread, call_id):
@@ -167,11 +202,7 @@
         out_shape=jax.ShapeDtypeStruct((size,) + block, values.dtype),
         in_specs=[pl.BlockSpec(memory_space=pltpu.VMEM)],
         out_specs=pl.BlockSpec(memory_space=pltpu.VMEM),
-        scratch_shapes=[
-            pltpu.SemaphoreType.DMA((size,)),
-            pltpu.SemaphoreType.DMA((size,)),
-            pltpu.SemaphoreType.DMA,
-        ],
+        scratch_shapes=crowd_scratch(size),
         compiler_params=pltpu.CompilerParams(
             collective_id=call_id, has_side_effects=True, vmem_limit_bytes=32 * 2**20
         ),
@@ -1021,6 +1052,386 @@
     )(d_residual, mod_vec, *saved, *weights, *terms)
 
 
+def dense_nt(left_op, right_op):
+    return lax.dot_general(
+        left_op,
+        right_op,
+        (((1,), (1,)), ((), ())),
+        precision=PRECISE,
+        preferred_element_type=jnp.float32,
+    )
+
+
+def dense_tn(left_op, right_op):
+    return lax.dot_general(
+        left_op,
+        right_op,
+        (((0,), (0,)), ((), ())),
+        precision=PRECISE,
+        preferred_element_type=jnp.float32,
+    )
+
+
+def chosen(shape, rule, kind):
+    row = lax.broadcasted_iota(jnp.int32, shape, 0)
+    col = lax.broadcasted_iota(jnp.int32, shape, 1)
+    return jnp.where(rule(row, col), 1.0, 0.0).astype(kind)
+
+
+def fold(values):
+    groups = values.shape[-2] // 8
+    pieces = [values[..., 8 * at : 8 * at + 8, :] for at in range(groups)]
+    used = groups * values.shape[-1]
+    if used % 128:
+        pieces.append(jnp.zeros(values.shape[:-2] + (8, 128 - used % 128), values.dtype))
+    return jnp.concatenate(pieces, axis=-1)
+
+
+def folded_lanes(cols, count):
+    return -(-(cols // 8 * count) // 128) * 128
+
+
+def unfold(values, cols, count):
+    pieces = [values[..., at * count : (at + 1) * count] for at in range(cols // 8)]
+    return jnp.concatenate(pieces, axis=-2)
+
+
+def slots_of(images):
+    return -(-LAYERS * images // 16) * 16
+
+
+def head_kernel(
+    images,
+    small_ref,
+    feats_ref,
+    table_ref,
+    time_ref,
+    second_ref,
+    shift_ref,
+    scale_ref,
+    bias_ref,
+    mod_ref,
+    *rest,
+):
+    shards = rest[0:3]
+    (
+        small_all,
+        feats_out,
+        pre_time_out,
+        hidden_out,
+        pre_signal_out,
+        signal_out,
+        final_all,
+        mod_all,
+    ) = rest[3:11]
+    wholes = rest[11:14]
+    (
+        feats_all,
+        hidden_own,
+        hidden_all,
+        signal_own,
+        signal_all,
+        final_own,
+        mod_part,
+        mod_in,
+        mod_own,
+        small_dp,
+    ) = rest[14:24]
+    crowds = [rest[24 + 3 * index : 27 + 3 * index] for index in range(8)]
+    gather_sems = rest[48:]
+    dp_size = lax.axis_size("dp")
+    tensor_size = lax.axis_size("tensor")
+    dp_rank = lax.axis_index("dp")
+    images_all = images * dp_size
+    slots = mod_own.shape[0]
+    greet_group("all")
+    gather = Gather(Line(), shards, wholes, *gather_sems)
+    feats = Crowd("dp", lambda place: feats_ref, feats_all, *crowds[0])
+    small = Crowd("dp", lambda place: small_ref, small_dp, *crowds[1])
+    small_spread = Crowd("tensor", lambda place: small_dp, small_all, *crowds[7])
+    hidden = Crowd("all", lambda place: hidden_own, hidden_all, *crowds[2])
+    signal = Crowd("all", lambda place: signal_own, signal_all, *crowds[3])
+    final = Crowd("all", lambda place: final_own.at[place // tensor_size], final_all, *crowds[4])
+    mod_sum = Crowd("dp", lambda place: mod_part.at[place], mod_in, *crowds[5])
+    feats.start()
+    small.start()
+    gather.start()
+    feats.wait()
+    pick = chosen(
+        (images_all, 8 * dp_size),
+        lambda row, col: (row // images == col // 8) & (lax.rem(row, images) == lax.rem(col, 8)),
+        jnp.float32,
+    )
+    feats_sum = dense(pick, feats_all[...].reshape(8 * dp_size, feats_all.shape[2]))
+    feats_out[...] = feats_sum
+    pre_time = dense_nt(time_ref[...], feats_sum[:, 0:FREQ]) + bias_ref[:, 1:2]
+    pre_time_out[...] = pre_time
+    hidden_own[...] = fold(jax.nn.silu(pre_time))
+    hidden.start()
+    class_lanes = -(-CLASSES // 128) * 128
+    labels = jnp.round(feats_sum[:, FREQ : FREQ + 1]).astype(jnp.int32)
+    lane = lax.broadcasted_iota(jnp.int32, (images_all, class_lanes), 1)
+    onehot = jnp.where(lane == labels, 1.0, 0.0)
+    class_part = dense_nt(table_ref[:, 0:class_lanes], onehot) + bias_ref[:, 2:3]
+    gather.tick(1)
+    hidden.wait()
+    cols = second_ref.shape[0]
+    hidden_full = unfold(hidden_all[...], cols, images_all).reshape(D, images_all)
+    hidden_out[...] = hidden_full
+    pre_signal = dense(second_ref[...], hidden_full) + class_part
+    pre_signal_out[...] = pre_signal
+    signal_own[...] = fold(jax.nn.silu(pre_signal))
+    signal.start()
+    gather.tick(2)
+    signal.wait()
+    signal_full = unfold(signal_all[...], cols, images_all).reshape(D, images_all)
+    signal_out[...] = signal_full
+    mod_rows = mod_ref.shape[1]
+    own_rows = pl.ds(pl.multiple_of(dp_rank * mod_rows, 8), mod_rows)
+    signal_low = signal_out[own_rows, :].astype(jnp.bfloat16)
+    total = None
+    for layer_idx in range(LAYERS):
+        pick = chosen(
+            (images_all, dp_size * slots),
+            lambda row, col: (
+                (row // images == col // slots)
+                & (lax.rem(row, images) + layer_idx * images == lax.rem(col, slots))
+            ),
+            jnp.bfloat16,
+        )
+        placed = dot_nn(signal_low, pick).astype(jnp.bfloat16)
+        term = dot_tn(placed, mod_ref[layer_idx])
+        total = term if total is None else total + term
+    mod_part[...] = total.reshape(mod_part.shape)
+    mod_sum.start()
+    small.wait()
+    small_spread.start()
+    finals = jnp.concatenate(
+        [
+            dense(shift_ref[...], signal_full) + bias_ref[:, 3:4],
+            dense(scale_ref[...], signal_full) + bias_ref[:, 4:5],
+            jnp.zeros((128 - 2 * shift_ref.shape[0], images_all), jnp.float32),
+        ],
+        axis=0,
+    )
+    pick = chosen(
+        (8 * dp_size, images_all),
+        lambda row, col: (row // 8 == col // images) & (lax.rem(row, 8) == lax.rem(col, images)),
+        jnp.float32,
+    )
+    final_own[...] = dense_nt(pick, finals).reshape(final_own.shape)
+    final.start()
+    run_ticks(gather, 3, min(4, dp_size // 2))
+    mod_sum.wait()
+    mod_own[...] = jnp.sum(mod_in[...], axis=0)
+    mod_spread = Crowd("tensor", lambda place: mod_own, mod_all, *crowds[6])
+    mod_spread.start()
+    each(max(dp_size // 2 - 4, 0), lambda step: gather.tick(step + 4))
+    small_spread.wait()
+    final.wait()
+    mod_spread.wait()
+    gather.finish()
+
+
+def head_call(small, feats, table, times, second, shift, scale, bias, mod_low, shards, images):
+    dp_size, tensor_size = lax.axis_size("dp"), lax.axis_size("tensor")
+    size = dp_size * tensor_size
+    images_all = images * dp_size
+    cols = table.shape[0]
+    slots = slots_of(images)
+    folded = folded_lanes(cols, images_all)
+    full, low = jnp.float32, jnp.bfloat16
+    shapes = [
+        ((tensor_size, dp_size) + small.shape, full),
+        ((images_all, feats.shape[1]), full),
+        ((cols, images_all), full),
+        ((D, images_all), full),
+        ((cols, images_all), full),
+        ((D, images_all), full),
+        ((size, 8, 128), full),
+        ((tensor_size, slots, mod_low.shape[2]), full),
+    ] + [((dp_size,) + shard.shape, low) for shard in shards]
+    scratch = [
+        pltpu.VMEM((dp_size,) + feats.shape, full),
+        pltpu.VMEM((8, folded), full),
+        pltpu.VMEM((size, 8, folded), full),
+        pltpu.VMEM((8, folded), full),
+        pltpu.VMEM((size, 8, folded), full),
+        pltpu.VMEM((dp_size, 8, 128), full),
+        pltpu.VMEM((dp_size, slots, mod_low.shape[2]), full),
+        pltpu.VMEM((dp_size, slots, mod_low.shape[2]), full),
+        pltpu.VMEM((slots, mod_low.shape[2]), full),
+        pltpu.VMEM((dp_size,) + small.shape, full),
+    ]
+    for count in (dp_size, dp_size, size, size, size, dp_size, tensor_size, tensor_size):
+        scratch += crowd_scratch(count)
+    scratch += [
+        pltpu.SemaphoreType.DMA((3, dp_size // 2, 3)),
+        pltpu.SemaphoreType.DMA((3, dp_size // 2, 3)),
+        pltpu.SemaphoreType.DMA((3,)),
+    ]
+    return pl.pallas_call(
+        functools.partial(head_kernel, images),
+        out_shape=[jax.ShapeDtypeStruct(*shape) for shape in shapes],
+        in_specs=[pl.BlockSpec(memory_space=pltpu.VMEM)] * (9 + len(shards)),
+        out_specs=[pl.BlockSpec(memory_space=pltpu.VMEM)] * len(shapes),
+        scratch_shapes=scratch,
+        compiler_params=pltpu.CompilerParams(
+            collective_id=30, has_side_effects=True, vmem_limit_bytes=ACT_VMEM
+        ),
+        name="head",
+    )(small, feats, table, times, second, shift, scale, bias, mod_low, *shards)
+
+
+def tail_kernel(
+    images,
+    final_at,
+    row_ref,
+    mod_ref,
+    weight_ref,
+    second_ref,
+    shift_ref,
+    scale_ref,
+    pre_signal_ref,
+    pre_time_ref,
+    *rest,
+):
+    terms = rest[0:3]
+    row_sums, d_final, d_mod_all, d_signal_own, d_hidden_own = rest[3:8]
+    totals = rest[8:11]
+    row_in, mod_in, mod_low, signal_part, signal_out, signal_in, hidden_out, hidden_in = rest[11:19]
+    pair_in, way_in, way_out = rest[19:22], rest[22:25], rest[25:28]
+    crowds = [rest[28 + 3 * index : 31 + 3 * index] for index in range(5)]
+    reduce_sems = rest[43:]
+    dp_size = lax.axis_size("dp")
+    tensor_size = lax.axis_size("tensor")
+    dp_rank = lax.axis_index("dp")
+    images_all = images * dp_size
+    cols, lanes = row_ref.shape[1:]
+    mod_rows = weight_ref.shape[1]
+    slots = mod_low.shape[0]
+    last_step = dp_size // 2
+    greet_group("all")
+    reduce = Reduce(Line(), terms, totals, pair_in, way_in, way_out, *reduce_sems)
+
+    mod_sum = Crowd("tensor", lambda place: mod_ref.at[place], mod_in, *crowds[0])
+    rows = Crowd("all", lambda place: row_ref.at[place], row_in, *crowds[1])
+    mod_spread = Crowd("dp", lambda place: mod_low, d_mod_all, *crowds[2])
+    signal = Crowd("all", lambda place: signal_out.at[place], signal_in, *crowds[3])
+    hidden = Crowd("all", lambda place: hidden_out.at[place], hidden_in, *crowds[4])
+    mod_sum.start()
+    rows.start()
+    reduce.start()
+    mod_sum.wait()
+    mod_low[...] = jnp.sum(mod_in[...], axis=0).astype(jnp.bfloat16)
+    mod_spread.start()
+    rows.wait()
+    row_sums[...] = jnp.sum(row_in[...], axis=0)
+    group_sums = [
+        jnp.sum(row_in[at * tensor_size : (at + 1) * tensor_size], axis=0)
+        for at in range(dp_size)
+    ]
+    joined = jnp.concatenate(group_sums, axis=1)
+
+    def final_of(piece):
+        return dense(
+            joined,
+            chosen(
+                (dp_size * lanes, images_all),
+                lambda row, col: (
+                    (row // lanes == col // images)
+                    & (lax.rem(row, lanes) == final_at + piece * images + lax.rem(col, images))
+                ),
+                jnp.float32,
+            ),
+        )
+
+    d_shift, d_scale = final_of(0), final_of(1)
+    d_final[0] = d_shift
+    d_final[1] = d_scale
+    signal_part[...] = dense_tn(shift_ref[...], d_shift) + dense_tn(scale_ref[...], d_scale)
+    run_ticks(reduce, 0, min(1, last_step))
+    mod_spread.wait()
+    d_mod = d_mod_all[...].reshape(dp_size * slots, mod_low.shape[1])
+    own_rows = pl.ds(pl.multiple_of(dp_rank * mod_rows, 8), mod_rows)
+    for layer_idx in range(LAYERS):
+        pick = chosen(
+            (dp_size * slots, images_all),
+            lambda row, col: (
+                (row // slots == col // images)
+                & (lax.rem(row, slots) == layer_idx * images + lax.rem(col, images))
+            ),
+            jnp.float32,
+        )
+        signal_part[own_rows, :] += dense(dot_nt(weight_ref[layer_idx], d_mod), pick)
+    places = dp_size * tensor_size
+    signal_out[...] = fold(signal_part[...].reshape(places, cols, images_all))
+    signal.start()
+    run_ticks(reduce, 1, min(2, last_step))
+    signal.wait()
+    d_signal = unfold(jnp.sum(signal_in[...], axis=0), cols, images_all)
+    d_signal = d_signal * silu_slope(pre_signal_ref[...])
+    d_signal_own[...] = d_signal
+    d_hidden = dense_tn(second_ref[...], d_signal)
+    hidden_out[...] = fold(d_hidden.reshape(places, cols, images_all))
+    hidden.start()
+    run_ticks(reduce, 2, min(3, last_step))
+    hidden.wait()
+    d_hidden = unfold(jnp.sum(hidden_in[...], axis=0), cols, images_all)
+    d_hidden_own[...] = d_hidden * silu_slope(pre_time_ref[...])
+    run_ticks(reduce, 3, min(4, last_step))
+    each(max(last_step - 4, 0), lambda step: reduce.tick(step + 4))
+    reduce.finish()
+
+
+def tail_call(rows, mods, mod_low, second, shift, scale, pre_signal, pre_time, terms, images, at):
+    dp_size, tensor_size = lax.axis_size("dp"), lax.axis_size("tensor")
+    size = dp_size * tensor_size
+    images_all = images * dp_size
+    cols, lanes = rows.shape[1:]
+    folded = folded_lanes(cols, images_all)
+    full, low = jnp.float32, jnp.bfloat16
+    spots = dp_size // 2
+    blocks = [term.shape[1:] for term in terms]
+    shapes = [
+        ((cols, lanes), full),
+        ((2, cols, images_all), full),
+        ((dp_size,) + mods.shape[1:], low),
+        ((cols, images_all), full),
+        ((cols, images_all), full),
+    ] + [(block, full) for block in blocks]
+    scratch = [
+        pltpu.VMEM(rows.shape, full),
+        pltpu.VMEM(mods.shape, full),
+        pltpu.VMEM(mods.shape[1:], low),
+        pltpu.VMEM((D, images_all), full),
+        pltpu.VMEM((size, 8, folded), full),
+        pltpu.VMEM((size, 8, folded), full),
+        pltpu.VMEM((size, 8, folded), full),
+        pltpu.VMEM((size, 8, folded), full),
+    ]
+    scratch += [pltpu.VMEM((spots,) + block, low) for block in blocks]
+    scratch += [pltpu.VMEM((2, spots) + block, low) for block in blocks]
+    scratch += [pltpu.VMEM((2, spots) + block, low) for block in blocks]
+    for count in (tensor_size, size, dp_size, size, size):
+        scratch += crowd_scratch(count)
+    scratch += [
+        pltpu.SemaphoreType.DMA((3, spots, 3)),
+        pltpu.SemaphoreType.DMA((3, spots, 3)),
+    ]
+    return pl.pallas_call(
+        functools.partial(tail_kernel, images, at),
+        out_shape=[jax.ShapeDtypeStruct(*shape) for shape in shapes],
+        in_specs=[pl.BlockSpec(memory_space=pltpu.VMEM)] * (8 + len(terms)),
+        out_specs=[pl.BlockSpec(memory_space=pltpu.VMEM)] * len(shapes),
+        scratch_shapes=scratch,
+        compiler_params=pltpu.CompilerParams(
+            collective_id=31, has_side_effects=True, vmem_limit_bytes=ACT_VMEM
+        ),
+        name="tail",
+    )(rows, mods, mod_low, second, shift, scale, pre_signal, pre_time, *terms)
+
+
 def adam_update(weight, first, second, grad, factor, first_fix, second_fix):
     clipped = grad * factor
     first_new = BETA_ONE * first + (1.0 - BETA_ONE) * clipped
@@ -1069,7 +1480,7 @@
     dp_size = lax.axis_size("dp")
     place_count = dp_size * tensor_size
     images_all = images * dp_size
-    table_cols = embed_table.T.astype(jnp.bfloat16).astype(jnp.float32)
+    table_cols = lax.reduce_precision(embed_table.T, 8, 7)
     cols = table_cols.shape[0]
     mod_rows = layer_ada.shape[1]
     mod_cols = layer_ada.shape[2]
@@ -1081,62 +1492,117 @@
     vector_count = 5 + LAYERS * layer_rows
     small_count = 2 * patch_in + vector_count
     lanes = -(-(small_count + 2 * images) // 128) * 128
-    scalar_lanes = jnp.concatenate([timesteps, labels]).astype(jnp.float32)
-    small_send = jnp.concatenate(
-        [
-            col_block(patch_start, patch_in),
-            col_block(head_start, patch_in + vector_count),
-            jnp.broadcast_to(scalar_lanes[None, :], (cols, 2 * images)),
-            jnp.zeros((cols, lanes - small_count - 2 * images), jnp.float32),
-        ],
-        axis=1,
-    )
-    small_all = exchange(small_send, "all", False, 1)
+    shards_all = []
+    for layer_idx in range(LAYERS):
+        shard_in = layer_in[layer_idx, :, 0].astype(jnp.bfloat16)
+        shard_out = layer_out[layer_idx, 0].astype(jnp.bfloat16)
+        shards_all.append(
+            (shard_in[:, : 3 * group_width], shard_in[:, 3 * group_width :], shard_out)
+        )
+    second_cols = col_block(second_start, D)
+    shift_cols = col_block(final_start, D)
+    scale_cols = col_block(final_start + D, D)
+    fused = cols % 8 == 0 and images <= 8
+    if fused:
+        small_send = jnp.concatenate(
+            [
+                col_block(patch_start, patch_in),
+                col_block(head_start, patch_in + vector_count),
+                jnp.zeros((cols, lanes - small_count), jnp.float32),
+            ],
+            axis=1,
+        )
+        feats_send = jnp.concatenate(
+            [
+                time_features(timesteps),
+                jnp.broadcast_to(labels.astype(jnp.float32)[:, None], (images, 128)),
+            ],
+            axis=1,
+        )
+        feats_send = jnp.pad(feats_send, ((0, 8 - images), (0, 0)))
+        outs = head_call(
+            small_send,
+            feats_send,
+            table_cols,
+            col_block(time_start, FREQ),
+            second_cols,
+            shift_cols,
+            scale_cols,
+            col_block(vector_start, 5),
+            mod_low,
+            shards_all[0],
+            images,
+        )
+        small_all, feats_all, pre_time, hidden, pre_signal, signal, final_all, mod_full = outs[:8]
+        wholes = outs[8:]
+        small_all = small_all.transpose(1, 0, 2, 3)
+        time_feats = feats_all[:, :FREQ]
+        labels_all = jnp.round(feats_all[:, FREQ]).astype(jnp.int32)
+        signal_low = lax.dynamic_slice_in_dim(
+            signal.astype(jnp.bfloat16), dp_rank * mod_rows, mod_rows, 0
+        )
+        final_own = final_all[:, :images, : 2 * cols].reshape(place_count, images, 2, cols)
+        final_own = final_own.transpose(2, 1, 0, 3).reshape(2, images, D)
+        mod_full = mod_full[:, : LAYERS * images].reshape(tensor_size, LAYERS, images, mod_cols)
+        mod_full = mod_full.transpose(1, 2, 0, 3).reshape(LAYERS, images, tensor_size * mod_cols)
+    else:
+        scalar_lanes = jnp.concatenate([timesteps, labels]).astype(jnp.float32)
+        small_send = jnp.concatenate(
+            [
+                col_block(patch_start, patch_in),
+                col_block(head_start, patch_in + vector_count),
+                jnp.broadcast_to(scalar_lanes[None, :], (cols, 2 * images)),
+                jnp.zeros((cols, lanes - small_count - 2 * images), jnp.float32),
+            ],
+            axis=1,
+        )
+        small_all = exchange(small_send, "all", False, 1)
+        scalars_all = small_all[::tensor_size, 0, small_count : small_count + 2 * images].astype(
+            jnp.int32
+        )
+        timesteps_all = scalars_all[:, :images].reshape(images_all)
+        labels_all = scalars_all[:, images:].reshape(images_all)
+        time_feats = time_features(timesteps_all)
+        onehot = (labels_all[:, None] == jnp.arange(CLASSES, dtype=jnp.int32)[None, :]).astype(
+            jnp.float32
+        )
+        pre_time = dense(col_block(time_start, FREQ), time_feats.T) + col_block(vector_start + 1, 1)
+        hidden = exchange(jax.nn.silu(pre_time), "all", False, 2).reshape(D, images_all)
+        pre_signal = (
+            dense(second_cols, hidden)
+            + col_block(vector_start + 2, 1)
+            + dense(col_block(0, CLASSES), onehot.T)
+        )
+        signal = exchange(jax.nn.silu(pre_signal), "all", False, 3).reshape(D, images_all)
+        final_send = jnp.concatenate(
+            [
+                dense(shift_cols, signal) + col_block(vector_start + 3, 1),
+                dense(scale_cols, signal) + col_block(vector_start + 4, 1),
+            ],
+            axis=0,
+        )
+        final_all = exchange(final_send, "all", False, 4).reshape(place_count, 2, cols, images_all)
+        final_own = lax.dynamic_slice_in_dim(final_all, dp_rank * images, images, 3)
+        final_own = final_own.transpose(1, 3, 0, 2).reshape(2, images, D)
+        signal_low = lax.dynamic_slice_in_dim(
+            signal.astype(jnp.bfloat16), dp_rank * mod_rows, mod_rows, 0
+        )
+        mod_part = jnp.einsum("db,lde->ble", signal_low, mod_low, preferred_element_type=jnp.float32)
+        mod_part = mod_part.reshape(dp_size, images * LAYERS, mod_cols)
+        mod_local = jnp.sum(exchange(mod_part, "dp", True, 5), axis=0)
+        mod_full = exchange(mod_local, "tensor", False, 6)
+        mod_full = mod_full.reshape(tensor_size, images, LAYERS, mod_cols)
+        mod_full = mod_full.transpose(2, 1, 0, 3).reshape(LAYERS, images, tensor_size * mod_cols)
+        wholes = [lax.all_gather(shard, "dp") for shard in shards_all[0]]
     small_rows = small_all.reshape(D, lanes).T
     patch_w = small_rows[0:patch_in]
     head_w = small_rows[patch_in : 2 * patch_in]
     vectors = small_rows[2 * patch_in : 2 * patch_in + 5]
     bias_all = small_rows[2 * patch_in + 5 : small_count]
-    scalars_all = small_all[::tensor_size, 0, small_count : small_count + 2 * images].astype(
-        jnp.int32
-    )
-    timesteps_all = scalars_all[:, :images].reshape(images_all)
-    labels_all = scalars_all[:, images:].reshape(images_all)
-    time_feats = time_features(timesteps_all)
     onehot = (labels_all[:, None] == jnp.arange(CLASSES, dtype=jnp.int32)[None, :]).astype(
         jnp.float32
     )
-    pre_time = dense(col_block(time_start, FREQ), time_feats.T) + col_block(vector_start + 1, 1)
-    hidden = exchange(jax.nn.silu(pre_time), "all", False, 2).reshape(D, images_all)
-    second_cols = col_block(second_start, D)
-    shift_cols = col_block(final_start, D)
-    scale_cols = col_block(final_start + D, D)
-    pre_signal = (
-        dense(second_cols, hidden)
-        + col_block(vector_start + 2, 1)
-        + dense(col_block(0, CLASSES), onehot.T)
-    )
-    signal = exchange(jax.nn.silu(pre_signal), "all", False, 3).reshape(D, images_all)
-    final_send = jnp.concatenate(
-        [
-            dense(shift_cols, signal) + col_block(vector_start + 3, 1),
-            dense(scale_cols, signal) + col_block(vector_start + 4, 1),
-        ],
-        axis=0,
-    )
-    final_all = exchange(final_send, "all", False, 4).reshape(place_count, 2, cols, images_all)
-    final_own = lax.dynamic_slice_in_dim(final_all, dp_rank * images, images, 3)
-    final_own = final_own.transpose(1, 3, 0, 2).reshape(2, images, D)
     final_shift, final_scale = final_own[0], final_own[1]
-    signal_low = lax.dynamic_slice_in_dim(
-        signal.astype(jnp.bfloat16), dp_rank * mod_rows, mod_rows, 0
-    )
-    mod_part = jnp.einsum("db,lde->ble", signal_low, mod_low, preferred_element_type=jnp.float32)
-    mod_part = mod_part.reshape(dp_size, images * LAYERS, mod_cols)
-    mod_local = jnp.sum(exchange(mod_part, "dp", True, 5), axis=0)
-    mod_full = exchange(mod_local, "tensor", False, 6)
-    mod_full = mod_full.reshape(tensor_size, images, LAYERS, mod_cols)
-    mod_full = mod_full.transpose(2, 1, 0, 3).reshape(LAYERS, images, tensor_size * mod_cols)
     pixels = patchify(latents, local_rows)
     targets = patchify(target_noise, local_rows)
     keep_coef, drop_coef = noise_levels(timesteps)
@@ -1147,14 +1613,6 @@
         + position_table(tensor_rank * local_rows, local_rows)[None]
     )
     saved_acts = []
-    shards_all = []
-    for layer_idx in range(LAYERS):
-        shard_in = layer_in[layer_idx, :, 0].astype(jnp.bfloat16)
-        shard_out = layer_out[layer_idx, 0].astype(jnp.bfloat16)
-        shards_all.append(
-            (shard_in[:, : 3 * group_width], shard_in[:, 3 * group_width :], shard_out)
-        )
-    wholes = [lax.all_gather(shard, "dp") for shard in shards_all[0]]
     for layer_idx in range(LAYERS):
         bias_rows = bias_all[layer_idx * layer_rows : (layer_idx + 1) * layer_rows]
         up_all = bias_rows[10:].reshape(FF)
@@ -1237,13 +1695,6 @@
                 axis=0,
             ),
         )
-    totals.insert(
-        0,
-        [
-            lax.psum_scatter(term, "dp", scatter_dimension=0).astype(jnp.float32)
-            for term in terms
-        ],
-    )
     d_patch_w = jnp.einsum("btp,btd->pd", noisy, d_residual, precision=PRECISE)
     d_patch_b = jnp.sum(d_residual, axis=(0, 1))
     row_parts = jnp.concatenate(
@@ -1253,38 +1704,69 @@
     row_count = row_parts.shape[0]
     row_lanes = -(-row_count // 128) * 128
     row_parts = jnp.pad(row_parts, ((0, row_lanes - row_count), (0, 0)))
-    row_all = exchange(row_parts.T.reshape(place_count, cols, row_lanes), "all", True, 7)
-    row_sums = jnp.sum(row_all, axis=0)
     final_at = row_count - 2 * images
-    final_sums = jnp.sum(
-        row_all[:, :, final_at:row_count].reshape(dp_size, tensor_size, cols, 2, images), axis=1
-    )
-    final_sums = final_sums.transpose(2, 1, 0, 3).reshape(2, cols, images_all)
-    d_shift_cols, d_scale_cols = final_sums[0], final_sums[1]
-    mod_parts = jnp.stack(mod_parts).reshape(LAYERS * images, tensor_size, mod_cols)
-    d_mod_own = jnp.sum(exchange(mod_parts.transpose(1, 0, 2), "tensor", True, 8), axis=0)
-    d_mod_low = exchange(d_mod_own.astype(jnp.bfloat16), "dp", False, 9)
-    d_mod_low = d_mod_low.reshape(dp_size, LAYERS, images, mod_cols)
-    d_mod_low = d_mod_low.transpose(1, 0, 2, 3).reshape(LAYERS, images_all, mod_cols)
+    row_send = row_parts.T.reshape(place_count, cols, row_lanes)
+    mod_send = jnp.stack(mod_parts).reshape(LAYERS * images, tensor_size, mod_cols)
+    mod_send = mod_send.transpose(1, 0, 2)
+    if fused:
+        slots = slots_of(images)
+        outs = tail_call(
+            row_send,
+            jnp.pad(mod_send, ((0, 0), (0, slots - LAYERS * images), (0, 0))),
+            mod_low,
+            second_cols,
+            shift_cols,
+            scale_cols,
+            pre_signal,
+            pre_time,
+            terms,
+            images,
+            final_at,
+        )
+        row_sums, final_sums, d_mod_low, d_pre_signal, d_hidden = outs[:5]
+        totals.insert(0, outs[5:])
+        d_shift_cols, d_scale_cols = final_sums[0], final_sums[1]
+        d_mod_low = d_mod_low[:, : LAYERS * images]
+        d_mod_low = d_mod_low.reshape(dp_size, LAYERS, images, mod_cols)
+        d_mod_low = d_mod_low.transpose(1, 0, 2, 3).reshape(LAYERS, images_all, mod_cols)
+    else:
+        totals.insert(
+            0,
+            [
+                lax.psum_scatter(term, "dp", scatter_dimension=0).astype(jnp.float32)
+                for term in terms
+            ],
+        )
+        row_all = exchange(row_send, "all", True, 7)
+        row_sums = jnp.sum(row_all, axis=0)
+        final_sums = jnp.sum(
+            row_all[:, :, final_at:row_count].reshape(dp_size, tensor_size, cols, 2, images), axis=1
+        )
+        final_sums = final_sums.transpose(2, 1, 0, 3).reshape(2, cols, images_all)
+        d_shift_cols, d_scale_cols = final_sums[0], final_sums[1]
+        d_mod_own = jnp.sum(exchange(mod_send, "tensor", True, 8), axis=0)
+        d_mod_low = exchange(d_mod_own.astype(jnp.bfloat16), "dp", False, 9)
+        d_mod_low = d_mod_low.reshape(dp_size, LAYERS, images, mod_cols)
+        d_mod_low = d_mod_low.transpose(1, 0, 2, 3).reshape(LAYERS, images_all, mod_cols)
+        d_signal_rows = jnp.einsum(
+            "lbe,lde->db", d_mod_low, mod_low, preferred_element_type=jnp.float32
+        )
+        d_signal_part = dense(shift_cols.T, d_shift_cols) + dense(scale_cols.T, d_scale_cols)
+        d_signal_part = d_signal_part + lax.dynamic_update_slice_in_dim(
+            jnp.zeros((D, images_all), jnp.float32), d_signal_rows, dp_rank * mod_rows, 0
+        )
+        d_signal_cols = jnp.sum(
+            exchange(d_signal_part.reshape(place_count, cols, images_all), "all", True, 10), axis=0
+        )
+        d_pre_signal = d_signal_cols * silu_slope(pre_signal)
+        d_hidden_part = dense(second_cols.T, d_pre_signal)
+        d_hidden_cols = jnp.sum(
+            exchange(d_hidden_part.reshape(place_count, cols, images_all), "all", True, 11), axis=0
+        )
+        d_hidden = d_hidden_cols * silu_slope(pre_time)
     mod_grad = jnp.einsum(
         "db,lbe->lde", signal_low, d_mod_low, preferred_element_type=jnp.float32
     )
-    d_signal_rows = jnp.einsum(
-        "lbe,lde->db", d_mod_low, mod_low, preferred_element_type=jnp.float32
-    )
-    d_signal_part = dense(shift_cols.T, d_shift_cols) + dense(scale_cols.T, d_scale_cols)
-    d_signal_part = d_signal_part + lax.dynamic_update_slice_in_dim(
-        jnp.zeros((D, images_all), jnp.float32), d_signal_rows, dp_rank * mod_rows, 0
-    )
-    d_signal_cols = jnp.sum(
-        exchange(d_signal_part.reshape(place_count, cols, images_all), "all", True, 10), axis=0
-    )
-    d_pre_signal = d_signal_cols * silu_slope(pre_signal)
-    d_hidden_part = dense(second_cols.T, d_pre_signal)
-    d_hidden_cols = jnp.sum(
-        exchange(d_hidden_part.reshape(place_count, cols, images_all), "all", True, 11), axis=0
-    )
-    d_hidden = d_hidden_cols * silu_slope(pre_time)
     table_grad = jnp.concatenate(
         [
             dense(d_pre_signal, onehot),

time: 806 us -> 631 us (0.78)
  waiting for transfers between devices: 118 us -> 0 us
  blocking collectives: 37.2 us -> 0 us
  between operations: 21.8 us -> 8.23 us
    pallas_call x12 -> x1, Pallas kernels: 190 us -> 10.1 us  [exchange(): pl.pallas_call(functools.partial(exchange_kernel, group, spread), out_sha...]
    pallas_call x0 -> x2, Pallas kernels: none -> 173 us  [the longest x1 102 us: tail_call(): pl.pallas_call(functools.partial(tail_kernel, images, at), out_shape=[jax...]
    reduce_scatter x3 -> x0, waiting for transfers between devices: 118 us -> none  [local(): lax.psum_scatter(term, 'dp', scatter_dimension=0).astype(jnp.float32)]
    all_gather x1 -> x0, blocking collectives: 37.2 us -> none  [local(): wholes = [lax.all_gather(shard, 'dp') for shard in shards_all[0]]]
  transfers between devices with their start and end apart: 5 -> 0, of which waited for: 2 -> 0; matrix products, arithmetic and copies ran while one was open for 5% -> 0% of each run, Pallas kernels for 23% -> 0%
where the time goes in v4:
time: 631 us; the launch traced here: 623 us
  Pallas kernels  526 us (83%)
  local copies, waits for them, and re-layouts  43.6 us (7%)
  other arithmetic  32.6 us (5%)
  matrix products  12.6 us (2%)
  between operations  8.23 us (1%)
    pallas_call x3, Pallas kernels, backward_layer(): pl.pallas_call(backward_kernel, out_shape=[jax.ShapeDtypeStruct(*shape) f...  186 us
    pallas_call x3, Pallas kernels, forward_layer(): pl.pallas_call(forward_kernel, out_shape=[jax.ShapeDtypeStruct(*shape) fo...  157 us
    pallas_call x1, Pallas kernels, tail_call(): pl.pallas_call(functools.partial(tail_kernel, images, at), out_shape=[jax...  102 us
    pallas_call x1, Pallas kernels, head_call(): pl.pallas_call(functools.partial(head_kernel, images), out_shape=[jax.Sha...  70.8 us

profile of v4, /device:TPU:0, one launch (start us, length us, event | category | flops | bytes accessed | tf_op | source)
XLA Modules:
  0.0 622.6 jit_solution(8518699316133655245)
XLA Ops:
  1.4 0.7 convert_element_type.75
  2.0 0.7 convert_element_type.74
  2.8 0.7 fusion.54
  5.0 1.0 reduce-precision_bitcast_fusion.table_ref
  6.0 0.7 slice.318.bias_ref
  6.8 0.7 maximum_maximum_fusion.small_ref
  7.5 0.7 slice.314.time_ref
  8.2 0.8 fusion.59
  11.4 0.8 slice_bitcast_fusion.3
  12.8 0.9 convert_element_type.76.mod_ref.weight_ref
  13.9 0.7 slice.344.rest_0_
  14.5 0.8 slice.345.rest_1_
  15.3 0.7 slice.333.rest_0_
  16.0 0.8 slice.334.rest_1_
  16.7 0.7 slice.320.rest_0_
  17.4 0.8 slice.321.rest_1_
  18.2 70.8 %head.1 = (f32[4,8,24,128]{3,2,1,0:T(8,128)}, f32[24,384]{1,0:T(8,128)}, f32[24,24]{1,0:T(8,128)}, f32[768,24]{1,0:T(8,128)}, f32[24,24]{1,0:T(8,128)}, /*index=...) custom-call(f32[24,128]{1,0:T(8,128)} %maximum_maximum_fusion.small_, ...), custom_call_target="tpu_custom_call" | custom-call | tf_op jit(solution)/shard_map/head/pallas_call | solution.py:1273
  89.0 1.1 copy.58
  90.3 1.5 convert_reduce_fusion
  97.9 0.7 broadcast_add_fusion.1
  98.6 0.7 slice.330.w_attn_ref
  99.3 1.1 slice.331.w_down_ref
  100.4 1.6 fusion.2.res_ref
  102.0 59.2 %block_forward.3 = (f32[3,64,768]{2,1,0:T(8,128)}, bf16[3,256,768]{2,1,0:T(8,128)(2,1)}, bf16[3,256,576]{2,1,0:T(8,128)(2,1)}, bf16[3,256,192]{2,1,0:T(8,128)(2,...) custom-call(f32[3,64,768]{2,1,0:T(8,128)} %fusion.2.res_ref, ...), custom_call_target="tpu_custom_call" | custom-call | flops 30000001024 | bytes 15728640 | tf_op jit(solution)/shard_map/block_forward/pallas_call | solution.py:759
  161.2 1.7 slice.341.w_attn_ref
  162.9 2.4 slice.342.w_down_ref
  165.3 54.5 %block_forward.4 = (f32[3,64,768]{2,1,0:T(8,128)}, bf16[3,256,768]{2,1,0:T(8,128)(2,1)}, bf16[3,256,576]{2,1,0:T(8,128)(2,1)}, bf16[3,256,192]{2,1,0:T(8,128)(2,...) custom-call(f32[3,64,768]{2,1,0:T(8,128)} %get-tuple-element.104.res, ...), custom_call_target="tpu_custom_call" | custom-call | flops 30000001024 | bytes 15728640 | tf_op jit(solution)/shard_map/block_forward/pallas_call | solution.py:759
  219.8 1.7 slice.352.w_attn_ref
  221.5 2.4 slice.353.w_down_ref
  223.9 42.9 %block_forward.5 = (f32[3,64,768]{2,1,0:T(8,128)}, bf16[3,256,768]{2,1,0:T(8,128)(2,1)}, bf16[3,256,576]{2,1,0:T(8,128)(2,1)}, bf16[3,256,192]{2,1,0:T(8,128)(2,...) custom-call(f32[3,64,768]{2,1,0:T(8,128)} %get-tuple-element.108.res, ...), custom_call_target="tpu_custom_call" | custom-call | flops 30000001024 | bytes 15728640 | tf_op jit(solution)/shard_map/block_forward/pallas_call | solution.py:759
  266.8 1.2 reduce_sum.196
  268.0 1.3 multiply_reduce_fusion.5
  269.3 2.5 multiply_reduce_fusion.7
  272.5 1.2 convolution_bitcast_fusion
  273.6 0.8 multiply_reduce_fusion.4
  274.4 1.0 multiply_reduce_fusion.3
  275.4 1.0 broadcast_add_fusion.d_res_ref
  276.4 49.7 %block_backward.3 = (f32[3,64,768]{2,1,0:T(8,128)}, bf16[768,576]{1,0:T(8,128)(2,1)}, bf16[768,768]{1,0:T(8,128)(2,1)}, bf16[960,768]{1,0:T(8,128)(2,1)}, f32[3,...) custom-call(f32[3,64,768]{2,1,0:T(8,128)} %broadcast_add_fusion.d_res_ref, ...), custom_call_target="tpu_custom_call" | custom-call | flops 60000002048 | bytes 26214400 | tf_op jit(solution)/shard_map/block_backward/pallas_call | solution.py:1029
  326.2 61.6 %block_backward.4 = (f32[3,64,768]{2,1,0:T(8,128)}, bf16[768,576]{1,0:T(8,128)(2,1)}, bf16[768,768]{1,0:T(8,128)(2,1)}, bf16[960,768]{1,0:T(8,128)(2,1)}, f32[3,...) custom-call(f32[3,64,768]{2,1,0:T(8,128)} %get-tuple-element.122.d_r, ...), custom_call_target="tpu_custom_call" | custom-call | flops 60000002048 | bytes 26214400 | tf_op jit(solution)/shard_map/block_backward/pallas_call | solution.py:1029
  387.8 74.9 %block_backward.5 = (f32[3,64,768]{2,1,0:T(8,128)}, bf16[768,576]{1,0:T(8,128)(2,1)}, bf16[768,768]{1,0:T(8,128)(2,1)}, bf16[960,768]{1,0:T(8,128)(2,1)}, f32[3,...) custom-call(f32[3,64,768]{2,1,0:T(8,128)} %get-tuple-element.134.d_r, ...), custom_call_target="tpu_custom_call" | custom-call | flops 60000002048 | bytes 26214400 | tf_op jit(solution)/shard_map/block_backward/pallas_call | solution.py:1029
  462.9 1.6 convolution_bitcast_fusion.1
  464.5 0.7 fusion.63
  466.3 1.1 reduce_sum.201
  468.7 0.7 concatenate.76
  469.7 0.9 copy.64
  470.6 0.7 pad.14.mod_ref
  471.4 101.8 %tail.1 = (f32[24,128]{1,0:T(8,128)}, f32[2,24,24]{2,1,0:T(8,128)}, bf16[8,16,1152]{2,1,0:T(8,128)(2,1)}, f32[24,24]{1,0:T(8,128)}, f32[24,24]{1,0:T(8,128)}, /*...) custom-call(f32[32,24,128]{2,1,0:T(8,128)} %bitcast.147, f32[4,16,1152]{2,1,0:T(8,128)} %pad.14.mod_ref, ...), custom_call_target="tpu_custom_call" | custom-call | tf_op jit(solution)/shard_map/tail/pallas_call | solution.py:1422
  573.2 1.2 fusion.65
  574.4 0.9 fusion.26
  575.3 0.8 reduce_sum.207
  576.1 0.8 reduce_sum.208
  577.0 1.9 multiply_reduce_fusion.2
  581.1 0.7 multiply_reduce_fusion.6
  582.4 1.0 multiply_reduce_fusion
  585.4 1.9 multiply_reduce_fusion.1
  587.9 10.1 %exchange_all.1 = f32[32,8,128]{2,1,0:T(8,128)S(1)} custom-call(f32[8,128]{1,0:T(8,128)S(1)} %iota.39.source), custom_call_target="tpu_custom_call" | custom-call | tf_op jit(solution)/shard_map/exchange_all/pallas_call | solution.py:200
  599.4 2.6 fusion.20
  602.0 4.3 fusion.50
  606.3 3.0 fusion.48
  609.3 1.1 copy-done.10
  610.4 2.2 fusion.52
  612.6 2.8 copy.77
  615.4 2.8 copy.79
  618.2 2.8 copy.78
  (234 shorter events, 16.8 us)
Async XLA Ops:
  0.7 8.3 %copy-start.43 = (f32[3,1024]{1,0:T(4,128)S(1)}, f32[3,1024]{1,0:T(4,128)}, u32[]{:S(2)}) copy-start(f32[3,1024]{1,0:T(4,128)} %param.17) | copy-start | bytes 36868
  3.5 96.9 %copy-start.52 = (f32[3]{0:T(128)}, f32[3]{0:T(128)S(1)}, u32[]{:S(2)}) copy-start(f32[3]{0:T(128)S(1)} %get-tuple-element.232) | copy-start | bytes 40
  3.5 96.9 %copy-start.54 = (f32[3]{0:T(128)}, f32[3]{0:T(128)S(1)}, u32[]{:S(2)}) copy-start(f32[3]{0:T(128)S(1)} %subtract_sqrt_fusion) | copy-start | bytes 40
  4.9 5.2 copy-start.44
  6.0 5.2 copy-start.7
  6.0 5.2 copy-start.5
  10.1 90.3 %copy-start.33 = (f32[3,64,16]{1,2,0:T(8,128)}, f32[3,64,16]{1,2,0:T(8,128)S(1)}, u32[]{:S(2)}) copy-start(f32[3,64,16]{1,2,0:T(8,128)S(1)} %reshape.550) | copy-start | bytes 36868
  11.3 258.0 %copy-start.19 = (f32[3,64,16]{1,2,0:T(8,128)}, f32[3,64,16]{1,2,0:T(8,128)S(1)}, u32[]{:S(2)}) copy-start(f32[3,64,16]{1,2,0:T(8,128)S(1)} %reshape.552) | copy-start | bytes 36868
  11.3 1.5 copy-start.3
  11.3 2.4 copy-start.1
  89.0 1.3 copy-start.23
  89.0 7.7 %copy-start.42 = (f32[32,8,128]{2,1,0:T(8,128)S(1)}, f32[32,8,128]{2,1,0:T(8,128)}, u32[]{:S(2)}) copy-start(f32[32,8,128]{2,1,0:T(8,128)} %get-tuple-element.113) | copy-start | bytes 393220
  90.3 8.3 %copy-start.11 = (bf16[8,120,768]{2,1,0:T(8,128)(2,1)S(1)}, bf16[8,120,768]{2,1,0:T(8,128)(2,1)}, u32[]{:S(2)}) copy-start(bf16[8,120,768]{2,1,0:T(8,128)(2,1)} %get-tuple-element.103) | copy-start | bytes 4423684
  266.8 5.7 copy-start
  387.8 75.1 %copy-start.20 = (f32[3,64,16]{1,2,0:T(8,128)S(1)}, f32[3,64,16]{1,2,0:T(8,128)}, u32[]{:S(2)}) copy-start(f32[3,64,16]{1,2,0:T(8,128)} %copy-done.19) | copy-start | bytes 36868
  387.8 75.1 %copy-start.34 = (f32[3,64,16]{1,2,0:T(8,128)S(1)}, f32[3,64,16]{1,2,0:T(8,128)}, u32[]{:S(2)}) copy-start(f32[3,64,16]{1,2,0:T(8,128)} %copy-done.33) | copy-start | bytes 36868
  387.8 75.1 %copy-start.53 = (f32[3]{0:T(128)S(1)}, f32[3]{0:T(128)}, u32[]{:S(2)}) copy-start(f32[3]{0:T(128)} %copy-done.52) | copy-start | bytes 40
  387.8 75.1 %copy-start.55 = (f32[3]{0:T(128)S(1)}, f32[3]{0:T(128)}, u32[]{:S(2)}) copy-start(f32[3]{0:T(128)} %copy-done.54) | copy-start | bytes 40
  387.8 77.7 %copy-start.57 = (f32[1,576]{1,0:T(1,128)S(1)}, f32[1,576]{1,0:T(1,128)}, u32[]{:S(2)}) copy-start(f32[1,576]{1,0:T(1,128)} %get-tuple-element.153) | copy-start | bytes 6916
  387.8 78.1 %copy-start.56 = (f32[1,576]{1,0:T(1,128)S(1)}, f32[1,576]{1,0:T(1,128)}, u32[]{:S(2)}) copy-start(f32[1,576]{1,0:T(1,128)} %get-tuple-element.157) | copy-start | bytes 6916
  462.8 4.7 copy-start.50
  462.8 5.0 copy-start.49
  462.8 5.4 copy-start.48
  462.8 5.7 copy-start.26
  462.8 5.7 copy-start.25
  462.8 5.8 copy-start.24
  462.8 5.8 copy-start.35
  462.8 5.8 copy-start.39
  462.8 5.8 copy-start.40
  462.9 5.8 copy-start.45
  462.9 5.8 copy-start.46
  462.9 5.8 copy-start.47
  471.4 101.8 %copy-start.21 = (f32[768,24]{1,0:T(8,128)S(1)}, f32[768,24]{1,0:T(8,128)}, u32[]{:S(2)}) copy-start(f32[768,24]{1,0:T(8,128)} %get-tuple-element.168) | copy-start | bytes 221188
  471.4 103.1 %copy-start.41 = (f32[24,384]{1,0:T(8,128)S(1)}, f32[24,384]{1,0:T(8,128)}, u32[]{:S(2)}) copy-start(f32[24,384]{1,0:T(8,128)} %get-tuple-element.165) | copy-start | bytes 110596
  471.4 105.6 %copy-start.12 = (f32[120,768]{1,0:T(8,128)S(1)}, f32[120,768]{1,0:T(8,128)}, u32[]{:S(2)}) copy-start(f32[120,768]{1,0:T(8,128)} %get-tuple-element.179) | copy-start | bytes 1105924
  471.4 105.6 %copy-start.14 = (f32[120,768]{1,0:T(8,128)S(1)}, f32[120,768]{1,0:T(8,128)}, u32[]{:S(2)}) copy-start(f32[120,768]{1,0:T(8,128)} %get-tuple-element.178) | copy-start | bytes 1105924
  573.2 5.7 copy-start.29
  573.2 5.7 copy-start.32
  573.2 5.9 copy-start.38
  573.2 6.3 %copy-start.36 = (f32[24,128]{1,0:T(8,128)S(1)}, f32[24,128]{1,0:T(8,128)}, u32[]{:S(2)}) copy-start(f32[24,128]{1,0:T(8,128)} %get-tuple-element.166) | copy-start | bytes 36868
  574.4 5.3 copy-start.8
  578.9 1.7 copy-start.37
  578.9 1.7 copy-start.51
  579.0 2.7 copy-start.22
  580.6 1.5 copy-start.28
  580.6 1.5 copy-start.31
  581.0 1.2 copy-start.27
  581.0 1.2 copy-start.30
  599.3 2.6 copy-start.6
  599.4 2.6 copy-start.13
  599.4 2.6 copy-start.15
  599.4 2.6 copy-start.16
  602.0 4.3 copy-start.4
  602.0 4.3 copy-start.17
  602.0 4.3 copy-start.18
  606.3 3.0 copy-start.2
  606.3 3.0 copy-start.9
  606.3 4.1 copy-start.10

commit v5 on v4

--- a/solution.py
+++ b/solution.py
@@ -443,25 +443,38 @@
             self.copy(part, PAIR, line.at, line.place, True).start()
             self.local_copy(part).start()
 
+    def came(self, way, step):
+        there = -step if way == UP else step
+        spot = self.line.at + there
+        return self.line.place + 2 * there, spot, (spot >= 0) & (spot < self.line.size)
+
+    def hand_on(self, step, way):
+        line = self.line
+        owner, _, real = self.came(way, step)
+        can = line.has_up if way == UP else line.has_down
+
+        @pl.when(real)
+        def _():
+            for part in range(len(self.shards)):
+                self.copy(part, way, step - 1, owner).wait_recv()
+
+            @pl.when(can)
+            def _():
+                for part in range(len(self.shards)):
+                    self.copy(part, way, step, owner).start()
+
+    def hand_over(self, step, way, when=True):
+        owner, spot, real = self.came(way, step)
+
+        @pl.when(real & when)
+        def _():
+            for part in range(len(self.shards)):
+                self.copy(part, PAIR, spot, owner).start()
+
     def tick(self, step):
-        line = self.line
-        parts = range(len(self.shards))
-        for way, there, can in ((UP, -step, line.has_up), (DOWN, step, line.has_down)):
-            owner = line.place + 2 * there
-            spot = line.at + there
-
-            @pl.when((spot >= 0) & (spot < line.size))
-            def _(way=way, can=can, owner=owner, spot=spot):
-                for part in parts:
-                    self.copy(part, way, step - 1, owner).wait_recv()
-
-                @pl.when(can)
-                def _():
-                    for part in parts:
-                        self.copy(part, way, step, owner).start()
-
-                for part in parts:
-                    self.copy(part, PAIR, spot, owner).start()
+        for way in (UP, DOWN):
+            self.hand_on(step, way)
+            self.hand_over(step, way)
 
     def finish(self):
         line = self.line
@@ -515,18 +528,21 @@
         )
 
     def start(self):
-        last = self.line.size - 1
-
-        def outer(step):
+        each(self.line.size, self.send_pair)
+
+    def send_pair(self, step):
+        line = self.line
+        far = line.size - 1 - step
+
+        @pl.when(line.at + far < line.size)
+        def _():
             for part in range(len(self.terms)):
-                self.pair_copy(part, last - step).start()
-
-            @pl.when(last - step > step)
-            def _():
-                for part in range(len(self.terms)):
-                    self.pair_copy(part, step).start()
-
-        each((self.line.size + 1) // 2, outer)
+                self.pair_copy(part, line.at + far).start()
+
+        @pl.when((line.at - far >= 0) & (far > 0))
+        def _():
+            for part in range(len(self.terms)):
+                self.pair_copy(part, line.at - far).start()
 
     def pair_sum(self, part, spot):
         own = self.terms[part][2 * spot + self.line.side].astype(jnp.float32)
@@ -548,15 +564,15 @@
 
     def tick(self, step):
         line = self.line
-        last = line.size - 1
-
-        @pl.when(last - step > line.at)
+        far = line.size - 1 - step
+
+        @pl.when(line.at + far < line.size)
         def _():
-            self.pass_on(UP, last - step, line.has_down)
-
-        @pl.when(line.at > step)
+            self.pass_on(UP, line.at + far, line.has_down)
+
+        @pl.when(line.at - far >= 0)
         def _():
-            self.pass_on(DOWN, step, line.has_up)
+            self.pass_on(DOWN, line.at - far, line.has_up)
 
     def finish(self):
         line = self.line
@@ -602,6 +618,7 @@
 
 
 def forward_kernel(
+    layer_idx,
     res_ref,
     mod_ref,
     vec_ref,
@@ -609,12 +626,13 @@
     up_bias_ref,
     w_qkv_ref,
     w_up_ref,
-    w_attn_ref,
-    w_down_ref,
+    w_out_ref,
     *rest,
 ):
     with_gather = len(rest) > 19
     shards, rest = (rest[:3], rest[3:]) if with_gather else ((), rest)
+    group_width = w_qkv_ref.shape[1] // 3
+    w_attn_ref, w_down_ref = w_out_ref.at[0:group_width, :], w_out_ref.at[group_width:, :]
     (
         res_out,
         rows_a,
@@ -640,12 +658,12 @@
     recvs,
     ) = rest[:10]
     images = res_ref.shape[0]
-    group_width = w_attn_ref.shape[0]
     gather, last_step = None, 0
     if with_gather:
         line = Line()
         greet(line)
-        gather = Gather(line, shards, wholes, *rest[10:])
+        own = [shard.at[layer_idx + 1] for shard in shards]
+        gather = Gather(line, own, wholes, *rest[10:])
         last_step = line.size
     else:
         greet(None)
@@ -707,9 +725,9 @@
         collect_a.close(image)
         collect_m.close(image)
 
-    each(images, start_norm)
     if with_gather:
         gather.start()
+    each(images, start_norm)
     each(images, spread_a.forward)
     each(images, attend)
     run_ticks(gather, 1, min(2, last_step))
@@ -728,7 +746,7 @@
 
 
 def forward_layer(
-    residual, mod_vec, vec_bias, qkv_bias, up_bias, w_qkv, w_up, w_attn, w_down, shards
+    residual, mod_vec, vec_bias, qkv_bias, up_bias, w_qkv, w_up, w_out, shards, layer_idx
 ):
     images, count, _ = residual.shape
     tokens = 4 * count
@@ -737,7 +755,7 @@
         ((images, count, D), full),
         ((images, tokens, D), low),
         ((images, tokens, w_qkv.shape[1]), low),
-        ((images, tokens, w_attn.shape[0]), low),
+        ((images, tokens, w_qkv.shape[1] // 3), low),
         ((images, count, D), full),
         ((images, count, D), full),
         ((images, tokens, D), low),
@@ -750,26 +768,27 @@
     ]
     if shards:
         dp_size = lax.axis_size("dp")
-        shapes += [((dp_size,) + shard.shape, low) for shard in shards]
+        shapes += [((dp_size,) + shard.shape[1:], low) for shard in shards]
         scratch += [
             pltpu.SemaphoreType.DMA((3, dp_size // 2, 3)),
             pltpu.SemaphoreType.DMA((3, dp_size // 2, 3)),
             pltpu.SemaphoreType.DMA((3,)),
         ]
     return pl.pallas_call(
-        forward_kernel,
+        functools.partial(forward_kernel, layer_idx),
         out_shape=[jax.ShapeDtypeStruct(*shape) for shape in shapes],
-        in_specs=[pl.BlockSpec(memory_space=pltpu.VMEM)] * (9 + len(shards)),
+        in_specs=[pl.BlockSpec(memory_space=pltpu.VMEM)] * 8
+        + [pl.BlockSpec(memory_space=pl.ANY)] * len(shards),
         out_specs=[pl.BlockSpec(memory_space=pltpu.VMEM)] * len(shapes),
         scratch_shapes=collect_scratch(images, tokens) + collect_scratch(images, tokens) + scratch,
         compiler_params=pltpu.CompilerParams(
-            collective_id=20 if shards else 22, has_side_effects=True, vmem_limit_bytes=ACT_VMEM
+            collective_id=16 + layer_idx, has_side_effects=True, vmem_limit_bytes=ACT_VMEM
         ),
         cost_estimate=pl.CostEstimate(
             flops=30 * 10**9, bytes_accessed=15 * 2**20, transcendentals=0
         ),
         name="block_forward",
-    )(residual, mod_vec, vec_bias, qkv_bias, up_bias, w_qkv, w_up, w_attn, w_down, *shards)
+    )(residual, mod_vec, vec_bias, qkv_bias, up_bias, w_qkv, w_up, w_out, *shards)
 
 
 def gelu_slope(values):
@@ -805,11 +824,12 @@
     down_ref,
     w_qkv_ref,
     w_up_ref,
-    w_attn_ref,
-    w_down_ref,
+    w_out_ref,
     *rest,
 ):
     with_reduce = len(rest) > 24
+    group_width = w_qkv_ref.shape[1] // 3
+    w_attn_ref, w_down_ref = w_out_ref.at[0:group_width, :], w_out_ref.at[group_width:, :]
     terms, rest = (rest[:3], rest[3:]) if with_reduce else ((), rest)
     (
         d_res_out,
@@ -842,7 +862,6 @@
     ) = rest[:16]
     images = res_ref.shape[0]
     tokens = rows_a.shape[1]
-    group_width = w_attn_ref.shape[0]
     qkv_width = 3 * group_width
     units = w_up_ref.shape[1]
     reduce, last_step = None, 0
@@ -977,21 +996,20 @@
         reduce.start()
     each(images, spread_m.forward)
     each(images, feed)
+    run_ticks(reduce, 0, min(1, last_step - 1))
     each(images, collect_m.forward)
     feed_weights()
-    run_ticks(reduce, 0, min(1, last_step))
+    run_ticks(reduce, 1, min(2, last_step - 1))
     each(images, middle)
     each(images, spread_a.forward)
-    run_ticks(reduce, 1, min(2, last_step))
     each(images, attend)
-    run_ticks(reduce, 2, min(3, last_step))
     each(images, collect_a.forward)
+    run_ticks(reduce, 2, min(3, last_step - 1))
     attend_weights()
-    run_ticks(reduce, 3, min(4, last_step))
     each(images, finish)
     each(images, close)
     if with_reduce:
-        each(max(last_step - 4, 0), lambda step: reduce.tick(step + 4))
+        each(max(last_step - 4, 0), lambda step: reduce.tick(step + 3))
         reduce.finish()
 
 
@@ -999,8 +1017,8 @@
     images, count, _ = d_residual.shape
     tokens = 4 * count
     low, full = jnp.bfloat16, jnp.float32
-    w_qkv, w_up, w_attn, w_down = weights
-    group_width, units = w_attn.shape[0], w_up.shape[1]
+    w_qkv, w_up, w_out = weights
+    group_width, units = w_qkv.shape[1] // 3, w_up.shape[1]
     shapes = [
         ((images, count, D), full),
         ((D, 3 * group_width), low),
@@ -1029,7 +1047,7 @@
     return pl.pallas_call(
         backward_kernel,
         out_shape=[jax.ShapeDtypeStruct(*shape) for shape in shapes],
-        in_specs=[pl.BlockSpec(memory_space=pltpu.VMEM)] * (15 + len(terms)),
+        in_specs=[pl.BlockSpec(memory_space=pltpu.VMEM)] * (14 + len(terms)),
         out_specs=[pl.BlockSpec(memory_space=pltpu.VMEM)] * len(shapes),
         scratch_shapes=[
             pltpu.VMEM((images, count, D), full),
@@ -1145,7 +1163,7 @@
     images_all = images * dp_size
     slots = mod_own.shape[0]
     greet_group("all")
-    gather = Gather(Line(), shards, wholes, *gather_sems)
+    gather = Gather(Line(), [shard.at[0] for shard in shards], wholes, *gather_sems)
     feats = Crowd("dp", lambda place: feats_ref, feats_all, *crowds[0])
     small = Crowd("dp", lambda place: small_ref, small_dp, *crowds[1])
     small_spread = Crowd("tensor", lambda place: small_dp, small_all, *crowds[7])
@@ -1153,8 +1171,9 @@
     signal = Crowd("all", lambda place: signal_own, signal_all, *crowds[3])
     final = Crowd("all", lambda place: final_own.at[place // tensor_size], final_all, *crowds[4])
     mod_sum = Crowd("dp", lambda place: mod_part.at[place], mod_in, *crowds[5])
+    line = gather.line
+    first, last = line.at == 0, line.at == line.size - 1
     feats.start()
-    small.start()
     gather.start()
     feats.wait()
     pick = chosen(
@@ -1173,7 +1192,11 @@
     lane = lax.broadcasted_iota(jnp.int32, (images_all, class_lanes), 1)
     onehot = jnp.where(lane == labels, 1.0, 0.0)
     class_part = dense_nt(table_ref[:, 0:class_lanes], onehot) + bias_ref[:, 2:3]
-    gather.tick(1)
+    small.start()
+    for way in (UP, DOWN):
+        gather.hand_on(1, way)
+    gather.hand_over(1, UP)
+    gather.hand_over(1, DOWN, first)
     hidden.wait()
     cols = second_ref.shape[0]
     hidden_full = unfold(hidden_all[...], cols, images_all).reshape(D, images_all)
@@ -1182,7 +1205,13 @@
     pre_signal_out[...] = pre_signal
     signal_own[...] = fold(jax.nn.silu(pre_signal))
     signal.start()
-    gather.tick(2)
+    for way in (UP, DOWN):
+        gather.hand_on(2, way)
+    gather.hand_over(1, DOWN, jnp.logical_not(first))
+    gather.hand_over(2, UP, last)
+    gather.hand_over(2, DOWN, first)
+    small.wait()
+    small_spread.start()
     signal.wait()
     signal_full = unfold(signal_all[...], cols, images_all).reshape(D, images_all)
     signal_out[...] = signal_full
@@ -1204,8 +1233,8 @@
         total = term if total is None else total + term
     mod_part[...] = total.reshape(mod_part.shape)
     mod_sum.start()
-    small.wait()
-    small_spread.start()
+    gather.hand_over(2, UP, jnp.logical_not(last))
+    gather.hand_over(2, DOWN, jnp.logical_not(first))
     finals = jnp.concatenate(
         [
             dense(shift_ref[...], signal_full) + bias_ref[:, 3:4],
@@ -1250,7 +1279,7 @@
         ((D, images_all), full),
         ((size, 8, 128), full),
         ((tensor_size, slots, mod_low.shape[2]), full),
-    ] + [((dp_size,) + shard.shape, low) for shard in shards]
+    ] + [((dp_size,) + shard.shape[1:], low) for shard in shards]
     scratch = [
         pltpu.VMEM((dp_size,) + feats.shape, full),
         pltpu.VMEM((8, folded), full),
@@ -1273,7 +1302,8 @@
     return pl.pallas_call(
         functools.partial(head_kernel, images),
         out_shape=[jax.ShapeDtypeStruct(*shape) for shape in shapes],
-        in_specs=[pl.BlockSpec(memory_space=pltpu.VMEM)] * (9 + len(shards)),
+        in_specs=[pl.BlockSpec(memory_space=pltpu.VMEM)] * 9
+        + [pl.BlockSpec(memory_space=pl.ANY)] * len(shards),
         out_specs=[pl.BlockSpec(memory_space=pltpu.VMEM)] * len(shapes),
         scratch_shapes=scratch,
         compiler_params=pltpu.CompilerParams(
@@ -1281,6 +1311,10 @@
         ),
         name="head",
     )(small, feats, table, times, second, shift, scale, bias, mod_low, *shards)
+
+
+def square_sum(values):
+    return jnp.sum(jnp.sum(values * values, axis=0, keepdims=True), axis=1, keepdims=True)
 
 
 def tail_kernel(
@@ -1294,44 +1328,77 @@
     scale_ref,
     pre_signal_ref,
     pre_time_ref,
+    feats_ref,
+    hidden_ref,
+    signal_ref,
+    loss_ref,
     *rest,
 ):
-    terms = rest[0:3]
-    row_sums, d_final, d_mod_all, d_signal_own, d_hidden_own = rest[3:8]
-    totals = rest[8:11]
-    row_in, mod_in, mod_low, signal_part, signal_out, signal_in, hidden_out, hidden_in = rest[11:19]
-    pair_in, way_in, way_out = rest[19:22], rest[22:25], rest[25:28]
-    crowds = [rest[28 + 3 * index : 31 + 3 * index] for index in range(5)]
-    reduce_sems = rest[43:]
+    terms, others = rest[0:3], rest[3 : 3 * LAYERS]
+    rest = rest[3 * LAYERS :]
+    (
+        row_sums,
+        vector_sums,
+        class_grad,
+        time_grad,
+        second_grad,
+        shift_grad,
+        scale_grad,
+        mod_grad,
+        scalar_sums,
+    ) = rest[0:9]
+    totals = rest[9:12]
+    (
+        row_in,
+        row_mid,
+        row_fin,
+        mod_in,
+        mod_low,
+        d_mod_all,
+        signal_part,
+        signal_out,
+        signal_in,
+        hidden_out,
+        hidden_in,
+        scalar_own,
+        scalar_in,
+    ) = rest[12:25]
+    pair_in, way_in, way_out = rest[25:28], rest[28:31], rest[31:34]
+    crowds = [rest[34 + 3 * index : 37 + 3 * index] for index in range(7)]
+    reduce_sems = rest[55:]
     dp_size = lax.axis_size("dp")
     tensor_size = lax.axis_size("tensor")
+    places = dp_size * tensor_size
     dp_rank = lax.axis_index("dp")
     images_all = images * dp_size
-    cols, lanes = row_ref.shape[1:]
+    cols, lanes = row_ref.shape[2:]
     mod_rows = weight_ref.shape[1]
     slots = mod_low.shape[0]
     last_step = dp_size // 2
     greet_group("all")
     reduce = Reduce(Line(), terms, totals, pair_in, way_in, way_out, *reduce_sems)
-
     mod_sum = Crowd("tensor", lambda place: mod_ref.at[place], mod_in, *crowds[0])
-    rows = Crowd("all", lambda place: row_ref.at[place], row_in, *crowds[1])
+    rows = Crowd("tensor", lambda place: row_ref.at[:, place], row_in, *crowds[1])
     mod_spread = Crowd("dp", lambda place: mod_low, d_mod_all, *crowds[2])
     signal = Crowd("all", lambda place: signal_out.at[place], signal_in, *crowds[3])
     hidden = Crowd("all", lambda place: hidden_out.at[place], hidden_in, *crowds[4])
+    row_cross = Crowd("dp", lambda place: row_mid.at[place], row_fin, *crowds[5])
+    scalars = Crowd("all", lambda place: scalar_own, scalar_in, *crowds[6])
     mod_sum.start()
     rows.start()
-    reduce.start()
+    reduce.send_pair(0)
     mod_sum.wait()
     mod_low[...] = jnp.sum(mod_in[...], axis=0).astype(jnp.bfloat16)
     mod_spread.start()
     rows.wait()
-    row_sums[...] = jnp.sum(row_in[...], axis=0)
-    group_sums = [
-        jnp.sum(row_in[at * tensor_size : (at + 1) * tensor_size], axis=0)
-        for at in range(dp_size)
-    ]
-    joined = jnp.concatenate(group_sums, axis=1)
+    row_mid[...] = jnp.sum(row_in[...], axis=0)
+    row_cross.start()
+    reduce.send_pair(1)
+    other_squares = sum(square_sum(other[...]) for other in others)
+    row_cross.wait()
+    row_total = jnp.sum(row_fin[...], axis=0)
+    row_sums[...] = row_total
+    joined = jnp.concatenate([row_fin[at] for at in range(dp_size)], axis=1)
 
     def final_of(piece):
         return dense(
@@ -1347,73 +1414,126 @@
         )
 
     d_shift, d_scale = final_of(0), final_of(1)
-    d_final[0] = d_shift
-    d_final[1] = d_scale
     signal_part[...] = dense_tn(shift_ref[...], d_shift) + dense_tn(scale_ref[...], d_scale)
-    run_ticks(reduce, 0, min(1, last_step))
     mod_spread.wait()
     d_mod = d_mod_all[...].reshape(dp_size * slots, mod_low.shape[1])
     own_rows = pl.ds(pl.multiple_of(dp_rank * mod_rows, 8), mod_rows)
-    for layer_idx in range(LAYERS):
-        pick = chosen(
+
+    def layer_pick(layer_idx, kind):
+        return chosen(
             (dp_size * slots, images_all),
             lambda row, col: (
                 (row // slots == col // images)
                 & (lax.rem(row, slots) == layer_idx * images + lax.rem(col, images))
             ),
-            jnp.float32,
-        )
-        signal_part[own_rows, :] += dense(dot_nt(weight_ref[layer_idx], d_mod), pick)
-    places = dp_size * tensor_size
+            kind,
+        )
+
+    for layer_idx in range(LAYERS):
+        signal_part[own_rows, :] += dense(
+            dot_nt(weight_ref[layer_idx], d_mod), layer_pick(layer_idx, jnp.float32)
+        )
     signal_out[...] = fold(signal_part[...].reshape(places, cols, images_all))
     signal.start()
-    run_ticks(reduce, 1, min(2, last_step))
+    reduce.send_pair(2)
+    run_ticks(reduce, 0, min(1, last_step - 1))
+    signal_low = signal_ref[own_rows, :].astype(jnp.bfloat16)
+    for layer_idx in range(LAYERS):
+        placed = dot_nt(signal_low, layer_pick(layer_idx, jnp.bfloat16)).astype(jnp.bfloat16)
+        grad = dot_nn(placed, d_mod)
+        mod_grad[layer_idx] = grad
+        other_squares = other_squares + square_sum(grad)
+    grad = dense_nt(d_shift, signal_ref[...])
+    shift_grad[...] = grad
+    other_squares = other_squares + square_sum(grad)
+    grad = dense_nt(d_scale, signal_ref[...])
+    scale_grad[...] = grad
+    other_squares = other_squares + square_sum(grad)
+    lane = lax.broadcasted_iota(jnp.int32, row_total.shape, 1)
+    other_squares = other_squares + square_sum(jnp.where(lane < final_at, row_total, 0.0))
     signal.wait()
     d_signal = unfold(jnp.sum(signal_in[...], axis=0), cols, images_all)
     d_signal = d_signal * silu_slope(pre_signal_ref[...])
-    d_signal_own[...] = d_signal
     d_hidden = dense_tn(second_ref[...], d_signal)
     hidden_out[...] = fold(d_hidden.reshape(places, cols, images_all))
     hidden.start()
-    run_ticks(reduce, 2, min(3, last_step))
+    each(max(last_step - 3, 0), lambda step: reduce.send_pair(step + 3))
+    run_ticks(reduce, 1, min(2, last_step - 1))
+    labels = jnp.round(feats_ref[:, FREQ : FREQ + 1]).astype(jnp.int32)
+    class_lane = lax.broadcasted_iota(jnp.int32, (images_all, class_grad.shape[1]), 1)
+    grad = dense(d_signal, jnp.where(class_lane == labels, 1.0, 0.0))
+    class_grad[...] = grad
+    other_squares = other_squares + square_sum(grad)
+    grad = dense_nt(d_signal, hidden_ref[...])
+    second_grad[...] = grad
+    other_squares = other_squares + square_sum(grad)
     hidden.wait()
     d_hidden = unfold(jnp.sum(hidden_in[...], axis=0), cols, images_all)
-    d_hidden_own[...] = d_hidden * silu_slope(pre_time_ref[...])
-    run_ticks(reduce, 3, min(4, last_step))
-    each(max(last_step - 4, 0), lambda step: reduce.tick(step + 4))
+    d_hidden = d_hidden * silu_slope(pre_time_ref[...])
+    grad = dense(d_hidden, feats_ref[:, 0:FREQ])
+    time_grad[...] = grad
+    other_squares = other_squares + square_sum(grad)
+    vectors = [
+        jnp.sum(values, axis=1, keepdims=True) for values in (d_hidden, d_signal, d_shift, d_scale)
+    ]
+    lane = lax.broadcasted_iota(jnp.int32, vector_sums.shape, 1)
+    grad = sum(jnp.where(lane == at, vector, 0.0) for at, vector in enumerate(vectors))
+    vector_sums[...] = grad
+    other_squares = other_squares + square_sum(grad)
+    run_ticks(reduce, 2, min(3, last_step - 1))
+    each(max(last_step - 4, 0), lambda step: reduce.tick(step + 3))
     reduce.finish()
-
-
-def tail_call(rows, mods, mod_low, second, shift, scale, pre_signal, pre_time, terms, images, at):
+    for total in totals:
+        other_squares = other_squares + square_sum(total[...])
+    lane = lax.broadcasted_iota(jnp.int32, scalar_own.shape, 1)
+    scalar_own[...] = jnp.where(lane == 0, loss_ref[...], other_squares)
+    scalars.start()
+    scalars.wait()
+    scalar_sums[...] = jnp.sum(scalar_in[...], axis=0)
+
+
+def tail_call(
+    rows, mods, mod_low, second, shift, scale, pre_signal, pre_time, feats, hidden, signal, loss,
+    terms, others, images, at,
+):
     dp_size, tensor_size = lax.axis_size("dp"), lax.axis_size("tensor")
     size = dp_size * tensor_size
     images_all = images * dp_size
-    cols, lanes = rows.shape[1:]
+    cols, lanes = rows.shape[2:]
     folded = folded_lanes(cols, images_all)
     full, low = jnp.float32, jnp.bfloat16
     spots = dp_size // 2
     blocks = [term.shape[1:] for term in terms]
     shapes = [
         ((cols, lanes), full),
-        ((2, cols, images_all), full),
-        ((dp_size,) + mods.shape[1:], low),
-        ((cols, images_all), full),
-        ((cols, images_all), full),
+        ((cols, 128), full),
+        ((cols, -(-CLASSES // 128) * 128), full),
+        ((cols, FREQ), full),
+        ((cols, D), full),
+        ((cols, D), full),
+        ((cols, D), full),
+        (mod_low.shape, full),
+        ((8, 128), full),
     ] + [(block, full) for block in blocks]
     scratch = [
-        pltpu.VMEM(rows.shape, full),
+        pltpu.VMEM((tensor_size, dp_size, cols, lanes), full),
+        pltpu.VMEM((dp_size, cols, lanes), full),
+        pltpu.VMEM((dp_size, cols, lanes), full),
         pltpu.VMEM(mods.shape, full),
         pltpu.VMEM(mods.shape[1:], low),
+        pltpu.VMEM((dp_size,) + mods.shape[1:], low),
         pltpu.VMEM((D, images_all), full),
         pltpu.VMEM((size, 8, folded), full),
         pltpu.VMEM((size, 8, folded), full),
         pltpu.VMEM((size, 8, folded), full),
         pltpu.VMEM((size, 8, folded), full),
+        pltpu.VMEM((8, 128), full),
+        pltpu.VMEM((size, 8, 128), full),
     ]
     scratch += [pltpu.VMEM((spots,) + block, low) for block in blocks]
     scratch += [pltpu.VMEM((2, spots) + block, low) for block in blocks]
     scratch += [pltpu.VMEM((2, spots) + block, low) for block in blocks]
-    for count in (tensor_size, size, dp_size, size, size):
+    for count in (tensor_size, tensor_size, dp_size, size, size, dp_size, size):
         scratch += crowd_scratch(count)
     scratch += [
         pltpu.SemaphoreType.DMA((3, spots, 3)),
@@ -1422,14 +1542,17 @@
     return pl.pallas_call(
         functools.partial(tail_kernel, images, at),
         out_shape=[jax.ShapeDtypeStruct(*shape) for shape in shapes],
-        in_specs=[pl.BlockSpec(memory_space=pltpu.VMEM)] * (8 + len(terms)),
+        in_specs=[pl.BlockSpec(memory_space=pltpu.VMEM)] * (12 + len(terms) + len(others)),
         out_specs=[pl.BlockSpec(memory_space=pltpu.VMEM)] * len(shapes),
         scratch_shapes=scratch,
         compiler_params=pltpu.CompilerParams(
             collective_id=31, has_side_effects=True, vmem_limit_bytes=ACT_VMEM
         ),
         name="tail",
-    )(rows, mods, mod_low, second, shift, scale, pre_signal, pre_time, *terms)
+    )(
+        rows, mods, mod_low, second, shift, scale, pre_signal, pre_time, feats, hidden, signal,
+        loss, *terms, *others,
+    )
 
 
 def adam_update(weight, first, second, grad, factor, first_fix, second_fix):
@@ -1492,13 +1615,12 @@
     vector_count = 5 + LAYERS * layer_rows
     small_count = 2 * patch_in + vector_count
     lanes = -(-(small_count + 2 * images) // 128) * 128
-    shards_all = []
-    for layer_idx in range(LAYERS):
-        shard_in = layer_in[layer_idx, :, 0].astype(jnp.bfloat16)
-        shard_out = layer_out[layer_idx, 0].astype(jnp.bfloat16)
-        shards_all.append(
-            (shard_in[:, : 3 * group_width], shard_in[:, 3 * group_width :], shard_out)
-        )
+    shards_in = layer_in[:, :, 0].astype(jnp.bfloat16)
+    shards = (
+        shards_in[:, :, : 3 * group_width],
+        shards_in[:, :, 3 * group_width :],
+        layer_out[:, 0].astype(jnp.bfloat16),
+    )
     second_cols = col_block(second_start, D)
     shift_cols = col_block(final_start, D)
     scale_cols = col_block(final_start + D, D)
@@ -1530,7 +1652,7 @@
             scale_cols,
             col_block(vector_start, 5),
             mod_low,
-            shards_all[0],
+            shards,
             images,
         )
         small_all, feats_all, pre_time, hidden, pre_signal, signal, final_all, mod_full = outs[:8]
@@ -1593,7 +1715,7 @@
         mod_full = exchange(mod_local, "tensor", False, 6)
         mod_full = mod_full.reshape(tensor_size, images, LAYERS, mod_cols)
         mod_full = mod_full.transpose(2, 1, 0, 3).reshape(LAYERS, images, tensor_size * mod_cols)
-        wholes = [lax.all_gather(shard, "dp") for shard in shards_all[0]]
+        wholes = [lax.all_gather(shard[0], "dp") for shard in shards]
     small_rows = small_all.reshape(D, lanes).T
     patch_w = small_rows[0:patch_in]
     head_w = small_rows[patch_in : 2 * patch_in]
@@ -1613,37 +1735,35 @@
         + position_table(tensor_rank * local_rows, local_rows)[None]
     )
     saved_acts = []
+    bias_all = bias_all.reshape(LAYERS, layer_rows, D)
+    mod_vecs = mod_full.reshape(LAYERS, images, 6, D) + bias_all[:, None, 0:6]
+    part_bias = lax.dynamic_slice_in_dim(
+        bias_all[:, 8:10], tensor_rank * group_width, group_width, 2
+    )
+    qkv_bias = jnp.concatenate(
+        [part_bias[:, 0], jnp.zeros((LAYERS, group_width), jnp.float32), part_bias[:, 1]], axis=1
+    )
+    up_bias = lax.dynamic_slice_in_dim(
+        bias_all[:, 10:].reshape(LAYERS, FF), tensor_rank * unit_count, unit_count, 1
+    )
     for layer_idx in range(LAYERS):
-        bias_rows = bias_all[layer_idx * layer_rows : (layer_idx + 1) * layer_rows]
-        up_all = bias_rows[10:].reshape(FF)
-        ada_bias = bias_rows[0:6].reshape(6 * D)
-        out_bias = bias_rows[6]
-        down_bias = bias_rows[7]
-        query_bias = lax.dynamic_slice_in_dim(bias_rows[8], tensor_rank * group_width, group_width)
-        value_bias = lax.dynamic_slice_in_dim(bias_rows[9], tensor_rank * group_width, group_width)
-        up_bias = lax.dynamic_slice_in_dim(up_all, tensor_rank * unit_count, unit_count)
-        mod_vec = (mod_full[layer_idx] + ada_bias).reshape(images, 6, D)
-        weight_out = wholes[2].reshape(group_width + unit_count, D)
         weights = (
             wholes[0].reshape(D, 3 * group_width),
             wholes[1].reshape(D, unit_count),
-            weight_out[:group_width],
-            weight_out[group_width:],
-        )
-        qkv_bias = jnp.concatenate(
-            [query_bias, jnp.zeros((group_width,), jnp.float32), value_bias]
-        )[None]
+            wholes[2].reshape(group_width + unit_count, D),
+        )
         outs = forward_layer(
             residual,
-            mod_vec,
-            jnp.stack([out_bias, down_bias]),
-            qkv_bias,
-            up_bias[None],
+            mod_vecs[layer_idx],
+            bias_all[layer_idx, 6:8],
+            qkv_bias[layer_idx : layer_idx + 1],
+            up_bias[layer_idx : layer_idx + 1],
             *weights,
-            shards_all[layer_idx + 1] if layer_idx + 1 < LAYERS else (),
+            shards if layer_idx + 1 < LAYERS else (),
+            layer_idx,
         )
         wholes = outs[9:]
-        saved_acts.append((mod_vec, (residual,) + tuple(outs[1:9]), weights))
+        saved_acts.append((mod_vecs[layer_idx], (residual,) + tuple(outs[1:9]), weights))
         residual = outs[0]
     final_in, final_norm_pull = jax.vjp(modulate, residual, final_shift, final_scale)
     predicted = jnp.einsum("btd,pd->btp", final_in, head_w, precision=PRECISE)
@@ -1655,8 +1775,7 @@
     d_residual, d_final_shift, d_final_scale = final_norm_pull(d_final)
     totals = []
     terms = ()
-    mod_parts = []
-    bias_blocks = []
+    bias_parts = []
     for layer_idx in reversed(range(LAYERS)):
         mod_vec, saved, weights = saved_acts[layer_idx]
         outs = backward_layer(d_residual, mod_vec, saved, weights, terms)
@@ -1666,47 +1785,34 @@
         terms = [
             term.reshape((dp_size, -1) + term.shape[1:]) for term in (d_w_qkv, d_w_up, d_w_out)
         ]
-        d_modulation = d_mod_vec.reshape(images, 6 * D)
-        d_out_bias, d_down_bias = d_vec[0], d_vec[1]
-        d_query_bias = d_qkv_bias[0, :group_width]
-        d_value_bias = d_qkv_bias[0, 2 * group_width :]
-        d_up_bias = d_up_bias[0]
-        mod_parts.insert(0, d_modulation)
-        query_row = lax.dynamic_update_slice_in_dim(
-            jnp.zeros((D,), jnp.float32), d_query_bias, tensor_rank * group_width, 0
-        )
-        value_row = lax.dynamic_update_slice_in_dim(
-            jnp.zeros((D,), jnp.float32), d_value_bias, tensor_rank * group_width, 0
-        )
-        up_rows = lax.dynamic_update_slice_in_dim(
-            jnp.zeros((FF,), jnp.float32), d_up_bias, tensor_rank * unit_count, 0
-        ).reshape(FF // D, D)
-        bias_blocks.insert(
-            0,
-            jnp.concatenate(
-                [
-                    jnp.sum(d_modulation, axis=0).reshape(6, D),
-                    d_out_bias[None],
-                    d_down_bias[None],
-                    query_row[None],
-                    value_row[None],
-                    up_rows,
-                ],
-                axis=0,
+        bias_parts.insert(0, (d_mod_vec, d_vec, d_qkv_bias, d_up_bias))
+    d_mods, d_vecs, d_qkv_rows, d_up_rows = [jnp.stack(parts) for parts in zip(*bias_parts)]
+    part_rows = jnp.stack([d_qkv_rows[:, 0, :group_width], d_qkv_rows[:, 0, 2 * group_width :]], 1)
+    bias_blocks = jnp.concatenate(
+        [
+            jnp.sum(d_mods, axis=1),
+            d_vecs,
+            lax.dynamic_update_slice_in_dim(
+                jnp.zeros((LAYERS, 2, D), jnp.float32), part_rows, tensor_rank * group_width, 2
             ),
-        )
+            lax.dynamic_update_slice_in_dim(
+                jnp.zeros((LAYERS, FF), jnp.float32), d_up_rows[:, 0], tensor_rank * unit_count, 1
+            ).reshape(LAYERS, FF // D, D),
+        ],
+        axis=1,
+    ).reshape(LAYERS * layer_rows, D)
     d_patch_w = jnp.einsum("btp,btd->pd", noisy, d_residual, precision=PRECISE)
     d_patch_b = jnp.sum(d_residual, axis=(0, 1))
     row_parts = jnp.concatenate(
-        [d_patch_w, d_head, d_patch_b[None]] + bias_blocks + [d_final_shift, d_final_scale],
+        [d_patch_w, d_head, d_patch_b[None], bias_blocks, d_final_shift, d_final_scale],
         axis=0,
     )
     row_count = row_parts.shape[0]
     row_lanes = -(-row_count // 128) * 128
     row_parts = jnp.pad(row_parts, ((0, row_lanes - row_count), (0, 0)))
     final_at = row_count - 2 * images
-    row_send = row_parts.T.reshape(place_count, cols, row_lanes)
-    mod_send = jnp.stack(mod_parts).reshape(LAYERS * images, tensor_size, mod_cols)
+    row_send = row_parts.T.reshape(dp_size, tensor_size, cols, row_lanes)
+    mod_send = d_mods.reshape(LAYERS * images, tensor_size, mod_cols)
     mod_send = mod_send.transpose(1, 0, 2)
     if fused:
         slots = slots_of(images)
@@ -1719,16 +1825,21 @@
             scale_cols,
             pre_signal,
             pre_time,
+            feats_all,
+            hidden,
+            signal,
+            loss_part.reshape(1, 1),
             terms,
+            [block for total in totals for block in total],
             images,
             final_at,
         )
-        row_sums, final_sums, d_mod_low, d_pre_signal, d_hidden = outs[:5]
-        totals.insert(0, outs[5:])
-        d_shift_cols, d_scale_cols = final_sums[0], final_sums[1]
-        d_mod_low = d_mod_low[:, : LAYERS * images]
-        d_mod_low = d_mod_low.reshape(dp_size, LAYERS, images, mod_cols)
-        d_mod_low = d_mod_low.transpose(1, 0, 2, 3).reshape(LAYERS, images_all, mod_cols)
+        row_sums, vector_sums, class_grad, time_grad, second_grad, shift_grad, scale_grad = outs[:7]
+        mod_grad, scalar_sums = outs[7:9]
+        totals.insert(0, outs[9:])
+        vector_sums = vector_sums[:, 0:4]
+        class_grad = class_grad[:, :CLASSES]
+        scalar_sums = scalar_sums[0]
     else:
         totals.insert(
             0,
@@ -1737,7 +1848,7 @@
                 for term in terms
             ],
         )
-        row_all = exchange(row_send, "all", True, 7)
+        row_all = exchange(row_send.reshape(place_count, cols, row_lanes), "all", True, 7)
         row_sums = jnp.sum(row_all, axis=0)
         final_sums = jnp.sum(
             row_all[:, :, final_at:row_count].reshape(dp_size, tensor_size, cols, 2, images), axis=1
@@ -1764,22 +1875,31 @@
             exchange(d_hidden_part.reshape(place_count, cols, images_all), "all", True, 11), axis=0
         )
         d_hidden = d_hidden_cols * silu_slope(pre_time)
-    mod_grad = jnp.einsum(
-        "db,lbe->lde", signal_low, d_mod_low, preferred_element_type=jnp.float32
-    )
+        mod_grad = jnp.einsum(
+            "db,lbe->lde", signal_low, d_mod_low, preferred_element_type=jnp.float32
+        )
+        class_grad = dense(d_pre_signal, onehot)
+        time_grad = dense(d_hidden, time_feats)
+        second_grad = dense(d_pre_signal, hidden.T)
+        shift_grad = dense(d_shift_cols, signal.T)
+        scale_grad = dense(d_scale_cols, signal.T)
+        vector_sums = jnp.stack(
+            [
+                jnp.sum(values, axis=1)
+                for values in (d_hidden, d_pre_signal, d_shift_cols, d_scale_cols)
+            ],
+            axis=1,
+        )
     table_grad = jnp.concatenate(
         [
-            dense(d_pre_signal, onehot),
+            class_grad,
             row_sums[:, 0:patch_in],
-            dense(d_hidden, time_feats),
-            dense(d_pre_signal, hidden.T),
-            dense(d_shift_cols, signal.T),
-            dense(d_scale_cols, signal.T),
+            time_grad,
+            second_grad,
+            shift_grad,
+            scale_grad,
             row_sums[:, patch_in : 2 * patch_in + 1],
-            jnp.sum(d_hidden, axis=1, keepdims=True),
-            jnp.sum(d_pre_signal, axis=1, keepdims=True),
-            jnp.sum(d_shift_cols, axis=1, keepdims=True),
-            jnp.sum(d_scale_cols, axis=1, keepdims=True),
+            vector_sums,
             row_sums[:, 2 * patch_in + 1 : final_at],
         ],
         axis=1,
@@ -1787,16 +1907,17 @@
     input_grad = jnp.stack([jnp.concatenate(total[0:2], axis=1) for total in totals])
     input_grad = input_grad.reshape(layer_in.shape)
     output_grad = jnp.stack([total[2] for total in totals]).reshape(layer_out.shape)
-    local_squares = (
-        jnp.sum(table_grad * table_grad)
-        + jnp.sum(input_grad * input_grad)
-        + jnp.sum(output_grad * output_grad)
-        + jnp.sum(mod_grad * mod_grad)
-    )
-    scalar_send = jnp.where(
-        lax.broadcasted_iota(jnp.int32, (8, 128), 1) == 0, loss_part, local_squares
-    )
-    scalar_sums = jnp.sum(exchange(scalar_send, "all", False, 12)[:, 0, 0:2], axis=0)
+    if not fused:
+        local_squares = (
+            jnp.sum(table_grad * table_grad)
+            + jnp.sum(input_grad * input_grad)
+            + jnp.sum(output_grad * output_grad)
+            + jnp.sum(mod_grad * mod_grad)
+        )
+        scalar_send = jnp.where(
+            lax.broadcasted_iota(jnp.int32, (8, 128), 1) == 0, loss_part, local_squares
+        )
+        scalar_sums = jnp.sum(exchange(scalar_send, "all", False, 12)[:, 0, 0:2], axis=0)
     loss_value = scalar_sums[0]
     square_total = scalar_sums[1]
     grad_norm = jnp.sqrt(square_total)

time: 631 us -> 551 us (0.87)
  Pallas kernels: 526 us -> 474 us
  local copies, waits for them, and re-layouts: 43.6 us -> 30 us
  other arithmetic: 32.6 us -> 25.5 us
    pallas_call x1, Pallas kernels: 102 us -> 73.3 us  [tail_call(): pl.pallas_call(functools.partial(tail_kernel, images, at), out_shape=[jax...]
    pallas_call x4 -> x3, Pallas kernels: 167 us -> 153 us  [forward_layer(): pl.pallas_call(functools.partial(forward_kernel, layer_idx), out_shape=[j...]
    slice x20 -> x9, local copies, waits for them, and re-layouts: 15 us -> 3.16 us  [the longest x1 0.96 us: local(): shards_in[:, :, 3 * group_width:]]
    pallas_call x3, Pallas kernels: 186 us -> 175 us  [backward_layer(): pl.pallas_call(backward_kernel, out_shape=[jax.ShapeDtypeStruct(*shape) f...]
where the time goes in v5:
time: 551 us; the launch traced here: 542 us
  Pallas kernels  474 us (86%)
  local copies, waits for them, and re-layouts  30 us (5%)
  other arithmetic  25.5 us (5%)
  matrix products  7.57 us (1%)
    pallas_call x3, Pallas kernels, backward_layer(): pl.pallas_call(backward_kernel, out_shape=[jax.ShapeDtypeStruct(*shape) f...  175 us
    pallas_call x3, Pallas kernels, forward_layer(): pl.pallas_call(functools.partial(forward_kernel, layer_idx), out_shape=[j...  153 us
    pallas_call x1, Pallas kernels, head_call(): pl.pallas_call(functools.partial(head_kernel, images), out_shape=[jax.Sha...  73.3 us
    pallas_call x1, Pallas kernels, tail_call(): pl.pallas_call(functools.partial(tail_kernel, images, at), out_shape=[jax...  73.3 us
    unnamed x110, local copies, waits for them, and re-layouts  12 us

profile of v5, /device:TPU:0, one launch (start us, length us, event | category | flops | bytes accessed | tf_op | source)
XLA Modules:
  0.0 542.4 jit_solution(15594030770397074420)
XLA Ops:
  1.4 0.7 convert_element_type.57
  2.0 0.7 convert_element_type.56
  2.8 1.2 fusion.42
  4.0 0.5 subtract_sqrt_fusion
  4.8 0.6 select_maximum_fusion.feats_ref
  5.4 0.5 multiply_sine_fusion.1
  6.1 1.0 reduce-precision_bitcast_fusion.table_ref
  7.1 0.7 slice.190.bias_ref
  7.9 0.7 maximum_maximum_fusion.small_ref
  8.6 0.7 slice.186.time_ref
  9.3 0.8 fusion.43
  10.1 0.6 reshape.382
  10.7 0.4 copy.52
  11.1 0.7 reshape.383
  11.8 0.6 reshape.384
  12.4 0.4 copy.53
  13.0 0.9 fusion.5.rest_2_
  13.8 0.9 convert_element_type.58.mod_ref.weight_ref
  14.7 0.8 copy-done.1
  15.6 0.8 slice.191.rest_0_
  16.4 1.0 slice.192.rest_1_
  17.3 73.3 %head.1 = (f32[4,8,24,128]{3,2,1,0:T(8,128)}, f32[24,384]{1,0:T(8,128)}, f32[24,24]{1,0:T(8,128)}, f32[768,24]{1,0:T(8,128)}, f32[24,24]{1,0:T(8,128)}, /*index=...) custom-call(f32[24,128]{1,0:T(8,128)} %maximum_maximum_fusion.small_, ...), custom_call_target="tpu_custom_call" | custom-call | tf_op jit(solution)/shard_map/head/pallas_call | solution.py:1302
  90.7 1.1 copy.56
  92.8 0.6 fusion.45
  93.4 0.6 slice_bitcast_fusion.9
  94.1 0.7 slice_bitcast_fusion
  94.8 0.7 fusion.44
  95.5 1.6 fusion.2.res_ref
  97.1 56.2 %block_forward.3 = (f32[3,64,768]{2,1,0:T(8,128)}, bf16[3,256,768]{2,1,0:T(8,128)(2,1)}, bf16[3,256,576]{2,1,0:T(8,128)(2,1)}, bf16[3,256,192]{2,1,0:T(8,128)(2,...) custom-call(f32[3,64,768]{2,1,0:T(8,128)} %fusion.2.res_ref, ...), custom_call_target="tpu_custom_call" | custom-call | flops 30000001024 | bytes 15728640 | tf_op jit(solution)/shard_map/block_forward/pallas_call | solution.py:777
  153.2 53.9 %block_forward.4 = (f32[3,64,768]{2,1,0:T(8,128)}, bf16[3,256,768]{2,1,0:T(8,128)(2,1)}, bf16[3,256,576]{2,1,0:T(8,128)(2,1)}, bf16[3,256,192]{2,1,0:T(8,128)(2,...) custom-call(f32[3,64,768]{2,1,0:T(8,128)} %get-tuple-element.108.res, ...), custom_call_target="tpu_custom_call" | custom-call | flops 30000001024 | bytes 15728640 | tf_op jit(solution)/shard_map/block_forward/pallas_call | solution.py:777
  207.2 42.9 %block_forward.5 = (f32[3,64,768]{2,1,0:T(8,128)}, bf16[3,256,768]{2,1,0:T(8,128)(2,1)}, bf16[3,256,576]{2,1,0:T(8,128)(2,1)}, bf16[3,256,192]{2,1,0:T(8,128)(2,...) custom-call(f32[3,64,768]{2,1,0:T(8,128)} %get-tuple-element.112.res, ...), custom_call_target="tpu_custom_call" | custom-call | flops 30000001024 | bytes 15728640 | tf_op jit(solution)/shard_map/block_forward/pallas_call | solution.py:777
  250.1 1.2 reduce_sum.78
  251.3 1.3 multiply_reduce_fusion.2
  252.6 2.5 multiply_reduce_fusion.3
  255.8 1.2 convolution_bitcast_fusion
  256.9 0.8 multiply_reduce_fusion.1
  257.7 1.0 multiply_reduce_fusion
  258.7 1.0 broadcast_add_fusion.d_res_ref
  259.7 50.7 %block_backward.3 = (f32[3,64,768]{2,1,0:T(8,128)}, bf16[768,576]{1,0:T(8,128)(2,1)}, bf16[768,768]{1,0:T(8,128)(2,1)}, bf16[960,768]{1,0:T(8,128)(2,1)}, f32[3,...) custom-call(f32[3,64,768]{2,1,0:T(8,128)} %broadcast_add_fusion.d_res_ref, ...), custom_call_target="tpu_custom_call" | custom-call | flops 60000002048 | bytes 26214400 | tf_op jit(solution)/shard_map/block_backward/pallas_call | solution.py:1047
  310.4 60.7 %block_backward.4 = (f32[3,64,768]{2,1,0:T(8,128)}, bf16[768,576]{1,0:T(8,128)(2,1)}, bf16[768,768]{1,0:T(8,128)(2,1)}, bf16[960,768]{1,0:T(8,128)(2,1)}, f32[3,...) custom-call(f32[3,64,768]{2,1,0:T(8,128)} %get-tuple-element.126.d_r, ...), custom_call_target="tpu_custom_call" | custom-call | flops 60000002048 | bytes 26214400 | tf_op jit(solution)/shard_map/block_backward/pallas_call | solution.py:1047
  371.3 63.2 %block_backward.5 = (f32[3,64,768]{2,1,0:T(8,128)}, bf16[768,576]{1,0:T(8,128)(2,1)}, bf16[768,768]{1,0:T(8,128)(2,1)}, bf16[960,768]{1,0:T(8,128)(2,1)}, f32[3,...) custom-call(f32[3,64,768]{2,1,0:T(8,128)} %get-tuple-element.138.d_r, ...), custom_call_target="tpu_custom_call" | custom-call | flops 60000002048 | bytes 26214400 | tf_op jit(solution)/shard_map/block_backward/pallas_call | solution.py:1047
  434.6 1.6 convolution_bitcast_fusion.1
  436.2 0.7 fusion.25
  437.0 0.7 fusion.28
  437.7 0.2 dynamic_update_slice.6
  438.3 0.4 concatenate.57
  438.7 0.9 copy.63
  439.6 0.7 pad.14.mod_ref
  440.4 73.3 %tail.1 = (f32[24,128]{1,0:T(8,128)}, f32[24,128]{1,0:T(8,128)}, f32[24,1024]{1,0:T(8,128)}, f32[24,256]{1,0:T(8,128)}, f32[24,768]{1,0:T(8,128)}, /*index=5*/f3...) custom-call(f32[8,4,24,128]{3,2,1,0:T(8,128)} %bitcast.147, ...), custom_call_target="tpu_custom_call" | custom-call | tf_op jit(solution)/shard_map/tail/pallas_call | solution.py:1542
  514.1 1.3 fusion.46
  516.2 0.7 slice.183
  516.9 0.7 slice.181
  517.6 1.2 concatenate.58
  518.8 1.2 maximum_bitcast_fusion
  520.1 2.4 fusion.21
  522.5 2.6 fusion.38
  525.1 0.9 copy-done.15
  526.0 0.4 copy-done.16
  526.4 2.9 fusion.36
  529.4 1.1 copy-done.10
  530.5 2.2 fusion.40
  532.6 2.8 copy.69
  535.5 2.8 copy.71
  538.3 2.8 copy.70
  (152 shorter events, 2.7 us)
Async XLA Ops:
  0.7 9.4 %copy-start.39 = (f32[3,1024]{1,0:T(4,128)S(1)}, f32[3,1024]{1,0:T(4,128)}, u32[]{:S(2)}) copy-start(f32[3,1024]{1,0:T(4,128)} %param.17) | copy-start | bytes 36868
  5.9 5.9 %copy-start.40 = (f32[3,1024]{1,0:T(4,128)S(1)}, f32[3,1024]{1,0:T(4,128)}, u32[]{:S(2)}) copy-start(f32[3,1024]{1,0:T(4,128)} %param.18) | copy-start | bytes 36868
  7.1 5.8 %copy-start.7 = (f32[24,3640]{1,0:T(8,128)}, f32[24,3640]{1,0:T(8,128)S(1)}, u32[]{:S(2)}) copy-start(f32[24,3640]{1,0:T(8,128)S(1)} %reduce-precision_bitcast_fusion.table_ref) | copy-start | bytes 1048324
  7.1 5.8 %copy-start.5 = (f32[3,1,120,768]{3,2,1,0:T(8,128)S(1)}, f32[3,1,120,768]{3,2,1,0:T(8,128)}, u32[]{:S(2)}) copy-start(f32[3,1,120,768]{3,2,1,0:T(8,128)} %param.24) | copy-start | bytes 3317764
  11.8 2.0 copy-start.3
  12.9 239.7 %copy-start.23 = (f32[3,64,16]{1,2,0:T(8,128)}, f32[3,64,16]{1,2,0:T(8,128)S(1)}, u32[]{:S(2)}) copy-start(f32[3,64,16]{1,2,0:T(8,128)S(1)} %reshape.385) | copy-start | bytes 36868
  13.8 1.7 copy-start.1
  90.6 1.3 copy-start.27
  90.7 1.5 copy-start.38
  92.1 3.4 copy-start.29
  92.2 3.3 copy-start.48
  92.2 3.3 copy-start.50
  250.1 5.7 %copy-start = (f32[3,64,768]{2,1,0:T(8,128)S(1)}, f32[3,64,768]{2,1,0:T(8,128)}, u32[]{:S(2)}) copy-start(f32[3,64,768]{2,1,0:T(8,128)} %get-tuple-element.116) | copy-start | bytes 1769476
  371.2 63.4 %copy-start.24 = (f32[3,64,16]{1,2,0:T(8,128)S(1)}, f32[3,64,16]{1,2,0:T(8,128)}, u32[]{:S(2)}) copy-start(f32[3,64,16]{1,2,0:T(8,128)} %copy-done.23) | copy-start | bytes 36868
  371.2 63.4 %copy-start.30 = (f32[3,64,16]{1,2,0:T(8,128)S(1)}, f32[3,64,16]{1,2,0:T(8,128)}, u32[]{:S(2)}) copy-start(f32[3,64,16]{1,2,0:T(8,128)} %reshape.383) | copy-start | bytes 36868
  371.2 63.4 %copy-start.49 = (f32[3]{0:T(128)S(1)}, f32[3]{0:T(128)}, u32[]{:S(2)}) copy-start(f32[3]{0:T(128)} %get-tuple-element.238) | copy-start | bytes 40
  371.2 63.4 %copy-start.51 = (f32[3]{0:T(128)S(1)}, f32[3]{0:T(128)}, u32[]{:S(2)}) copy-start(f32[3]{0:T(128)} %subtract_sqrt_fusion) | copy-start | bytes 40
  371.2 65.0 %copy-start.44 = (f32[1,768]{1,0:T(1,128)S(1)}, f32[1,768]{1,0:T(1,128)}, u32[]{:S(2)}) copy-start(f32[1,768]{1,0:T(1,128)} %get-tuple-element.162) | copy-start | bytes 9220
  371.2 65.0 %copy-start.45 = (f32[1,768]{1,0:T(1,128)S(1)}, f32[1,768]{1,0:T(1,128)}, u32[]{:S(2)}) copy-start(f32[1,768]{1,0:T(1,128)} %get-tuple-element.161) | copy-start | bytes 9220
  371.2 65.8 %copy-start.46 = (f32[1,576]{1,0:T(1,128)S(1)}, f32[1,576]{1,0:T(1,128)}, u32[]{:S(2)}) copy-start(f32[1,576]{1,0:T(1,128)} %get-tuple-element.159) | copy-start | bytes 6916
  371.2 65.8 %copy-start.47 = (f32[1,576]{1,0:T(1,128)S(1)}, f32[1,576]{1,0:T(1,128)}, u32[]{:S(2)}) copy-start(f32[1,576]{1,0:T(1,128)} %get-tuple-element.158) | copy-start | bytes 6916
  434.5 3.4 copy-start.8
  434.5 3.5 copy-start.33
  434.5 3.5 copy-start.34
  434.5 3.5 copy-start.35
  434.5 3.6 copy-start.41
  434.5 3.6 copy-start.42
  434.5 3.6 copy-start.43
  436.2 2.1 copy-start.31
  436.2 2.1 copy-start.36
  436.2 2.1 copy-start.37
  440.4 73.4 %copy-start.17 = (f32[96,768]{1,0:T(8,128)S(1)}, f32[96,768]{1,0:T(8,128)}, u32[]{:S(2)}) copy-start(f32[96,768]{1,0:T(8,128)} %get-tuple-element.175.rest_7_) | copy-start | bytes 884740
  440.4 73.4 %copy-start.21 = (f32[96,576]{1,0:T(8,128)S(1)}, f32[96,576]{1,0:T(8,128)}, u32[]{:S(2)}) copy-start(f32[96,576]{1,0:T(8,128)} %get-tuple-element.174.rest_6_) | copy-start | bytes 663556
  440.4 73.5 %copy-start.18 = (f32[96,768]{1,0:T(8,128)S(1)}, f32[96,768]{1,0:T(8,128)}, u32[]{:S(2)}) copy-start(f32[96,768]{1,0:T(8,128)} %get-tuple-element.172.rest_4_) | copy-start | bytes 884740
  440.4 73.6 %copy-start.22 = (f32[96,576]{1,0:T(8,128)S(1)}, f32[96,576]{1,0:T(8,128)}, u32[]{:S(2)}) copy-start(f32[96,576]{1,0:T(8,128)} %get-tuple-element.171.rest_3_) | copy-start | bytes 663556
  440.4 82.0 %copy-start.19 = (f32[3,1,120,768]{3,2,1,0:T(8,128)S(1)}, f32[3,1,120,768]{3,2,1,0:T(8,128)}, u32[]{:S(2)}) copy-start(f32[3,1,120,768]{3,2,1,0:T(8,128)} %param.31) | copy-start | bytes 3317764
  513.7 2.5 copy-start.32
  513.7 5.1 copy-start.28
  513.9 6.1 %copy-start.13 = (f32[3640,24]{0,1:T(8,128)S(1)}, f32[3640,24]{0,1:T(8,128)}, u32[]{:S(2)}) copy-start(f32[3640,24]{0,1:T(8,128)} %param.22) | copy-start | bytes 1048324
  513.9 6.1 %copy-start.26 = (f32[3640,24]{0,1:T(8,128)S(1)}, f32[3640,24]{0,1:T(8,128)}, u32[]{:S(2)}) copy-start(f32[3640,24]{0,1:T(8,128)} %param.27) | copy-start | bytes 1048324
  518.8 3.6 copy-start.20
  520.0 2.4 copy-start.6
  520.0 2.4 copy-start.11
  520.0 2.4 copy-start.12
  520.1 2.4 copy-start.25
  522.5 2.6 copy-start.4
  522.5 2.6 copy-start.14
  522.5 3.5 copy-start.15
  522.5 3.9 copy-start.16
  526.4 3.0 copy-start.2
  526.4 3.0 copy-start.9
  526.4 4.1 copy-start.10

commit v6 on v5

--- a/solution.py
+++ b/solution.py
@@ -130,6 +130,22 @@
     pl.semaphore_wait(barrier, size - 1)
 
 
+def greet_groups(*groups):
+    barrier = pltpu.get_barrier_semaphore()
+    count = 0
+    for group in groups:
+        place, size, coords = group_place(group)
+
+        def greet_one(step, carry, place=place, size=size, coords=coords):
+            peer = coords(lax.rem(place + step, size))
+            pl.semaphore_signal(barrier, inc=1, device_id=peer, device_id_type=pl.DeviceIdType.MESH)
+            return carry
+
+        lax.fori_loop(1, size, greet_one, 0)
+        count += size - 1
+    pl.semaphore_wait(barrier, count)
+
+
 class Crowd:
     def __init__(self, group, source_at, target, send_sems, recv_sems, local_sem):
         self.place, self.size, self.coords = group_place(group)
@@ -167,6 +183,41 @@
 
         self.own_copy().wait()
         lax.fori_loop(1, self.size, finish, 0)
+
+
+class Relay:
+    def __init__(self, source_at, middle, whole, sems_dp, sems_tensor):
+        self.first = Crowd("dp", source_at, middle, *sems_dp)
+        self.second = Crowd("tensor", lambda place: middle, whole, *sems_tensor)
+
+    def start(self):
+        self.first.start()
+
+    def hand_on(self):
+        self.first.wait()
+        self.second.start()
+
+    def wait(self):
+        self.second.wait()
+
+
+class Funnel:
+    def __init__(self, source, across, middle, along, sems_tensor, sems_dp):
+        self.across, self.middle, self.along = across, middle, along
+        self.first = Crowd("tensor", lambda place: source.at[:, place], across, *sems_tensor)
+        self.second = Crowd("dp", lambda place: middle.at[place], along, *sems_dp)
+
+    def start(self):
+        self.first.start()
+
+    def hand_on(self):
+        self.first.wait()
+        self.middle[...] = jnp.sum(self.across[...], axis=0)
+        self.second.start()
+
+    def take(self):
+        self.second.wait()
+        return jnp.sum(self.along[...], axis=0)
 
 
 def crowd_scratch(size):
@@ -230,6 +281,10 @@
     )
 
 
+def square_sum(values):
+    return jnp.sum(jnp.sum(values * values, axis=0, keepdims=True), axis=1, keepdims=True)
+
+
 def norm_parts(values):
     center = values - jnp.mean(values, axis=-1, keepdims=True)
     rstd = lax.rsqrt(jnp.mean(center * center, axis=-1, keepdims=True) + EPS_NORM)
@@ -372,6 +427,22 @@
     lax.fori_loop(0, count, step, 0)
 
 
+class Moves:
+    def __init__(self, pairs, sems):
+        self.copies = [
+            pltpu.make_async_copy(source, target, sems.at[at])
+            for at, (source, target) in enumerate(pairs)
+        ]
+
+    def start(self, *which):
+        for at in which:
+            self.copies[at].start()
+
+    def wait(self, *which):
+        for at in which:
+            self.copies[at].wait()
+
+
 class Line:
     def __init__(self):
         self.size = lax.axis_size("dp") // 2
@@ -501,8 +572,9 @@
 
 
 class Reduce:
-    def __init__(self, line, terms, totals, pair_in, way_in, way_out, sends, recvs):
-        self.line, self.terms, self.totals = line, terms, totals
+    def __init__(self, line, terms, totals, own, pair_in, way_in, way_out, sends, recvs, own_sems):
+        self.line, self.terms, self.totals, self.own = line, terms, totals, own
+        self.own_sems = own_sems
         self.pair_in, self.way_in, self.way_out = pair_in, way_in, way_out
         self.sends, self.recvs = sends, recvs
 
@@ -528,7 +600,29 @@
         )
 
     def start(self):
+        self.load_own()
         each(self.line.size, self.send_pair)
+
+    def own_copy(self, part, spot):
+        return pltpu.make_async_copy(
+            self.terms[part].at[2 * spot + self.line.side],
+            self.own[part].at[spot],
+            self.own_sems.at[part, spot],
+        )
+
+    def load_own(self):
+        def load(spot):
+            for part in range(len(self.terms)):
+                self.own_copy(part, spot).start()
+
+        each(self.line.size, load)
+
+    def wait_own(self):
+        def wait(spot):
+            for part in range(len(self.terms)):
+                self.own_copy(part, spot).wait()
+
+        each(self.line.size, wait)
 
     def send_pair(self, step):
         line = self.line
@@ -545,7 +639,7 @@
                 self.pair_copy(part, line.at - far).start()
 
     def pair_sum(self, part, spot):
-        own = self.terms[part][2 * spot + self.line.side].astype(jnp.float32)
+        own = self.own[part][spot].astype(jnp.float32)
         return own + self.pair_in[part][spot].astype(jnp.float32)
 
     def pass_on(self, way, spot, more):
@@ -624,46 +718,43 @@
     vec_ref,
     qkv_bias_ref,
     up_bias_ref,
-    w_qkv_ref,
-    w_up_ref,
-    w_out_ref,
+    w_qkv_far,
+    w_up_far,
+    w_out_far,
     *rest,
 ):
-    with_gather = len(rest) > 19
+    with_gather = len(rest) > 31
     shards, rest = (rest[:3], rest[3:]) if with_gather else ((), rest)
+    res_out, kept = rest[0], rest[1:9]
+    wholes, rest = (rest[9:12], rest[12:]) if with_gather else ((), rest[9:])
+    rows_a, qkv_out, mixed_out, branch_out, mid_out, rows_m, upper_out, down_out = rest[:8]
+    w_qkv_ref, w_up_ref, w_out_ref = rest[8:11]
+    (
+        part_a,
+        near_a,
+        far_out_a,
+        far_in_a,
+        part_m,
+        near_m,
+        far_out_m,
+        far_in_m,
+        sends,
+        recvs,
+        move_sems,
+    ) = rest[11:22]
     group_width = w_qkv_ref.shape[1] // 3
     w_attn_ref, w_down_ref = w_out_ref.at[0:group_width, :], w_out_ref.at[group_width:, :]
-    (
-        res_out,
-        rows_a,
-        qkv_out,
-        mixed_out,
-        branch_out,
-        mid_out,
-        rows_m,
-        upper_out,
-        down_out,
-    ) = rest[:9]
-    wholes, rest = (rest[9:12], rest[12:]) if with_gather else ((), rest[9:])
-    (
-    part_a,
-    near_a,
-    far_out_a,
-    far_in_a,
-    part_m,
-    near_m,
-    far_out_m,
-    far_in_m,
-    sends,
-    recvs,
-    ) = rest[:10]
+    far = (w_qkv_far, w_out_far, w_up_far)
+    pairs = list(zip(far, (w_qkv_ref, w_out_ref, w_up_ref))) + list(zip(rest[:8], kept))
+    moves = Moves(pairs, move_sems)
+    moves.start(0, 1, 2)
     images = res_ref.shape[0]
     gather, last_step = None, 0
     if with_gather:
         line = Line()
         greet(line)
         own = [shard.at[layer_idx + 1] for shard in shards]
-        gather = Gather(line, own, wholes, *rest[10:])
+        gather = Gather(line, own, wholes, *rest[22:])
         last_step = line.size
     else:
         greet(None)
@@ -729,17 +820,24 @@
         gather.start()
     each(images, start_norm)
     each(images, spread_a.forward)
+    moves.wait(0, 1)
     each(images, attend)
+    moves.start(3, 4, 5)
     run_ticks(gather, 1, min(2, last_step))
     each(images, collect_a.forward)
     each(images, middle)
+    moves.start(6, 7)
     each(images, spread_m.forward)
     run_ticks(gather, 2, min(3, last_step))
+    moves.wait(2)
     each(images, feed)
+    moves.start(8, 9)
     run_ticks(gather, 3, min(4, last_step))
     each(images, collect_m.forward)
     each(images, finish)
+    moves.start(10)
     each(images, close)
+    moves.wait(*range(3, 11))
     if with_gather:
         each(max(last_step - 4, 0), lambda step: gather.tick(step + 4))
         gather.finish()
@@ -765,7 +863,10 @@
     scratch = [
         pltpu.SemaphoreType.DMA((4, images, 3)),
         pltpu.SemaphoreType.DMA((4, images, 3)),
+        pltpu.SemaphoreType.DMA((11,)),
     ]
+    near = [pltpu.VMEM(*shape) for shape in shapes[1:]]
+    near += [pltpu.VMEM(weight.shape, low) for weight in (w_qkv, w_up, w_out)]
     if shards:
         dp_size = lax.axis_size("dp")
         shapes += [((dp_size,) + shard.shape[1:], low) for shard in shards]
@@ -777,10 +878,14 @@
     return pl.pallas_call(
         functools.partial(forward_kernel, layer_idx),
         out_shape=[jax.ShapeDtypeStruct(*shape) for shape in shapes],
-        in_specs=[pl.BlockSpec(memory_space=pltpu.VMEM)] * 8
-        + [pl.BlockSpec(memory_space=pl.ANY)] * len(shards),
-        out_specs=[pl.BlockSpec(memory_space=pltpu.VMEM)] * len(shapes),
-        scratch_shapes=collect_scratch(images, tokens) + collect_scratch(images, tokens) + scratch,
+        in_specs=[pl.BlockSpec(memory_space=pltpu.VMEM)] * 5
+        + [pl.BlockSpec(memory_space=pl.ANY)] * (3 + len(shards)),
+        out_specs=[pl.BlockSpec(memory_space=pltpu.VMEM)]
+        + [pl.BlockSpec(memory_space=pl.ANY)] * (len(shapes) - 1),
+        scratch_shapes=near
+        + collect_scratch(images, tokens)
+        + collect_scratch(images, tokens)
+        + scratch,
         compiler_params=pltpu.CompilerParams(
             collective_id=16 + layer_idx, has_side_effects=True, vmem_limit_bytes=ACT_VMEM
         ),
@@ -810,56 +915,54 @@
     return (inner - mean_one - normed * mean_two) * rstd, d_shift, d_scale
 
 
-def backward_kernel(
-    d_res_ref,
-    mod_ref,
-    res_ref,
-    rows_a,
-    qkv_ref,
-    mixed_ref,
-    branch_ref,
-    mid_ref,
-    rows_m,
-    upper_ref,
-    down_ref,
-    w_qkv_ref,
-    w_up_ref,
-    w_out_ref,
-    *rest,
-):
-    with_reduce = len(rest) > 24
-    group_width = w_qkv_ref.shape[1] // 3
-    w_attn_ref, w_down_ref = w_out_ref.at[0:group_width, :], w_out_ref.at[group_width:, :]
+def backward_kernel(d_res_ref, mod_ref, *rest):
+    kept, rest = rest[:12], rest[12:]
+    with_reduce = len(rest) > 40
     terms, rest = (rest[:3], rest[3:]) if with_reduce else ((), rest)
+    d_res_out, d_far, (d_mod, d_vec, d_qkv_bias, d_up_bias) = rest[0], rest[1:4], rest[4:8]
+    totals, square_out = (rest[8:11], rest[11]) if with_reduce else ((), None)
+    rest = rest[12:] if with_reduce else rest[8:]
     (
-        d_res_out,
+        res_ref,
+        rows_a,
+        qkv_ref,
+        mixed_ref,
+        branch_ref,
+        mid_ref,
+        rows_m,
+        upper_ref,
+        down_ref,
+        w_qkv_ref,
+        w_up_ref,
+        w_out_ref,
         d_w_qkv,
         d_w_up,
         d_out,
-        d_mod,
-        d_vec,
-        d_qkv_bias,
-        d_up_bias,
-    ) = rest[:8]
-    totals, rest = (rest[8:11], rest[11:]) if with_reduce else ((), rest[8:])
+    ) = rest[:15]
     (
-    d_mid,
-    d_rows_m,
-    d_rows_a,
-    act_low,
-    d_upper,
-    d_qkv,
-    part_a,
-    near_a,
-    far_out_a,
-    far_in_a,
-    part_m,
-    near_m,
-    far_out_m,
-    far_in_m,
-    sends,
-    recvs,
-    ) = rest[:16]
+        d_mid,
+        d_rows_m,
+        d_rows_a,
+        act_low,
+        d_upper,
+        d_qkv,
+        part_a,
+        near_a,
+        far_out_a,
+        far_in_a,
+        part_m,
+        near_m,
+        far_out_m,
+        far_in_m,
+        sends,
+        recvs,
+        move_sems,
+    ) = rest[15:32]
+    group_width = w_qkv_ref.shape[1] // 3
+    w_attn_ref, w_down_ref = w_out_ref.at[0:group_width, :], w_out_ref.at[group_width:, :]
+    pairs = list(zip(kept, rest[:12])) + list(zip(rest[12:15], d_far))
+    moves = Moves(pairs, move_sems)
+    moves.start(8, 11, 7, 10, 6, 5, 4, 2, 9, 3, 1, 0)
     images = res_ref.shape[0]
     tokens = rows_a.shape[1]
     qkv_width = 3 * group_width
@@ -868,8 +971,8 @@
     if with_reduce:
         line = Line()
         greet(line)
-        pair_in, way_in, way_out = rest[16:19], rest[19:22], rest[22:25]
-        reduce = Reduce(line, terms, totals, pair_in, way_in, way_out, *rest[25:])
+        own, pair_in, way_in, way_out = rest[32:35], rest[35:38], rest[38:41], rest[41:44]
+        reduce = Reduce(line, terms, totals, own, pair_in, way_in, way_out, *rest[44:])
         last_step = line.size
     else:
         greet(None)
@@ -991,26 +1094,41 @@
         collect_a.close(image)
         collect_m.close(image)
 
-    each(images, start_down)
     if with_reduce:
         reduce.start()
+    moves.wait(8)
+    each(images, start_down)
     each(images, spread_m.forward)
+    moves.wait(11, 7, 10)
     each(images, feed)
+    if with_reduce:
+        reduce.wait_own()
     run_ticks(reduce, 0, min(1, last_step - 1))
     each(images, collect_m.forward)
+    moves.wait(6)
     feed_weights()
+    moves.start(13)
     run_ticks(reduce, 1, min(2, last_step - 1))
+    moves.wait(5, 4)
     each(images, middle)
     each(images, spread_a.forward)
+    moves.wait(2, 9)
     each(images, attend)
     each(images, collect_a.forward)
     run_ticks(reduce, 2, min(3, last_step - 1))
+    moves.wait(3, 1)
     attend_weights()
+    moves.start(12, 14)
+    moves.wait(0)
     each(images, finish)
     each(images, close)
     if with_reduce:
         each(max(last_step - 4, 0), lambda step: reduce.tick(step + 3))
         reduce.finish()
+        square_out[...] = jnp.broadcast_to(
+            sum(square_sum(total[...]) for total in totals), square_out.shape
+        )
+    moves.wait(12, 13, 14)
 
 
 def backward_layer(d_residual, mod_vec, saved, weights, terms):
@@ -1032,24 +1150,33 @@
     scratch = [
         pltpu.SemaphoreType.DMA((4, images, 3)),
         pltpu.SemaphoreType.DMA((4, images, 3)),
+        pltpu.SemaphoreType.DMA((15,)),
     ]
+    near = [pltpu.VMEM(kept.shape, kept.dtype) for kept in tuple(saved) + tuple(weights)]
+    near += [pltpu.VMEM(*shape) for shape in shapes[1:4]]
     if terms:
         spots = lax.axis_size("dp") // 2
         blocks = [term.shape[1:] for term in terms]
-        shapes += [(block, full) for block in blocks]
+        shapes += [(block, full) for block in blocks] + [((8, 128), full)]
+        scratch += [pltpu.VMEM((spots,) + block, low) for block in blocks]
         scratch += [pltpu.VMEM((spots,) + block, low) for block in blocks]
         scratch += [pltpu.VMEM((2, spots) + block, low) for block in blocks]
         scratch += [pltpu.VMEM((2, spots) + block, low) for block in blocks]
         scratch += [
             pltpu.SemaphoreType.DMA((3, spots, 3)),
             pltpu.SemaphoreType.DMA((3, spots, 3)),
+            pltpu.SemaphoreType.DMA((3, spots)),
         ]
     return pl.pallas_call(
         backward_kernel,
         out_shape=[jax.ShapeDtypeStruct(*shape) for shape in shapes],
-        in_specs=[pl.BlockSpec(memory_space=pltpu.VMEM)] * (14 + len(terms)),
-        out_specs=[pl.BlockSpec(memory_space=pltpu.VMEM)] * len(shapes),
-        scratch_shapes=[
+        in_specs=[pl.BlockSpec(memory_space=pltpu.VMEM)] * 2
+        + [pl.BlockSpec(memory_space=pl.ANY)] * (12 + len(terms)),
+        out_specs=[pl.BlockSpec(memory_space=pltpu.VMEM)]
+        + [pl.BlockSpec(memory_space=pl.ANY)] * 3
+        + [pl.BlockSpec(memory_space=pltpu.VMEM)] * (len(shapes) - 4),
+        scratch_shapes=near
+        + [
             pltpu.VMEM((images, count, D), full),
             pltpu.VMEM((images, tokens, D), low),
             pltpu.VMEM((images, tokens, D), low),
@@ -1107,6 +1234,15 @@
 
 def folded_lanes(cols, count):
     return -(-(cols // 8 * count) // 128) * 128
+
+
+def unfold_all(values, cols, count):
+    ordered = [
+        values[tensor_at, dp_at]
+        for dp_at in range(values.shape[1])
+        for tensor_at in range(values.shape[0])
+    ]
+    return jnp.concatenate([unfold(value, cols, count) for value in ordered], axis=0)
 
 
 def unfold(values, cols, count):
@@ -1146,31 +1282,34 @@
     (
         feats_all,
         hidden_own,
+        hidden_dp,
         hidden_all,
         signal_own,
+        signal_dp,
         signal_all,
         final_own,
+        final_dp,
         mod_part,
         mod_in,
         mod_own,
         small_dp,
-    ) = rest[14:24]
-    crowds = [rest[24 + 3 * index : 27 + 3 * index] for index in range(8)]
-    gather_sems = rest[48:]
+    ) = rest[14:27]
+    crowds = [rest[27 + 3 * index : 30 + 3 * index] for index in range(11)]
+    gather_sems = rest[60:]
     dp_size = lax.axis_size("dp")
     tensor_size = lax.axis_size("tensor")
     dp_rank = lax.axis_index("dp")
     images_all = images * dp_size
     slots = mod_own.shape[0]
-    greet_group("all")
+    greet_groups("dp", "tensor")
     gather = Gather(Line(), [shard.at[0] for shard in shards], wholes, *gather_sems)
     feats = Crowd("dp", lambda place: feats_ref, feats_all, *crowds[0])
-    small = Crowd("dp", lambda place: small_ref, small_dp, *crowds[1])
-    small_spread = Crowd("tensor", lambda place: small_dp, small_all, *crowds[7])
-    hidden = Crowd("all", lambda place: hidden_own, hidden_all, *crowds[2])
-    signal = Crowd("all", lambda place: signal_own, signal_all, *crowds[3])
-    final = Crowd("all", lambda place: final_own.at[place // tensor_size], final_all, *crowds[4])
-    mod_sum = Crowd("dp", lambda place: mod_part.at[place], mod_in, *crowds[5])
+    mod_sum = Crowd("dp", lambda place: mod_part.at[place], mod_in, *crowds[1])
+    mod_spread = Crowd("tensor", lambda place: mod_own, mod_all, *crowds[2])
+    small = Relay(lambda place: small_ref, small_dp, small_all, *crowds[3:5])
+    hidden = Relay(lambda place: hidden_own, hidden_dp, hidden_all, *crowds[5:7])
+    signal = Relay(lambda place: signal_own, signal_dp, signal_all, *crowds[7:9])
+    final = Relay(lambda place: final_own.at[place], final_dp, final_all, *crowds[9:11])
     line = gather.line
     first, last = line.at == 0, line.at == line.size - 1
     feats.start()
@@ -1193,27 +1332,28 @@
     onehot = jnp.where(lane == labels, 1.0, 0.0)
     class_part = dense_nt(table_ref[:, 0:class_lanes], onehot) + bias_ref[:, 2:3]
     small.start()
+    hidden.hand_on()
     for way in (UP, DOWN):
         gather.hand_on(1, way)
     gather.hand_over(1, UP)
     gather.hand_over(1, DOWN, first)
     hidden.wait()
     cols = second_ref.shape[0]
-    hidden_full = unfold(hidden_all[...], cols, images_all).reshape(D, images_all)
+    hidden_full = unfold_all(hidden_all[...], cols, images_all)
     hidden_out[...] = hidden_full
     pre_signal = dense(second_ref[...], hidden_full) + class_part
     pre_signal_out[...] = pre_signal
     signal_own[...] = fold(jax.nn.silu(pre_signal))
     signal.start()
+    small.hand_on()
+    signal.hand_on()
     for way in (UP, DOWN):
         gather.hand_on(2, way)
     gather.hand_over(1, DOWN, jnp.logical_not(first))
     gather.hand_over(2, UP, last)
     gather.hand_over(2, DOWN, first)
-    small.wait()
-    small_spread.start()
     signal.wait()
-    signal_full = unfold(signal_all[...], cols, images_all).reshape(D, images_all)
+    signal_full = unfold_all(signal_all[...], cols, images_all)
     signal_out[...] = signal_full
     mod_rows = mod_ref.shape[1]
     own_rows = pl.ds(pl.multiple_of(dp_rank * mod_rows, 8), mod_rows)
@@ -1231,7 +1371,7 @@
         placed = dot_nn(signal_low, pick).astype(jnp.bfloat16)
         term = dot_tn(placed, mod_ref[layer_idx])
         total = term if total is None else total + term
-    mod_part[...] = total.reshape(mod_part.shape)
+    mod_part[...] = total.reshape(mod_part.shape).astype(mod_part.dtype)
     mod_sum.start()
     gather.hand_over(2, UP, jnp.logical_not(last))
     gather.hand_over(2, DOWN, jnp.logical_not(first))
@@ -1252,11 +1392,11 @@
     final.start()
     run_ticks(gather, 3, min(4, dp_size // 2))
     mod_sum.wait()
-    mod_own[...] = jnp.sum(mod_in[...], axis=0)
-    mod_spread = Crowd("tensor", lambda place: mod_own, mod_all, *crowds[6])
+    mod_own[...] = jnp.sum(mod_in[...].astype(jnp.float32), axis=0)
     mod_spread.start()
+    final.hand_on()
     each(max(dp_size // 2 - 4, 0), lambda step: gather.tick(step + 4))
-    small_spread.wait()
+    small.wait()
     final.wait()
     mod_spread.wait()
     gather.finish()
@@ -1264,7 +1404,6 @@
 
 def head_call(small, feats, table, times, second, shift, scale, bias, mod_low, shards, images):
     dp_size, tensor_size = lax.axis_size("dp"), lax.axis_size("tensor")
-    size = dp_size * tensor_size
     images_all = images * dp_size
     cols = table.shape[0]
     slots = slots_of(images)
@@ -1277,22 +1416,25 @@
         ((D, images_all), full),
         ((cols, images_all), full),
         ((D, images_all), full),
-        ((size, 8, 128), full),
+        ((tensor_size, dp_size, 8, 128), full),
         ((tensor_size, slots, mod_low.shape[2]), full),
     ] + [((dp_size,) + shard.shape[1:], low) for shard in shards]
     scratch = [
         pltpu.VMEM((dp_size,) + feats.shape, full),
         pltpu.VMEM((8, folded), full),
-        pltpu.VMEM((size, 8, folded), full),
+        pltpu.VMEM((dp_size, 8, folded), full),
+        pltpu.VMEM((tensor_size, dp_size, 8, folded), full),
         pltpu.VMEM((8, folded), full),
-        pltpu.VMEM((size, 8, folded), full),
+        pltpu.VMEM((dp_size, 8, folded), full),
+        pltpu.VMEM((tensor_size, dp_size, 8, folded), full),
         pltpu.VMEM((dp_size, 8, 128), full),
-        pltpu.VMEM((dp_size, slots, mod_low.shape[2]), full),
-        pltpu.VMEM((dp_size, slots, mod_low.shape[2]), full),
+        pltpu.VMEM((dp_size, 8, 128), full),
+        pltpu.VMEM((dp_size, slots, mod_low.shape[2]), low),
+        pltpu.VMEM((dp_size, slots, mod_low.shape[2]), low),
         pltpu.VMEM((slots, mod_low.shape[2]), full),
         pltpu.VMEM((dp_size,) + small.shape, full),
     ]
-    for count in (dp_size, dp_size, size, size, size, dp_size, tensor_size, tensor_size):
+    for count in (dp_size, dp_size) + (tensor_size, dp_size) * 4 + (tensor_size,):
         scratch += crowd_scratch(count)
     scratch += [
         pltpu.SemaphoreType.DMA((3, dp_size // 2, 3)),
@@ -1304,17 +1446,14 @@
         out_shape=[jax.ShapeDtypeStruct(*shape) for shape in shapes],
         in_specs=[pl.BlockSpec(memory_space=pltpu.VMEM)] * 9
         + [pl.BlockSpec(memory_space=pl.ANY)] * len(shards),
-        out_specs=[pl.BlockSpec(memory_space=pltpu.VMEM)] * len(shapes),
+        out_specs=[pl.BlockSpec(memory_space=pltpu.VMEM)] * 8
+        + [pl.BlockSpec(memory_space=pl.ANY)] * len(shards),
         scratch_shapes=scratch,
         compiler_params=pltpu.CompilerParams(
             collective_id=30, has_side_effects=True, vmem_limit_bytes=ACT_VMEM
         ),
         name="head",
     )(small, feats, table, times, second, shift, scale, bias, mod_low, *shards)
-
-
-def square_sum(values):
-    return jnp.sum(jnp.sum(values * values, axis=0, keepdims=True), axis=1, keepdims=True)
 
 
 def tail_kernel(
@@ -1334,8 +1473,8 @@
     loss_ref,
     *rest,
 ):
-    terms, others = rest[0:3], rest[3 : 3 * LAYERS]
-    rest = rest[3 * LAYERS :]
+    terms, others = rest[0:3], rest[3 : 2 + LAYERS]
+    rest = rest[2 + LAYERS :]
     (
         row_sums,
         vector_sums,
@@ -1356,16 +1495,16 @@
         mod_low,
         d_mod_all,
         signal_part,
-        signal_out,
-        signal_in,
-        hidden_out,
-        hidden_in,
         scalar_own,
         scalar_in,
-    ) = rest[12:25]
-    pair_in, way_in, way_out = rest[25:28], rest[28:31], rest[31:34]
-    crowds = [rest[34 + 3 * index : 37 + 3 * index] for index in range(7)]
-    reduce_sems = rest[55:]
+        scalar_mid,
+        scalar_fin,
+    ) = rest[12:23]
+    signal_refs, hidden_refs = rest[23:27], rest[27:31]
+    own, pair_in, way_in, way_out = rest[31:34], rest[34:37], rest[37:40], rest[40:43]
+    crowds = [rest[43 + 3 * index : 46 + 3 * index] for index in range(10)]
+    reduce_sems = rest[73:]
+    signal_out, hidden_out = signal_refs[0], hidden_refs[0]
     dp_size = lax.axis_size("dp")
     tensor_size = lax.axis_size("tensor")
     places = dp_size * tensor_size
@@ -1375,28 +1514,27 @@
     mod_rows = weight_ref.shape[1]
     slots = mod_low.shape[0]
     last_step = dp_size // 2
-    greet_group("all")
-    reduce = Reduce(Line(), terms, totals, pair_in, way_in, way_out, *reduce_sems)
+    greet_groups("tensor", "dp")
+    reduce = Reduce(Line(), terms, totals, own, pair_in, way_in, way_out, *reduce_sems)
     mod_sum = Crowd("tensor", lambda place: mod_ref.at[place], mod_in, *crowds[0])
-    rows = Crowd("tensor", lambda place: row_ref.at[:, place], row_in, *crowds[1])
-    mod_spread = Crowd("dp", lambda place: mod_low, d_mod_all, *crowds[2])
-    signal = Crowd("all", lambda place: signal_out.at[place], signal_in, *crowds[3])
-    hidden = Crowd("all", lambda place: hidden_out.at[place], hidden_in, *crowds[4])
-    row_cross = Crowd("dp", lambda place: row_mid.at[place], row_fin, *crowds[5])
-    scalars = Crowd("all", lambda place: scalar_own, scalar_in, *crowds[6])
+    mod_spread = Crowd("dp", lambda place: mod_low, d_mod_all, *crowds[1])
+    rows = Funnel(row_ref, row_in, row_mid, row_fin, *crowds[2:4])
+    signal = Funnel(*signal_refs, *crowds[4:6])
+    hidden = Funnel(*hidden_refs, *crowds[6:8])
+    scalars = Crowd("tensor", lambda place: scalar_own, scalar_in, *crowds[8])
+    scalars_dp = Crowd("dp", lambda place: scalar_mid, scalar_fin, *crowds[9])
     mod_sum.start()
     rows.start()
     reduce.send_pair(0)
+    reduce.load_own()
     mod_sum.wait()
     mod_low[...] = jnp.sum(mod_in[...], axis=0).astype(jnp.bfloat16)
     mod_spread.start()
-    rows.wait()
-    row_mid[...] = jnp.sum(row_in[...], axis=0)
-    row_cross.start()
+    rows.hand_on()
     reduce.send_pair(1)
-    other_squares = sum(square_sum(other[...]) for other in others)
-    row_cross.wait()
-    row_total = jnp.sum(row_fin[...], axis=0)
+    other_squares = sum(other[0:1, 0:1] for other in others)
+    reduce.wait_own()
+    row_total = rows.take()
     row_sums[...] = row_total
     joined = jnp.concatenate([row_fin[at] for at in range(dp_size)], axis=1)
 
@@ -1433,8 +1571,11 @@
         signal_part[own_rows, :] += dense(
             dot_nt(weight_ref[layer_idx], d_mod), layer_pick(layer_idx, jnp.float32)
         )
-    signal_out[...] = fold(signal_part[...].reshape(places, cols, images_all))
+    signal_out[...] = fold(signal_part[...].reshape(places, cols, images_all)).reshape(
+        signal_out.shape
+    )
     signal.start()
+    signal.hand_on()
     reduce.send_pair(2)
     run_ticks(reduce, 0, min(1, last_step - 1))
     signal_low = signal_ref[own_rows, :].astype(jnp.bfloat16)
@@ -1451,12 +1592,12 @@
     other_squares = other_squares + square_sum(grad)
     lane = lax.broadcasted_iota(jnp.int32, row_total.shape, 1)
     other_squares = other_squares + square_sum(jnp.where(lane < final_at, row_total, 0.0))
-    signal.wait()
-    d_signal = unfold(jnp.sum(signal_in[...], axis=0), cols, images_all)
+    d_signal = unfold(signal.take(), cols, images_all)
     d_signal = d_signal * silu_slope(pre_signal_ref[...])
     d_hidden = dense_tn(second_ref[...], d_signal)
-    hidden_out[...] = fold(d_hidden.reshape(places, cols, images_all))
+    hidden_out[...] = fold(d_hidden.reshape(places, cols, images_all)).reshape(hidden_out.shape)
     hidden.start()
+    hidden.hand_on()
     each(max(last_step - 3, 0), lambda step: reduce.send_pair(step + 3))
     run_ticks(reduce, 1, min(2, last_step - 1))
     labels = jnp.round(feats_ref[:, FREQ : FREQ + 1]).astype(jnp.int32)
@@ -1467,8 +1608,7 @@
     grad = dense_nt(d_signal, hidden_ref[...])
     second_grad[...] = grad
     other_squares = other_squares + square_sum(grad)
-    hidden.wait()
-    d_hidden = unfold(jnp.sum(hidden_in[...], axis=0), cols, images_all)
+    d_hidden = unfold(hidden.take(), cols, images_all)
     d_hidden = d_hidden * silu_slope(pre_time_ref[...])
     grad = dense(d_hidden, feats_ref[:, 0:FREQ])
     time_grad[...] = grad
@@ -1489,7 +1629,10 @@
     scalar_own[...] = jnp.where(lane == 0, loss_ref[...], other_squares)
     scalars.start()
     scalars.wait()
-    scalar_sums[...] = jnp.sum(scalar_in[...], axis=0)
+    scalar_mid[...] = jnp.sum(scalar_in[...], axis=0)
+    scalars_dp.start()
+    scalars_dp.wait()
+    scalar_sums[...] = jnp.sum(scalar_fin[...], axis=0)
 
 
 def tail_call(
@@ -1497,7 +1640,6 @@
     terms, others, images, at,
 ):
     dp_size, tensor_size = lax.axis_size("dp"), lax.axis_size("tensor")
-    size = dp_size * tensor_size
     images_all = images * dp_size
     cols, lanes = rows.shape[2:]
     folded = folded_lanes(cols, images_all)
@@ -1523,26 +1665,35 @@
         pltpu.VMEM(mods.shape[1:], low),
         pltpu.VMEM((dp_size,) + mods.shape[1:], low),
         pltpu.VMEM((D, images_all), full),
-        pltpu.VMEM((size, 8, folded), full),
-        pltpu.VMEM((size, 8, folded), full),
-        pltpu.VMEM((size, 8, folded), full),
-        pltpu.VMEM((size, 8, folded), full),
         pltpu.VMEM((8, 128), full),
-        pltpu.VMEM((size, 8, 128), full),
+        pltpu.VMEM((tensor_size, 8, 128), full),
+        pltpu.VMEM((8, 128), full),
+        pltpu.VMEM((dp_size, 8, 128), full),
     ]
+    for _ in range(2):
+        scratch += [
+            pltpu.VMEM((dp_size, tensor_size, 8, folded), full),
+            pltpu.VMEM((tensor_size, dp_size, 8, folded), full),
+            pltpu.VMEM((dp_size, 8, folded), full),
+            pltpu.VMEM((dp_size, 8, folded), full),
+        ]
+    scratch += [pltpu.VMEM((spots,) + block, low) for block in blocks]
     scratch += [pltpu.VMEM((spots,) + block, low) for block in blocks]
     scratch += [pltpu.VMEM((2, spots) + block, low) for block in blocks]
     scratch += [pltpu.VMEM((2, spots) + block, low) for block in blocks]
-    for count in (tensor_size, tensor_size, dp_size, size, size, dp_size, size):
+    for count in (tensor_size, dp_size) * 5:
         scratch += crowd_scratch(count)
     scratch += [
         pltpu.SemaphoreType.DMA((3, spots, 3)),
         pltpu.SemaphoreType.DMA((3, spots, 3)),
+        pltpu.SemaphoreType.DMA((3, spots)),
     ]
     return pl.pallas_call(
         functools.partial(tail_kernel, images, at),
         out_shape=[jax.ShapeDtypeStruct(*shape) for shape in shapes],
-        in_specs=[pl.BlockSpec(memory_space=pltpu.VMEM)] * (12 + len(terms) + len(others)),
+        in_specs=[pl.BlockSpec(memory_space=pltpu.VMEM)] * 12
+        + [pl.BlockSpec(memory_space=pl.ANY)] * len(terms)
+        + [pl.BlockSpec(memory_space=pltpu.VMEM)] * len(others),
         out_specs=[pl.BlockSpec(memory_space=pltpu.VMEM)] * len(shapes),
         scratch_shapes=scratch,
         compiler_params=pltpu.CompilerParams(
@@ -1663,7 +1814,8 @@
         signal_low = lax.dynamic_slice_in_dim(
             signal.astype(jnp.bfloat16), dp_rank * mod_rows, mod_rows, 0
         )
-        final_own = final_all[:, :images, : 2 * cols].reshape(place_count, images, 2, cols)
+        final_all = final_all.transpose(1, 0, 2, 3)[:, :, :images, : 2 * cols]
+        final_own = final_all.reshape(place_count, images, 2, cols)
         final_own = final_own.transpose(2, 1, 0, 3).reshape(2, images, D)
         mod_full = mod_full[:, : LAYERS * images].reshape(tensor_size, LAYERS, images, mod_cols)
         mod_full = mod_full.transpose(1, 2, 0, 3).reshape(LAYERS, images, tensor_size * mod_cols)
@@ -1774,6 +1926,7 @@
     d_final = jnp.einsum("btp,pd->btd", d_pred, head_w, precision=PRECISE)
     d_residual, d_final_shift, d_final_scale = final_norm_pull(d_final)
     totals = []
+    squares = []
     terms = ()
     bias_parts = []
     for layer_idx in reversed(range(LAYERS)):
@@ -1781,7 +1934,8 @@
         outs = backward_layer(d_residual, mod_vec, saved, weights, terms)
         d_residual, d_w_qkv, d_w_up, d_w_out, d_mod_vec, d_vec, d_qkv_bias, d_up_bias = outs[:8]
         if terms:
-            totals.insert(0, outs[8:])
+            totals.insert(0, outs[8:11])
+            squares.append(outs[11])
         terms = [
             term.reshape((dp_size, -1) + term.shape[1:]) for term in (d_w_qkv, d_w_up, d_w_out)
         ]
@@ -1830,7 +1984,7 @@
             signal,
             loss_part.reshape(1, 1),
             terms,
-            [block for total in totals for block in total],
+            squares,
             images,
             final_at,
         )

time: 551 us -> 509 us (0.924)
  Pallas kernels: 474 us -> 432 us
    pallas_call x3, Pallas kernels: 175 us -> 156 us  [backward_layer(): pl.pallas_call(backward_kernel, out_shape=[jax.ShapeDtypeStruct(*shape) f...]
    pallas_call x1, Pallas kernels: 73.3 us -> 59.8 us  [head_call(): pl.pallas_call(functools.partial(head_kernel, images), out_shape=[jax.Sha...]
    pallas_call x3, Pallas kernels: 153 us -> 146 us  [forward_layer(): pl.pallas_call(functools.partial(forward_kernel, layer_idx), out_shape=[j...]
    unnamed x110 -> x108, local copies, waits for them, and re-layouts: 12 us -> 13.6 us
where the time goes in v6:
time: 509 us; the launch traced here: 499 us
  Pallas kernels  432 us (85%)
  local copies, waits for them, and re-layouts  31.1 us (6%)
  other arithmetic  23.7 us (5%)
  matrix products  7.56 us (1%)
  between operations  5.22 us (1%)
    pallas_call x3, Pallas kernels, backward_layer(): pl.pallas_call(backward_kernel, out_shape=[jax.ShapeDtypeStruct(*shape) f...  156 us
    pallas_call x3, Pallas kernels, forward_layer(): pl.pallas_call(functools.partial(forward_kernel, layer_idx), out_shape=[j...  146 us
    pallas_call x1, Pallas kernels, tail_call(): pl.pallas_call(functools.partial(tail_kernel, images, at), out_shape=[jax...  69.7 us
    pallas_call x1, Pallas kernels, head_call(): pl.pallas_call(functools.partial(head_kernel, images), out_shape=[jax.Sha...  59.8 us
    unnamed x108, local copies, waits for them, and re-layouts  13.6 us

profile of v6, /device:TPU:0, one launch (start us, length us, event | category | flops | bytes accessed | tf_op | source)
XLA Modules:
  0.0 499.5 jit_solution(1581538328818379401)
XLA Ops:
  1.4 0.7 convert_element_type.57
  2.0 0.7 convert_element_type.56
  2.8 0.7 fusion.43
  3.8 0.6 select_maximum_fusion.feats_ref
  4.4 0.5 multiply_sine_fusion.1
  5.1 1.0 reduce-precision_bitcast_fusion.table_ref
  6.1 0.7 slice.190.bias_ref
  6.9 0.7 maximum_maximum_fusion.small_ref
  7.6 0.7 slice.186.time_ref
  8.3 0.8 fusion.44
  9.1 0.6 reshape.382
  9.7 0.4 copy.50
  10.2 0.6 reshape.384
  10.8 0.4 copy.51
  11.4 0.9 fusion.5.rest_2_
  12.2 0.9 convert_element_type.58.mod_ref.weight_ref
  13.2 0.8 copy-done.1
  14.0 0.8 slice.191.rest_0_
  14.8 1.0 slice.192.rest_1_
  15.7 59.8 %head.1 = (f32[4,8,24,128]{3,2,1,0:T(8,128)}, f32[24,384]{1,0:T(8,128)}, f32[24,24]{1,0:T(8,128)}, f32[768,24]{1,0:T(8,128)}, f32[24,24]{1,0:T(8,128)}, /*index=...) custom-call(f32[24,128]{1,0:T(8,128)} %maximum_maximum_fusion.small_, ...), custom_call_target="tpu_custom_call" | custom-call | tf_op jit(solution)/shard_map/head/pallas_call | solution.py:1444
  75.6 1.1 copy.54
  77.2 0.3 fusion.22
  77.9 0.6 fusion.46
  78.5 0.6 slice_bitcast_fusion.9
  79.1 0.7 slice_bitcast_fusion
  79.8 0.7 fusion.45
  80.5 1.6 fusion.2.res_ref.rest_0_
  82.1 55.7 %block_forward.3 = (f32[3,64,768]{2,1,0:T(8,128)}, bf16[3,256,768]{2,1,0:T(8,128)(2,1)}, bf16[3,256,576]{2,1,0:T(8,128)(2,1)}, bf16[3,256,192]{2,1,0:T(8,128)(2,...) custom-call(f32[3,64,768]{2,1,0:T(8,128)} %fusion.2.res_ref.rest_0_,, ...), custom_call_target="tpu_custom_call" | custom-call | flops 30000001024 | bytes 15728640 | tf_op jit(solution)/shard_map/block_forward/pallas_call | solution.py:878
  137.8 50.3 %block_forward.4 = (f32[3,64,768]{2,1,0:T(8,128)}, bf16[3,256,768]{2,1,0:T(8,128)(2,1)}, bf16[3,256,576]{2,1,0:T(8,128)(2,1)}, bf16[3,256,192]{2,1,0:T(8,128)(2,...) custom-call(f32[3,64,768]{2,1,0:T(8,128)} %get-tuple-element.110.res, ...), custom_call_target="tpu_custom_call" | custom-call | flops 30000001024 | bytes 15728640 | tf_op jit(solution)/shard_map/block_forward/pallas_call | solution.py:878
  188.2 39.9 %block_forward.5 = (f32[3,64,768]{2,1,0:T(8,128)}, bf16[3,256,768]{2,1,0:T(8,128)(2,1)}, bf16[3,256,576]{2,1,0:T(8,128)(2,1)}, bf16[3,256,192]{2,1,0:T(8,128)(2,...) custom-call(f32[3,64,768]{2,1,0:T(8,128)} %get-tuple-element.114.res, ...), custom_call_target="tpu_custom_call" | custom-call | flops 30000001024 | bytes 15728640 | tf_op jit(solution)/shard_map/block_forward/pallas_call | solution.py:878
  228.1 1.2 reduce_sum.78
  229.4 1.3 multiply_reduce_fusion.2
  230.7 2.5 multiply_reduce_fusion.3
  233.8 1.2 convolution_bitcast_fusion
  235.0 0.8 multiply_reduce_fusion.1
  235.8 0.9 multiply_reduce_fusion
  236.7 1.0 broadcast_add_fusion.d_res_ref
  237.8 44.9 %block_backward.3 = (f32[3,64,768]{2,1,0:T(8,128)}, bf16[768,576]{1,0:T(8,128)(2,1)}, bf16[768,768]{1,0:T(8,128)(2,1)}, bf16[960,768]{1,0:T(8,128)(2,1)}, f32[3,...) custom-call(f32[3,64,768]{2,1,0:T(8,128)} %broadcast_add_fusion.d_res_ref, ...), custom_call_target="tpu_custom_call" | custom-call | flops 60000002048 | bytes 26214400 | tf_op jit(solution)/shard_map/block_backward/pallas_call | solution.py:1170
  282.7 55.0 %block_backward.4 = (f32[3,64,768]{2,1,0:T(8,128)}, bf16[768,576]{1,0:T(8,128)(2,1)}, bf16[768,768]{1,0:T(8,128)(2,1)}, bf16[960,768]{1,0:T(8,128)(2,1)}, f32[3,...) custom-call(f32[3,64,768]{2,1,0:T(8,128)} %get-tuple-element.128.d_r, ...), custom_call_target="tpu_custom_call" | custom-call | flops 60000002048 | bytes 26214400 | tf_op jit(solution)/shard_map/block_backward/pallas_call | solution.py:1170
  337.7 56.5 %block_backward.5 = (f32[3,64,768]{2,1,0:T(8,128)}, bf16[768,576]{1,0:T(8,128)(2,1)}, bf16[768,768]{1,0:T(8,128)(2,1)}, bf16[960,768]{1,0:T(8,128)(2,1)}, f32[3,...) custom-call(f32[3,64,768]{2,1,0:T(8,128)} %get-tuple-element.140.d_r, ...), custom_call_target="tpu_custom_call" | custom-call | flops 60000002048 | bytes 26214400 | tf_op jit(solution)/shard_map/block_backward/pallas_call | solution.py:1170
  394.4 1.6 convolution_bitcast_fusion.1
  396.1 0.7 fusion.26
  396.8 0.7 fusion.29
  398.1 0.4 concatenate.57
  398.5 0.9 copy.59
  399.5 0.7 pad.14.mod_ref
  400.2 69.7 %tail.1 = (f32[24,128]{1,0:T(8,128)}, f32[24,128]{1,0:T(8,128)}, f32[24,1024]{1,0:T(8,128)}, f32[24,256]{1,0:T(8,128)}, f32[24,768]{1,0:T(8,128)}, /*index=5*/f3...) custom-call(f32[8,4,24,128]{3,2,1,0:T(8,128)} %bitcast.147, ...), custom_call_target="tpu_custom_call" | custom-call | tf_op jit(solution)/shard_map/tail/pallas_call | solution.py:1691
  469.9 1.3 fusion.47
  472.0 0.8 slice.183
  472.8 0.8 slice.181
  473.6 1.3 concatenate.58
  474.9 1.2 maximum_bitcast_fusion
  476.5 0.6 copy-done.11
  477.3 1.2 fusion.21
  478.8 0.6 copy-done.15
  479.4 2.5 fusion.39
  481.9 1.0 copy-done.13
  482.9 0.4 copy-done.14
  483.3 3.0 fusion.37
  486.3 1.1 copy-done.10
  487.4 2.1 fusion.41
  489.5 2.8 copy.65
  492.3 2.8 copy.67
  495.1 2.8 copy.66
  (149 shorter events, 3.3 us)
Async XLA Ops:
  0.7 8.4 %copy-start.38 = (f32[3,1024]{1,0:T(4,128)S(1)}, f32[3,1024]{1,0:T(4,128)}, u32[]{:S(2)}) copy-start(f32[3,1024]{1,0:T(4,128)} %param.17) | copy-start | bytes 36868
  3.5 77.0 %copy-start.47 = (f32[3]{0:T(128)}, f32[3]{0:T(128)S(1)}, u32[]{:S(2)}) copy-start(f32[3]{0:T(128)S(1)} %get-tuple-element.244) | copy-start | bytes 40
  3.5 77.0 %copy-start.49 = (f32[3]{0:T(128)}, f32[3]{0:T(128)S(1)}, u32[]{:S(2)}) copy-start(f32[3]{0:T(128)S(1)} %subtract_sqrt_fusion) | copy-start | bytes 40
  4.9 5.2 %copy-start.39 = (f32[3,1024]{1,0:T(4,128)S(1)}, f32[3,1024]{1,0:T(4,128)}, u32[]{:S(2)}) copy-start(f32[3,1024]{1,0:T(4,128)} %param.18) | copy-start | bytes 36868
  6.1 5.3 %copy-start.7 = (f32[24,3640]{1,0:T(8,128)}, f32[24,3640]{1,0:T(8,128)S(1)}, u32[]{:S(2)}) copy-start(f32[24,3640]{1,0:T(8,128)S(1)} %reduce-precision_bitcast_fusion.table_ref) | copy-start | bytes 1048324
  6.1 5.3 %copy-start.5 = (f32[3,1,120,768]{3,2,1,0:T(8,128)S(1)}, f32[3,1,120,768]{3,2,1,0:T(8,128)}, u32[]{:S(2)}) copy-start(f32[3,1,120,768]{3,2,1,0:T(8,128)} %param.24) | copy-start | bytes 3317764
  10.2 70.3 %copy-start.29 = (f32[3,64,16]{1,2,0:T(8,128)}, f32[3,64,16]{1,2,0:T(8,128)S(1)}, u32[]{:S(2)}) copy-start(f32[3,64,16]{1,2,0:T(8,128)S(1)} %reshape.383) | copy-start | bytes 36868
  10.2 2.0 copy-start.3
  11.4 219.3 %copy-start.17 = (f32[3,64,16]{1,2,0:T(8,128)}, f32[3,64,16]{1,2,0:T(8,128)S(1)}, u32[]{:S(2)}) copy-start(f32[3,64,16]{1,2,0:T(8,128)S(1)} %reshape.385) | copy-start | bytes 36868
  12.2 1.7 copy-start.1
  75.5 1.3 copy-start.24
  75.5 1.5 copy-start.37
  228.1 5.7 %copy-start = (f32[3,64,768]{2,1,0:T(8,128)S(1)}, f32[3,64,768]{2,1,0:T(8,128)}, u32[]{:S(2)}) copy-start(f32[3,64,768]{2,1,0:T(8,128)} %get-tuple-element.118) | copy-start | bytes 1769476
  337.7 56.7 %copy-start.18 = (f32[3,64,16]{1,2,0:T(8,128)S(1)}, f32[3,64,16]{1,2,0:T(8,128)}, u32[]{:S(2)}) copy-start(f32[3,64,16]{1,2,0:T(8,128)} %copy-done.17) | copy-start | bytes 36868
  337.7 56.7 %copy-start.30 = (f32[3,64,16]{1,2,0:T(8,128)S(1)}, f32[3,64,16]{1,2,0:T(8,128)}, u32[]{:S(2)}) copy-start(f32[3,64,16]{1,2,0:T(8,128)} %copy-done.29) | copy-start | bytes 36868
  337.7 56.7 %copy-start.48 = (f32[3]{0:T(128)S(1)}, f32[3]{0:T(128)}, u32[]{:S(2)}) copy-start(f32[3]{0:T(128)} %copy-done.47) | copy-start | bytes 40
  337.7 56.7 %copy-start.50 = (f32[3]{0:T(128)S(1)}, f32[3]{0:T(128)}, u32[]{:S(2)}) copy-start(f32[3]{0:T(128)} %copy-done.49) | copy-start | bytes 40
  337.7 58.3 %copy-start.43 = (f32[1,768]{1,0:T(1,128)S(1)}, f32[1,768]{1,0:T(1,128)}, u32[]{:S(2)}) copy-start(f32[1,768]{1,0:T(1,128)} %get-tuple-element.164) | copy-start | bytes 9220
  337.7 58.3 %copy-start.44 = (f32[1,768]{1,0:T(1,128)S(1)}, f32[1,768]{1,0:T(1,128)}, u32[]{:S(2)}) copy-start(f32[1,768]{1,0:T(1,128)} %get-tuple-element.163) | copy-start | bytes 9220
  337.7 59.1 %copy-start.45 = (f32[1,576]{1,0:T(1,128)S(1)}, f32[1,576]{1,0:T(1,128)}, u32[]{:S(2)}) copy-start(f32[1,576]{1,0:T(1,128)} %get-tuple-element.161) | copy-start | bytes 6916
  337.7 59.1 %copy-start.46 = (f32[1,576]{1,0:T(1,128)S(1)}, f32[1,576]{1,0:T(1,128)}, u32[]{:S(2)}) copy-start(f32[1,576]{1,0:T(1,128)} %get-tuple-element.160) | copy-start | bytes 6916
  394.3 3.5 copy-start.8
  394.3 3.5 copy-start.32
  394.3 3.5 copy-start.33
  394.3 3.5 copy-start.34
  394.3 3.6 copy-start.40
  394.3 3.6 copy-start.41
  394.4 3.6 copy-start.42
  396.0 2.1 copy-start.31
  396.0 2.1 copy-start.35
  396.0 2.1 copy-start.36
  400.2 78.4 %copy-start.16 = (f32[3,1,120,768]{3,2,1,0:T(8,128)S(1)}, f32[3,1,120,768]{3,2,1,0:T(8,128)}, u32[]{:S(2)}) copy-start(f32[3,1,120,768]{3,2,1,0:T(8,128)} %param.30) | copy-start | bytes 3317764
  469.9 6.2 %copy-start.26 = (f32[96,768]{1,0:T(8,128)S(1)}, f32[96,768]{1,0:T(8,128)}, u32[]{:S(2)}) copy-start(f32[96,768]{1,0:T(8,128)} %get-tuple-element.186) | copy-start | bytes 884740
  469.9 6.2 %copy-start.28 = (f32[96,576]{1,0:T(8,128)S(1)}, f32[96,576]{1,0:T(8,128)}, u32[]{:S(2)}) copy-start(f32[96,576]{1,0:T(8,128)} %get-tuple-element.185) | copy-start | bytes 663556
  473.6 2.8 copy-start.25
  473.6 2.8 copy-start.27
  474.9 3.7 copy-start.19
  476.1 1.0 copy-start.11
  476.1 1.1 copy-start.22
  476.2 1.2 copy-start.23
  476.4 2.2 copy-start.20
  476.4 2.2 copy-start.21
  477.3 1.4 copy-start.6
  477.3 2.0 copy-start.15
  479.4 2.6 copy-start.4
  479.4 2.6 copy-start.12
  479.4 3.5 copy-start.13
  479.4 3.9 copy-start.14
  483.3 3.0 copy-start.2
  483.3 3.0 copy-start.9
  483.3 4.1 copy-start.10

commit v7 on v6

--- a/solution.py
+++ b/solution.py
@@ -896,6 +896,265 @@
     )(residual, mod_vec, vec_bias, qkv_bias, up_bias, w_qkv, w_up, w_out, *shards)
 
 
+def flat(ref):
+    value = ref[...]
+    return value.reshape(-1, value.shape[-1])
+
+
+def forward_all_kernel(
+    res_ref,
+    mod_ref,
+    vec_ref,
+    qkv_bias_ref,
+    up_bias_ref,
+    qkv_far,
+    up_far,
+    out_far,
+    *rest,
+):
+    shards, res_out, kept_far, whole_far = rest[0:3], rest[3], rest[4:13], rest[13:16]
+    kept, rest = rest[16:25], rest[25:]
+    res_all, rows_a_all, qkv_all, mixed_all, branch_all, mid_all, rows_m_all, upper_all, down_all = kept
+    w_qkv_all, w_up_all, w_blocks_all, w_out_all = rest[0:4]
+    part_a, near_a, far_out_a, far_in_a, part_m, near_m, far_out_m, far_in_m = rest[4:12]
+    sends, recvs, keep_sems, load_sems, whole_sems, gather_sends, gather_recvs, local_sems = rest[12:]
+    images = res_ref.shape[0]
+    group_width = w_qkv_all.shape[-1] // 3
+    line = Line()
+    last_step = line.size
+    loads = Moves(
+        [(qkv_far, w_qkv_all.at[0]), (out_far, w_blocks_all.at[0]), (up_far, w_up_all.at[0])],
+        load_sems,
+    )
+    loads.start(0, 1, 2)
+    greet(line)
+    gathers = [None]
+    for layer_idx in range(1, LAYERS):
+        gathers.append(
+            Gather(
+                line,
+                [shard.at[layer_idx] for shard in shards],
+                [whole.at[layer_idx] for whole in (w_qkv_all, w_up_all, w_blocks_all)],
+                gather_sends.at[layer_idx],
+                gather_recvs.at[layer_idx],
+                local_sems.at[layer_idx],
+            )
+        )
+    gathers.append(None)
+
+    def join_blocks(layer_idx):
+        rows = w_blocks_all.shape[2]
+        for pair in range(w_blocks_all.shape[1] // 2):
+            halves = [
+                w_blocks_all[layer_idx, 2 * pair + side].astype(jnp.float32) for side in range(2)
+            ]
+            w_out_all[layer_idx, 2 * rows * pair : 2 * rows * (pair + 1), :] = jnp.concatenate(
+                halves, axis=0
+            ).astype(jnp.bfloat16)
+
+    def mod_row(layer_idx, image, piece):
+        return mod_ref[layer_idx, image, pl.ds(piece, 1), :]
+
+    for layer_idx in range(LAYERS):
+        res, rows_a, qkv_out, mixed_out, branch_out, mid_out, rows_m, upper_out, down_out = [
+            ref.at[layer_idx] for ref in kept
+        ]
+        w_qkv, w_up, w_out = w_qkv_all.at[layer_idx], w_up_all.at[layer_idx], w_out_all.at[layer_idx]
+        w_attn, w_down = w_out.at[0:group_width, :], w_out.at[group_width:, :]
+        spread_a = Spread(rows_a, sends.at[layer_idx, 0], recvs.at[layer_idx, 0])
+        spread_m = Spread(rows_m, sends.at[layer_idx, 1], recvs.at[layer_idx, 1])
+        collect_a = Collect(
+            part_a,
+            near_a.at[layer_idx],
+            far_out_a.at[layer_idx],
+            far_in_a.at[layer_idx],
+            sends.at[layer_idx, 2],
+            recvs.at[layer_idx, 2],
+        )
+        collect_m = Collect(
+            part_m,
+            near_m.at[layer_idx],
+            far_out_m.at[layer_idx],
+            far_in_m.at[layer_idx],
+            sends.at[layer_idx, 3],
+            recvs.at[layer_idx, 3],
+        )
+        keep = Moves(
+            [(ref.at[layer_idx], far.at[layer_idx]) for ref, far in zip(kept, kept_far)],
+            keep_sems.at[layer_idx],
+        )
+        keep_whole = Moves(
+            [
+                (ref.at[layer_idx], far.at[layer_idx])
+                for ref, far in zip((w_qkv_all, w_up_all, w_out_all), whole_far)
+            ],
+            whole_sems.at[layer_idx],
+        )
+        gather = gathers[layer_idx + 1]
+
+        def start_norm(image, at, values, target):
+            normed, _ = norm_parts(values)
+            normed = normed * (1.0 + mod_row(at, image, 1)) + mod_row(at, image, 0)
+            target.put(image, normed.astype(jnp.bfloat16))
+
+        def first_norm(image, res=res, spread_a=spread_a):
+            res[image] = res_ref[image]
+            start_norm(image, 0, res_ref[image], spread_a)
+
+        def attend(image):
+            spread_a.wait(image)
+            projected = dot_nn(rows_a[image], flat(w_qkv)) + qkv_bias_ref[layer_idx]
+            qkv = projected.astype(jnp.bfloat16)
+            qkv_out[image] = qkv
+            heads = []
+            for head in range(group_width // HEAD_DIM):
+                probs = soft_rows(
+                    head_slice(qkv[:, :group_width], head),
+                    head_slice(qkv[:, group_width : 2 * group_width], head),
+                )
+                heads.append(
+                    dot_nn(probs.astype(jnp.bfloat16), head_slice(qkv[:, 2 * group_width :], head))
+                )
+            mixed = jnp.concatenate(heads, axis=1).astype(jnp.bfloat16)
+            mixed_out[image] = mixed
+            collect_a.put(image, dot_nn(mixed, w_attn[...]))
+
+        def middle(image):
+            branch = collect_a.take(image) + vec_ref[layer_idx, 0:1, :]
+            branch_out[image] = branch
+            mid = res[image] + mod_row(layer_idx, image, 2) * branch
+            mid_out[image] = mid
+            normed, _ = norm_parts(mid)
+            normed = normed * (1.0 + mod_row(layer_idx, image, 4)) + mod_row(layer_idx, image, 3)
+            spread_m.put(image, normed.astype(jnp.bfloat16))
+
+        def feed(image):
+            spread_m.wait(image)
+            upper = dot_nn(rows_m[image], flat(w_up)) + up_bias_ref[layer_idx]
+            upper_out[image] = upper
+            collect_m.put(image, dot_nn(gelu_tanh(upper).astype(jnp.bfloat16), w_down[...]))
+
+        def finish(image):
+            down = collect_m.take(image) + vec_ref[layer_idx, 1:2, :]
+            down_out[image] = down
+            value = mid_out[image] + mod_row(layer_idx, image, 5) * down
+            if layer_idx + 1 < LAYERS:
+                res_all[layer_idx + 1, image] = value
+                following = Spread(
+                    rows_a_all.at[layer_idx + 1],
+                    sends.at[layer_idx + 1, 0],
+                    recvs.at[layer_idx + 1, 0],
+                )
+                start_norm(image, layer_idx + 1, value, following)
+            else:
+                res_out[image] = value
+
+        def close(image):
+            spread_a.close(image)
+            spread_m.close(image)
+            collect_a.close(image)
+            collect_m.close(image)
+
+        if layer_idx == 0:
+            gather.start()
+            each(images, first_norm)
+        each(images, spread_a.forward)
+        if layer_idx == 0:
+            loads.wait(0, 1)
+            join_blocks(0)
+        each(images, attend)
+        keep.start(0, 1, 2, 3)
+        run_ticks(gather, 1, min(2, last_step))
+        each(images, collect_a.forward)
+        each(images, middle)
+        keep.start(4, 5)
+        each(images, spread_m.forward)
+        run_ticks(gather, 2, min(3, last_step))
+        if layer_idx == 0:
+            loads.wait(2)
+        each(images, feed)
+        keep.start(6, 7)
+        run_ticks(gather, 3, min(4, last_step))
+        each(images, collect_m.forward)
+        each(images, finish)
+        keep.start(8)
+        keep_whole.start(0, 1, 2)
+        each(images, close)
+        if gather is not None:
+            each(max(last_step - 4, 0), lambda step, gather=gather: gather.tick(step + 4))
+            if gathers[layer_idx + 2] is not None:
+                gathers[layer_idx + 2].start()
+            gather.finish()
+            join_blocks(layer_idx + 1)
+        keep.wait(*range(9))
+        keep_whole.wait(0, 1, 2)
+
+
+def forward_all(residual, mod_vecs, vec_bias, qkv_bias, up_bias, wholes, shards):
+    images, count, _ = residual.shape
+    tokens = 4 * count
+    low, full = jnp.bfloat16, jnp.float32
+    dp_size = lax.axis_size("dp")
+    qkv_width, units = wholes[0].shape[-1], wholes[1].shape[-1]
+    own = (images, count, D)
+    kept = [
+        (own, full),
+        ((images, tokens, D), low),
+        ((images, tokens, qkv_width), low),
+        ((images, tokens, qkv_width // 3), low),
+        (own, full),
+        (own, full),
+        ((images, tokens, D), low),
+        ((images, tokens, units), full),
+        (own, full),
+    ]
+    kept = [((LAYERS,) + shape, kind) for shape, kind in kept]
+    out_rows = wholes[2].shape[0] * wholes[2].shape[1]
+    matrices = [
+        ((LAYERS,) + wholes[0].shape, low),
+        ((LAYERS,) + wholes[1].shape, low),
+        ((LAYERS, out_rows, D), low),
+    ]
+    shapes = [(own, full)] + kept + matrices
+    collect = [
+        pltpu.VMEM((images, tokens, D), low),
+        pltpu.VMEM((LAYERS, images, 2, count, D), low),
+        pltpu.VMEM((LAYERS, images, count, D), low),
+        pltpu.VMEM((LAYERS, images, count, D), low),
+    ]
+    return pl.pallas_call(
+        forward_all_kernel,
+        out_shape=[jax.ShapeDtypeStruct(*shape) for shape in shapes],
+        in_specs=[pl.BlockSpec(memory_space=pltpu.VMEM)] * 5
+        + [pl.BlockSpec(memory_space=pl.ANY)] * 6,
+        out_specs=[pl.BlockSpec(memory_space=pltpu.VMEM)]
+        + [pl.BlockSpec(memory_space=pl.ANY)] * (len(shapes) - 1),
+        scratch_shapes=[pltpu.VMEM(*shape) for shape in kept]
+        + [
+            pltpu.VMEM(*matrices[0]),
+            pltpu.VMEM(*matrices[1]),
+            pltpu.VMEM((LAYERS,) + wholes[2].shape, low),
+            pltpu.VMEM(*matrices[2]),
+        ]
+        + collect
+        + collect
+        + [
+            pltpu.SemaphoreType.DMA((LAYERS, 4, images, 3)),
+            pltpu.SemaphoreType.DMA((LAYERS, 4, images, 3)),
+            pltpu.SemaphoreType.DMA((LAYERS, 9)),
+            pltpu.SemaphoreType.DMA((3,)),
+            pltpu.SemaphoreType.DMA((LAYERS, 3)),
+            pltpu.SemaphoreType.DMA((LAYERS, 3, dp_size // 2, 3)),
+            pltpu.SemaphoreType.DMA((LAYERS, 3, dp_size // 2, 3)),
+            pltpu.SemaphoreType.DMA((LAYERS, 3)),
+        ],
+        compiler_params=pltpu.CompilerParams(
+            collective_id=24, has_side_effects=True, vmem_limit_bytes=ACT_VMEM
+        ),
+        name="blocks_forward",
+    )(residual, mod_vecs, vec_bias, qkv_bias, up_bias, *wholes, *shards)
+
+
 def gelu_slope(values):
     root = math.sqrt(2.0 / math.pi)
     square = values * values
@@ -915,8 +1174,10 @@
     return (inner - mean_one - normed * mean_two) * rstd, d_shift, d_scale
 
 
-def backward_kernel(d_res_ref, mod_ref, *rest):
+def backward_kernel(layer_idx, d_res_ref, mod_ref, *rest):
     kept, rest = rest[:12], rest[12:]
+    if layer_idx is not None:
+        kept = [ref.at[layer_idx] for ref in kept]
     with_reduce = len(rest) > 40
     terms, rest = (rest[:3], rest[3:]) if with_reduce else ((), rest)
     d_res_out, d_far, (d_mod, d_vec, d_qkv_bias, d_up_bias) = rest[0], rest[1:4], rest[4:8]
@@ -958,7 +1219,7 @@
         recvs,
         move_sems,
     ) = rest[15:32]
-    group_width = w_qkv_ref.shape[1] // 3
+    group_width = w_qkv_ref.shape[-1] // 3
     w_attn_ref, w_down_ref = w_out_ref.at[0:group_width, :], w_out_ref.at[group_width:, :]
     pairs = list(zip(kept, rest[:12])) + list(zip(rest[12:15], d_far))
     moves = Moves(pairs, move_sems)
@@ -966,7 +1227,7 @@
     images = res_ref.shape[0]
     tokens = rows_a.shape[1]
     qkv_width = 3 * group_width
-    units = w_up_ref.shape[1]
+    units = w_up_ref.shape[-1]
     reduce, last_step = None, 0
     if with_reduce:
         line = Line()
@@ -1003,7 +1264,7 @@
         d_up_bias[...] += jnp.sum(d_up, axis=0, keepdims=True)
         d_up_low = d_up.astype(jnp.bfloat16)
         d_upper[image] = d_up_low
-        collect_m.put(image, dot_nt(d_up_low, w_up_ref[...]))
+        collect_m.put(image, dot_nt(d_up_low, flat(w_up_ref)))
 
     def rows_of(ref, width):
         return ref[...].reshape(images * tokens, width)
@@ -1062,7 +1323,7 @@
         d_qkv_bias[...] += jnp.sum(joined, axis=0, keepdims=True)
         joined = joined.astype(jnp.bfloat16)
         d_qkv[image] = joined
-        collect_a.put(image, dot_nt(joined, w_qkv_ref[...]))
+        collect_a.put(image, dot_nt(joined, flat(w_qkv_ref)))
 
     def attend_weights():
         d_out[0:group_width, :] = dot_tn(
@@ -1131,12 +1392,12 @@
     moves.wait(12, 13, 14)
 
 
-def backward_layer(d_residual, mod_vec, saved, weights, terms):
+def backward_layer(d_residual, mod_vec, saved, weights, terms, layer_idx, stacked):
     images, count, _ = d_residual.shape
     tokens = 4 * count
     low, full = jnp.bfloat16, jnp.float32
     w_qkv, w_up, w_out = weights
-    group_width, units = w_qkv.shape[1] // 3, w_up.shape[1]
+    group_width, units = w_qkv.shape[-1] // 3, w_up.shape[-1]
     shapes = [
         ((images, count, D), full),
         ((D, 3 * group_width), low),
@@ -1152,7 +1413,10 @@
         pltpu.SemaphoreType.DMA((4, images, 3)),
         pltpu.SemaphoreType.DMA((15,)),
     ]
-    near = [pltpu.VMEM(kept.shape, kept.dtype) for kept in tuple(saved) + tuple(weights)]
+    near = [
+        pltpu.VMEM(kept.shape[1:] if stacked else kept.shape, kept.dtype)
+        for kept in tuple(saved) + tuple(weights)
+    ]
     near += [pltpu.VMEM(*shape) for shape in shapes[1:4]]
     if terms:
         spots = lax.axis_size("dp") // 2
@@ -1168,7 +1432,7 @@
             pltpu.SemaphoreType.DMA((3, spots)),
         ]
     return pl.pallas_call(
-        backward_kernel,
+        functools.partial(backward_kernel, layer_idx if stacked else None),
         out_shape=[jax.ShapeDtypeStruct(*shape) for shape in shapes],
         in_specs=[pl.BlockSpec(memory_space=pltpu.VMEM)] * 2
         + [pl.BlockSpec(memory_space=pl.ANY)] * (12 + len(terms)),
@@ -1188,7 +1452,7 @@
         + collect_scratch(images, tokens)
         + scratch,
         compiler_params=pltpu.CompilerParams(
-            collective_id=21 if terms else 23, has_side_effects=True, vmem_limit_bytes=ACT_VMEM
+            collective_id=20 + layer_idx if stacked else (21 if terms else 23), has_side_effects=True, vmem_limit_bytes=ACT_VMEM
         ),
         cost_estimate=pl.CostEstimate(
             flops=60 * 10**9, bytes_accessed=25 * 2**20, transcendentals=0
@@ -1898,25 +2162,39 @@
     up_bias = lax.dynamic_slice_in_dim(
         bias_all[:, 10:].reshape(LAYERS, FF), tensor_rank * unit_count, unit_count, 1
     )
-    for layer_idx in range(LAYERS):
-        weights = (
-            wholes[0].reshape(D, 3 * group_width),
-            wholes[1].reshape(D, unit_count),
-            wholes[2].reshape(group_width + unit_count, D),
-        )
-        outs = forward_layer(
+    joined = fused and shards[0].shape[1] % 16 == 0 and shards[2].shape[1] % 8 == 0
+    if joined:
+        outs = forward_all(
             residual,
-            mod_vecs[layer_idx],
-            bias_all[layer_idx, 6:8],
-            qkv_bias[layer_idx : layer_idx + 1],
-            up_bias[layer_idx : layer_idx + 1],
-            *weights,
-            shards if layer_idx + 1 < LAYERS else (),
-            layer_idx,
-        )
-        wholes = outs[9:]
-        saved_acts.append((mod_vecs[layer_idx], (residual,) + tuple(outs[1:9]), weights))
+            mod_vecs,
+            bias_all[:, 6:8],
+            qkv_bias[:, None],
+            up_bias[:, None],
+            wholes,
+            shards,
+        )
         residual = outs[0]
+        saved_acts = [(mod_vecs[layer_idx], outs[1:10], outs[10:13]) for layer_idx in range(LAYERS)]
+    else:
+        for layer_idx in range(LAYERS):
+            weights = (
+                wholes[0].reshape(D, 3 * group_width),
+                wholes[1].reshape(D, unit_count),
+                wholes[2].reshape(group_width + unit_count, D),
+            )
+            outs = forward_layer(
+                residual,
+                mod_vecs[layer_idx],
+                bias_all[layer_idx, 6:8],
+                qkv_bias[layer_idx : layer_idx + 1],
+                up_bias[layer_idx : layer_idx + 1],
+                *weights,
+                shards if layer_idx + 1 < LAYERS else (),
+                layer_idx,
+            )
+            wholes = outs[9:]
+            saved_acts.append((mod_vecs[layer_idx], (residual,) + tuple(outs[1:9]), weights))
+            residual = outs[0]
     final_in, final_norm_pull = jax.vjp(modulate, residual, final_shift, final_scale)
     predicted = jnp.einsum("btd,pd->btp", final_in, head_w, precision=PRECISE)
     error_all = predicted - targets
@@ -1931,7 +2209,9 @@
     bias_parts = []
     for layer_idx in reversed(range(LAYERS)):
         mod_vec, saved, weights = saved_acts[layer_idx]
-        outs = backward_layer(d_residual, mod_vec, saved, weights, terms)
+        outs = backward_layer(
+            d_residual, mod_vec, saved, weights, terms, layer_idx, joined
+        )
         d_residual, d_w_qkv, d_w_up, d_w_out, d_mod_vec, d_vec, d_qkv_bias, d_up_bias = outs[:8]
         if terms:
             totals.insert(0, outs[8:11])

time: 509 us -> 494 us (0.971)
  Pallas kernels: 432 us -> 420 us
    pallas_call x6 -> x4, Pallas kernels: 302 us -> 290 us  [the longest x3 156 us: backward_layer(): pl.pallas_call(functools.partial(backward_kernel, layer_idx if stacked el...]
    unnamed x108 -> x110, local copies, waits for them, and re-layouts: 13.6 us -> 13.6 us
where the time goes in v7:
time: 494 us; the launch traced here: 488 us
  Pallas kernels  420 us (85%)
  local copies, waits for them, and re-layouts  31 us (6%)
  other arithmetic  23.7 us (5%)
  matrix products  7.56 us (2%)
  between operations  5.27 us (1%)
    pallas_call x3, Pallas kernels, backward_layer(): pl.pallas_call(functools.partial(backward_kernel, layer_idx if stacked el...  156 us
    pallas_call x1, Pallas kernels, forward_all(): pl.pallas_call(forward_all_kernel, out_shape=[jax.ShapeDtypeStruct(*shape...  134 us
    pallas_call x1, Pallas kernels, tail_call(): pl.pallas_call(functools.partial(tail_kernel, images, at), out_shape=[jax...  70.9 us
    pallas_call x1, Pallas kernels, head_call(): pl.pallas_call(functools.partial(head_kernel, images), out_shape=[jax.Sha...  59.8 us
    unnamed x110, local copies, waits for them, and re-layouts  13.6 us

profile of v7, /device:TPU:0, one launch (start us, length us, event | category | flops | bytes accessed | tf_op | source)
XLA Modules:
  0.0 487.9 jit_solution(2188231030937990767)
XLA Ops:
  1.4 0.7 convert_element_type.57
  2.0 0.7 convert_element_type.56
  2.8 0.7 fusion.43
  3.8 0.6 select_maximum_fusion.feats_ref
  4.4 0.5 multiply_sine_fusion.1
  5.1 1.0 reduce-precision_bitcast_fusion.table_ref
  6.1 0.7 slice.155.bias_ref
  6.9 0.7 maximum_maximum_fusion.small_ref
  7.6 0.7 slice.151.time_ref
  8.3 0.8 fusion.44
  9.1 0.6 reshape.355
  9.7 0.4 copy.51
  10.2 0.6 reshape.357
  10.8 0.4 copy.52
  11.4 0.9 fusion.5.rest_2_
  12.2 0.9 convert_element_type.58.mod_ref.weight_ref
  13.2 0.8 copy-done.1
  14.0 0.8 slice.156.rest_0_
  14.8 1.0 slice.157.rest_1_
  15.7 59.8 %head.1 = (f32[4,8,24,128]{3,2,1,0:T(8,128)}, f32[24,384]{1,0:T(8,128)}, f32[24,24]{1,0:T(8,128)}, f32[768,24]{1,0:T(8,128)}, f32[24,24]{1,0:T(8,128)}, /*index=...) custom-call(f32[24,128]{1,0:T(8,128)} %maximum_maximum_fusion.small_, ...), custom_call_target="tpu_custom_call" | custom-call | tf_op jit(solution)/shard_map/head/pallas_call | solution.py:1708
  75.5 1.1 copy.55
  77.2 0.3 fusion.22
  77.8 0.6 broadcast_in_dim.24.up_bias_ref
  78.4 0.6 fusion.45
  79.1 0.6 broadcast_in_dim.23.qkv_bias_ref
  79.8 0.7 slice_bitcast_fusion
  80.5 1.6 fusion.2.res_ref
  82.0 133.8 %blocks_forward.1 = (f32[3,64,768]{2,1,0:T(8,128)}, f32[3,3,64,768]{3,2,1,0:T(8,128)}, bf16[3,3,256,768]{3,2,1,0:T(8,128)(2,1)}, bf16[3,3,256,576]{3,2,1,0:T(8,1...) custom-call(f32[3,64,768]{2,1,0:T(8,128)} %fusion.2.res_ref, ...), custom_call_target="tpu_custom_call" | custom-call | tf_op jit(solution)/shard_map/blocks_forward/pallas_call | solution.py:1125
  215.8 1.2 reduce_sum.78
  217.1 1.3 multiply_reduce_fusion.2
  218.4 2.5 multiply_reduce_fusion.3
  221.5 1.2 convolution_bitcast_fusion
  222.7 0.8 multiply_reduce_fusion.1
  223.5 0.9 multiply_reduce_fusion
  224.4 1.0 broadcast_add_fusion.d_res_ref
  225.5 45.0 %block_backward.3 = (f32[3,64,768]{2,1,0:T(8,128)}, bf16[768,576]{1,0:T(8,128)(2,1)}, bf16[768,768]{1,0:T(8,128)(2,1)}, bf16[960,768]{1,0:T(8,128)(2,1)}, f32[3,...) custom-call(f32[3,64,768]{2,1,0:T(8,128)} %broadcast_add_fusion.d_res_ref, ...), custom_call_target="tpu_custom_call" | custom-call | flops 60000002048 | bytes 26214400 | tf_op jit(solution)/shard_map/block_backward/pallas_call | solution.py:1434
  270.5 55.0 %block_backward.4 = (f32[3,64,768]{2,1,0:T(8,128)}, bf16[768,576]{1,0:T(8,128)(2,1)}, bf16[768,768]{1,0:T(8,128)(2,1)}, bf16[960,768]{1,0:T(8,128)(2,1)}, f32[3,...) custom-call(f32[3,64,768]{2,1,0:T(8,128)} %get-tuple-element.104.d_r, ...), custom_call_target="tpu_custom_call" | custom-call | flops 60000002048 | bytes 26214400 | tf_op jit(solution)/shard_map/block_backward/pallas_call | solution.py:1434
  325.5 56.0 %block_backward.5 = (f32[3,64,768]{2,1,0:T(8,128)}, bf16[768,576]{1,0:T(8,128)(2,1)}, bf16[768,768]{1,0:T(8,128)(2,1)}, bf16[960,768]{1,0:T(8,128)(2,1)}, f32[3,...) custom-call(f32[3,64,768]{2,1,0:T(8,128)} %get-tuple-element.108.d_r, ...), custom_call_target="tpu_custom_call" | custom-call | flops 60000002048 | bytes 26214400 | tf_op jit(solution)/shard_map/block_backward/pallas_call | solution.py:1434
  381.6 1.6 convolution_bitcast_fusion.1
  383.3 0.7 fusion.26
  384.1 0.7 fusion.29
  384.8 0.2 dynamic_update_slice.6
  385.3 0.4 concatenate.57
  385.7 0.9 copy.60
  386.7 0.7 pad.14.mod_ref
  387.4 70.9 %tail.1 = (f32[24,128]{1,0:T(8,128)}, f32[24,128]{1,0:T(8,128)}, f32[24,1024]{1,0:T(8,128)}, f32[24,256]{1,0:T(8,128)}, f32[24,768]{1,0:T(8,128)}, /*index=5*/f3...) custom-call(f32[8,4,24,128]{3,2,1,0:T(8,128)} %bitcast.132, ...), custom_call_target="tpu_custom_call" | custom-call | tf_op jit(solution)/shard_map/tail/pallas_call | solution.py:1955
  458.3 1.3 fusion.46
  460.4 0.8 slice.148
  461.2 0.8 slice.146
  461.9 1.3 concatenate.58
  463.2 1.2 maximum_bitcast_fusion
  464.9 0.6 copy-done.12
  465.7 1.2 fusion.21
  466.9 0.2 copy-done.6
  467.1 0.6 copy-done.16
  467.7 2.5 fusion.39
  470.3 1.0 copy-done.14
  471.2 0.4 copy-done.15
  471.6 3.0 fusion.37
  474.7 1.1 copy-done.11
  475.7 2.1 fusion.41
  477.8 2.8 copy.66
  480.7 2.8 copy.68
  483.5 2.8 copy.67
  (149 shorter events, 3.0 us)
Async XLA Ops:
  0.7 8.4 %copy-start.39 = (f32[3,1024]{1,0:T(4,128)S(1)}, f32[3,1024]{1,0:T(4,128)}, u32[]{:S(2)}) copy-start(f32[3,1024]{1,0:T(4,128)} %param.17) | copy-start | bytes 36868
  3.5 76.9 %copy-start.48 = (f32[3]{0:T(128)}, f32[3]{0:T(128)S(1)}, u32[]{:S(2)}) copy-start(f32[3]{0:T(128)S(1)} %get-tuple-element.204) | copy-start | bytes 40
  3.5 76.9 %copy-start.50 = (f32[3]{0:T(128)}, f32[3]{0:T(128)S(1)}, u32[]{:S(2)}) copy-start(f32[3]{0:T(128)S(1)} %subtract_sqrt_fusion) | copy-start | bytes 40
  4.9 5.2 %copy-start.40 = (f32[3,1024]{1,0:T(4,128)S(1)}, f32[3,1024]{1,0:T(4,128)}, u32[]{:S(2)}) copy-start(f32[3,1024]{1,0:T(4,128)} %param.18) | copy-start | bytes 36868
  6.1 5.3 %copy-start.7 = (f32[24,3640]{1,0:T(8,128)}, f32[24,3640]{1,0:T(8,128)S(1)}, u32[]{:S(2)}) copy-start(f32[24,3640]{1,0:T(8,128)S(1)} %reduce-precision_bitcast_fusion.table_ref) | copy-start | bytes 1048324
  6.1 5.3 %copy-start.5 = (f32[3,1,120,768]{3,2,1,0:T(8,128)S(1)}, f32[3,1,120,768]{3,2,1,0:T(8,128)}, u32[]{:S(2)}) copy-start(f32[3,1,120,768]{3,2,1,0:T(8,128)} %param.24) | copy-start | bytes 3317764
  10.2 70.3 %copy-start.30 = (f32[3,64,16]{1,2,0:T(8,128)}, f32[3,64,16]{1,2,0:T(8,128)S(1)}, u32[]{:S(2)}) copy-start(f32[3,64,16]{1,2,0:T(8,128)S(1)} %reshape.356) | copy-start | bytes 36868
  10.2 2.0 copy-start.3
  11.4 207.0 %copy-start.18 = (f32[3,64,16]{1,2,0:T(8,128)}, f32[3,64,16]{1,2,0:T(8,128)S(1)}, u32[]{:S(2)}) copy-start(f32[3,64,16]{1,2,0:T(8,128)S(1)} %reshape.358) | copy-start | bytes 36868
  12.2 1.7 copy-start.1
  75.5 1.3 copy-start.25
  75.5 1.5 copy-start.38
  79.0 3.0 copy-start.9
  215.8 5.7 %copy-start = (f32[3,64,768]{2,1,0:T(8,128)S(1)}, f32[3,64,768]{2,1,0:T(8,128)}, u32[]{:S(2)}) copy-start(f32[3,64,768]{2,1,0:T(8,128)} %get-tuple-element.90) | copy-start | bytes 1769476
  325.5 56.1 %copy-start.19 = (f32[3,64,16]{1,2,0:T(8,128)S(1)}, f32[3,64,16]{1,2,0:T(8,128)}, u32[]{:S(2)}) copy-start(f32[3,64,16]{1,2,0:T(8,128)} %copy-done.18) | copy-start | bytes 36868
  325.5 56.1 %copy-start.31 = (f32[3,64,16]{1,2,0:T(8,128)S(1)}, f32[3,64,16]{1,2,0:T(8,128)}, u32[]{:S(2)}) copy-start(f32[3,64,16]{1,2,0:T(8,128)} %copy-done.30) | copy-start | bytes 36868
  325.5 56.1 %copy-start.49 = (f32[3]{0:T(128)S(1)}, f32[3]{0:T(128)}, u32[]{:S(2)}) copy-start(f32[3]{0:T(128)} %copy-done.48) | copy-start | bytes 40
  325.5 56.1 %copy-start.51 = (f32[3]{0:T(128)S(1)}, f32[3]{0:T(128)}, u32[]{:S(2)}) copy-start(f32[3]{0:T(128)} %copy-done.50) | copy-start | bytes 40
  325.5 57.8 %copy-start.44 = (f32[1,768]{1,0:T(1,128)S(1)}, f32[1,768]{1,0:T(1,128)}, u32[]{:S(2)}) copy-start(f32[1,768]{1,0:T(1,128)} %get-tuple-element.124) | copy-start | bytes 9220
  325.5 57.8 %copy-start.45 = (f32[1,768]{1,0:T(1,128)S(1)}, f32[1,768]{1,0:T(1,128)}, u32[]{:S(2)}) copy-start(f32[1,768]{1,0:T(1,128)} %get-tuple-element.123) | copy-start | bytes 9220
  325.5 58.5 %copy-start.46 = (f32[1,576]{1,0:T(1,128)S(1)}, f32[1,576]{1,0:T(1,128)}, u32[]{:S(2)}) copy-start(f32[1,576]{1,0:T(1,128)} %get-tuple-element.121) | copy-start | bytes 6916
  325.5 58.5 %copy-start.47 = (f32[1,576]{1,0:T(1,128)S(1)}, f32[1,576]{1,0:T(1,128)}, u32[]{:S(2)}) copy-start(f32[1,576]{1,0:T(1,128)} %get-tuple-element.120) | copy-start | bytes 6916
  381.5 3.4 copy-start.8
  381.5 3.5 copy-start.33
  381.5 3.5 copy-start.34
  381.6 3.5 copy-start.35
  381.6 3.6 copy-start.41
  381.6 3.6 copy-start.42
  381.6 3.6 copy-start.43
  383.2 2.1 copy-start.32
  383.2 2.1 copy-start.36
  383.2 2.1 copy-start.37
  387.4 79.5 %copy-start.17 = (f32[3,1,120,768]{3,2,1,0:T(8,128)S(1)}, f32[3,1,120,768]{3,2,1,0:T(8,128)}, u32[]{:S(2)}) copy-start(f32[3,1,120,768]{3,2,1,0:T(8,128)} %param.30) | copy-start | bytes 3317764
  458.3 6.2 %copy-start.27 = (f32[96,768]{1,0:T(8,128)S(1)}, f32[96,768]{1,0:T(8,128)}, u32[]{:S(2)}) copy-start(f32[96,768]{1,0:T(8,128)} %get-tuple-element.146) | copy-start | bytes 884740
  458.3 6.2 %copy-start.29 = (f32[96,576]{1,0:T(8,128)S(1)}, f32[96,576]{1,0:T(8,128)}, u32[]{:S(2)}) copy-start(f32[96,576]{1,0:T(8,128)} %get-tuple-element.145) | copy-start | bytes 663556
  461.9 2.8 copy-start.26
  461.9 2.8 copy-start.28
  463.2 3.7 copy-start.20
  464.5 1.0 copy-start.12
  464.5 1.1 copy-start.23
  464.5 1.2 copy-start.24
  464.7 2.2 copy-start.21
  464.7 2.2 copy-start.22
  465.7 1.4 copy-start.6
  465.7 2.0 copy-start.16
  467.7 2.6 copy-start.4
  467.7 2.6 copy-start.13
  467.7 3.5 copy-start.14
  467.7 3.9 copy-start.15
  471.6 3.0 copy-start.2
  471.6 3.0 copy-start.10
  471.6 4.1 copy-start.11

commit v8 on v7

--- a/solution.py
+++ b/solution.py
@@ -902,18 +902,25 @@
 
 
 def forward_all_kernel(
+    count_all,
     res_ref,
     mod_ref,
     vec_ref,
     qkv_bias_ref,
     up_bias_ref,
+    final_shift_ref,
+    final_scale_ref,
+    head_ref,
+    targets_ref,
     qkv_far,
     up_far,
     out_far,
     *rest,
 ):
-    shards, res_out, kept_far, whole_far = rest[0:3], rest[3], rest[4:13], rest[13:16]
-    kept, rest = rest[16:25], rest[25:]
+    shards, rest = rest[0:3], rest[3:]
+    d_res_out, d_head_out, loss_out, d_shift_out, d_scale_out = rest[0:5]
+    kept_far, whole_far = rest[5:14], rest[14:17]
+    kept, rest = rest[17:26], rest[26:]
     res_all, rows_a_all, qkv_all, mixed_all, branch_all, mid_all, rows_m_all, upper_all, down_all = kept
     w_qkv_all, w_up_all, w_blocks_all, w_out_all = rest[0:4]
     part_a, near_a, far_out_a, far_in_a, part_m, near_m, far_out_m, far_in_m = rest[4:12]
@@ -954,6 +961,23 @@
 
     def mod_row(layer_idx, image, piece):
         return mod_ref[layer_idx, image, pl.ds(piece, 1), :]
+
+    d_head_out[...] = jnp.zeros_like(d_head_out)
+    loss_out[...] = jnp.zeros_like(loss_out)
+
+    def final_loss(image, value):
+        normed, _ = norm_parts(value)
+        final_in = normed * (1.0 + final_scale_ref[image]) + final_shift_ref[image]
+        error_all = dense_nt(final_in, head_ref[...]) - targets_ref[image]
+        loss_out[...] += square_sum(error_all) / count_all
+        d_pred = 2.0 * error_all / count_all
+        d_head_out[...] += dense_tn(d_pred, final_in)
+        d_value, d_shift, d_scale = norm_pull(
+            value, final_scale_ref[image], dense(d_pred, head_ref[...])
+        )
+        d_shift_out[image] = d_shift
+        d_scale_out[image] = d_scale
+        d_res_out[image] = d_value
 
     for layer_idx in range(LAYERS):
         res, rows_a, qkv_out, mixed_out, branch_out, mid_out, rows_m, upper_out, down_out = [
@@ -1047,7 +1071,7 @@
                 )
                 start_norm(image, layer_idx + 1, value, following)
             else:
-                res_out[image] = value
+                final_loss(image, value)
 
         def close(image):
             spread_a.close(image)
@@ -1090,7 +1114,9 @@
         keep_whole.wait(0, 1, 2)
 
 
-def forward_all(residual, mod_vecs, vec_bias, qkv_bias, up_bias, wholes, shards):
+def forward_all(
+    count_all, residual, mod_vecs, vec_bias, qkv_bias, up_bias, finals, wholes, shards
+):
     images, count, _ = residual.shape
     tokens = 4 * count
     low, full = jnp.bfloat16, jnp.float32
@@ -1115,7 +1141,9 @@
         ((LAYERS,) + wholes[1].shape, low),
         ((LAYERS, out_rows, D), low),
     ]
-    shapes = [(own, full)] + kept + matrices
+    shapes = [(own, full), (finals[2].shape, full), ((1, 1), full)]
+    shapes += [(finals[0].shape, full), (finals[1].shape, full)]
+    shapes += kept + matrices
     collect = [
         pltpu.VMEM((images, tokens, D), low),
         pltpu.VMEM((LAYERS, images, 2, count, D), low),
@@ -1123,12 +1151,12 @@
         pltpu.VMEM((LAYERS, images, count, D), low),
     ]
     return pl.pallas_call(
-        forward_all_kernel,
+        functools.partial(forward_all_kernel, count_all),
         out_shape=[jax.ShapeDtypeStruct(*shape) for shape in shapes],
-        in_specs=[pl.BlockSpec(memory_space=pltpu.VMEM)] * 5
+        in_specs=[pl.BlockSpec(memory_space=pltpu.VMEM)] * 9
         + [pl.BlockSpec(memory_space=pl.ANY)] * 6,
-        out_specs=[pl.BlockSpec(memory_space=pltpu.VMEM)]
-        + [pl.BlockSpec(memory_space=pl.ANY)] * (len(shapes) - 1),
+        out_specs=[pl.BlockSpec(memory_space=pltpu.VMEM)] * 5
+        + [pl.BlockSpec(memory_space=pl.ANY)] * (len(shapes) - 5),
         scratch_shapes=[pltpu.VMEM(*shape) for shape in kept]
         + [
             pltpu.VMEM(*matrices[0]),
@@ -1152,7 +1180,7 @@
             collective_id=24, has_side_effects=True, vmem_limit_bytes=ACT_VMEM
         ),
         name="blocks_forward",
-    )(residual, mod_vecs, vec_bias, qkv_bias, up_bias, *wholes, *shards)
+    )(residual, mod_vecs, vec_bias, qkv_bias, up_bias, *finals, *wholes, *shards)
 
 
 def gelu_slope(values):
@@ -1739,18 +1767,8 @@
 ):
     terms, others = rest[0:3], rest[3 : 2 + LAYERS]
     rest = rest[2 + LAYERS :]
-    (
-        row_sums,
-        vector_sums,
-        class_grad,
-        time_grad,
-        second_grad,
-        shift_grad,
-        scale_grad,
-        mod_grad,
-        scalar_sums,
-    ) = rest[0:9]
-    totals = rest[9:12]
+    table_grad, mod_grad, scalar_sums = rest[0:3]
+    totals, rest = rest[3:6], rest[6:]
     (
         row_in,
         row_mid,
@@ -1763,11 +1781,11 @@
         scalar_in,
         scalar_mid,
         scalar_fin,
-    ) = rest[12:23]
-    signal_refs, hidden_refs = rest[23:27], rest[27:31]
-    own, pair_in, way_in, way_out = rest[31:34], rest[34:37], rest[37:40], rest[40:43]
-    crowds = [rest[43 + 3 * index : 46 + 3 * index] for index in range(10)]
-    reduce_sems = rest[73:]
+    ) = rest[0:11]
+    signal_refs, hidden_refs = rest[11:15], rest[15:19]
+    own, pair_in, way_in, way_out = rest[19:22], rest[22:25], rest[25:28], rest[28:31]
+    crowds = [rest[31 + 3 * index : 34 + 3 * index] for index in range(10)]
+    reduce_sems = rest[61:]
     signal_out, hidden_out = signal_refs[0], hidden_refs[0]
     dp_size = lax.axis_size("dp")
     tensor_size = lax.axis_size("tensor")
@@ -1799,7 +1817,18 @@
     other_squares = sum(other[0:1, 0:1] for other in others)
     reduce.wait_own()
     row_total = rows.take()
-    row_sums[...] = row_total
+    patch_start, time_start, second_start, final_start, head_start, vector_start, layer_start = (
+        table_starts()
+    )
+    patch_in = time_start - patch_start
+    layer_at = 2 * patch_in + 1
+
+    def put(start, values):
+        table_grad[:, start : start + values.shape[1]] = values
+
+    put(patch_start, row_total[:, 0:patch_in])
+    put(head_start, row_total[:, patch_in:layer_at])
+    put(layer_start, row_total[:, layer_at:final_at])
     joined = jnp.concatenate([row_fin[at] for at in range(dp_size)], axis=1)
 
     def final_of(piece):
@@ -1849,10 +1878,10 @@
         mod_grad[layer_idx] = grad
         other_squares = other_squares + square_sum(grad)
     grad = dense_nt(d_shift, signal_ref[...])
-    shift_grad[...] = grad
+    put(final_start, grad)
     other_squares = other_squares + square_sum(grad)
     grad = dense_nt(d_scale, signal_ref[...])
-    scale_grad[...] = grad
+    put(final_start + D, grad)
     other_squares = other_squares + square_sum(grad)
     lane = lax.broadcasted_iota(jnp.int32, row_total.shape, 1)
     other_squares = other_squares + square_sum(jnp.where(lane < final_at, row_total, 0.0))
@@ -1865,24 +1894,24 @@
     each(max(last_step - 3, 0), lambda step: reduce.send_pair(step + 3))
     run_ticks(reduce, 1, min(2, last_step - 1))
     labels = jnp.round(feats_ref[:, FREQ : FREQ + 1]).astype(jnp.int32)
-    class_lane = lax.broadcasted_iota(jnp.int32, (images_all, class_grad.shape[1]), 1)
+    class_lane = lax.broadcasted_iota(jnp.int32, (images_all, -(-CLASSES // 128) * 128), 1)
     grad = dense(d_signal, jnp.where(class_lane == labels, 1.0, 0.0))
-    class_grad[...] = grad
+    put(0, grad[:, 0:CLASSES])
     other_squares = other_squares + square_sum(grad)
     grad = dense_nt(d_signal, hidden_ref[...])
-    second_grad[...] = grad
+    put(second_start, grad)
     other_squares = other_squares + square_sum(grad)
     d_hidden = unfold(hidden.take(), cols, images_all)
     d_hidden = d_hidden * silu_slope(pre_time_ref[...])
     grad = dense(d_hidden, feats_ref[:, 0:FREQ])
-    time_grad[...] = grad
+    put(time_start, grad)
     other_squares = other_squares + square_sum(grad)
     vectors = [
         jnp.sum(values, axis=1, keepdims=True) for values in (d_hidden, d_signal, d_shift, d_scale)
     ]
-    lane = lax.broadcasted_iota(jnp.int32, vector_sums.shape, 1)
+    lane = lax.broadcasted_iota(jnp.int32, (cols, 128), 1)
     grad = sum(jnp.where(lane == at, vector, 0.0) for at, vector in enumerate(vectors))
-    vector_sums[...] = grad
+    put(vector_start + 1, grad[:, 0:4])
     other_squares = other_squares + square_sum(grad)
     run_ticks(reduce, 2, min(3, last_step - 1))
     each(max(last_step - 4, 0), lambda step: reduce.tick(step + 3))
@@ -1910,14 +1939,9 @@
     full, low = jnp.float32, jnp.bfloat16
     spots = dp_size // 2
     blocks = [term.shape[1:] for term in terms]
+    table_rows = table_starts()[-1] + LAYERS * (10 + FF // D)
     shapes = [
-        ((cols, lanes), full),
-        ((cols, 128), full),
-        ((cols, -(-CLASSES // 128) * 128), full),
-        ((cols, FREQ), full),
-        ((cols, D), full),
-        ((cols, D), full),
-        ((cols, D), full),
+        ((cols, table_rows), full),
         (mod_low.shape, full),
         ((8, 128), full),
     ] + [(block, full) for block in blocks]
@@ -2165,16 +2189,22 @@
     joined = fused and shards[0].shape[1] % 16 == 0 and shards[2].shape[1] % 8 == 0
     if joined:
         outs = forward_all(
+            count_all,
             residual,
             mod_vecs,
             bias_all[:, 6:8],
             qkv_bias[:, None],
             up_bias[:, None],
+            (final_shift[:, None], final_scale[:, None], head_w, targets),
             wholes,
             shards,
         )
-        residual = outs[0]
-        saved_acts = [(mod_vecs[layer_idx], outs[1:10], outs[10:13]) for layer_idx in range(LAYERS)]
+        d_residual, d_head, loss_part, d_final_shift, d_final_scale = outs[:5]
+        loss_part = loss_part[0, 0]
+        d_final_shift, d_final_scale = d_final_shift[:, 0], d_final_scale[:, 0]
+        saved_acts = [
+            (mod_vecs[layer_idx], outs[5:14], outs[14:17]) for layer_idx in range(LAYERS)
+        ]
     else:
         for layer_idx in range(LAYERS):
             weights = (
@@ -2195,14 +2225,14 @@
             wholes = outs[9:]
             saved_acts.append((mod_vecs[layer_idx], (residual,) + tuple(outs[1:9]), weights))
             residual = outs[0]
-    final_in, final_norm_pull = jax.vjp(modulate, residual, final_shift, final_scale)
-    predicted = jnp.einsum("btd,pd->btp", final_in, head_w, precision=PRECISE)
-    error_all = predicted - targets
-    loss_part = jnp.sum(error_all * error_all) / count_all
-    d_pred = 2.0 * error_all / count_all
-    d_head = jnp.einsum("btp,btd->pd", d_pred, final_in, precision=PRECISE)
-    d_final = jnp.einsum("btp,pd->btd", d_pred, head_w, precision=PRECISE)
-    d_residual, d_final_shift, d_final_scale = final_norm_pull(d_final)
+        final_in, final_norm_pull = jax.vjp(modulate, residual, final_shift, final_scale)
+        predicted = jnp.einsum("btd,pd->btp", final_in, head_w, precision=PRECISE)
+        error_all = predicted - targets
+        loss_part = jnp.sum(error_all * error_all) / count_all
+        d_pred = 2.0 * error_all / count_all
+        d_head = jnp.einsum("btp,btd->pd", d_pred, final_in, precision=PRECISE)
+        d_final = jnp.einsum("btp,pd->btd", d_pred, head_w, precision=PRECISE)
+        d_residual, d_final_shift, d_final_scale = final_norm_pull(d_final)
     totals = []
     squares = []
     terms = ()
@@ -2268,11 +2298,8 @@
             images,
             final_at,
         )
-        row_sums, vector_sums, class_grad, time_grad, second_grad, shift_grad, scale_grad = outs[:7]
-        mod_grad, scalar_sums = outs[7:9]
-        totals.insert(0, outs[9:])
-        vector_sums = vector_sums[:, 0:4]
-        class_grad = class_grad[:, :CLASSES]
+        table_grad, mod_grad, scalar_sums = outs[:3]
+        totals.insert(0, outs[3:])
         scalar_sums = scalar_sums[0]
     else:
         totals.insert(
@@ -2324,20 +2351,20 @@
             ],
             axis=1,
         )
-    table_grad = jnp.concatenate(
-        [
-            class_grad,
-            row_sums[:, 0:patch_in],
-            time_grad,
-            second_grad,
-            shift_grad,
-            scale_grad,
-            row_sums[:, patch_in : 2 * patch_in + 1],
-            vector_sums,
-            row_sums[:, 2 * patch_in + 1 : final_at],
-        ],
-        axis=1,
-    )
+        table_grad = jnp.concatenate(
+            [
+                class_grad,
+                row_sums[:, 0:patch_in],
+                time_grad,
+                second_grad,
+                shift_grad,
+                scale_grad,
+                row_sums[:, patch_in : 2 * patch_in + 1],
+                vector_sums,
+                row_sums[:, 2 * patch_in + 1 : final_at],
+            ],
+            axis=1,
+        )
     input_grad = jnp.stack([jnp.concatenate(total[0:2], axis=1) for total in totals])
     input_grad = input_grad.reshape(layer_in.shape)
     output_grad = jnp.stack([total[2] for total in totals]).reshape(layer_out.shape)

time: 494 us -> 483 us (0.978)
  matrix products: 7.56 us -> 2 us
where the time goes in v8:
time: 483 us; the launch traced here: 476 us
  Pallas kernels  421 us (87%)
  local copies, waits for them, and re-layouts  29.1 us (6%)
  other arithmetic  20 us (4%)
    pallas_call x3, Pallas kernels, backward_layer(): pl.pallas_call(functools.partial(backward_kernel, layer_idx if stacked el...  156 us
    pallas_call x1, Pallas kernels, forward_all(): pl.pallas_call(functools.partial(forward_all_kernel, count_all), out_shap...  134 us
    pallas_call x1, Pallas kernels, tail_call(): pl.pallas_call(functools.partial(tail_kernel, images, at), out_shape=[jax...  71.3 us
    pallas_call x1, Pallas kernels, head_call(): pl.pallas_call(functools.partial(head_kernel, images), out_shape=[jax.Sha...  59.8 us
    unnamed x110, local copies, waits for them, and re-layouts  11.7 us

profile of v8, /device:TPU:0, one launch (start us, length us, event | category | flops | bytes accessed | tf_op | source)
XLA Modules:
  0.0 476.5 jit_solution(967993422224774477)
XLA Ops:
  0.7 1.0 reduce-precision_bitcast_fusion.table_ref
  1.9 0.7 maximum_maximum_fusion.small_ref
  2.6 0.8 fusion.24
  3.4 0.7 slice.131.time_ref
  4.1 0.7 slice.135.bias_ref
  4.7 1.5 copy.99
  6.3 1.0 slice.137.rest_1_
  7.3 0.8 slice.136.rest_0_
  8.0 0.1 multiply_cosine_fusion.2
  8.2 0.6 select_maximum_fusion.feats_ref
  8.9 0.9 convert_element_type.58.mod_ref.weight_ref
  9.8 0.9 fusion.5.rest_2_
  10.6 59.8 %head.1 = (f32[4,8,24,128]{3,2,1,0:T(8,128)}, f32[24,384]{1,0:T(8,128)}, f32[24,24]{1,0:T(8,128)}, f32[768,24]{1,0:T(8,128)}, f32[24,24]{1,0:T(8,128)}, /*index=...) custom-call(f32[24,128]{1,0:T(8,128)} %maximum_maximum_fusion.small_, ...), custom_call_target="tpu_custom_call" | custom-call | tf_op jit(solution)/shard_map/head/pallas_call | solution.py:1736
  70.5 1.0 copy.59
  71.5 0.2 copy.60
  71.7 0.6 fusion.25
  72.5 0.6 broadcast_in_dim.19.qkv_bias_ref
  73.2 0.5 multiply_sine_fusion.1
  73.7 0.1 pad_maximum_fusion.1
  73.8 0.6 reshape.314
  74.5 0.4 copy.56
  74.8 0.1 reshape.315
  75.1 0.6 reshape.312
  75.7 0.4 copy.55
  76.1 0.1 reshape.313
  76.2 1.6 fusion.2.res_ref
  77.9 0.1 reshape_reshape.3
  78.0 0.7 broadcast_add_fusion.mod_ref
  78.7 0.6 broadcast_in_dim.20.up_bias_ref
  79.3 0.6 slice.148.head_ref
  80.0 0.1 reshape.320
  80.1 0.3 slice_reduce_fusion
  80.4 0.7 broadcast_in_dim_squeeze.7.final_shift_ref
  81.1 0.7 broadcast_in_dim_squeeze.8.final_scale_ref
  81.8 0.7 copy.64.targets_ref
  82.6 134.0 %blocks_forward.1 = (f32[3,64,768]{2,1,0:T(8,128)}, f32[16,768]{1,0:T(8,128)}, f32[1,1]{1,0:T(1,128)}, f32[3,1,768]{2,1,0:T(1,128)}, f32[3,1,768]{2,1,0:T(1,128)...) custom-call(f32[3,64,768]{2,1,0:T(8,128)} %fusion.2.res_ref, ...), custom_call_target="tpu_custom_call" | custom-call | tf_op jit(solution)/shard_map/blocks_forward/pallas_call | solution.py:1153
  216.6 0.7 slice_bitcast_fusion
  217.2 45.0 %block_backward.3 = (f32[3,64,768]{2,1,0:T(8,128)}, bf16[768,576]{1,0:T(8,128)(2,1)}, bf16[768,768]{1,0:T(8,128)(2,1)}, bf16[960,768]{1,0:T(8,128)(2,1)}, f32[3,...) custom-call(f32[3,64,768]{2,1,0:T(8,128)} %get-tuple-element.89.d_res_ref, ...), custom_call_target="tpu_custom_call" | custom-call | flops 60000002048 | bytes 26214400 | tf_op jit(solution)/shard_map/block_backward/pallas_call | solution.py:1462
  262.3 55.0 %block_backward.4 = (f32[3,64,768]{2,1,0:T(8,128)}, bf16[768,576]{1,0:T(8,128)(2,1)}, bf16[768,768]{1,0:T(8,128)(2,1)}, bf16[960,768]{1,0:T(8,128)(2,1)}, f32[3,...) custom-call(f32[3,64,768]{2,1,0:T(8,128)} %get-tuple-element.102.d_r, ...), custom_call_target="tpu_custom_call" | custom-call | flops 60000002048 | bytes 26214400 | tf_op jit(solution)/shard_map/block_backward/pallas_call | solution.py:1462
  317.3 56.0 %block_backward.5 = (f32[3,64,768]{2,1,0:T(8,128)}, bf16[768,576]{1,0:T(8,128)(2,1)}, bf16[768,768]{1,0:T(8,128)(2,1)}, bf16[960,768]{1,0:T(8,128)(2,1)}, f32[3,...) custom-call(f32[3,64,768]{2,1,0:T(8,128)} %get-tuple-element.106.d_r, ...), custom_call_target="tpu_custom_call" | custom-call | flops 60000002048 | bytes 26214400 | tf_op jit(solution)/shard_map/block_backward/pallas_call | solution.py:1462
  373.4 1.0 pad_maximum_fusion
  374.4 0.7 fusion.12
  375.1 0.2 dynamic_update_slice.6
  375.3 0.7 fusion.11
  376.1 0.7 pad_maximum_fusion.2
  376.9 0.5 convolution_bitcast_fusion
  377.5 0.4 concatenate.54
  377.9 0.9 copy.65
  378.8 0.1 reshape.330
  378.9 0.7 pad.14.mod_ref
  379.7 71.3 %tail.1 = (f32[24,3640]{1,0:T(8,128)}, f32[3,96,1152]{2,1,0:T(8,128)}, f32[8,128]{1,0:T(8,128)}, f32[96,576]{1,0:T(8,128)}, f32[96,768]{1,0:T(8,128)}, /*index=5*/f32[120,768]{1,0:T(8,128)}) custom-call(f32[8,4,24,128]{3,2,1,0:T(8,128)} %bitcast.124, f32[4,16,1152]{2,1,0:T(8,128)} %pad.14.mod_ref, ...), custom_call_target="tpu_custom_call" | custom-call | tf_op jit(solution)/shard_map/tail/pallas_call | solution.py:1979
  450.9 1.3 fusion.26
  453.8 4.8 %fusion.17 = (bf16[3,96,1152]{2,1,0:T(8,128)(2,1)}, f32[3,96,1152]{2,1,0:T(8,128)}, f32[3,96,1152]{2,1,0:T(8,128)}, f32[3,96,1152]{2,1,0:T(8,128)}) fusion(f32[3,96,1152]{2,1,0:T(8,128)S(1)} %copy-done.2, f32[]{:T(128)S(6)} %sub.15, f32[3,96,1152]{2,1,0:T(8,128)} %get-tuple-element.148, f32[]{:T(128)S(6)} %min.3, f32[3,96,1152]{2,1,0:T(8,128)S(1)} %copy-done.11, ...), kind=kLoop, calls=%fused_computation.88 | loop fusion | flops 5308416 | bytes 9953288 | tf_op jit(solution)/shard_map/convert_element_type | solution.py:2004
  458.7 2.6 fusion.19
  461.3 0.2 maximum_bitcast_fusion
  461.5 0.2 maximum_bitcast_fusion.1
  461.6 0.2 maximum_bitcast_fusion.2
  461.8 1.0 copy-done.8
  462.8 0.5 copy-done
  463.3 2.1 fusion.21
  465.4 2.8 copy.71
  468.2 2.8 copy.72
  471.1 2.8 copy.73
  473.9 1.2 fusion.10
  (137 shorter events, 1.2 us)
Async XLA Ops:
  1.7 4.6 copy-start.5
  6.3 1.8 copy-start.50
  6.3 1.9 copy-start.49
  6.3 2.6 copy-start.1
  7.3 2.5 copy-start.3
  71.5 2.3 copy-start.35
  71.7 3.4 copy-start.36
  74.4 3.3 copy-start.22
  75.0 6.9 %copy-start.14 = (f32[3,64,16]{1,2,0:T(8,128)}, f32[3,64,16]{1,2,0:T(8,128)S(1)}, u32[]{:S(2)}) copy-start(f32[3,64,16]{1,2,0:T(8,128)S(1)} %reshape.315) | copy-start | bytes 36868
  75.0 2.9 copy-start.45
  75.0 2.9 copy-start.47
  76.2 1.7 copy-start.29
  76.2 3.8 copy-start.34
  82.6 134.0 %copy-start.7 = (f32[3,3,6,768]{3,2,1,0:T(8,128)S(1)}, f32[3,3,6,768]{3,2,1,0:T(8,128)}, u32[]{:S(2)}) copy-start(f32[3,3,6,768]{3,2,1,0:T(8,128)} %broadcast_add_fusion.mod_ref) | copy-start | bytes 497668
  317.2 56.1 %copy-start.31 = (f32[3,6,768]{2,1,0:T(8,128)S(1)}, f32[3,6,768]{2,1,0:T(8,128)}, u32[]{:S(2)}) copy-start(f32[3,6,768]{2,1,0:T(8,128)} %get-tuple-element.114) | copy-start | bytes 165892
  317.2 56.1 %copy-start.32 = (f32[3,6,768]{2,1,0:T(8,128)S(1)}, f32[3,6,768]{2,1,0:T(8,128)}, u32[]{:S(2)}) copy-start(f32[3,6,768]{2,1,0:T(8,128)} %get-tuple-element.113) | copy-start | bytes 165892
  317.3 57.1 %copy-start.43 = (f32[1,576]{1,0:T(1,128)S(1)}, f32[1,576]{1,0:T(1,128)}, u32[]{:S(2)}) copy-start(f32[1,576]{1,0:T(1,128)} %get-tuple-element.120) | copy-start | bytes 6916
  317.3 57.1 %copy-start.44 = (f32[1,576]{1,0:T(1,128)S(1)}, f32[1,576]{1,0:T(1,128)}, u32[]{:S(2)}) copy-start(f32[1,576]{1,0:T(1,128)} %get-tuple-element.119) | copy-start | bytes 6916
  317.3 58.0 %copy-start.41 = (f32[1,768]{1,0:T(1,128)S(1)}, f32[1,768]{1,0:T(1,128)}, u32[]{:S(2)}) copy-start(f32[1,768]{1,0:T(1,128)} %get-tuple-element.123) | copy-start | bytes 9220
  317.3 58.0 %copy-start.42 = (f32[1,768]{1,0:T(1,128)S(1)}, f32[1,768]{1,0:T(1,128)}, u32[]{:S(2)}) copy-start(f32[1,768]{1,0:T(1,128)} %get-tuple-element.122) | copy-start | bytes 9220
  317.3 58.8 %copy-start.39 = (f32[2,768]{1,0:T(2,128)S(1)}, f32[2,768]{1,0:T(2,128)}, u32[]{:S(2)}) copy-start(f32[2,768]{1,0:T(2,128)} %get-tuple-element.117) | copy-start | bytes 18436
  317.3 58.8 %copy-start.40 = (f32[2,768]{1,0:T(2,128)S(1)}, f32[2,768]{1,0:T(2,128)}, u32[]{:S(2)}) copy-start(f32[2,768]{1,0:T(2,128)} %get-tuple-element.116) | copy-start | bytes 18436
  373.3 3.6 copy-start.6
  373.3 3.6 copy-start.15
  373.3 3.6 copy-start.30
  373.3 3.6 copy-start.46
  373.3 3.6 copy-start.48
  373.3 4.1 copy-start.38
  373.4 4.1 copy-start.37
  373.4 4.1 copy-start.33
  379.7 74.0 %copy-start.2 = (f32[3,96,1152]{2,1,0:T(8,128)S(1)}, f32[3,96,1152]{2,1,0:T(8,128)}, u32[]{:S(2)}) copy-start(f32[3,96,1152]{2,1,0:T(8,128)} %param.25) | copy-start | bytes 3981316
  379.7 74.0 %copy-start.11 = (f32[3,96,1152]{2,1,0:T(8,128)S(1)}, f32[3,96,1152]{2,1,0:T(8,128)}, u32[]{:S(2)}) copy-start(f32[3,96,1152]{2,1,0:T(8,128)} %param.33) | copy-start | bytes 3981316
  453.7 4.9 %copy-start.4 = (f32[3,1,120,768]{3,2,1,0:T(8,128)S(1)}, f32[3,1,120,768]{3,2,1,0:T(8,128)}, u32[]{:S(2)}) copy-start(f32[3,1,120,768]{3,2,1,0:T(8,128)} %param.24) | copy-start | bytes 3317764
  453.7 4.8 %copy-start.12 = (f32[3,1,120,768]{3,2,1,0:T(8,128)S(1)}, f32[3,1,120,768]{3,2,1,0:T(8,128)}, u32[]{:S(2)}) copy-start(f32[3,1,120,768]{3,2,1,0:T(8,128)} %param.31) | copy-start | bytes 3317764
  453.7 4.8 %copy-start.13 = (f32[3,1,120,768]{3,2,1,0:T(8,128)S(1)}, f32[3,1,120,768]{3,2,1,0:T(8,128)}, u32[]{:S(2)}) copy-start(f32[3,1,120,768]{3,2,1,0:T(8,128)} %param.30) | copy-start | bytes 3317764
  453.7 4.8 %copy-start.16 = (f32[120,768]{1,0:T(8,128)S(1)}, f32[120,768]{1,0:T(8,128)}, u32[]{:S(2)}) copy-start(f32[120,768]{1,0:T(8,128)} %get-tuple-element.147) | copy-start | bytes 1105924
  453.8 4.8 %copy-start.17 = (f32[120,768]{1,0:T(8,128)S(1)}, f32[120,768]{1,0:T(8,128)}, u32[]{:S(2)}) copy-start(f32[120,768]{1,0:T(8,128)} %get-tuple-element.146) | copy-start | bytes 1105924
  453.8 4.8 %copy-start.18 = (f32[120,768]{1,0:T(8,128)S(1)}, f32[120,768]{1,0:T(8,128)}, u32[]{:S(2)}) copy-start(f32[120,768]{1,0:T(8,128)} %get-tuple-element.145) | copy-start | bytes 1105924
  458.6 2.7 copy-start.25
  458.6 2.6 copy-start.28
  458.6 2.8 copy-start.24
  458.6 2.8 copy-start.27
  458.6 3.0 copy-start.23
  458.7 3.0 copy-start.26
  458.7 3.1 copy-start.9
  461.3 1.5 copy-start.8
  461.4 1.8 copy-start
  471.0 2.8 copy-start.10
  471.0 2.8 copy-start.19
  471.1 2.8 copy-start.20
  471.1 2.8 copy-start.21

commit v9 on v8

--- a/solution.py
+++ b/solution.py
@@ -1082,23 +1082,30 @@
         if layer_idx == 0:
             gather.start()
             each(images, first_norm)
+        if layer_idx > 0:
+            run_ticks(gather, 1, min(2, last_step))
         each(images, spread_a.forward)
         if layer_idx == 0:
             loads.wait(0, 1)
             join_blocks(0)
         each(images, attend)
         keep.start(0, 1, 2, 3)
-        run_ticks(gather, 1, min(2, last_step))
+        at = 1 if layer_idx == 0 else 2
+        run_ticks(gather, at, min(at + 1, last_step))
         each(images, collect_a.forward)
         each(images, middle)
         keep.start(4, 5)
         each(images, spread_m.forward)
-        run_ticks(gather, 2, min(3, last_step))
+        at = 2 if layer_idx == 0 else 3
+        run_ticks(gather, at, min(at + 1, last_step))
         if layer_idx == 0:
             loads.wait(2)
         each(images, feed)
         keep.start(6, 7)
-        run_ticks(gather, 3, min(4, last_step))
+        if layer_idx == 0:
+            run_ticks(gather, 3, min(4, last_step))
+        if gather is not None and gathers[layer_idx + 2] is not None:
+            gathers[layer_idx + 2].start()
         each(images, collect_m.forward)
         each(images, finish)
         keep.start(8)
@@ -1106,8 +1113,6 @@
         each(images, close)
         if gather is not None:
             each(max(last_step - 4, 0), lambda step, gather=gather: gather.tick(step + 4))
-            if gathers[layer_idx + 2] is not None:
-                gathers[layer_idx + 2].start()
             gather.finish()
             join_blocks(layer_idx + 1)
         keep.wait(*range(9))
@@ -1397,14 +1402,16 @@
     moves.wait(6)
     feed_weights()
     moves.start(13)
+    moves.wait(5, 4)
+    each(images - 1, middle)
     run_ticks(reduce, 1, min(2, last_step - 1))
-    moves.wait(5, 4)
-    each(images, middle)
+    middle(images - 1)
     each(images, spread_a.forward)
     moves.wait(2, 9)
-    each(images, attend)
+    each(images - 1, attend)
+    run_ticks(reduce, 2, min(3, last_step - 1))
+    attend(images - 1)
     each(images, collect_a.forward)
-    run_ticks(reduce, 2, min(3, last_step - 1))
     moves.wait(3, 1)
     attend_weights()
     moves.start(12, 14)

time: 483 us -> 463 us (0.959)
  Pallas kernels: 421 us -> 401 us
    pallas_call x3, Pallas kernels: 156 us -> 139 us  [backward_layer(): pl.pallas_call(functools.partial(backward_kernel, layer_idx if stacked el...]
where the time goes in v9:
time: 463 us; the launch traced here: 457 us
  Pallas kernels  401 us (87%)
  local copies, waits for them, and re-layouts  29.1 us (6%)
  other arithmetic  20 us (4%)
  between operations  4.65 us (1%)
    pallas_call x3, Pallas kernels, backward_layer(): pl.pallas_call(functools.partial(backward_kernel, layer_idx if stacked el...  139 us
    pallas_call x1, Pallas kernels, forward_all(): pl.pallas_call(functools.partial(forward_all_kernel, count_all), out_shap...  130 us
    pallas_call x1, Pallas kernels, tail_call(): pl.pallas_call(functools.partial(tail_kernel, images, at), out_shape=[jax...  72 us
    pallas_call x1, Pallas kernels, head_call(): pl.pallas_call(functools.partial(head_kernel, images), out_shape=[jax.Sha...  59.8 us
    unnamed x110, local copies, waits for them, and re-layouts  11.7 us
    convert_element_type x3, other arithmetic, adam_update(): return (master, first_new, second_new, master.astype(jnp.bfloat16), change)  9.5 us

profile of v9, /device:TPU:0, one launch (start us, length us, event | category | flops | bytes accessed | tf_op | source)
XLA Modules:
  0.0 456.6 jit_solution(3985609681198908991)
XLA Ops:
  0.7 1.0 reduce-precision_bitcast_fusion.table_ref
  1.9 0.7 maximum_maximum_fusion.small_ref
  2.6 0.8 fusion.24
  3.4 0.7 slice.131.time_ref
  4.1 0.7 slice.135.bias_ref
  4.7 1.5 copy.99
  6.3 1.0 slice.137.rest_1_
  7.3 0.8 slice.136.rest_0_
  8.0 0.1 multiply_cosine_fusion.2
  8.2 0.6 select_maximum_fusion.feats_ref
  8.9 0.9 convert_element_type.58.mod_ref.weight_ref
  9.8 0.9 fusion.5.rest_2_
  10.6 59.8 %head.1 = (f32[4,8,24,128]{3,2,1,0:T(8,128)}, f32[24,384]{1,0:T(8,128)}, f32[24,24]{1,0:T(8,128)}, f32[768,24]{1,0:T(8,128)}, f32[24,24]{1,0:T(8,128)}, /*index=...) custom-call(f32[24,128]{1,0:T(8,128)} %maximum_maximum_fusion.small_, ...), custom_call_target="tpu_custom_call" | custom-call | tf_op jit(solution)/shard_map/head/pallas_call | solution.py:1743
  70.5 1.0 copy.59
  71.5 0.2 copy.60
  71.7 0.6 fusion.25
  72.5 0.6 broadcast_in_dim.19.qkv_bias_ref
  73.2 0.5 multiply_sine_fusion.1
  73.7 0.1 pad_maximum_fusion.1
  73.8 0.6 reshape.314
  74.5 0.4 copy.56
  74.8 0.1 reshape.315
  75.1 0.6 reshape.312
  75.7 0.4 copy.55
  76.1 0.1 reshape.313
  76.2 1.6 fusion.2.res_ref
  77.9 0.1 reshape_reshape.3
  78.0 0.7 broadcast_add_fusion.mod_ref
  78.7 0.6 broadcast_in_dim.20.up_bias_ref
  79.3 0.6 slice.148.head_ref
  80.0 0.1 reshape.320
  80.1 0.3 slice_reduce_fusion
  80.4 0.7 broadcast_in_dim_squeeze.7.final_shift_ref
  81.1 0.7 broadcast_in_dim_squeeze.8.final_scale_ref
  81.8 0.7 copy.64.targets_ref
  82.6 129.7 %blocks_forward.1 = (f32[3,64,768]{2,1,0:T(8,128)}, f32[16,768]{1,0:T(8,128)}, f32[1,1]{1,0:T(1,128)}, f32[3,1,768]{2,1,0:T(1,128)}, f32[3,1,768]{2,1,0:T(1,128)...) custom-call(f32[3,64,768]{2,1,0:T(8,128)} %fusion.2.res_ref, ...), custom_call_target="tpu_custom_call" | custom-call | tf_op jit(solution)/shard_map/blocks_forward/pallas_call | solution.py:1158
  212.3 0.7 slice_bitcast_fusion
  213.0 43.6 %block_backward.3 = (f32[3,64,768]{2,1,0:T(8,128)}, bf16[768,576]{1,0:T(8,128)(2,1)}, bf16[768,768]{1,0:T(8,128)(2,1)}, bf16[960,768]{1,0:T(8,128)(2,1)}, f32[3,...) custom-call(f32[3,64,768]{2,1,0:T(8,128)} %get-tuple-element.89.d_res_ref, ...), custom_call_target="tpu_custom_call" | custom-call | flops 60000002048 | bytes 26214400 | tf_op jit(solution)/shard_map/block_backward/pallas_call | solution.py:1469
  256.6 48.1 %block_backward.4 = (f32[3,64,768]{2,1,0:T(8,128)}, bf16[768,576]{1,0:T(8,128)(2,1)}, bf16[768,768]{1,0:T(8,128)(2,1)}, bf16[960,768]{1,0:T(8,128)(2,1)}, f32[3,...) custom-call(f32[3,64,768]{2,1,0:T(8,128)} %get-tuple-element.102.d_r, ...), custom_call_target="tpu_custom_call" | custom-call | flops 60000002048 | bytes 26214400 | tf_op jit(solution)/shard_map/block_backward/pallas_call | solution.py:1469
  304.8 47.7 %block_backward.5 = (f32[3,64,768]{2,1,0:T(8,128)}, bf16[768,576]{1,0:T(8,128)(2,1)}, bf16[768,768]{1,0:T(8,128)(2,1)}, bf16[960,768]{1,0:T(8,128)(2,1)}, f32[3,...) custom-call(f32[3,64,768]{2,1,0:T(8,128)} %get-tuple-element.106.d_r, ...), custom_call_target="tpu_custom_call" | custom-call | flops 60000002048 | bytes 26214400 | tf_op jit(solution)/shard_map/block_backward/pallas_call | solution.py:1469
  352.6 1.0 pad_maximum_fusion
  353.6 0.7 fusion.12
  354.3 0.2 dynamic_update_slice.6
  354.5 0.7 fusion.11
  355.3 0.7 pad_maximum_fusion.2
  356.1 0.5 convolution_bitcast_fusion
  356.7 0.4 concatenate.54
  357.1 0.9 copy.65
  358.0 0.1 reshape.330
  358.1 0.7 pad.14.mod_ref
  358.9 72.0 %tail.1 = (f32[24,3640]{1,0:T(8,128)}, f32[3,96,1152]{2,1,0:T(8,128)}, f32[8,128]{1,0:T(8,128)}, f32[96,576]{1,0:T(8,128)}, f32[96,768]{1,0:T(8,128)}, /*index=5*/f32[120,768]{1,0:T(8,128)}) custom-call(f32[8,4,24,128]{3,2,1,0:T(8,128)} %bitcast.124, f32[4,16,1152]{2,1,0:T(8,128)} %pad.14.mod_ref, ...), custom_call_target="tpu_custom_call" | custom-call | tf_op jit(solution)/shard_map/tail/pallas_call | solution.py:1986
  430.9 1.3 fusion.26
  433.7 4.8 %fusion.17 = (bf16[3,96,1152]{2,1,0:T(8,128)(2,1)}, f32[3,96,1152]{2,1,0:T(8,128)}, f32[3,96,1152]{2,1,0:T(8,128)}, f32[3,96,1152]{2,1,0:T(8,128)}) fusion(f32[3,96,1152]{2,1,0:T(8,128)S(1)} %copy-done.2, f32[]{:T(128)S(6)} %sub.15, f32[3,96,1152]{2,1,0:T(8,128)} %get-tuple-element.148, f32[]{:T(128)S(6)} %min.3, f32[3,96,1152]{2,1,0:T(8,128)S(1)} %copy-done.11, ...), kind=kLoop, calls=%fused_computation.88 | loop fusion | flops 5308416 | bytes 9953288 | tf_op jit(solution)/shard_map/convert_element_type | solution.py:2011
  438.6 2.6 fusion.19
  441.2 0.2 maximum_bitcast_fusion
  441.4 0.2 maximum_bitcast_fusion.1
  441.6 0.2 maximum_bitcast_fusion.2
  441.7 1.0 copy-done.8
  442.7 0.5 copy-done
  443.2 2.1 fusion.21
  445.3 2.8 copy.71
  448.2 2.8 copy.72
  451.0 2.8 copy.73
  453.8 1.2 fusion.10
  (137 shorter events, 1.2 us)
Async XLA Ops:
  1.7 4.6 %copy-start.5 = (f32[24,3640]{1,0:T(8,128)}, f32[24,3640]{1,0:T(8,128)S(1)}, u32[]{:S(2)}) copy-start(f32[24,3640]{1,0:T(8,128)S(1)} %reduce-precision_bitcast_fusion.table_ref) | copy-start | bytes 1048324
  6.3 1.8 copy-start.50
  6.3 1.9 copy-start.49
  6.3 2.6 copy-start.1
  7.3 2.5 copy-start.3
  71.5 2.3 copy-start.35
  71.7 3.4 copy-start.36
  74.4 3.3 copy-start.22
  75.0 6.9 %copy-start.14 = (f32[3,64,16]{1,2,0:T(8,128)}, f32[3,64,16]{1,2,0:T(8,128)S(1)}, u32[]{:S(2)}) copy-start(f32[3,64,16]{1,2,0:T(8,128)S(1)} %reshape.315) | copy-start | bytes 36868
  75.0 2.9 copy-start.45
  75.0 2.9 copy-start.47
  76.2 1.7 copy-start.29
  76.2 3.8 copy-start.34
  82.6 129.7 %copy-start.7 = (f32[3,3,6,768]{3,2,1,0:T(8,128)S(1)}, f32[3,3,6,768]{3,2,1,0:T(8,128)}, u32[]{:S(2)}) copy-start(f32[3,3,6,768]{3,2,1,0:T(8,128)} %broadcast_add_fusion.mod_ref) | copy-start | bytes 497668
  304.7 47.9 %copy-start.31 = (f32[3,6,768]{2,1,0:T(8,128)S(1)}, f32[3,6,768]{2,1,0:T(8,128)}, u32[]{:S(2)}) copy-start(f32[3,6,768]{2,1,0:T(8,128)} %get-tuple-element.114) | copy-start | bytes 165892
  304.7 47.9 %copy-start.32 = (f32[3,6,768]{2,1,0:T(8,128)S(1)}, f32[3,6,768]{2,1,0:T(8,128)}, u32[]{:S(2)}) copy-start(f32[3,6,768]{2,1,0:T(8,128)} %get-tuple-element.113) | copy-start | bytes 165892
  304.7 48.9 %copy-start.43 = (f32[1,576]{1,0:T(1,128)S(1)}, f32[1,576]{1,0:T(1,128)}, u32[]{:S(2)}) copy-start(f32[1,576]{1,0:T(1,128)} %get-tuple-element.120) | copy-start | bytes 6916
  304.7 48.9 %copy-start.44 = (f32[1,576]{1,0:T(1,128)S(1)}, f32[1,576]{1,0:T(1,128)}, u32[]{:S(2)}) copy-start(f32[1,576]{1,0:T(1,128)} %get-tuple-element.119) | copy-start | bytes 6916
  304.7 49.8 %copy-start.41 = (f32[1,768]{1,0:T(1,128)S(1)}, f32[1,768]{1,0:T(1,128)}, u32[]{:S(2)}) copy-start(f32[1,768]{1,0:T(1,128)} %get-tuple-element.123) | copy-start | bytes 9220
  304.7 49.8 %copy-start.42 = (f32[1,768]{1,0:T(1,128)S(1)}, f32[1,768]{1,0:T(1,128)}, u32[]{:S(2)}) copy-start(f32[1,768]{1,0:T(1,128)} %get-tuple-element.122) | copy-start | bytes 9220
  304.7 50.5 %copy-start.39 = (f32[2,768]{1,0:T(2,128)S(1)}, f32[2,768]{1,0:T(2,128)}, u32[]{:S(2)}) copy-start(f32[2,768]{1,0:T(2,128)} %get-tuple-element.117) | copy-start | bytes 18436
  304.7 50.5 %copy-start.40 = (f32[2,768]{1,0:T(2,128)S(1)}, f32[2,768]{1,0:T(2,128)}, u32[]{:S(2)}) copy-start(f32[2,768]{1,0:T(2,128)} %get-tuple-element.116) | copy-start | bytes 18436
  352.5 3.6 copy-start.6
  352.5 3.6 copy-start.15
  352.5 3.6 copy-start.30
  352.5 3.6 copy-start.46
  352.5 3.6 copy-start.48
  352.5 4.1 copy-start.38
  352.6 4.1 copy-start.37
  352.6 4.1 copy-start.33
  358.8 74.8 %copy-start.2 = (f32[3,96,1152]{2,1,0:T(8,128)S(1)}, f32[3,96,1152]{2,1,0:T(8,128)}, u32[]{:S(2)}) copy-start(f32[3,96,1152]{2,1,0:T(8,128)} %param.25) | copy-start | bytes 3981316
  358.8 74.8 %copy-start.11 = (f32[3,96,1152]{2,1,0:T(8,128)S(1)}, f32[3,96,1152]{2,1,0:T(8,128)}, u32[]{:S(2)}) copy-start(f32[3,96,1152]{2,1,0:T(8,128)} %param.33) | copy-start | bytes 3981316
  433.6 4.9 %copy-start.4 = (f32[3,1,120,768]{3,2,1,0:T(8,128)S(1)}, f32[3,1,120,768]{3,2,1,0:T(8,128)}, u32[]{:S(2)}) copy-start(f32[3,1,120,768]{3,2,1,0:T(8,128)} %param.24) | copy-start | bytes 3317764
  433.7 4.8 %copy-start.12 = (f32[3,1,120,768]{3,2,1,0:T(8,128)S(1)}, f32[3,1,120,768]{3,2,1,0:T(8,128)}, u32[]{:S(2)}) copy-start(f32[3,1,120,768]{3,2,1,0:T(8,128)} %param.31) | copy-start | bytes 3317764
  433.7 4.8 %copy-start.13 = (f32[3,1,120,768]{3,2,1,0:T(8,128)S(1)}, f32[3,1,120,768]{3,2,1,0:T(8,128)}, u32[]{:S(2)}) copy-start(f32[3,1,120,768]{3,2,1,0:T(8,128)} %param.30) | copy-start | bytes 3317764
  433.7 4.8 %copy-start.16 = (f32[120,768]{1,0:T(8,128)S(1)}, f32[120,768]{1,0:T(8,128)}, u32[]{:S(2)}) copy-start(f32[120,768]{1,0:T(8,128)} %get-tuple-element.147) | copy-start | bytes 1105924
  433.7 4.8 %copy-start.17 = (f32[120,768]{1,0:T(8,128)S(1)}, f32[120,768]{1,0:T(8,128)}, u32[]{:S(2)}) copy-start(f32[120,768]{1,0:T(8,128)} %get-tuple-element.146) | copy-start | bytes 1105924
  433.7 4.8 %copy-start.18 = (f32[120,768]{1,0:T(8,128)S(1)}, f32[120,768]{1,0:T(8,128)}, u32[]{:S(2)}) copy-start(f32[120,768]{1,0:T(8,128)} %get-tuple-element.145) | copy-start | bytes 1105924
  438.5 2.7 copy-start.25
  438.5 2.6 copy-start.28
  438.6 2.8 copy-start.24
  438.6 2.8 copy-start.27
  438.6 3.0 copy-start.23
  438.6 3.0 copy-start.26
  438.6 3.1 copy-start.9
  441.2 1.5 copy-start.8
  441.4 1.8 copy-start
  451.0 2.8 copy-start.10
  451.0 2.8 copy-start.19
  451.0 2.8 copy-start.20
  451.0 2.8 copy-start.21

commit v10 on v9

--- a/solution.py
+++ b/solution.py
@@ -1088,16 +1088,18 @@
         if layer_idx == 0:
             loads.wait(0, 1)
             join_blocks(0)
-        each(images, attend)
-        keep.start(0, 1, 2, 3)
+        each(images - 1, attend)
         at = 1 if layer_idx == 0 else 2
         run_ticks(gather, at, min(at + 1, last_step))
+        attend(images - 1)
+        keep.start(0, 1, 2, 3)
         each(images, collect_a.forward)
-        each(images, middle)
+        each(images - 1, middle)
+        at = 2 if layer_idx == 0 else 3
+        run_ticks(gather, at, min(at + 1, last_step))
+        middle(images - 1)
         keep.start(4, 5)
         each(images, spread_m.forward)
-        at = 2 if layer_idx == 0 else 3
-        run_ticks(gather, at, min(at + 1, last_step))
         if layer_idx == 0:
             loads.wait(2)
         each(images, feed)

time: 463 us -> 459 us (level)
  no operation moved by 1% of the time
where the time goes in v10:
time: 459 us; the launch traced here: 453 us
  Pallas kernels  398 us (87%)
  local copies, waits for them, and re-layouts  29.1 us (6%)
  other arithmetic  20 us (4%)
  between operations  4.65 us (1%)
    pallas_call x3, Pallas kernels, backward_layer(): pl.pallas_call(functools.partial(backward_kernel, layer_idx if stacked el...  139 us
    pallas_call x1, Pallas kernels, forward_all(): pl.pallas_call(functools.partial(forward_all_kernel, count_all), out_shap...  126 us
    pallas_call x1, Pallas kernels, tail_call(): pl.pallas_call(functools.partial(tail_kernel, images, at), out_shape=[jax...  72 us
    pallas_call x1, Pallas kernels, head_call(): pl.pallas_call(functools.partial(head_kernel, images), out_shape=[jax.Sha...  59.8 us
    unnamed x110, local copies, waits for them, and re-layouts  11.7 us
    convert_element_type x3, other arithmetic, adam_update(): return (master, first_new, second_new, master.astype(jnp.bfloat16), change)  9.5 us

profile of v10, /device:TPU:0, one launch (start us, length us, event | category | flops | bytes accessed | tf_op | source)
XLA Modules:
  0.0 453.2 jit_solution(5820958659442221540)
XLA Ops:
  0.7 1.0 reduce-precision_bitcast_fusion.table_ref
  1.9 0.7 maximum_maximum_fusion.small_ref
  2.6 0.8 fusion.24
  3.4 0.7 slice.131.time_ref
  4.1 0.7 slice.135.bias_ref
  4.7 1.5 copy.99
  6.3 1.0 slice.137.rest_1_
  7.3 0.8 slice.136.rest_0_
  8.0 0.1 multiply_cosine_fusion.2
  8.2 0.6 select_maximum_fusion.feats_ref
  8.9 0.9 convert_element_type.58.mod_ref.weight_ref
  9.8 0.9 fusion.5.rest_2_
  10.6 59.8 %head.1 = (f32[4,8,24,128]{3,2,1,0:T(8,128)}, f32[24,384]{1,0:T(8,128)}, f32[24,24]{1,0:T(8,128)}, f32[768,24]{1,0:T(8,128)}, f32[24,24]{1,0:T(8,128)}, /*index=...) custom-call(f32[24,128]{1,0:T(8,128)} %maximum_maximum_fusion.small_, ...), custom_call_target="tpu_custom_call" | custom-call | tf_op jit(solution)/shard_map/head/pallas_call | solution.py:1745
  70.5 1.0 copy.59
  71.5 0.2 copy.60
  71.7 0.6 fusion.25
  72.5 0.6 broadcast_in_dim.19.qkv_bias_ref
  73.2 0.5 multiply_sine_fusion.1
  73.7 0.1 pad_maximum_fusion.1
  73.8 0.6 reshape.314
  74.5 0.4 copy.56
  74.8 0.1 reshape.315
  75.1 0.6 reshape.312
  75.7 0.4 copy.55
  76.1 0.1 reshape.313
  76.2 1.6 fusion.2.res_ref
  77.9 0.1 reshape_reshape.3
  78.0 0.7 broadcast_add_fusion.mod_ref
  78.7 0.6 broadcast_in_dim.20.up_bias_ref
  79.3 0.6 slice.148.head_ref
  80.0 0.1 reshape.320
  80.1 0.3 slice_reduce_fusion
  80.4 0.7 broadcast_in_dim_squeeze.7.final_shift_ref
  81.1 0.7 broadcast_in_dim_squeeze.8.final_scale_ref
  81.8 0.7 copy.64.targets_ref
  82.6 126.3 %blocks_forward.1 = (f32[3,64,768]{2,1,0:T(8,128)}, f32[16,768]{1,0:T(8,128)}, f32[1,1]{1,0:T(1,128)}, f32[3,1,768]{2,1,0:T(1,128)}, f32[3,1,768]{2,1,0:T(1,128)...) custom-call(f32[3,64,768]{2,1,0:T(8,128)} %fusion.2.res_ref, ...), custom_call_target="tpu_custom_call" | custom-call | tf_op jit(solution)/shard_map/blocks_forward/pallas_call | solution.py:1160
  208.9 0.7 slice_bitcast_fusion
  209.6 43.3 %block_backward.3 = (f32[3,64,768]{2,1,0:T(8,128)}, bf16[768,576]{1,0:T(8,128)(2,1)}, bf16[768,768]{1,0:T(8,128)(2,1)}, bf16[960,768]{1,0:T(8,128)(2,1)}, f32[3,...) custom-call(f32[3,64,768]{2,1,0:T(8,128)} %get-tuple-element.89.d_res_ref, ...), custom_call_target="tpu_custom_call" | custom-call | flops 60000002048 | bytes 26214400 | tf_op jit(solution)/shard_map/block_backward/pallas_call | solution.py:1471
  252.9 48.2 %block_backward.4 = (f32[3,64,768]{2,1,0:T(8,128)}, bf16[768,576]{1,0:T(8,128)(2,1)}, bf16[768,768]{1,0:T(8,128)(2,1)}, bf16[960,768]{1,0:T(8,128)(2,1)}, f32[3,...) custom-call(f32[3,64,768]{2,1,0:T(8,128)} %get-tuple-element.102.d_r, ...), custom_call_target="tpu_custom_call" | custom-call | flops 60000002048 | bytes 26214400 | tf_op jit(solution)/shard_map/block_backward/pallas_call | solution.py:1471
  301.2 48.0 %block_backward.5 = (f32[3,64,768]{2,1,0:T(8,128)}, bf16[768,576]{1,0:T(8,128)(2,1)}, bf16[768,768]{1,0:T(8,128)(2,1)}, bf16[960,768]{1,0:T(8,128)(2,1)}, f32[3,...) custom-call(f32[3,64,768]{2,1,0:T(8,128)} %get-tuple-element.106.d_r, ...), custom_call_target="tpu_custom_call" | custom-call | flops 60000002048 | bytes 26214400 | tf_op jit(solution)/shard_map/block_backward/pallas_call | solution.py:1471
  349.2 1.0 pad_maximum_fusion
  350.3 0.7 fusion.12
  350.9 0.2 dynamic_update_slice.6
  351.2 0.7 fusion.11
  351.9 0.7 pad_maximum_fusion.2
  352.8 0.5 convolution_bitcast_fusion
  353.4 0.4 concatenate.54
  353.7 0.9 copy.65
  354.7 0.1 reshape.330
  354.8 0.7 pad.14.mod_ref
  355.5 72.0 %tail.1 = (f32[24,3640]{1,0:T(8,128)}, f32[3,96,1152]{2,1,0:T(8,128)}, f32[8,128]{1,0:T(8,128)}, f32[96,576]{1,0:T(8,128)}, f32[96,768]{1,0:T(8,128)}, /*index=5*/f32[120,768]{1,0:T(8,128)}) custom-call(f32[8,4,24,128]{3,2,1,0:T(8,128)} %bitcast.124, f32[4,16,1152]{2,1,0:T(8,128)} %pad.14.mod_ref, ...), custom_call_target="tpu_custom_call" | custom-call | tf_op jit(solution)/shard_map/tail/pallas_call | solution.py:1988
  427.5 1.3 fusion.26
  430.3 4.8 %fusion.17 = (bf16[3,96,1152]{2,1,0:T(8,128)(2,1)}, f32[3,96,1152]{2,1,0:T(8,128)}, f32[3,96,1152]{2,1,0:T(8,128)}, f32[3,96,1152]{2,1,0:T(8,128)}) fusion(f32[3,96,1152]{2,1,0:T(8,128)S(1)} %copy-done.2, f32[]{:T(128)S(6)} %sub.15, f32[3,96,1152]{2,1,0:T(8,128)} %get-tuple-element.148, f32[]{:T(128)S(6)} %min.3, f32[3,96,1152]{2,1,0:T(8,128)S(1)} %copy-done.11, ...), kind=kLoop, calls=%fused_computation.88 | loop fusion | flops 5308416 | bytes 9953288 | tf_op jit(solution)/shard_map/convert_element_type | solution.py:2013
  435.2 2.6 fusion.19
  437.8 0.2 maximum_bitcast_fusion
  438.0 0.2 maximum_bitcast_fusion.1
  438.2 0.2 maximum_bitcast_fusion.2
  438.4 1.0 copy-done.8
  439.3 0.5 copy-done
  439.8 2.1 fusion.21
  441.9 2.8 copy.71
  444.8 2.8 copy.72
  447.6 2.8 copy.73
  450.4 1.2 fusion.10
  (137 shorter events, 1.2 us)
Async XLA Ops:
  1.7 4.6 %copy-start.5 = (f32[24,3640]{1,0:T(8,128)}, f32[24,3640]{1,0:T(8,128)S(1)}, u32[]{:S(2)}) copy-start(f32[24,3640]{1,0:T(8,128)S(1)} %reduce-precision_bitcast_fusion.table_ref) | copy-start | bytes 1048324
  6.3 1.8 copy-start.50
  6.3 1.9 copy-start.49
  6.3 2.6 copy-start.1
  7.3 2.5 copy-start.3
  71.5 2.3 copy-start.35
  71.7 3.4 copy-start.36
  74.4 3.3 copy-start.22
  75.0 6.9 %copy-start.14 = (f32[3,64,16]{1,2,0:T(8,128)}, f32[3,64,16]{1,2,0:T(8,128)S(1)}, u32[]{:S(2)}) copy-start(f32[3,64,16]{1,2,0:T(8,128)S(1)} %reshape.315) | copy-start | bytes 36868
  75.0 2.9 copy-start.45
  75.0 2.9 copy-start.47
  76.2 1.7 copy-start.29
  76.2 3.8 copy-start.34
  82.6 126.4 %copy-start.7 = (f32[3,3,6,768]{3,2,1,0:T(8,128)S(1)}, f32[3,3,6,768]{3,2,1,0:T(8,128)}, u32[]{:S(2)}) copy-start(f32[3,3,6,768]{3,2,1,0:T(8,128)} %broadcast_add_fusion.mod_ref) | copy-start | bytes 497668
  301.1 48.1 %copy-start.31 = (f32[3,6,768]{2,1,0:T(8,128)S(1)}, f32[3,6,768]{2,1,0:T(8,128)}, u32[]{:S(2)}) copy-start(f32[3,6,768]{2,1,0:T(8,128)} %get-tuple-element.114) | copy-start | bytes 165892
  301.1 48.1 %copy-start.32 = (f32[3,6,768]{2,1,0:T(8,128)S(1)}, f32[3,6,768]{2,1,0:T(8,128)}, u32[]{:S(2)}) copy-start(f32[3,6,768]{2,1,0:T(8,128)} %get-tuple-element.113) | copy-start | bytes 165892
  301.1 49.1 %copy-start.43 = (f32[1,576]{1,0:T(1,128)S(1)}, f32[1,576]{1,0:T(1,128)}, u32[]{:S(2)}) copy-start(f32[1,576]{1,0:T(1,128)} %get-tuple-element.120) | copy-start | bytes 6916
  301.1 49.1 %copy-start.44 = (f32[1,576]{1,0:T(1,128)S(1)}, f32[1,576]{1,0:T(1,128)}, u32[]{:S(2)}) copy-start(f32[1,576]{1,0:T(1,128)} %get-tuple-element.119) | copy-start | bytes 6916
  301.1 50.0 %copy-start.41 = (f32[1,768]{1,0:T(1,128)S(1)}, f32[1,768]{1,0:T(1,128)}, u32[]{:S(2)}) copy-start(f32[1,768]{1,0:T(1,128)} %get-tuple-element.123) | copy-start | bytes 9220
  301.1 50.0 %copy-start.42 = (f32[1,768]{1,0:T(1,128)S(1)}, f32[1,768]{1,0:T(1,128)}, u32[]{:S(2)}) copy-start(f32[1,768]{1,0:T(1,128)} %get-tuple-element.122) | copy-start | bytes 9220
  301.2 50.8 %copy-start.39 = (f32[2,768]{1,0:T(2,128)S(1)}, f32[2,768]{1,0:T(2,128)}, u32[]{:S(2)}) copy-start(f32[2,768]{1,0:T(2,128)} %get-tuple-element.117) | copy-start | bytes 18436
  301.2 50.8 %copy-start.40 = (f32[2,768]{1,0:T(2,128)S(1)}, f32[2,768]{1,0:T(2,128)}, u32[]{:S(2)}) copy-start(f32[2,768]{1,0:T(2,128)} %get-tuple-element.116) | copy-start | bytes 18436
  349.1 3.6 copy-start.6
  349.2 3.6 copy-start.15
  349.2 3.6 copy-start.30
  349.2 3.6 copy-start.46
  349.2 3.6 copy-start.48
  349.2 4.1 copy-start.38
  349.2 4.1 copy-start.37
  349.2 4.1 copy-start.33
  355.5 74.7 %copy-start.2 = (f32[3,96,1152]{2,1,0:T(8,128)S(1)}, f32[3,96,1152]{2,1,0:T(8,128)}, u32[]{:S(2)}) copy-start(f32[3,96,1152]{2,1,0:T(8,128)} %param.25) | copy-start | bytes 3981316
  355.5 74.7 %copy-start.11 = (f32[3,96,1152]{2,1,0:T(8,128)S(1)}, f32[3,96,1152]{2,1,0:T(8,128)}, u32[]{:S(2)}) copy-start(f32[3,96,1152]{2,1,0:T(8,128)} %param.33) | copy-start | bytes 3981316
  430.3 4.9 %copy-start.4 = (f32[3,1,120,768]{3,2,1,0:T(8,128)S(1)}, f32[3,1,120,768]{3,2,1,0:T(8,128)}, u32[]{:S(2)}) copy-start(f32[3,1,120,768]{3,2,1,0:T(8,128)} %param.24) | copy-start | bytes 3317764
  430.3 4.8 %copy-start.12 = (f32[3,1,120,768]{3,2,1,0:T(8,128)S(1)}, f32[3,1,120,768]{3,2,1,0:T(8,128)}, u32[]{:S(2)}) copy-start(f32[3,1,120,768]{3,2,1,0:T(8,128)} %param.31) | copy-start | bytes 3317764
  430.3 4.8 %copy-start.13 = (f32[3,1,120,768]{3,2,1,0:T(8,128)S(1)}, f32[3,1,120,768]{3,2,1,0:T(8,128)}, u32[]{:S(2)}) copy-start(f32[3,1,120,768]{3,2,1,0:T(8,128)} %param.30) | copy-start | bytes 3317764
  430.3 4.8 %copy-start.16 = (f32[120,768]{1,0:T(8,128)S(1)}, f32[120,768]{1,0:T(8,128)}, u32[]{:S(2)}) copy-start(f32[120,768]{1,0:T(8,128)} %get-tuple-element.147) | copy-start | bytes 1105924
  430.3 4.8 %copy-start.17 = (f32[120,768]{1,0:T(8,128)S(1)}, f32[120,768]{1,0:T(8,128)}, u32[]{:S(2)}) copy-start(f32[120,768]{1,0:T(8,128)} %get-tuple-element.146) | copy-start | bytes 1105924
  430.3 4.8 %copy-start.18 = (f32[120,768]{1,0:T(8,128)S(1)}, f32[120,768]{1,0:T(8,128)}, u32[]{:S(2)}) copy-start(f32[120,768]{1,0:T(8,128)} %get-tuple-element.145) | copy-start | bytes 1105924
  435.2 2.7 copy-start.25
  435.2 2.6 copy-start.28
  435.2 2.8 copy-start.24
  435.2 2.8 copy-start.27
  435.2 3.0 copy-start.23
  435.2 3.0 copy-start.26
  435.2 3.1 copy-start.9
  437.8 1.5 copy-start.8
  438.0 1.8 copy-start
  447.6 2.8 copy-start.10
  447.6 2.8 copy-start.19
  447.6 2.8 copy-start.20
  447.6 2.8 copy-start.21
